TPU v7x, 32 devices: a whole 2x2x4 slice. The times are simulated.
32 devices in a mesh: groups: 2 (over x), seq: 8 (over z, y), head: 2 (over core).
Axes of the slice: x: 2, y: 2, z: 4, core: 2. Of those that a mesh axis runs over, the one named last changes fastest.
Arguments:
- query_rows: bfloat16 [2048, 6144], P(('groups', 'seq'), 'head'), parts along dimension 0
- key_rows: bfloat16 [2048, 6144], P(('groups', 'seq'), 'head'), parts along dimension 0, may hold values from -6 to 6
- value_rows: bfloat16 [2048, 6144], P(('groups', 'seq'), 'head'), parts along dimension 0, may hold values from -6 to 6
- key_len: int32 [16], P('groups'), parts along dimension 0, may hold values from 2 to 128, as said below
- linear_scale: float32 [48], P('head'), may hold values from 0.5 to 2
Outputs:
- attended: bfloat16 [2048, 6144], P(('groups', 'seq'), 'head'), parts along dimension 0
There are 2 independent parts, one for each index of `groups`. A program takes and returns all parts, laid end to end along the dimension named above; an argument that names none is the same for every part. Nothing has to cross between parts.
Inputs may be any that keep to these rules, and one draw needn't show every extreme that they name: `key_len`: one block has exactly 128 valid keys in every draw.
All inputs are finite; a program needn't handle non-finite values.
Results may differ from a plain program's by a relative error of at most 0.00135.
Values may be sent and summed in bfloat16 or wider, within the bound.
No kernel may reach another device: no remote copies, remote signals or barrier semaphores. Data moves between devices by JAX's collectives and lax.ppermute only.
A program may use at most 256 MiB of HBM per device.

v0:
```python
import math

import jax
import jax.numpy as jnp
from jax import lax
from jax.sharding import PartitionSpec as P


def swapped(shard, axis, apart):
    return lax.ppermute(shard, axis, [(i, i ^ 1 << apart) for i in range(lax.axis_size(axis))])


def prefix_2(value, axis, join, neutral):
    count, mine = (lax.axis_size(axis), lax.axis_index(axis))
    pieces = lax.all_gather(value, axis)
    running = jnp.full_like(value, 0) + jnp.asarray(neutral, value.dtype)

    def turn(position, running):
        longer = join(running, pieces[position])
        return jnp.where(position < mine, longer, running)

    return lax.fori_loop(0, count - 1, turn, running)


def feature(inputs):
    return jnp.where(inputs > 0.0, inputs + 1.0, jnp.exp(jnp.minimum(inputs, 0.0)))


def partial_block(query_block, key_block, value_block, live_count, causal):
    scores = jnp.einsum(
        "rhd,chd->hrc", query_block, key_block, preferred_element_type=jnp.float32
    ) * (1.0 / math.sqrt(query_block.shape[2]))
    columns = lax.broadcasted_iota(jnp.int32, scores.shape, 2)
    allowed = columns < live_count
    if causal:
        allowed = allowed & (columns <= lax.broadcasted_iota(jnp.int32, scores.shape, 1))
    row_peak = jnp.max(jnp.where(allowed, scores, -jnp.inf), axis=2)
    weights = jnp.where(allowed, jnp.exp(scores - row_peak[:, :, None]), 0.0).astype(jnp.bfloat16)
    row_total = jnp.sum(weights.astype(jnp.float32), axis=2)
    numerator = jnp.einsum("hrc,chd->rhd", weights, value_block, preferred_element_type=jnp.float32)
    return (numerator, row_peak, row_total)


def combine(pieces):
    row_peak = pieces[0][1]
    for one_piece in pieces[1:]:
        row_peak = jnp.maximum(row_peak, one_piece[1])
    numerator = jnp.zeros_like(pieces[0][0])
    denominator = jnp.zeros_like(pieces[0][2])
    for one_piece in pieces:
        factor = jnp.exp(one_piece[1] - row_peak)
        numerator = numerator + jnp.transpose(factor)[:, :, None] * one_piece[0]
        denominator = denominator + factor * one_piece[2]
    return numerator / jnp.transpose(denominator)[:, :, None]


def add_terms(earlier, later):
    return earlier + later


def shards(query_rows, key_rows, value_rows, key_len, linear_scale):
    row_count = query_rows.shape[0]
    head_count = linear_scale.shape[0]
    head_width = query_rows.shape[1] // head_count
    queries = query_rows.reshape(row_count, head_count, head_width)
    key_heads = key_rows.reshape(row_count, head_count, head_width)
    value_heads = value_rows.reshape(row_count, head_count, head_width)
    my_index = lax.axis_index("seq")
    seq_count = lax.axis_size("seq")
    levels = seq_count.bit_length() - 1
    own_count = key_len[my_index]
    pieces = [partial_block(queries, key_heads, value_heads, own_count, True)]
    for bit_level in range(levels):
        far_keys, far_values = swapped((key_rows, value_rows), "seq", bit_level)
        partner = jnp.bitwise_xor(my_index, 1 << bit_level)
        pieces.append(
            partial_block(
                queries,
                far_keys.reshape(row_count, head_count, head_width),
                far_values.reshape(row_count, head_count, head_width),
                key_len[partner],
                False,
            )
        )
    live_rows = (lax.iota(jnp.int32, row_count) < own_count)[:, None, None]
    mapped = jnp.where(live_rows, feature(key_heads.astype(jnp.float32)), 0.0)
    local_sum = jnp.einsum(
        "rhd,rhe->hde", mapped, value_heads.astype(jnp.float32), precision=lax.Precision.HIGHEST
    )
    prefix = prefix_2(local_sum, "seq", add_terms, jnp.zeros_like(local_sum))
    tokens_all = row_count * seq_count
    linear = jnp.einsum(
        "rhd,hde->rhe",
        feature(queries.astype(jnp.float32)),
        prefix,
        precision=lax.Precision.HIGHEST,
    )
    linear = linear * (linear_scale[None, :, None] / (head_width * math.sqrt(tokens_all)))
    attended = (combine(pieces) + linear).astype(jnp.bfloat16)
    return attended.reshape(row_count, head_count * head_width)


def solution(mesh):
    return jax.shard_map(
        shards,
        mesh=mesh,
        in_specs=(
            P(("groups", "seq"), "head"),
            P(("groups", "seq"), "head"),
            P(("groups", "seq"), "head"),
            P("groups"),
            P("head"),
        ),
        out_specs=P(("groups", "seq"), "head"),
        check_vma=False,
    )
```

profile of v0, /device:TPU:0, one launch (start us, length us, event | category | flops | bytes accessed | tf_op | source)
XLA Modules:
  0.0 270.9 jit_solution(16982039009425216038)
XLA Ops:
  6.5 1.5 fusion.58
  8.0 0.6 iota_compare_fusion.4
  8.6 4.2 %fusion.2 = f32[24,128,128]{2,1,0:T(8,128)} fusion(pred[128]{0:T(512)(128)(4,1)S(1)} %iota_compare_fusion.4, bf16[128,3072]{1,0:T(8,128)(2,1)} %param.9, bf16[128,3072]{1,0:T(8,128)(2,1)} %param.8), kind=kOutput, calls=%fused_computation.9 | convolution fusion | flops 606339072 | bytes 3145856 | tf_op jit(solution)/shard_map/rhd,rhe->hde/dot_general | solution.py:87
  12.8 0.0 all-gather.3.cloned.1.call-update
  12.9 1.1 copy-done.5
  14.0 1.2 copy.52
  15.2 3.0 %collective-permute-start.1 = (bf16[128,3072]{0,1:T(8,128)(2,1)}, bf16[128,3072]{0,1:T(8,128)(2,1)}, u32[]{:S(2)}, u32[]{:S(2)}) collective-permute-start(bf16[128,3072]{0,1:T(8,128)(2,1)} %copy.52), channel_id=1, source_target_pairs={{0,4},{2,6},{4,0},{6,2},{8,12},{10,14},{12,8},{14,10},{1,5},{3,7},... | collective-permute-start | bytes 2359304 | tf_op jit(solution)/shard_map/ppermute | solution.py:10
  18.2 1.5 collective-permute-start
  19.7 0.5 collective-permute-start.3
  20.2 2.6 collective-permute-start.5
  22.8 0.4 collective-permute-start.4
  23.3 0.7 iota_compare_fusion.1
  23.9 0.7 iota_compare_fusion.3
  24.6 0.6 iota_compare_fusion.2
  25.3 0.0 copy-start.7
  25.3 0.7 select_reduce_fusion.3
  26.0 0.4 convert_reduce_fusion.3
  26.4 2.9 %fusion.17 = f32[24,128,128]{1,2,0:T(8,128)} fusion(bf16[24,128,128]{1,2,0:T(8,128)(2,1)S(1)} %get-tuple-element.114, bf16[128,3072]{1,0:T(8,128)(2,1)} %param.9), kind=kOutput, calls=%fused_computation.42 | convolution fusion | flops 100663296 | bytes 3145728 | tf_op jit(solution)/shard_map/hrc,chd->rhd/dot_general | solution.py:40
  29.3 41.9 %collective-permute-done.3 = bf16[128,3072]{1,0:T(8,128)(2,1)} collective-permute-done((bf16[128,3072]{1,0:T(8,128)(2,1)}, bf16[128,3072]{1,0:T(8,128)(2,1)}, u32[]{:S(2)}, u32[]{:S(2)}) %collective-permute-start.3) | collective-permute-done | bytes 786464 | tf_op jit(solution)/shard_map/ppermute | solution.py:10
  71.2 2.6 collective-permute-start.2
  73.8 1.5 copy.63
  75.3 9.8 %collective-permute-done.5 = bf16[128,3072]{1,0:T(8,128)(2,1)} collective-permute-done((bf16[128,3072]{1,0:T(8,128)(2,1)}, bf16[128,3072]{1,0:T(8,128)(2,1)}, u32[]{:S(2)}, u32[]{:S(2)}) %collective-permute-start.5) | collective-permute-done | bytes 786464 | tf_op jit(solution)/shard_map/ppermute | solution.py:10
  85.1 2.3 copy.67
  87.4 48.1 %collective-permute-done.4 = bf16[128,3072]{1,0:T(8,128)(2,1)} collective-permute-done((bf16[128,3072]{1,0:T(8,128)(2,1)}, bf16[128,3072]{1,0:T(8,128)(2,1)}, u32[]{:S(2)}, u32[]{:S(2)}) %collective-permute-start.4) | collective-permute-done | bytes 786464 | tf_op jit(solution)/shard_map/ppermute | solution.py:10
  135.5 2.5 copy.65
  138.0 0.0 collective-permute-done
  138.0 1.9 select_reduce_fusion.2
  139.9 0.3 convert_reduce_fusion.2
  140.2 1.8 select_reduce_fusion.1
  142.1 6.0 %collective-permute-done.2 = bf16[128,3072]{0,1:T(8,128)(2,1)} collective-permute-done((bf16[128,3072]{0,1:T(8,128)(2,1)}, bf16[128,3072]{0,1:T(8,128)(2,1)}, u32[]{:S(2)}, u32[]{:S(2)}) %collective-permute-start.2) | collective-permute-done | bytes 786464 | tf_op jit(solution)/shard_map/ppermute | solution.py:10
  148.1 1.8 select_reduce_fusion
  150.0 0.7 convert_reduce_fusion
  150.8 0.4 copy-done.1
  151.2 0.0 copy-start.3
  151.2 1.6 fusion.52
  152.8 1.6 fusion.53
  154.4 88.7 %all-gather.3.cloned.1.call-done = f32[192,128,128]{2,1,0:T(8,128)} async-done(((f32[24,128,128]{2,1,0:T(8,128)}), f32[192,128,128]{2,1,0:T(8,128)}) %all-gather.3.cloned.1.call-update) | async-done | bytes 12582928 | tf_op jit(solution)/shard_map/all_gather | solution.py:15
  243.1 13.8 %while.14 = (s32[]{:T(128)}, f32[24,128,128]{2,1,0:T(8,128)S(1)}, s32[]{:T(128)}, f32[8,24,128,128]{3,2,1,0:T(8,128)}, s32[]{:T(128)}, /*index=5*/s32[]{:T(128)}) while((s32[]{:T(128)}, f32[24,128,128]{2,1,0:T(8,128)S(1)}, s32[]{:T(128)}, f32[8,24,128,128]{3,2,1,0:T(8,128)}, s32[]{:T(128)}, /*index=5*/s32[]{:T(128)}) %tuple.50), condition=%wide.region_9.10_spmd.clone, body=%wide.region_8.9_spmd.clone.sunk | while | flops 1179652 | bytes 4718693 | solution.py:22
  243.1 1.9 add_select_fusion.2
  245.1 2.0 add_select_fusion.2
  247.1 2.0 add_select_fusion.2
  249.1 2.0 add_select_fusion.2
  251.0 2.0 add_select_fusion.2
  253.0 2.0 add_select_fusion.2
  255.0 2.0 add_select_fusion.2
  257.0 3.0 %fusion.7 = f32[24,128,128]{2,1,0:T(8,128)S(1)} fusion(f32[24,128,128]{2,1,0:T(8,128)S(1)} %get-tuple-element.84, bf16[128,3072]{1,0:T(8,128)(2,1)S(1)} %copy-done), kind=kOutput, calls=%fused_computation.12 | convolution fusion | flops 605945856 | bytes 3932160 | tf_op jit(solution)/shard_map/rhd,hde->rhe/dot_general | solution.py:92
  260.0 2.9 %fusion.11 = bf16[128,24,128]{0,2,1:T(8,128)(2,1)S(1)} fusion(f32[24,128,128]{1,2,0:T(8,128)} %fusion.53, f32[24,128,128]{1,2,0:T(8,128)S(1)} %copy-done.4, f32[24,128,128]{1,2,0:T(8,128)} %fusion.17, f32[24,128,128]{2,1,0:T(8,128)S(1)} %fusion.7, bf16[128,24,128]{0,2,1:T(8,128)(2,1)S(1)} %bitcast.168, f32[24]{0:T(128)S(1)} %broadcast_multiply_fusion, ...), kind=kOutput, calls=%fused_computation.15 | convolution fusion | flops 106168320 | bytes 9511136 | tf_op jit(solution)/shard_map/hrc,chd->rhd/dot_general | solution.py:40
  262.9 1.2 copy.74
  (17 shorter events, 0.1 us)
Async XLA Ops:
  6.5 18.7 %copy-start = (bf16[128,3072]{1,0:T(8,128)(2,1)S(1)}, bf16[128,3072]{1,0:T(8,128)(2,1)}, u32[]{:S(2)}) copy-start(bf16[128,3072]{1,0:T(8,128)(2,1)} %param.7) | copy-start | bytes 2359300
  6.5 236.6 %all-gather.3.cloned.1.call-start = ((), (), s32[]{:S(2)}) async-start(), calls=%async_computation | async-start | bytes 14155776 | tf_op jit(solution)/shard_map/all_gather | solution.py:15
  12.8 1.1 copy-start.5
  15.2 125.1 %collective-permute-start.1 = (bf16[128,3072]{0,1:T(8,128)(2,1)}, bf16[128,3072]{0,1:T(8,128)(2,1)}, u32[]{:S(2)}, u32[]{:S(2)}) collective-permute-start(bf16[128,3072]{0,1:T(8,128)(2,1)} %copy.52), channel_id=1, source_target_pairs={{0,4},{2,6},{4,0},{6,2},{8,12},{10,14},{12,8},{14,10},{1,5},{3,7},... | collective-permute-start | bytes 2359304 | tf_op jit(solution)/shard_map/ppermute | solution.py:10
  18.2 119.8 %collective-permute-start = (bf16[128,3072]{0,1:T(8,128)(2,1)}, bf16[128,3072]{0,1:T(8,128)(2,1)}, u32[]{:S(2)}, u32[]{:S(2)}) collective-permute-start(bf16[128,3072]{0,1:T(8,128)(2,1)} %copy.52), channel_id=1, source_target_pairs={{0,2},{2,0},{4,6},{6,4},{8,10},{10,8},{12,14},{14,12},{1,3},{3,1},... | collective-permute-start | bytes 2359304 | tf_op jit(solution)/shard_map/ppermute | solution.py:10
  19.7 51.5 %collective-permute-start.3 = (bf16[128,3072]{1,0:T(8,128)(2,1)}, bf16[128,3072]{1,0:T(8,128)(2,1)}, u32[]{:S(2)}, u32[]{:S(2)}) collective-permute-start(bf16[128,3072]{1,0:T(8,128)(2,1)} %param.9), channel_id=1, source_target_pairs={{0,2},{2,0},{4,6},{6,4},{8,10},{10,8},{12,14},{14,12},{1,3},{3,1},... | collective-permute-start | bytes 2359304 | tf_op jit(solution)/shard_map/ppermute | solution.py:10
  20.2 64.9 %collective-permute-start.5 = (bf16[128,3072]{1,0:T(8,128)(2,1)}, bf16[128,3072]{1,0:T(8,128)(2,1)}, u32[]{:S(2)}, u32[]{:S(2)}) collective-permute-start(bf16[128,3072]{1,0:T(8,128)(2,1)} %param.9), channel_id=1, source_target_pairs={{0,8},{2,10},{4,12},{6,14},{8,0},{10,2},{12,4},{14,6},{1,9},{3,11}... | collective-permute-start | bytes 2359304 | tf_op jit(solution)/shard_map/ppermute | solution.py:10
  22.8 112.7 %collective-permute-start.4 = (bf16[128,3072]{1,0:T(8,128)(2,1)}, bf16[128,3072]{1,0:T(8,128)(2,1)}, u32[]{:S(2)}, u32[]{:S(2)}) collective-permute-start(bf16[128,3072]{1,0:T(8,128)(2,1)} %param.9), channel_id=1, source_target_pairs={{0,4},{2,6},{4,0},{6,2},{8,12},{10,14},{12,8},{14,10},{1,5},{3,7},... | collective-permute-start | bytes 2359304 | tf_op jit(solution)/shard_map/ppermute | solution.py:10
  25.3 0.7 copy-start.7
  71.2 76.9 %collective-permute-start.2 = (bf16[128,3072]{0,1:T(8,128)(2,1)}, bf16[128,3072]{0,1:T(8,128)(2,1)}, u32[]{:S(2)}, u32[]{:S(2)}) collective-permute-start(bf16[128,3072]{0,1:T(8,128)(2,1)} %copy.52), channel_id=1, source_target_pairs={{0,8},{2,10},{4,12},{6,14},{8,0},{10,2},{12,4},{14,6},{1,9},{3,11}... | collective-permute-start | bytes 2359304 | tf_op jit(solution)/shard_map/ppermute | solution.py:10
  150.0 1.2 copy-start.1
  151.2 1.7 copy-start.3
  257.0 3.0 %copy-start.2 = (f32[24,128,128]{1,2,0:T(8,128)S(1)}, f32[24,128,128]{1,2,0:T(8,128)}, u32[]{:S(2)}) copy-start(f32[24,128,128]{1,2,0:T(8,128)} %copy-done.1) | copy-start | bytes 4718596
  257.0 3.0 %copy-start.4 = (f32[24,128,128]{1,2,0:T(8,128)S(1)}, f32[24,128,128]{1,2,0:T(8,128)}, u32[]{:S(2)}) copy-start(f32[24,128,128]{1,2,0:T(8,128)} %fusion.52) | copy-start | bytes 4718596
  257.0 3.0 %copy-start.6 = (bf16[128,3072]{0,1:T(8,128)(2,1)S(1)}, bf16[128,3072]{0,1:T(8,128)(2,1)}, u32[]{:S(2)}) copy-start(bf16[128,3072]{0,1:T(8,128)(2,1)} %copy.67) | copy-start | bytes 2359300
Sparse Core Ops, SparseCore 0:
  13.0 230.1 all-gather.2
where the time goes:
time: 272 us; the launch traced here: 271 us
  waiting for transfers between devices  195 us (72%)
  matrix products  22.5 us (8%)
  other arithmetic  17.8 us (7%)
  between operations  13.6 us (5%)
  local copies, waits for them, and re-layouts  11.7 us (4%)
  starting transfers between devices  10.7 us (4%)
    ppermute x6, waiting for transfers between devices, swapped(): lax.ppermute(shard, axis, [(i, i ^ 1 << apart) for i in range(lax.axis_si...  106 us
    all_gather x1, waiting for transfers between devices, prefix_2(): pieces = lax.all_gather(value, axis)  88.7 us
    select_n x7, other arithmetic, turn(): return jnp.where(position < mine, longer, running)  13.7 us
    ppermute x6, starting transfers between devices, swapped(): lax.ppermute(shard, axis, [(i, i ^ 1 << apart) for i in range(lax.axis_si...  10.7 us
    dot_general x4, matrix products, partial_block(): jnp.einsum('hrc,chd->rhd', weights, value_block, preferred_element_type=j...  9 us
    ppermute x3, local copies, waits for them, and re-layouts, swapped(): lax.ppermute(shard, axis, [(i, i ^ 1 << apart) for i in range(lax.axis_si...  6.31 us
    dot_general x4, matrix products, partial_block(): jnp.einsum('rhd,chd->hrc', query_block, key_block, preferred_element_type...  6.29 us
  transfers between devices with their start and end apart: 7, of which 5 were waited for; matrix products, arithmetic and copies ran while one was open for 9% of the time, Pallas kernels for 0%

commit v1 on v0

v1 whole, which is shorter than its diff:
```python
import functools
import math

import jax
import jax.numpy as jnp
from jax import lax
from jax.experimental import pallas as pl
from jax.experimental.pallas import tpu as pltpu
from jax.sharding import PartitionSpec as P

CENTER = 1.125
TERMS = 3
HEADS_A_STEP = 4
VMEM_BYTES = 40 * 1024 * 1024
F32 = jnp.float32
BF16 = jnp.bfloat16


def feature(x):
    return jnp.where(x > 0.0, x + 1.0, jnp.exp(jnp.minimum(x, 0.0)))


def halves(x):
    high = x.astype(BF16)
    return high, (x - high.astype(F32)).astype(BF16)


def padded(count):
    return -(-count // 16) * 16


def store_packed(ref, main, sums):
    rows, extra = main.shape[0], sums.shape[0]
    ref[0:rows, :] = main.astype(BF16)
    for term in range(TERMS):
        part = sums.astype(BF16)
        sums = sums - part.astype(F32)
        ref[rows + term * extra : rows + (term + 1) * extra, :] = part


def packed_sums(ref, rows, extra):
    total = ref[rows : rows + extra, :].astype(F32)
    for term in range(1, TERMS):
        total = total + ref[rows + term * extra : rows + (term + 1) * extra, :].astype(F32)
    return total


def block_sums_kernel(heads, width, where, lengths, k_ref, v_ref, send_ref, keep_ref):
    half_heads = heads // 2
    me = where[0]
    side = lax.rem(me, 2)
    length = lengths[me]
    rows = half_heads * width
    extra = padded(half_heads)
    live = lax.broadcasted_iota(jnp.int32, (k_ref.shape[0], width), 0) < length

    def one_half(first, store):
        sums = []
        for i in range(half_heads):
            columns = pl.ds(pl.multiple_of((first + i) * width, width), width)
            mapped = jnp.where(live, feature(k_ref[:, columns].astype(F32)) - CENTER, 0.0)
            values = jnp.where(live, v_ref[:, columns].astype(F32), 0.0)
            sums.append(jnp.sum(values, axis=0, keepdims=True))
            high, low = halves(mapped)
            values = values.astype(BF16)
            store(
                i,
                lax.dot_general(
                    jnp.concatenate([high, low], axis=0),
                    jnp.concatenate([values, values], axis=0),
                    (((0,), (0,)), ((), ())),
                    preferred_element_type=F32,
                ),
            )
        sums += [jnp.zeros((1, width), F32)] * (extra - half_heads)
        return jnp.concatenate(sums, axis=0)

    def store_send(i, value):
        send_ref[i * width : (i + 1) * width, :] = value.astype(BF16)

    def store_keep(i, value):
        keep_ref[i * width : (i + 1) * width, :] = value

    sums = one_half((1 - side) * half_heads, store_send)
    for term in range(TERMS):
        part = sums.astype(BF16)
        sums = sums - part.astype(F32)
        send_ref[rows + term * extra : rows + (term + 1) * extra, :] = part
    keep_ref[rows : rows + extra, :] = one_half(side * half_heads, store_keep)


def add_packed_kernel(rows, extra, count, where, keep_ref, *refs):
    flag = where[0].astype(F32)
    main = keep_ref[0:rows, :] * flag
    sums = keep_ref[rows : rows + extra, :] * flag
    for ref in refs[:count]:
        main = main + ref[0:rows, :].astype(F32)
        sums = sums + packed_sums(ref, rows, extra)
    store_packed(refs[count], main, sums)


def scores_kernel(heads, width, levels, hops, tokens, where, lengths, scale, *refs):
    step = pl.program_id(0)
    refs = list(refs)
    q_ref = refs.pop(0)
    key_refs = [refs.pop(0) for _ in range(levels + 1)]
    value_refs = [refs.pop(0) for _ in range(2)]
    hop_refs = [refs.pop(0) for _ in range(hops)]
    near_ref, far_ref = refs.pop(0), refs.pop(0)
    weight_refs = [refs.pop(0) for _ in range(levels - 1)]
    factor_ref, base_ref = refs
    me = where[0]
    side = lax.rem(me, 2)
    half_heads = heads // 2
    rows, extra = half_heads * width, padded(half_heads)
    row_count = q_ref.shape[0]
    a_step = q_ref.shape[1] // width
    first = step * a_step
    column = lax.broadcasted_iota(jnp.int32, (row_count, row_count), 1)
    row = lax.broadcasted_iota(jnp.int32, (row_count, row_count), 0)
    allowed = []
    for which in range(levels + 1):
        partner = me if which == 0 else jnp.bitwise_xor(me, 1 << (which - 1))
        fits = column < lengths[partner]
        allowed.append(fits & (column <= row) if which == 0 else fits)
    lane = lax.broadcasted_iota(jnp.int32, (row_count, 128), 1)
    factors = jnp.zeros((row_count, 128), F32)
    mine = (first // half_heads == side).astype(F32)
    upper = mine * side.astype(F32)
    in_half = lax.rem(first, half_heads)
    sums = (1.0 - mine) * packed_sums(far_ref, rows, extra) + upper * packed_sums(near_ref, rows, extra)
    for ref in hop_refs:
        sums = sums + mine * packed_sums(ref, rows, extra)
    sum_row = lax.broadcasted_iota(jnp.int32, sums.shape, 0)
    for h in range(a_step):
        at = slice(h * width, (h + 1) * width)
        queries = q_ref[:, at]
        peaks, totals, weights = [], [], []
        for which in range(levels + 1):
            s = lax.dot_general(
                queries, key_refs[which][:, at], (((1,), (1,)), ((), ())), preferred_element_type=F32
            ) * (1.0 / math.sqrt(width))
            s = jnp.where(allowed[which], s, -jnp.inf)
            peak = jnp.max(s, axis=1, keepdims=True)
            p = jnp.exp(s - peak).astype(BF16)
            peaks.append(peak)
            weights.append(p)
            totals.append(jnp.sum(p.astype(F32), axis=1, keepdims=True))
        peak = functools.reduce(jnp.maximum, peaks)
        shares = [jnp.exp(one - peak) for one in peaks]
        whole = functools.reduce(jnp.add, [a * b for a, b in zip(shares, totals)])
        shares = [share / whole for share in shares]
        base = shares[0] * jnp.dot(weights[0], value_refs[0][:, at], preferred_element_type=F32)
        base = base + shares[1] * jnp.dot(weights[1], value_refs[1][:, at], preferred_element_type=F32)
        for which in range(2, levels + 1):
            weight_refs[which - 2][:, at] = weights[which]
            factors = jnp.where(lane == (which - 2) * a_step + h, shares[which], factors)
        block = pl.ds(pl.multiple_of((in_half + h) * width, width), width)
        prefix = (1.0 - mine) * far_ref[block, :].astype(F32) + upper * near_ref[block, :].astype(F32)
        for ref in hop_refs:
            prefix = prefix + mine * ref[block, :].astype(F32)
        mapped = feature(queries.astype(F32))
        high, low = halves(mapped)
        prefix_high, prefix_low = halves(prefix)
        linear = jnp.dot(
            jnp.concatenate([high, low], axis=1),
            jnp.concatenate([prefix_high, prefix_high], axis=0),
            preferred_element_type=F32,
        ) + jnp.dot(high, prefix_low, preferred_element_type=F32)
        value_sum = jnp.sum(jnp.where(sum_row == in_half + h, sums, 0.0), axis=0, keepdims=True)
        linear = linear + jnp.sum(mapped, axis=1, keepdims=True) * (CENTER * value_sum)
        base_ref[:, at] = base + linear * (scale[first + h] * (1.0 / (width * math.sqrt(tokens))))
    factor_ref[...] = factors


def finish_kernel(late, width, factor_ref, base_ref, *refs):
    out_ref = refs[2 * late]
    a_step = base_ref.shape[1] // width
    for h in range(a_step):
        at = slice(h * width, (h + 1) * width)
        total = base_ref[:, at]
        for which in range(late):
            lane = which * a_step + h
            total = total + factor_ref[:, lane : lane + 1] * jnp.dot(
                refs[which][:, at], refs[late + which][:, at], preferred_element_type=F32
            )
        out_ref[:, at] = total.astype(BF16)


def params():
    return pltpu.CompilerParams(vmem_limit_bytes=VMEM_BYTES)


def shards(query_rows, key_rows, value_rows, key_len, linear_scale):
    row_count, columns = query_rows.shape
    heads = linear_scale.shape[0]
    width = columns // heads
    half_heads = heads // 2
    count = lax.axis_size("seq")
    levels = count.bit_length() - 1
    late = levels - 1
    me = lax.axis_index("seq").astype(jnp.int32)
    where = me.reshape(1)
    tokens = row_count * count
    rows, extra = half_heads * width, padded(half_heads)
    packed = jax.ShapeDtypeStruct((rows + TERMS * extra, width), BF16)
    smem = pl.BlockSpec(memory_space=pltpu.SMEM)
    vmem = pl.BlockSpec(memory_space=pltpu.VMEM)

    def swapped(x, level):
        return lax.ppermute(x, "seq", [(i, i ^ 1 << level) for i in range(count)])

    order = list(range(levels - 1, -1, -1))
    far_keys = {level: swapped(key_rows, level) for level in order}
    far_values = {level: swapped(value_rows, level) for level in order}

    send, keep = pl.pallas_call(
        functools.partial(block_sums_kernel, heads, width),
        in_specs=[smem, smem, vmem, vmem],
        out_specs=[vmem, vmem],
        out_shape=[packed, jax.ShapeDtypeStruct((rows + extra, width), F32)],
        compiler_params=params(),
        name="block_sums",
    )(where, key_len, key_rows, value_rows)
    near = swapped(send, 0)

    def add_packed(flag, *parts):
        return pl.pallas_call(
            functools.partial(add_packed_kernel, rows, extra, len(parts)),
            in_specs=[smem] + [vmem] * (1 + len(parts)),
            out_specs=vmem,
            out_shape=packed,
            compiler_params=params(),
            name="add_packed",
        )(flag, keep, *parts)

    one = jnp.ones((1,), jnp.int32)
    pairs_of_blocks = count // 2
    if pairs_of_blocks <= 4:
        steps = [[(z, z + 1)] for z in range(pairs_of_blocks - 1)]
    else:
        steps = [
            [(z, z + (1 << d)) for z in range(pairs_of_blocks - (1 << d))]
            for d in range((pairs_of_blocks - 1).bit_length())
        ]
    hops = []
    for pairs in steps:
        payload = add_packed(one, near, *hops)
        hops.append(
            lax.ppermute(payload, "seq", [(2 * a + y, 2 * b + y) for a, b in pairs for y in (0, 1)])
        )
    far = swapped(add_packed(1 - lax.rem(where, 2), *hops), 0)

    a_step = math.gcd(HEADS_A_STEP, half_heads)
    grid = (heads // a_step,)
    wide = pl.BlockSpec((row_count, a_step * width), lambda i, *_: (0, i))
    narrow = pl.BlockSpec((row_count, 128), lambda i, *_: (0, i))
    whole = pl.BlockSpec(packed.shape, lambda i, *_: (0, 0))
    full = jax.ShapeDtypeStruct((row_count, columns), BF16)
    *weights, factors, base = pl.pallas_call(
        functools.partial(scores_kernel, heads, width, levels, len(hops), tokens),
        grid_spec=pltpu.PrefetchScalarGridSpec(
            num_scalar_prefetch=3,
            grid=grid,
            in_specs=[wide] * (1 + levels + 1 + 2) + [whole] * (len(hops) + 2),
            out_specs=[wide] * late + [narrow, wide],
        ),
        out_shape=[full] * late
        + [
            jax.ShapeDtypeStruct((row_count, grid[0] * 128), F32),
            jax.ShapeDtypeStruct((row_count, columns), F32),
        ],
        compiler_params=params(),
        name="scores",
    )(
        where,
        key_len,
        linear_scale,
        query_rows,
        key_rows,
        *[far_keys[level] for level in range(levels)],
        value_rows,
        far_values[0],
        *hops,
        near,
        far,
    )
    return pl.pallas_call(
        functools.partial(finish_kernel, late, width),
        grid=grid,
        in_specs=[narrow, wide] + [wide] * (2 * late),
        out_specs=wide,
        out_shape=full,
        compiler_params=params(),
        name="finish",
    )(factors, base, *weights, *[far_values[level] for level in range(1, levels)])


def solution(mesh):
    return jax.shard_map(
        shards,
        mesh=mesh,
        in_specs=(
            P(("groups", "seq"), "head"),
            P(("groups", "seq"), "head"),
            P(("groups", "seq"), "head"),
            P("groups"),
            P("head"),
        ),
        out_specs=P(("groups", "seq"), "head"),
        check_vma=False,
    )
```

time: 272 us -> 113 us (0.42)
  waiting for transfers between devices: 195 us -> 64.2 us
  matrix products: 22.5 us -> 0 us
  other arithmetic: 17.8 us -> 0 us
  starting transfers between devices: 10.7 us -> 28.4 us
  Pallas kernels: 0 us -> 16.6 us
  between operations: 13.6 us -> 0.1 us
  local copies, waits for them, and re-layouts: 11.7 us -> 2.94 us
    all_gather x1 -> x0, waiting for transfers between devices: 88.7 us -> none  [prefix_2(): pieces = lax.all_gather(value, axis)]
    ppermute x6 -> x11, waiting for transfers between devices: 106 us -> 64.2 us  [the longest x8 56.5 us: swapped(): return lax.ppermute(x, 'seq', [(i, i ^ 1 << level) for i in range(count)])]
    dot_general x10 -> x0, matrix products: 22.5 us -> none  [the longest x4 9 us: partial_block(): jnp.einsum('hrc,chd->rhd', weights, value_block, preferred_element_type=j...]
    ppermute x6 -> x11, starting transfers between devices: 10.7 us -> 28.4 us  [the longest x8 23.1 us: swapped(): return lax.ppermute(x, 'seq', [(i, i ^ 1 << level) for i in range(count)])]
    pallas_call x0 -> x7, Pallas kernels: none -> 16.6 us  [the longest x1 10.7 us: shards(): pl.pallas_call(functools.partial(scores_kernel, heads, width, levels, len...]
    select_n x7 -> x0, other arithmetic: 13.7 us -> none  [turn(): return jnp.where(position < mine, longer, running)]
    ppermute x3 -> x0, local copies, waits for them, and re-layouts: 6.31 us -> none  [swapped(): lax.ppermute(shard, axis, [(i, i ^ 1 << apart) for i in range(lax.axis_si...]
  transfers between devices with their start and end apart: 7 -> 11, of which waited for: 5 -> 5; matrix products, arithmetic and copies ran while one was open for 9% -> 0% of each run, Pallas kernels for 0% -> 10%
where the time goes in v1:
time: 113 us; the launch traced here: 112 us
  waiting for transfers between devices  64.2 us (57%)
  starting transfers between devices  28.4 us (25%)
  Pallas kernels  16.6 us (15%)
  local copies, waits for them, and re-layouts  2.94 us (3%)
    ppermute x8, waiting for transfers between devices, swapped(): return lax.ppermute(x, 'seq', [(i, i ^ 1 << level) for i in range(count)])  56.5 us
    ppermute x8, starting transfers between devices, swapped(): return lax.ppermute(x, 'seq', [(i, i ^ 1 << level) for i in range(count)])  23.1 us
    pallas_call x1, Pallas kernels, shards(): pl.pallas_call(functools.partial(scores_kernel, heads, width, levels, len...  10.7 us
    ppermute x3, waiting for transfers between devices, shards(): lax.ppermute(payload, 'seq', [(2 * a + y, 2 * b + y) for a, b in pairs fo...  7.72 us
    ppermute x3, starting transfers between devices, shards(): lax.ppermute(payload, 'seq', [(2 * a + y, 2 * b + y) for a, b in pairs fo...  5.36 us
    pallas_call x1, Pallas kernels, shards(): pl.pallas_call(functools.partial(finish_kernel, late, width), grid=grid,...  3.23 us
    unnamed x12, local copies, waits for them, and re-layouts  2.94 us
  transfers between devices with their start and end apart: 11, of which 5 were waited for; matrix products, arithmetic and copies ran while one was open for 0% of the time, Pallas kernels for 10%

profile of v1, /device:TPU:0, one launch (start us, length us, event | category | flops | bytes accessed | tf_op | source)
XLA Modules:
  0.0 112.3 jit_solution(16407323745582296866)
XLA Ops:
  0.0 0.0 copy-start
  0.0 1.1 %copy-done = bf16[128,3072]{1,0:T(8,128)(2,1)S(1)} copy-done((bf16[128,3072]{1,0:T(8,128)(2,1)S(1)}, bf16[128,3072]{1,0:T(8,128)(2,1)}, u32[]{:S(2)}) %copy-start) | copy-done | bytes 786456
  1.1 0.0 copy-start.1
  1.1 1.1 %copy-done.1 = bf16[128,3072]{1,0:T(8,128)(2,1)S(1)} copy-done((bf16[128,3072]{1,0:T(8,128)(2,1)S(1)}, bf16[128,3072]{1,0:T(8,128)(2,1)}, u32[]{:S(2)}) %copy-start.1) | copy-done | bytes 786456
  2.3 0.0 copy-start.4
  2.3 0.7 copy-done.4
  2.9 1.9 %block_sums.1 = (bf16[1584,128]{1,0:T(8,128)(2,1)S(1)}, f32[1552,128]{1,0:T(8,128)S(1)}) custom-call(s32[1]{0:T(128)} %bitcast.where, s32[8]{0:T(128)S(1)} %copy-done.4, bf16[128,3072]{1,0:T(8,128)(2,1)S(1)} %copy-done, bf16[128,3072]{1,0:T(8,128)(2,1)S(1)} %copy-done.1), custom_call_target="tpu_custom_call" | custom-call | tf_op jit(solution)/shard_map/block_sums/pallas_call | solution.py:217
  4.8 3.0 %collective-permute-start.4 = (bf16[1584,128]{1,0:T(8,128)(2,1)S(1)}, bf16[1584,128]{1,0:T(8,128)(2,1)S(1)}, u32[]{:S(2)}, u32[]{:S(2)}) collective-permute-start(bf16[1584,128]{1,0:T(8,128)(2,1)S(1)} %get-tuple-element.12), channel_id=1, source_target_pairs={{0,2},{2,0},{4,6},{6,4},{8,10},{10,8},{12,14},{14,12},{1,3},{3,1},... | collective-permute-start | bytes 1216520 | tf_op jit(solution)/shard_map/ppermute | solution.py:211
  7.8 9.4 %collective-permute-done.4.refs_0_.refs_10_ = bf16[1584,128]{1,0:T(8,128)(2,1)S(1)} collective-permute-done((bf16[1584,128]{1,0:T(8,128)(2,1)S(1)}, bf16[1584,128]{1,0:T(8,128)(2,1)S(1)}, u32[]{:S(2)}, u32[]{:S(2)}) %collective-permute-start.4) | collective-permute-done | bytes 405536 | tf_op jit(solution)/shard_map/ppermute | solution.py:211
  17.2 0.1 add_packed.4
  17.3 3.7 %collective-permute-start.5 = (bf16[1584,128]{1,0:T(8,128)(2,1)S(1)}, bf16[1584,128]{1,0:T(8,128)(2,1)S(1)}, u32[]{:S(2)}, u32[]{:S(2)}) collective-permute-start(bf16[1584,128]{1,0:T(8,128)(2,1)S(1)} %add_packed.4), channel_id=1, source_target_pairs={{0,4},{2,6},{1,5},{3,7},{16,20},{18,22},{17,21},{19,23}} | collective-permute-start | bytes 1216520 | tf_op jit(solution)/shard_map/ppermute | solution.py:250
  21.0 7.7 %collective-permute-done.5.refs_1_.refs_0_.refs_7_ = bf16[1584,128]{1,0:T(8,128)(2,1)S(1)} collective-permute-done((bf16[1584,128]{1,0:T(8,128)(2,1)S(1)}, bf16[1584,128]{1,0:T(8,128)(2,1)S(1)}, u32[]{:S(2)}, u32[]{:S(2)}) %collective-permute-start.5) | collective-permute-done | bytes 405536 | tf_op jit(solution)/shard_map/ppermute | solution.py:250
  28.8 0.2 add_packed.5
  29.0 0.0 copy-start.2
  29.0 0.8 collective-permute-start.6
  29.8 1.6 %collective-permute-start = (bf16[128,3072]{1,0:T(8,128)(2,1)S(1)}, bf16[128,3072]{1,0:T(8,128)(2,1)S(1)}, u32[]{:S(2)}, u32[]{:S(2)}) collective-permute-start(bf16[128,3072]{1,0:T(8,128)(2,1)S(1)} %copy-done), channel_id=1, source_target_pairs={{0,2},{2,0},{4,6},{6,4},{8,10},{10,8},{12,14},{14,12},{1,3},{3,1},... | collective-permute-start | bytes 2359304 | tf_op jit(solution)/shard_map/ppermute | solution.py:211
  31.4 3.1 %collective-permute-start.1 = (bf16[128,3072]{1,0:T(8,128)(2,1)S(1)}, bf16[128,3072]{1,0:T(8,128)(2,1)S(1)}, u32[]{:S(2)}, u32[]{:S(2)}) collective-permute-start(bf16[128,3072]{1,0:T(8,128)(2,1)S(1)} %copy-done), channel_id=1, source_target_pairs={{0,4},{2,6},{4,0},{6,2},{8,12},{10,14},{12,8},{14,10},{1,5},{3,7},... | collective-permute-start | bytes 2359304 | tf_op jit(solution)/shard_map/ppermute | solution.py:211
  34.5 0.0 collective-permute-done.6.refs_2_.refs_1_.refs_8_
  34.5 0.2 add_packed.6
  34.7 0.0 copy-start.3
  34.7 0.0 copy-start.5
  34.7 0.8 collective-permute-start.7
  35.6 9.1 %collective-permute-start.2 = (bf16[128,3072]{1,0:T(8,128)(2,1)S(1)}, bf16[128,3072]{1,0:T(8,128)(2,1)S(1)}, u32[]{:S(2)}, u32[]{:S(2)}) collective-permute-start(bf16[128,3072]{1,0:T(8,128)(2,1)S(1)} %copy-done), channel_id=1, source_target_pairs={{0,8},{2,10},{4,12},{6,14},{8,0},{10,2},{12,4},{14,6},{1,9},{3,11}... | collective-permute-start | bytes 2359304 | tf_op jit(solution)/shard_map/ppermute | solution.py:211
  44.7 0.0 copy-done.2
  44.7 1.5 %collective-permute-start.3 = (bf16[128,3072]{1,0:T(8,128)(2,1)S(1)}, bf16[128,3072]{1,0:T(8,128)(2,1)S(1)}, u32[]{:S(2)}, u32[]{:S(2)}) collective-permute-start(bf16[128,3072]{1,0:T(8,128)(2,1)S(1)} %copy-done.2), channel_id=1, source_target_pairs={{0,2},{2,0},{4,6},{6,4},{8,10},{10,8},{12,14},{14,12},{1,3},{3,1},... | collective-permute-start | bytes 2359304 | tf_op jit(solution)/shard_map/ppermute | solution.py:211
  46.2 4.1 %collective-permute-done.refs_2_ = bf16[128,3072]{1,0:T(8,128)(2,1)S(1)} collective-permute-done((bf16[128,3072]{1,0:T(8,128)(2,1)S(1)}, bf16[128,3072]{1,0:T(8,128)(2,1)S(1)}, u32[]{:S(2)}, u32[]{:S(2)}) %collective-permute-start) | collective-permute-done | bytes 786464 | tf_op jit(solution)/shard_map/ppermute | solution.py:211
  50.3 0.0 collective-permute-start.10
  50.3 0.0 collective-permute-done.7.refs_2_.refs_9_
  50.3 3.1 %collective-permute-start.9 = (bf16[128,3072]{1,0:T(8,128)(2,1)S(1)}, bf16[128,3072]{1,0:T(8,128)(2,1)S(1)}, u32[]{:S(2)}, u32[]{:S(2)}) collective-permute-start(bf16[128,3072]{1,0:T(8,128)(2,1)S(1)} %copy-done.2), channel_id=1, source_target_pairs={{0,4},{2,6},{4,0},{6,2},{8,12},{10,14},{12,8},{14,10},{1,5},{3,7},... | collective-permute-start | bytes 2359304 | tf_op jit(solution)/shard_map/ppermute | solution.py:211
  53.5 0.2 add_packed.7
  53.7 0.0 collective-permute-done.1.refs_3_
  53.7 1.6 %collective-permute-start.8 = (bf16[1584,128]{1,0:T(8,128)(2,1)S(1)}, bf16[1584,128]{1,0:T(8,128)(2,1)S(1)}, u32[]{:S(2)}, u32[]{:S(2)}) collective-permute-start(bf16[1584,128]{1,0:T(8,128)(2,1)S(1)} %add_packed.7), channel_id=1, source_target_pairs={{0,2},{2,0},{4,6},{6,4},{8,10},{10,8},{12,14},{14,12},{1,3},{3,1},... | collective-permute-start | bytes 1216520 | tf_op jit(solution)/shard_map/ppermute | solution.py:211
  55.3 37.0 %collective-permute-done.2.refs_4_ = bf16[128,3072]{1,0:T(8,128)(2,1)S(1)} collective-permute-done((bf16[128,3072]{1,0:T(8,128)(2,1)S(1)}, bf16[128,3072]{1,0:T(8,128)(2,1)S(1)}, u32[]{:S(2)}, u32[]{:S(2)}) %collective-permute-start.2) | collective-permute-done | bytes 786464 | tf_op jit(solution)/shard_map/ppermute | solution.py:211
  92.3 0.0 collective-permute-done.3.refs_6_
  92.3 0.0 collective-permute-done.8.refs_11_
  92.3 0.0 copy-done.3
  92.3 0.0 copy-done.5
  92.3 10.7 %scores.1 = (bf16[128,3072]{1,0:T(8,128)(2,1)S(1)}, bf16[128,3072]{1,0:T(8,128)(2,1)S(1)}, f32[128,768]{1,0:T(8,128)S(1)}, f32[128,3072]{1,0:T(8,128)S(1)}) custom-call(s32[1]{0:T(128)} %bitcast.where, s32[8]{0:T(128)S(1)} %copy-done.4, f32[24]{0:T(128)S(1)} %copy-done.5, bf16[128,3072]{1,0:T(8,128)(2,1)S(1)} %copy-done.3, bf16[128,3072]{1,0:T(8,128)(2,1)S(1)} %copy-done, ...), custom_call_target="tpu_custom_call" | custom-call | tf_op jit(solution)/shard_map/scores/pallas_call | solution.py:260
  103.0 6.0 %collective-permute-done.10.refs_3_ = bf16[128,3072]{1,0:T(8,128)(2,1)S(1)} collective-permute-done((bf16[128,3072]{1,0:T(8,128)(2,1)S(1)}, bf16[128,3072]{1,0:T(8,128)(2,1)S(1)}, u32[]{:S(2)}, u32[]{:S(2)}) %collective-permute-start.10) | collective-permute-done | bytes 786464 | tf_op jit(solution)/shard_map/ppermute | solution.py:211
  109.0 0.0 collective-permute-done.9.refs_2_
  109.0 3.2 %finish.1 = bf16[128,3072]{1,0:T(8,128)(2,1)} custom-call(f32[128,768]{1,0:T(8,128)S(1)} %get-tuple-element.13.factor_ref, f32[128,3072]{1,0:T(8,128)S(1)} %get-tuple-element.14.base_ref, bf16[128,3072]{1,0:T(8,128)(2,1)S(1)} %get-tuple-element.15.refs_0_, bf16[128,3072]{1,0:T(8,128)(2,1)S(1)} %get-tuple-element.16.refs_1_, ...), custom_call_target="tpu_custom_call" | custom-call | tf_op jit(solution)/shard_map/finish/pallas_call | solution.py:288
Async XLA Ops:
  0.0 1.1 %copy-start = (bf16[128,3072]{1,0:T(8,128)(2,1)S(1)}, bf16[128,3072]{1,0:T(8,128)(2,1)}, u32[]{:S(2)}) copy-start(bf16[128,3072]{1,0:T(8,128)(2,1)} %refs_1_.1) | copy-start | bytes 2359300
  1.1 1.1 %copy-start.1 = (bf16[128,3072]{1,0:T(8,128)(2,1)S(1)}, bf16[128,3072]{1,0:T(8,128)(2,1)}, u32[]{:S(2)}) copy-start(bf16[128,3072]{1,0:T(8,128)(2,1)} %refs_5_.1) | copy-start | bytes 2359300
  2.3 0.7 copy-start.4
  4.8 12.4 %collective-permute-start.4 = (bf16[1584,128]{1,0:T(8,128)(2,1)S(1)}, bf16[1584,128]{1,0:T(8,128)(2,1)S(1)}, u32[]{:S(2)}, u32[]{:S(2)}) collective-permute-start(bf16[1584,128]{1,0:T(8,128)(2,1)S(1)} %get-tuple-element.12), channel_id=1, source_target_pairs={{0,2},{2,0},{4,6},{6,4},{8,10},{10,8},{12,14},{14,12},{1,3},{3,1},... | collective-permute-start | bytes 1216520 | tf_op jit(solution)/shard_map/ppermute | solution.py:211
  17.3 11.4 %collective-permute-start.5 = (bf16[1584,128]{1,0:T(8,128)(2,1)S(1)}, bf16[1584,128]{1,0:T(8,128)(2,1)S(1)}, u32[]{:S(2)}, u32[]{:S(2)}) collective-permute-start(bf16[1584,128]{1,0:T(8,128)(2,1)S(1)} %add_packed.4), channel_id=1, source_target_pairs={{0,4},{2,6},{1,5},{3,7},{16,20},{18,22},{17,21},{19,23}} | collective-permute-start | bytes 1216520 | tf_op jit(solution)/shard_map/ppermute | solution.py:250
  29.0 15.7 %copy-start.2 = (bf16[128,3072]{1,0:T(8,128)(2,1)S(1)}, bf16[128,3072]{1,0:T(8,128)(2,1)}, u32[]{:S(2)}) copy-start(bf16[128,3072]{1,0:T(8,128)(2,1)} %refs_5_.1) | copy-start | bytes 2359300
  29.0 5.5 %collective-permute-start.6 = (bf16[1584,128]{1,0:T(8,128)(2,1)S(1)}, bf16[1584,128]{1,0:T(8,128)(2,1)S(1)}, u32[]{:S(2)}, u32[]{:S(2)}) collective-permute-start(bf16[1584,128]{1,0:T(8,128)(2,1)S(1)} %add_packed.5), channel_id=1, source_target_pairs={{4,8},{6,10},{5,9},{7,11},{20,24},{22,26},{21,25},{23,27}} | collective-permute-start | bytes 1216520 | tf_op jit(solution)/shard_map/ppermute | solution.py:250
  29.8 20.5 %collective-permute-start = (bf16[128,3072]{1,0:T(8,128)(2,1)S(1)}, bf16[128,3072]{1,0:T(8,128)(2,1)S(1)}, u32[]{:S(2)}, u32[]{:S(2)}) collective-permute-start(bf16[128,3072]{1,0:T(8,128)(2,1)S(1)} %copy-done), channel_id=1, source_target_pairs={{0,2},{2,0},{4,6},{6,4},{8,10},{10,8},{12,14},{14,12},{1,3},{3,1},... | collective-permute-start | bytes 2359304 | tf_op jit(solution)/shard_map/ppermute | solution.py:211
  31.4 22.3 %collective-permute-start.1 = (bf16[128,3072]{1,0:T(8,128)(2,1)S(1)}, bf16[128,3072]{1,0:T(8,128)(2,1)S(1)}, u32[]{:S(2)}, u32[]{:S(2)}) collective-permute-start(bf16[128,3072]{1,0:T(8,128)(2,1)S(1)} %copy-done), channel_id=1, source_target_pairs={{0,4},{2,6},{4,0},{6,2},{8,12},{10,14},{12,8},{14,10},{1,5},{3,7},... | collective-permute-start | bytes 2359304 | tf_op jit(solution)/shard_map/ppermute | solution.py:211
  34.7 57.6 %copy-start.3 = (bf16[128,3072]{1,0:T(8,128)(2,1)S(1)}, bf16[128,3072]{1,0:T(8,128)(2,1)}, u32[]{:S(2)}) copy-start(bf16[128,3072]{1,0:T(8,128)(2,1)} %refs_0_.1) | copy-start | bytes 2359300
  34.7 57.6 %copy-start.5 = (f32[24]{0:T(128)S(1)}, f32[24]{0:T(128)}, u32[]{:S(2)}) copy-start(f32[24]{0:T(128)} %scale.1) | copy-start | bytes 292
  34.7 15.6 %collective-permute-start.7 = (bf16[1584,128]{1,0:T(8,128)(2,1)S(1)}, bf16[1584,128]{1,0:T(8,128)(2,1)S(1)}, u32[]{:S(2)}, u32[]{:S(2)}) collective-permute-start(bf16[1584,128]{1,0:T(8,128)(2,1)S(1)} %add_packed.6), channel_id=1, source_target_pairs={{8,12},{10,14},{9,13},{11,15},{24,28},{26,30},{25,29},{27,31}} | collective-permute-start | bytes 1216520 | tf_op jit(solution)/shard_map/ppermute | solution.py:250
  35.6 56.7 %collective-permute-start.2 = (bf16[128,3072]{1,0:T(8,128)(2,1)S(1)}, bf16[128,3072]{1,0:T(8,128)(2,1)S(1)}, u32[]{:S(2)}, u32[]{:S(2)}) collective-permute-start(bf16[128,3072]{1,0:T(8,128)(2,1)S(1)} %copy-done), channel_id=1, source_target_pairs={{0,8},{2,10},{4,12},{6,14},{8,0},{10,2},{12,4},{14,6},{1,9},{3,11}... | collective-permute-start | bytes 2359304 | tf_op jit(solution)/shard_map/ppermute | solution.py:211
  44.7 47.6 %collective-permute-start.3 = (bf16[128,3072]{1,0:T(8,128)(2,1)S(1)}, bf16[128,3072]{1,0:T(8,128)(2,1)S(1)}, u32[]{:S(2)}, u32[]{:S(2)}) collective-permute-start(bf16[128,3072]{1,0:T(8,128)(2,1)S(1)} %copy-done.2), channel_id=1, source_target_pairs={{0,2},{2,0},{4,6},{6,4},{8,10},{10,8},{12,14},{14,12},{1,3},{3,1},... | collective-permute-start | bytes 2359304 | tf_op jit(solution)/shard_map/ppermute | solution.py:211
  50.3 58.7 %collective-permute-start.10 = (bf16[128,3072]{1,0:T(8,128)(2,1)S(1)}, bf16[128,3072]{1,0:T(8,128)(2,1)S(1)}, u32[]{:S(2)}, u32[]{:S(2)}) collective-permute-start(bf16[128,3072]{1,0:T(8,128)(2,1)S(1)} %copy-done.2), channel_id=1, source_target_pairs={{0,8},{2,10},{4,12},{6,14},{8,0},{10,2},{12,4},{14,6},{1,9},{3,11}... | collective-permute-start | bytes 2359304 | tf_op jit(solution)/shard_map/ppermute | solution.py:211
  50.3 58.7 %collective-permute-start.9 = (bf16[128,3072]{1,0:T(8,128)(2,1)S(1)}, bf16[128,3072]{1,0:T(8,128)(2,1)S(1)}, u32[]{:S(2)}, u32[]{:S(2)}) collective-permute-start(bf16[128,3072]{1,0:T(8,128)(2,1)S(1)} %copy-done.2), channel_id=1, source_target_pairs={{0,4},{2,6},{4,0},{6,2},{8,12},{10,14},{12,8},{14,10},{1,5},{3,7},... | collective-permute-start | bytes 2359304 | tf_op jit(solution)/shard_map/ppermute | solution.py:211
  53.7 38.6 %collective-permute-start.8 = (bf16[1584,128]{1,0:T(8,128)(2,1)S(1)}, bf16[1584,128]{1,0:T(8,128)(2,1)S(1)}, u32[]{:S(2)}, u32[]{:S(2)}) collective-permute-start(bf16[1584,128]{1,0:T(8,128)(2,1)S(1)} %add_packed.7), channel_id=1, source_target_pairs={{0,2},{2,0},{4,6},{6,4},{8,10},{10,8},{12,14},{14,12},{1,3},{3,1},... | collective-permute-start | bytes 1216520 | tf_op jit(solution)/shard_map/ppermute | solution.py:211

commit v2 on v1

--- a/solution.py
+++ b/solution.py
@@ -210,31 +210,13 @@
     def swapped(x, level):
         return lax.ppermute(x, "seq", [(i, i ^ 1 << level) for i in range(count)])
 
-    order = list(range(levels - 1, -1, -1))
+    order = list(range(levels - 1, 0, -1))
     far_keys = {level: swapped(key_rows, level) for level in order}
+    neighbours = [[i, i + 1] for i in range(0, count, 2)]
+    both_keys = lax.all_gather(key_rows, "seq", axis_index_groups=neighbours)
+    both_values = lax.all_gather(value_rows, "seq", axis_index_groups=neighbours)
     far_values = {level: swapped(value_rows, level) for level in order}
 
-    send, keep = pl.pallas_call(
-        functools.partial(block_sums_kernel, heads, width),
-        in_specs=[smem, smem, vmem, vmem],
-        out_specs=[vmem, vmem],
-        out_shape=[packed, jax.ShapeDtypeStruct((rows + extra, width), F32)],
-        compiler_params=params(),
-        name="block_sums",
-    )(where, key_len, key_rows, value_rows)
-    near = swapped(send, 0)
-
-    def add_packed(flag, *parts):
-        return pl.pallas_call(
-            functools.partial(add_packed_kernel, rows, extra, len(parts)),
-            in_specs=[smem] + [vmem] * (1 + len(parts)),
-            out_specs=vmem,
-            out_shape=packed,
-            compiler_params=params(),
-            name="add_packed",
-        )(flag, keep, *parts)
-
-    one = jnp.ones((1,), jnp.int32)
     pairs_of_blocks = count // 2
     if pairs_of_blocks <= 4:
         steps = [[(z, z + 1)] for z in range(pairs_of_blocks - 1)]
@@ -243,17 +225,49 @@
             [(z, z + (1 << d)) for z in range(pairs_of_blocks - (1 << d))]
             for d in range((pairs_of_blocks - 1).bit_length())
         ]
-    hops = []
-    for pairs in steps:
-        payload = add_packed(one, near, *hops)
-        hops.append(
-            lax.ppermute(payload, "seq", [(2 * a + y, 2 * b + y) for a, b in pairs for y in (0, 1)])
-        )
-    far = swapped(add_packed(1 - lax.rem(where, 2), *hops), 0)
+
+    def prefix(where, key_len, key_rows, value_rows):
+        send, keep = pl.pallas_call(
+            functools.partial(block_sums_kernel, heads, width),
+            in_specs=[smem, smem, vmem, vmem],
+            out_specs=[vmem, vmem],
+            out_shape=[packed, jax.ShapeDtypeStruct((rows + extra, width), F32)],
+            compiler_params=params(),
+            name="block_sums",
+        )(where, key_len, key_rows, value_rows)
+        near = swapped(send, 0)
+
+        def add_packed(flag, *parts):
+            return pl.pallas_call(
+                functools.partial(add_packed_kernel, rows, extra, len(parts)),
+                in_specs=[smem] + [vmem] * (1 + len(parts)),
+                out_specs=vmem,
+                out_shape=packed,
+                compiler_params=params(),
+                name="add_packed",
+            )(flag, keep, *parts)
+
+        one = jnp.ones((1,), jnp.int32)
+        hops = []
+        for pairs in steps:
+            payload = add_packed(one, near, *hops)
+            hops.append(
+                lax.ppermute(payload, "seq", [(2 * a + y, 2 * b + y) for a, b in pairs for y in (0, 1)])
+            )
+        far = swapped(add_packed(1 - lax.rem(where, 2), *hops), 0)
+        return near, far, *hops
+
+    def nothing(*_):
+        return tuple(jnp.zeros(packed.shape, packed.dtype) for _ in range(2 + len(steps)))
+
+    near, far, *hops = lax.cond(key_len[0] > 0, prefix, nothing, where, key_len, key_rows, value_rows)
 
     a_step = math.gcd(HEADS_A_STEP, half_heads)
     grid = (heads // a_step,)
     wide = pl.BlockSpec((row_count, a_step * width), lambda i, *_: (0, i))
+    paired = pl.BlockSpec(
+        (None, row_count, a_step * width), lambda i, where, *_: (1 - lax.rem(where[0], 2), 0, i)
+    )
     narrow = pl.BlockSpec((row_count, 128), lambda i, *_: (0, i))
     whole = pl.BlockSpec(packed.shape, lambda i, *_: (0, 0))
     full = jax.ShapeDtypeStruct((row_count, columns), BF16)
@@ -262,7 +276,7 @@
         grid_spec=pltpu.PrefetchScalarGridSpec(
             num_scalar_prefetch=3,
             grid=grid,
-            in_specs=[wide] * (1 + levels + 1 + 2) + [whole] * (len(hops) + 2),
+            in_specs=[wide, wide, paired] + [wide] * late + [wide, paired] + [whole] * (len(hops) + 2),
             out_specs=[wide] * late + [narrow, wide],
         ),
         out_shape=[full] * late
@@ -271,6 +285,7 @@
             jax.ShapeDtypeStruct((row_count, columns), F32),
         ],
         compiler_params=params(),
+        cost_estimate=pl.CostEstimate(flops=1, bytes_accessed=1, transcendentals=1),
         name="scores",
     )(
         where,
@@ -278,9 +293,10 @@
         linear_scale,
         query_rows,
         key_rows,
-        *[far_keys[level] for level in range(levels)],
+        both_keys,
+        *[far_keys[level] for level in range(1, levels)],
         value_rows,
-        far_values[0],
+        both_values,
         *hops,
         near,
         far,

time: 113 us -> 146 us (1.29)
  the two profiles are of different devices: /device:TPU:0 before, /device:TPU:28 now
where the time goes in v2:
time: 146 us
  waiting for transfers between devices  96.3 us (66%)
  Pallas kernels  22.4 us (15%)
  between operations  13.5 us (9%)
  starting transfers between devices  10.5 us (7%)
  local copies, waits for them, and re-layouts  2.83 us (2%)
    ppermute x3, waiting for transfers between devices, prefix(): lax.ppermute(payload, 'seq', [(2 * a + y, 2 * b + y) for a, b in pairs fo...  68.1 us
    ppermute x6, waiting for transfers between devices, swapped(): return lax.ppermute(x, 'seq', [(i, i ^ 1 << level) for i in range(count)])  26.8 us
    pallas_call x1, Pallas kernels, shards(): pl.pallas_call(functools.partial(scores_kernel, heads, width, levels, len...  12.3 us
    ppermute x6, starting transfers between devices, swapped(): return lax.ppermute(x, 'seq', [(i, i ^ 1 << level) for i in range(count)])  6.16 us
    ppermute x3, starting transfers between devices, prefix(): lax.ppermute(payload, 'seq', [(2 * a + y, 2 * b + y) for a, b in pairs fo...  4.28 us
    pallas_call x4, Pallas kernels, add_packed(): pl.pallas_call(functools.partial(add_packed_kernel, rows, extra, len(part...  4.04 us
    pallas_call x1, Pallas kernels, shards(): pl.pallas_call(functools.partial(finish_kernel, late, width), grid=grid,...  3.24 us
  transfers between devices with their start and end apart: 11, of which 3 were waited for; matrix products, arithmetic and copies ran while one was open for 0% of the time, Pallas kernels for 13%

profile of v2, /device:TPU:28, one launch (start us, length us, event | category | flops | bytes accessed | tf_op | source)
XLA Modules:
  0.0 145.6 jit_solution(3131890072159195761)
XLA Ops:
  6.5 0.0 copy-start.6
  6.5 0.0 all-gather.5.cloned.1.call-start
  6.5 0.7 all-gather.5.cloned.1.call-update
  7.3 0.0 all-gather.7.cloned.1.call-start
  7.3 0.7 all-gather.7.cloned.1.call-update
  8.0 0.5 collective-permute-start.5
  8.5 0.3 collective-permute-start.6
  8.9 1.6 %collective-permute-start.7 = (bf16[128,3072]{1,0:T(8,128)(2,1)}, bf16[128,3072]{1,0:T(8,128)(2,1)S(1)}, u32[]{:S(2)}, u32[]{:S(2)}) collective-permute-start(bf16[128,3072]{1,0:T(8,128)(2,1)} %refs_5_.1), channel_id=1, source_target_pairs={{0,4},{2,6},{4,0},{6,2},{8,12},{10,14},{12,8},{14,10},{1,5},{3,7},... | collective-permute-start | bytes 2359304 | tf_op jit(solution)/shard_map/ppermute | solution.py:211
  10.4 2.6 %collective-permute-start.8 = (bf16[128,3072]{1,0:T(8,128)(2,1)}, bf16[128,3072]{1,0:T(8,128)(2,1)S(1)}, u32[]{:S(2)}, u32[]{:S(2)}) collective-permute-start(bf16[128,3072]{1,0:T(8,128)(2,1)} %refs_5_.1), channel_id=1, source_target_pairs={{0,8},{2,10},{4,12},{6,14},{8,0},{10,2},{12,4},{14,6},{1,9},{3,11}... | collective-permute-start | bytes 2359304 | tf_op jit(solution)/shard_map/ppermute | solution.py:211
  13.0 0.0 copy-done.6
  13.1 0.0 copy-start.2
  13.1 0.0 copy-start.3
  13.1 107.2 %conditional.1 = (bf16[1584,128]{1,0:T(8,128)(2,1)S(1)}, bf16[1584,128]{1,0:T(8,128)(2,1)}, bf16[1584,128]{1,0:T(8,128)(2,1)}, bf16[1584,128]{1,0:T(8,128)(2,1)}, bf16[1584,128]{1,0:T(8,128)(2,1)}) conditional(s32[]{:T(128)} %bitcast.3, () %tuple.13, (s32[1]{0:T(128)}, s32[8]{0:T(128)}, bf16[128,3072]{1,0:T(8,128)(2,1)}, ...), branch_computations={%region_0.0_spmd, %region_1.0_spmd} | conditional | flops 7 | bytes 11354483 | solution.py:263
  13.1 2.8 %block_sums.1 = (bf16[1584,128]{1,0:T(8,128)(2,1)S(1)}, f32[1552,128]{1,0:T(8,128)S(1)}) custom-call(s32[1]{0:T(128)} %get-tuple-element.13.where, s32[8]{0:T(128)} %get-tuple-element.14.lengths, bf16[128,3072]{1,0:T(8,128)(2,1)} %get-tuple-element.15.k_ref, bf16[128,3072]{1,0:T(8,128)(2,1)} %get-tuple-element.16.v_ref), custom_call_target="tpu_custom_call" | custom-call | tf_op jit(solution)/shard_map/cond/branch_1_fun/block_sums/pallas_call | solution.py:230
  15.9 0.6 collective-permute-start
  16.5 18.2 %collective-permute-done.refs_0_ = bf16[1584,128]{1,0:T(8,128)(2,1)S(1)} collective-permute-done((bf16[1584,128]{1,0:T(8,128)(2,1)S(1)}, bf16[1584,128]{1,0:T(8,128)(2,1)S(1)}, u32[]{:S(2)}, u32[]{:S(2)}) %collective-permute-start) | collective-permute-done | bytes 405536 | tf_op jit(solution)/shard_map/cond/branch_1_fun/ppermute | solution.py:211
  34.6 0.0 copy-start.4
  34.6 0.1 add_packed.4
  34.8 1.4 collective-permute-start.1
  36.2 0.0 collective-permute-done.1.refs_1_.refs_0_
  36.2 1.2 add_packed.5
  37.3 1.4 collective-permute-start.2
  38.8 0.0 collective-permute-done.2.refs_2_.refs_1_
  38.8 0.0 copy-done.4
  38.8 1.3 add_packed.6
  40.1 0.0 copy-start.5
  40.1 1.4 collective-permute-start.3
  41.6 68.1 %collective-permute-done.3.refs_2_ = bf16[1584,128]{1,0:T(8,128)(2,1)} collective-permute-done((bf16[1584,128]{1,0:T(8,128)(2,1)S(1)}, bf16[1584,128]{1,0:T(8,128)(2,1)}, u32[]{:S(2)}, u32[]{:S(2)}) %collective-permute-start.3) | collective-permute-done | bytes 405536 | tf_op jit(solution)/shard_map/cond/branch_1_fun/ppermute | solution.py:255
  109.7 1.4 add_packed.7
  111.1 0.6 collective-permute-start.4
  111.7 8.6 %collective-permute-done.4 = bf16[1584,128]{1,0:T(8,128)(2,1)} collective-permute-done((bf16[1584,128]{1,0:T(8,128)(2,1)S(1)}, bf16[1584,128]{1,0:T(8,128)(2,1)}, u32[]{:S(2)}, u32[]{:S(2)}) %collective-permute-start.4) | collective-permute-done | bytes 405536 | tf_op jit(solution)/shard_map/cond/branch_1_fun/ppermute | solution.py:211
  120.3 0.0 copy-done.5
  120.3 0.0 collective-permute-done.5.refs_3_
  120.3 0.0 collective-permute-done.6.refs_4_
  120.3 0.0 all-gather.5.cloned.1.call-done
  120.3 0.0 all-gather.7.cloned.1.call-done
  120.3 0.0 copy-done.2
  120.3 0.0 copy-done.3
  120.3 0.0 copy-start
  120.3 1.4 copy-done
  121.7 0.0 copy-start.1
  121.8 1.4 copy-done.1
  123.2 12.3 %scores.1 = (bf16[128,3072]{1,0:T(8,128)(2,1)S(1)}, bf16[128,3072]{1,0:T(8,128)(2,1)S(1)}, f32[128,768]{1,0:T(8,128)S(1)}, f32[128,3072]{1,0:T(8,128)S(1)}) custom-call(s32[1]{0:T(128)} %bitcast.where, s32[8]{0:T(128)} %lengths.1, f32[24]{0:T(128)S(1)} %copy-done.3, bf16[128,3072]{1,0:T(8,128)(2,1)S(1)} %copy-done.2, bf16[128,3072]{1,0:T(8,128)(2,1)} %refs_1_.1, ...), custom_call_target="tpu_custom_call" | custom-call | flops 1 | bytes 1 | tf_op jit(solution)/shard_map/scores/pallas_call | solution.py:274
  135.5 0.0 collective-permute-done.7.refs_2_
  135.5 0.0 collective-permute-done.8.refs_3_
  135.5 3.2 %finish.1 = bf16[128,3072]{1,0:T(8,128)(2,1)} custom-call(f32[128,768]{1,0:T(8,128)S(1)} %get-tuple-element.33.factor_ref, f32[128,3072]{1,0:T(8,128)S(1)} %get-tuple-element.34.base_ref, bf16[128,3072]{1,0:T(8,128)(2,1)S(1)} %get-tuple-element.35.refs_0_, bf16[128,3072]{1,0:T(8,128)(2,1)S(1)} %get-tuple-element.36.refs_1_, ...), custom_call_target="tpu_custom_call" | custom-call | tf_op jit(solution)/shard_map/finish/pallas_call | solution.py:304
Async XLA Ops:
  6.5 6.5 %copy-start.6 = (s32[8]{0:T(128)S(1)}, s32[8]{0:T(128)}, u32[]{:S(2)}) copy-start(s32[8]{0:T(128)} %lengths.1) | copy-start | bytes 100
  6.5 113.7 %all-gather.5.cloned.1.call-start = ((), (), s32[]{:S(2)}) async-start(), calls=%async_computation | async-start | bytes 2359296 | tf_op jit(solution)/shard_map/all_gather | solution.py:216
  7.3 113.1 %all-gather.7.cloned.1.call-start = ((), (), s32[]{:S(2)}) async-start(), calls=%async_computation.1 | async-start | bytes 2359296 | tf_op jit(solution)/shard_map/all_gather | solution.py:217
  8.0 112.2 %collective-permute-start.5 = (bf16[128,3072]{1,0:T(8,128)(2,1)}, bf16[128,3072]{1,0:T(8,128)(2,1)S(1)}, u32[]{:S(2)}, u32[]{:S(2)}) collective-permute-start(bf16[128,3072]{1,0:T(8,128)(2,1)} %refs_1_.1), channel_id=1, source_target_pairs={{0,4},{2,6},{4,0},{6,2},{8,12},{10,14},{12,8},{14,10},{1,5},{3,7},... | collective-permute-start | bytes 2359304 | tf_op jit(solution)/shard_map/ppermute | solution.py:211
  8.5 111.7 %collective-permute-start.6 = (bf16[128,3072]{1,0:T(8,128)(2,1)}, bf16[128,3072]{1,0:T(8,128)(2,1)}, u32[]{:S(2)}, u32[]{:S(2)}) collective-permute-start(bf16[128,3072]{1,0:T(8,128)(2,1)} %refs_1_.1), channel_id=1, source_target_pairs={{0,8},{2,10},{4,12},{6,14},{8,0},{10,2},{12,4},{14,6},{1,9},{3,11}... | collective-permute-start | bytes 2359304 | tf_op jit(solution)/shard_map/ppermute | solution.py:211
  8.9 126.6 %collective-permute-start.7 = (bf16[128,3072]{1,0:T(8,128)(2,1)}, bf16[128,3072]{1,0:T(8,128)(2,1)S(1)}, u32[]{:S(2)}, u32[]{:S(2)}) collective-permute-start(bf16[128,3072]{1,0:T(8,128)(2,1)} %refs_5_.1), channel_id=1, source_target_pairs={{0,4},{2,6},{4,0},{6,2},{8,12},{10,14},{12,8},{14,10},{1,5},{3,7},... | collective-permute-start | bytes 2359304 | tf_op jit(solution)/shard_map/ppermute | solution.py:211
  10.4 125.1 %collective-permute-start.8 = (bf16[128,3072]{1,0:T(8,128)(2,1)}, bf16[128,3072]{1,0:T(8,128)(2,1)S(1)}, u32[]{:S(2)}, u32[]{:S(2)}) collective-permute-start(bf16[128,3072]{1,0:T(8,128)(2,1)} %refs_5_.1), channel_id=1, source_target_pairs={{0,8},{2,10},{4,12},{6,14},{8,0},{10,2},{12,4},{14,6},{1,9},{3,11}... | collective-permute-start | bytes 2359304 | tf_op jit(solution)/shard_map/ppermute | solution.py:211
  13.1 107.3 %copy-start.2 = (bf16[128,3072]{1,0:T(8,128)(2,1)S(1)}, bf16[128,3072]{1,0:T(8,128)(2,1)}, u32[]{:S(2)}) copy-start(bf16[128,3072]{1,0:T(8,128)(2,1)} %refs_0_.1) | copy-start | bytes 2359300
  13.1 107.3 %copy-start.3 = (f32[24]{0:T(128)S(1)}, f32[24]{0:T(128)}, u32[]{:S(2)}) copy-start(f32[24]{0:T(128)} %scale.1) | copy-start | bytes 292
  15.9 18.8 %collective-permute-start = (bf16[1584,128]{1,0:T(8,128)(2,1)S(1)}, bf16[1584,128]{1,0:T(8,128)(2,1)S(1)}, u32[]{:S(2)}, u32[]{:S(2)}) collective-permute-start(bf16[1584,128]{1,0:T(8,128)(2,1)S(1)} %get-tuple-element.17), channel_id=1, source_target_pairs={{0,2},{2,0},{4,6},{6,4},{8,10},{10,8},{12,14},{14,12},{1,3},{3,1},... | collective-permute-start | bytes 1216520 | tf_op jit(solution)/shard_map/cond/branch_1_fun/ppermute | solution.py:211
  34.6 4.1 %copy-start.4 = (bf16[1584,128]{1,0:T(8,128)(2,1)}, bf16[1584,128]{1,0:T(8,128)(2,1)S(1)}, u32[]{:S(2)}) copy-start(bf16[1584,128]{1,0:T(8,128)(2,1)S(1)} %collective-permute-done.refs_0_) | copy-start | bytes 1216516 | tf_op jit(solution)/shard_map/cond
  34.8 1.4 collective-permute-start.1
  37.3 1.4 collective-permute-start.2
  40.1 80.1 %copy-start.5 = (bf16[1584,128]{1,0:T(8,128)(2,1)S(1)}, bf16[1584,128]{1,0:T(8,128)(2,1)}, u32[]{:S(2)}) copy-start(bf16[1584,128]{1,0:T(8,128)(2,1)} %copy-done.4) | copy-start | bytes 1216516 | tf_op jit(solution)/shard_map/cond
  40.1 69.6 %collective-permute-start.3 = (bf16[1584,128]{1,0:T(8,128)(2,1)S(1)}, bf16[1584,128]{1,0:T(8,128)(2,1)}, u32[]{:S(2)}, u32[]{:S(2)}) collective-permute-start(bf16[1584,128]{1,0:T(8,128)(2,1)S(1)} %add_packed.6), channel_id=1, source_target_pairs={{8,12},{10,14},{9,13},{11,15},{24,28},{26,30},{25,29},{27,31}} | collective-permute-start | bytes 1216520 | tf_op jit(solution)/shard_map/cond/branch_1_fun/ppermute | solution.py:255
  111.1 9.1 %collective-permute-start.4 = (bf16[1584,128]{1,0:T(8,128)(2,1)S(1)}, bf16[1584,128]{1,0:T(8,128)(2,1)}, u32[]{:S(2)}, u32[]{:S(2)}) collective-permute-start(bf16[1584,128]{1,0:T(8,128)(2,1)S(1)} %add_packed.7), channel_id=1, source_target_pairs={{0,2},{2,0},{4,6},{6,4},{8,10},{10,8},{12,14},{14,12},{1,3},{3,1},... | collective-permute-start | bytes 1216520 | tf_op jit(solution)/shard_map/cond/branch_1_fun/ppermute | solution.py:211
  120.3 1.4 copy-start
  121.7 1.4 copy-start.1
Sparse Core Ops, SparseCore 0:
  8.9 34.1 all-gather.4
  44.6 27.2 all-gather.6

commit v3 on v1

--- a/solution.py
+++ b/solution.py
@@ -99,39 +99,37 @@
     store_packed(refs[count], main, sums)
 
 
-def scores_kernel(heads, width, levels, hops, tokens, where, lengths, scale, *refs):
-    step = pl.program_id(0)
-    refs = list(refs)
-    q_ref = refs.pop(0)
-    key_refs = [refs.pop(0) for _ in range(levels + 1)]
-    value_refs = [refs.pop(0) for _ in range(2)]
-    hop_refs = [refs.pop(0) for _ in range(hops)]
-    near_ref, far_ref = refs.pop(0), refs.pop(0)
-    weight_refs = [refs.pop(0) for _ in range(levels - 1)]
-    factor_ref, base_ref = refs
-    me = where[0]
-    side = lax.rem(me, 2)
-    half_heads = heads // 2
-    rows, extra = half_heads * width, padded(half_heads)
+def partners(me, levels):
+    if levels != 3:
+        return [me] + [jnp.bitwise_xor(me, 1 << level) for level in range(levels)]
+    pair = me // 2
+    inner = lax.rem(pair + pair // 2, 2)
+    return [me, jnp.bitwise_xor(me, 1), jnp.bitwise_xor(me, 4 - 2 * inner), jnp.bitwise_xor(me, 2 + 2 * inner)]
+
+
+def exchanges(levels):
+    count = 1 << levels
+    if levels != 3:
+        return [[(i, i ^ 1 << level) for i in range(count)] for level in range(1, levels)]
+    cycle = [(0, 1), (1, 3), (3, 2), (2, 0)]
+    return [
+        [(2 * a + y, 2 * b + y) for a, b in cycle for y in (0, 1)],
+        [(2 * b + y, 2 * a + y) for a, b in cycle for y in (0, 1)],
+    ]
+
+
+def scores_kernel(width, levels, where, lengths, q_ref, *refs):
+    key_refs, refs = refs[: levels + 1], refs[levels + 1 :]
+    value_refs, refs = refs[:2], refs[2:]
+    weight_refs, (factor_ref, base_ref) = refs[: levels - 1], refs[levels - 1 :]
     row_count = q_ref.shape[0]
     a_step = q_ref.shape[1] // width
-    first = step * a_step
     column = lax.broadcasted_iota(jnp.int32, (row_count, row_count), 1)
     row = lax.broadcasted_iota(jnp.int32, (row_count, row_count), 0)
-    allowed = []
-    for which in range(levels + 1):
-        partner = me if which == 0 else jnp.bitwise_xor(me, 1 << (which - 1))
-        fits = column < lengths[partner]
-        allowed.append(fits & (column <= row) if which == 0 else fits)
+    allowed = [column < lengths[partner] for partner in partners(where[0], levels)]
+    allowed[0] = allowed[0] & (column <= row)
     lane = lax.broadcasted_iota(jnp.int32, (row_count, 128), 1)
     factors = jnp.zeros((row_count, 128), F32)
-    mine = (first // half_heads == side).astype(F32)
-    upper = mine * side.astype(F32)
-    in_half = lax.rem(first, half_heads)
-    sums = (1.0 - mine) * packed_sums(far_ref, rows, extra) + upper * packed_sums(near_ref, rows, extra)
-    for ref in hop_refs:
-        sums = sums + mine * packed_sums(ref, rows, extra)
-    sum_row = lax.broadcasted_iota(jnp.int32, sums.shape, 0)
     for h in range(a_step):
         at = slice(h * width, (h + 1) * width)
         queries = q_ref[:, at]
@@ -151,15 +149,34 @@
         whole = functools.reduce(jnp.add, [a * b for a, b in zip(shares, totals)])
         shares = [share / whole for share in shares]
         base = shares[0] * jnp.dot(weights[0], value_refs[0][:, at], preferred_element_type=F32)
-        base = base + shares[1] * jnp.dot(weights[1], value_refs[1][:, at], preferred_element_type=F32)
+        base_ref[:, at] = base + shares[1] * jnp.dot(weights[1], value_refs[1][:, at], preferred_element_type=F32)
         for which in range(2, levels + 1):
             weight_refs[which - 2][:, at] = weights[which]
             factors = jnp.where(lane == (which - 2) * a_step + h, shares[which], factors)
+    factor_ref[...] = factors
+
+
+def linear_kernel(heads, width, hops, tokens, where, scale, q_ref, *refs):
+    hop_refs, (near_ref, far_ref, out_ref) = refs[:hops], refs[hops:]
+    side = lax.rem(where[0], 2)
+    half_heads = heads // 2
+    rows, extra = half_heads * width, padded(half_heads)
+    a_step = q_ref.shape[1] // width
+    first = pl.program_id(0) * a_step
+    mine = (first // half_heads == side).astype(F32)
+    upper = mine * side.astype(F32)
+    in_half = lax.rem(first, half_heads)
+    sums = (1.0 - mine) * packed_sums(far_ref, rows, extra) + upper * packed_sums(near_ref, rows, extra)
+    for ref in hop_refs:
+        sums = sums + mine * packed_sums(ref, rows, extra)
+    sum_row = lax.broadcasted_iota(jnp.int32, sums.shape, 0)
+    for h in range(a_step):
+        at = slice(h * width, (h + 1) * width)
         block = pl.ds(pl.multiple_of((in_half + h) * width, width), width)
         prefix = (1.0 - mine) * far_ref[block, :].astype(F32) + upper * near_ref[block, :].astype(F32)
         for ref in hop_refs:
             prefix = prefix + mine * ref[block, :].astype(F32)
-        mapped = feature(queries.astype(F32))
+        mapped = feature(q_ref[:, at].astype(F32))
         high, low = halves(mapped)
         prefix_high, prefix_low = halves(prefix)
         linear = jnp.dot(
@@ -169,16 +186,15 @@
         ) + jnp.dot(high, prefix_low, preferred_element_type=F32)
         value_sum = jnp.sum(jnp.where(sum_row == in_half + h, sums, 0.0), axis=0, keepdims=True)
         linear = linear + jnp.sum(mapped, axis=1, keepdims=True) * (CENTER * value_sum)
-        base_ref[:, at] = base + linear * (scale[first + h] * (1.0 / (width * math.sqrt(tokens))))
-    factor_ref[...] = factors
-
-
-def finish_kernel(late, width, factor_ref, base_ref, *refs):
+        out_ref[:, at] = linear * (scale[first + h] * (1.0 / (width * math.sqrt(tokens))))
+
+
+def finish_kernel(late, width, factor_ref, base_ref, linear_ref, *refs):
     out_ref = refs[2 * late]
     a_step = base_ref.shape[1] // width
     for h in range(a_step):
         at = slice(h * width, (h + 1) * width)
-        total = base_ref[:, at]
+        total = base_ref[:, at] + linear_ref[:, at]
         for which in range(late):
             lane = which * a_step + h
             total = total + factor_ref[:, lane : lane + 1] * jnp.dot(
@@ -207,24 +223,44 @@
     smem = pl.BlockSpec(memory_space=pltpu.SMEM)
     vmem = pl.BlockSpec(memory_space=pltpu.VMEM)
 
-    def swapped(x, level):
-        return lax.ppermute(x, "seq", [(i, i ^ 1 << level) for i in range(count)])
-
-    order = list(range(levels - 1, -1, -1))
-    far_keys = {level: swapped(key_rows, level) for level in order}
-    far_values = {level: swapped(value_rows, level) for level in order}
-
-    send, keep = pl.pallas_call(
-        functools.partial(block_sums_kernel, heads, width),
-        in_specs=[smem, smem, vmem, vmem],
-        out_specs=[vmem, vmem],
-        out_shape=[packed, jax.ShapeDtypeStruct((rows + extra, width), F32)],
-        compiler_params=params(),
-        name="block_sums",
-    )(where, key_len, key_rows, value_rows)
-    near = swapped(send, 0)
-
-    def add_packed(flag, *parts):
+    pairs_of_blocks = count // 2
+    if pairs_of_blocks <= 4:
+        steps = [[(z, z + 1)] for z in range(pairs_of_blocks - 1)]
+    else:
+        steps = [
+            [(z, z + (1 << d)) for z in range(pairs_of_blocks - (1 << d))]
+            for d in range((pairs_of_blocks - 1).bit_length())
+        ]
+    steps = [[(2 * a + y, 2 * b + y) for a, b in pairs for y in (0, 1)] for pairs in steps]
+    swaps = [(i, i ^ 1) for i in range(count)]
+    turns = exchanges(levels)
+
+    def moved(x, pairs):
+        return lax.ppermute(x, "seq", pairs)
+
+    def after(x, *done):
+        return lax.optimization_barrier((x, *done))[0]
+
+    def fenced(run, *operands):
+        shapes = jax.eval_shape(run, *operands)
+
+        def nothing(*_):
+            return jax.tree.map(lambda leaf: jnp.zeros(leaf.shape, leaf.dtype), shapes)
+
+        return lax.cond(key_len[0] > 0, run, nothing, *operands)
+
+    def block_sums(where, key_len, key_rows, value_rows):
+        send, keep = pl.pallas_call(
+            functools.partial(block_sums_kernel, heads, width),
+            in_specs=[smem, smem, vmem, vmem],
+            out_specs=[vmem, vmem],
+            out_shape=[packed, jax.ShapeDtypeStruct((rows + extra, width), F32)],
+            compiler_params=params(),
+            name="block_sums",
+        )(where, key_len, key_rows, value_rows)
+        return keep, moved(send, swaps)
+
+    def add_packed(flag, keep, *parts):
         return pl.pallas_call(
             functools.partial(add_packed_kernel, rows, extra, len(parts)),
             in_specs=[smem] + [vmem] * (1 + len(parts)),
@@ -235,21 +271,26 @@
         )(flag, keep, *parts)
 
     one = jnp.ones((1,), jnp.int32)
-    pairs_of_blocks = count // 2
-    if pairs_of_blocks <= 4:
-        steps = [[(z, z + 1)] for z in range(pairs_of_blocks - 1)]
-    else:
-        steps = [
-            [(z, z + (1 << d)) for z in range(pairs_of_blocks - (1 << d))]
-            for d in range((pairs_of_blocks - 1).bit_length())
-        ]
-    hops = []
-    for pairs in steps:
-        payload = add_packed(one, near, *hops)
+    far_keys = [moved(key_rows, turns[0])]
+    keep, near = fenced(block_sums, where, key_len, key_rows, value_rows)
+    near_keys = moved(after(key_rows, near), swaps)
+    near_values = moved(after(value_rows, near), swaps)
+    hops = [moved(add_packed(one, keep, after(near, *far_keys)), steps[0])]
+    far_values = [moved(after(value_rows, near), turns[0])]
+    far_keys += [moved(after(key_rows, hops[0]), turn) for turn in turns[1:]]
+    for pairs in steps[1:]:
         hops.append(
-            lax.ppermute(payload, "seq", [(2 * a + y, 2 * b + y) for a, b in pairs for y in (0, 1)])
+            fenced(
+                lambda keep, *parts: moved(add_packed(one, keep, *parts), pairs), keep, near, *hops
+            )
         )
-    far = swapped(add_packed(1 - lax.rem(where, 2), *hops), 0)
+    far_values += [moved(after(value_rows, hops[-1]), turn) for turn in turns[1:]]
+    far = fenced(
+        lambda flag, keep, *parts: moved(add_packed(flag, keep, *parts), swaps),
+        1 - lax.rem(where, 2),
+        keep,
+        *hops,
+    )
 
     a_step = math.gcd(HEADS_A_STEP, half_heads)
     grid = (heads // a_step,)
@@ -257,43 +298,40 @@
     narrow = pl.BlockSpec((row_count, 128), lambda i, *_: (0, i))
     whole = pl.BlockSpec(packed.shape, lambda i, *_: (0, 0))
     full = jax.ShapeDtypeStruct((row_count, columns), BF16)
+    full_f32 = jax.ShapeDtypeStruct((row_count, columns), F32)
     *weights, factors, base = pl.pallas_call(
-        functools.partial(scores_kernel, heads, width, levels, len(hops), tokens),
+        functools.partial(scores_kernel, width, levels),
         grid_spec=pltpu.PrefetchScalarGridSpec(
-            num_scalar_prefetch=3,
+            num_scalar_prefetch=2,
             grid=grid,
-            in_specs=[wide] * (1 + levels + 1 + 2) + [whole] * (len(hops) + 2),
+            in_specs=[wide] * (1 + levels + 1 + 2),
             out_specs=[wide] * late + [narrow, wide],
         ),
-        out_shape=[full] * late
-        + [
-            jax.ShapeDtypeStruct((row_count, grid[0] * 128), F32),
-            jax.ShapeDtypeStruct((row_count, columns), F32),
-        ],
+        out_shape=[full] * late + [jax.ShapeDtypeStruct((row_count, grid[0] * 128), F32), full_f32],
         compiler_params=params(),
         name="scores",
-    )(
-        where,
-        key_len,
-        linear_scale,
-        query_rows,
-        key_rows,
-        *[far_keys[level] for level in range(levels)],
-        value_rows,
-        far_values[0],
-        *hops,
-        near,
-        far,
-    )
+    )(where, key_len, query_rows, key_rows, near_keys, *far_keys, value_rows, near_values)
+    linear = pl.pallas_call(
+        functools.partial(linear_kernel, heads, width, len(hops), tokens),
+        grid_spec=pltpu.PrefetchScalarGridSpec(
+            num_scalar_prefetch=2,
+            grid=grid,
+            in_specs=[wide] + [whole] * (len(hops) + 2),
+            out_specs=wide,
+        ),
+        out_shape=full_f32,
+        compiler_params=params(),
+        name="linear",
+    )(where, linear_scale, query_rows, *hops, near, far)
     return pl.pallas_call(
         functools.partial(finish_kernel, late, width),
         grid=grid,
-        in_specs=[narrow, wide] + [wide] * (2 * late),
+        in_specs=[narrow, wide, wide] + [wide] * (2 * late),
         out_specs=wide,
         out_shape=full,
         compiler_params=params(),
         name="finish",
-    )(factors, base, *weights, *[far_values[level] for level in range(1, levels)])
+    )(factors, base, linear, *weights, *far_values)
 
 
 def solution(mesh):

time: 113 us -> 112 us (level)
  waiting for transfers between devices: 64.2 us -> 45.3 us
  Pallas kernels: 16.6 us -> 27.1 us
  starting transfers between devices: 28.4 us -> 37.2 us
  local copies, waits for them, and re-layouts: 2.94 us -> 1.51 us
    ppermute x11, waiting for transfers between devices: 64.2 us -> 45.3 us  [moved(): return lax.ppermute(x, 'seq', pairs)]
    ppermute x11, starting transfers between devices: 28.4 us -> 37.2 us  [moved(): return lax.ppermute(x, 'seq', pairs)]
    pallas_call x2 -> x3, Pallas kernels: 12.6 us -> 18.2 us  [the longest x1 10.8 us: shards(): pl.pallas_call(functools.partial(scores_kernel, width, levels), grid_spec...]
    pallas_call x4, Pallas kernels: 0.76 us -> 5.59 us  [add_packed(): pl.pallas_call(functools.partial(add_packed_kernel, rows, extra, len(part...]
    unnamed x12 -> x10, local copies, waits for them, and re-layouts: 2.94 us -> 0.76 us
  transfers between devices with their start and end apart: 11 -> 11, of which waited for: 5 -> 4; matrix products, arithmetic and copies ran while one was open for 0% -> 0% of each run, Pallas kernels for 10% -> 20%
where the time goes in v3:
time: 112 us
  waiting for transfers between devices  45.3 us (40%)
  starting transfers between devices  37.2 us (33%)
  Pallas kernels  27.1 us (24%)
  local copies, waits for them, and re-layouts  1.51 us (1%)
    ppermute x11, waiting for transfers between devices, moved(): return lax.ppermute(x, 'seq', pairs)  45.3 us
    ppermute x11, starting transfers between devices, moved(): return lax.ppermute(x, 'seq', pairs)  37.2 us
    pallas_call x1, Pallas kernels, shards(): pl.pallas_call(functools.partial(scores_kernel, width, levels), grid_spec...  10.8 us
    pallas_call x4, Pallas kernels, add_packed(): pl.pallas_call(functools.partial(add_packed_kernel, rows, extra, len(part...  5.59 us
    pallas_call x1, Pallas kernels, shards(): pl.pallas_call(functools.partial(linear_kernel, heads, width, len(hops),...  4.74 us
    pallas_call x1, Pallas kernels, shards(): pl.pallas_call(functools.partial(finish_kernel, late, width), grid=grid,...  3.32 us
    pallas_call x1, Pallas kernels, block_sums(): pl.pallas_call(functools.partial(block_sums_kernel, heads, width), in_spe...  2.71 us
  transfers between devices with their start and end apart: 11, of which 4 were waited for; matrix products, arithmetic and copies ran while one was open for 0% of the time, Pallas kernels for 20%

profile of v3, /device:TPU:0, one launch (start us, length us, event | category | flops | bytes accessed | tf_op | source)
XLA Modules:
  0.0 112.0 jit_solution(6556573572134748568)
XLA Ops:
  0.0 3.0 %collective-permute-start.5 = (bf16[128,3072]{1,0:T(8,128)(2,1)}, bf16[128,3072]{1,0:T(8,128)(2,1)S(1)}, u32[]{:S(2)}, u32[]{:S(2)}) collective-permute-start(bf16[128,3072]{1,0:T(8,128)(2,1)} %refs_0_.1), channel_id=1, source_target_pairs={{0,4},{2,6},{4,12},{6,14},{12,8},{14,10},{8,0},{10,2},{1,5},{3,7},... | collective-permute-start | bytes 2359304 | tf_op jit(solution)/shard_map/ppermute | solution.py:239
  3.7 13.7 %conditional.4 = (f32[1552,128]{1,0:T(8,128)S(1)}, bf16[1584,128]{1,0:T(8,128)(2,1)}) conditional(s32[]{:T(128)} %bitcast.1, () %tuple.37, (s32[1]{0:T(128)}, s32[8]{0:T(128)}, bf16[128,3072]{1,0:T(8,128)(2,1)}, bf16[128,3072]{1,0:T(8,128)(2,1)}) %tuple.38), branch_computations={%region_0.0_spmd, %region_1.0_spmd} | conditional | bytes 1622072 | solution.py:250
  3.7 2.7 %block_sums.1 = (bf16[1584,128]{1,0:T(8,128)(2,1)S(1)}, f32[1552,128]{1,0:T(8,128)S(1)}) custom-call(s32[1]{0:T(128)} %get-tuple-element.60.where, s32[8]{0:T(128)} %get-tuple-element.61.lengths, bf16[128,3072]{1,0:T(8,128)(2,1)} %get-tuple-element.62.k_ref, bf16[128,3072]{1,0:T(8,128)(2,1)} %get-tuple-element.63.v_ref), custom_call_target="tpu_custom_call" | custom-call | tf_op jit(solution)/shard_map/cond/branch_1_fun/block_sums/pallas_call | solution.py:253
  6.4 1.6 %collective-permute-start = (bf16[1584,128]{1,0:T(8,128)(2,1)S(1)}, bf16[1584,128]{1,0:T(8,128)(2,1)}, u32[]{:S(2)}, u32[]{:S(2)}) collective-permute-start(bf16[1584,128]{1,0:T(8,128)(2,1)S(1)} %get-tuple-element.65), channel_id=1, source_target_pairs={{0,2},{2,0},{4,6},{6,4},{8,10},{10,8},{12,14},{14,12},{1,3},{3,1},... | collective-permute-start | bytes 1216520 | tf_op jit(solution)/shard_map/cond/branch_1_fun/ppermute | solution.py:239
  8.0 9.4 %collective-permute-done = bf16[1584,128]{1,0:T(8,128)(2,1)} collective-permute-done((bf16[1584,128]{1,0:T(8,128)(2,1)S(1)}, bf16[1584,128]{1,0:T(8,128)(2,1)}, u32[]{:S(2)}, u32[]{:S(2)}) %collective-permute-start) | collective-permute-done | bytes 405536 | tf_op jit(solution)/shard_map/cond/branch_1_fun/ppermute | solution.py:239
  17.4 0.0 copy-start.2
  17.4 4.4 %collective-permute-done.5.refs_2_ = bf16[128,3072]{1,0:T(8,128)(2,1)S(1)} collective-permute-done((bf16[128,3072]{1,0:T(8,128)(2,1)}, bf16[128,3072]{1,0:T(8,128)(2,1)S(1)}, u32[]{:S(2)}, u32[]{:S(2)}) %collective-permute-start.5) | collective-permute-done | bytes 786464 | tf_op jit(solution)/shard_map/ppermute | solution.py:239
  21.8 1.1 add_packed.7
  22.9 2.9 %collective-permute-start.6 = (bf16[1584,128]{1,0:T(8,128)(2,1)S(1)}, bf16[1584,128]{1,0:T(8,128)(2,1)S(1)}, u32[]{:S(2)}, u32[]{:S(2)}) collective-permute-start(bf16[1584,128]{1,0:T(8,128)(2,1)S(1)} %add_packed.7), channel_id=1, source_target_pairs={{0,4},{2,6},{1,5},{3,7},{16,20},{18,22},{17,21},{19,23}} | collective-permute-start | bytes 1216520 | tf_op jit(solution)/shard_map/ppermute | solution.py:239
  25.8 1.6 %collective-permute-start.8 = (bf16[128,3072]{1,0:T(8,128)(2,1)}, bf16[128,3072]{1,0:T(8,128)(2,1)S(1)}, u32[]{:S(2)}, u32[]{:S(2)}) collective-permute-start(bf16[128,3072]{1,0:T(8,128)(2,1)} %refs_4_.1), channel_id=1, source_target_pairs={{0,2},{2,0},{4,6},{6,4},{8,10},{10,8},{12,14},{14,12},{1,3},{3,1},... | collective-permute-start | bytes 2359304 | tf_op jit(solution)/shard_map/ppermute | solution.py:239
  27.4 0.0 collective-permute-start.9
  27.4 0.5 collective-permute-start.4
  27.9 7.7 %collective-permute-done.6.refs_0_ = bf16[1584,128]{1,0:T(8,128)(2,1)S(1)} collective-permute-done((bf16[1584,128]{1,0:T(8,128)(2,1)S(1)}, bf16[1584,128]{1,0:T(8,128)(2,1)S(1)}, u32[]{:S(2)}, u32[]{:S(2)}) %collective-permute-start.6) | collective-permute-done | bytes 405536 | tf_op jit(solution)/shard_map/ppermute | solution.py:239
  35.6 0.0 copy-start.3
  35.6 0.0 collective-permute-start.7
  35.6 0.7 copy-done.3
  36.3 3.4 %conditional.5 = (bf16[1584,128]{1,0:T(8,128)(2,1)}) conditional(s32[]{:T(128)} %bitcast.1, () %tuple.43, (f32[1552,128]{1,0:T(8,128)S(1)}, bf16[1584,128]{1,0:T(8,128)(2,1)}, bf16[1584,128]{1,0:T(8,128)(2,1)S(1)}) %tuple.44), branch_computations={%region_2.0_spmd, %region_3.0_spmd} | conditional | bytes 3244108 | solution.py:250
  36.3 0.0 copy-start.4
  36.3 0.7 copy-done.4
  37.1 1.3 %add_packed.4 = bf16[1584,128]{1,0:T(8,128)(2,1)S(1)} custom-call(s32[1]{0:T(128)} %constant.17.clone.where, f32[1552,128]{1,0:T(8,128)S(1)} %get-tuple-element.66.keep_ref, bf16[1584,128]{1,0:T(8,128)(2,1)} %get-tuple-element.67.refs_0_, bf16[1584,128]{1,0:T(8,128)(2,1)} %copy-done.4), custom_call_target="tpu_custom_call" | custom-call | tf_op jit(solution)/shard_map/cond/branch_1_fun/add_packed/pallas_call | solution.py:264
  38.3 1.4 %collective-permute-start.1 = (bf16[1584,128]{1,0:T(8,128)(2,1)S(1)}, bf16[1584,128]{1,0:T(8,128)(2,1)}, u32[]{:S(2)}, u32[]{:S(2)}) collective-permute-start(bf16[1584,128]{1,0:T(8,128)(2,1)S(1)} %add_packed.4), channel_id=1, source_target_pairs={{4,8},{6,10},{5,9},{7,11},{20,24},{22,26},{21,25},{23,27}} | collective-permute-start | bytes 1216520 | tf_op jit(solution)/shard_map/cond/branch_1_fun/ppermute | solution.py:239
  39.7 0.0 collective-permute-done.1
  39.7 0.0 copy-done.2
  39.8 2.9 %conditional.6 = (bf16[1584,128]{1,0:T(8,128)(2,1)}) conditional(s32[]{:T(128)} %bitcast.1, () %tuple.45, (f32[1552,128]{1,0:T(8,128)S(1)}, bf16[1584,128]{1,0:T(8,128)(2,1)}, bf16[1584,128]{1,0:T(8,128)(2,1)}, bf16[1584,128]{1,0:T(8,128)(2,1)}) %tuple.59), branch_computations={%region_4.0_spmd, %region_5.0_spmd} | conditional | bytes 1622064 | solution.py:250
  39.8 1.5 %add_packed.5 = bf16[1584,128]{1,0:T(8,128)(2,1)S(1)} custom-call(s32[1]{0:T(128)} %constant.25.clone.where, f32[1552,128]{1,0:T(8,128)S(1)} %get-tuple-element.69.keep_ref, bf16[1584,128]{1,0:T(8,128)(2,1)} %get-tuple-element.70.refs_0_, bf16[1584,128]{1,0:T(8,128)(2,1)} %get-tuple-element.71.refs_1_, bf16[1584,128]{1,0:T(8,128)(2,1)} %get-tuple-element.72.refs_2_), custom_call_target="tpu_custom_call" | custom-call | tf_op jit(solution)/shard_map/cond/branch_1_fun/add_packed/pallas_call | solution.py:264
  41.2 1.4 %collective-permute-start.2 = (bf16[1584,128]{1,0:T(8,128)(2,1)S(1)}, bf16[1584,128]{1,0:T(8,128)(2,1)}, u32[]{:S(2)}, u32[]{:S(2)}) collective-permute-start(bf16[1584,128]{1,0:T(8,128)(2,1)S(1)} %add_packed.5), channel_id=1, source_target_pairs={{8,12},{10,14},{9,13},{11,15},{24,28},{26,30},{25,29},{27,31}} | collective-permute-start | bytes 1216520 | tf_op jit(solution)/shard_map/cond/branch_1_fun/ppermute | solution.py:239
  42.6 0.0 collective-permute-done.2
  42.6 0.0 copy-start
  42.6 0.0 copy-start.1
  42.6 27.2 %conditional.7 = (bf16[1584,128]{1,0:T(8,128)(2,1)}) conditional(s32[]{:T(128)} %bitcast.1, () %tuple.47, (s32[1]{0:T(128)}, f32[1552,128]{1,0:T(8,128)}, bf16[1584,128]{1,0:T(8,128)(2,1)}, bf16[1584,128]{1,0:T(8,128)(2,1)}, bf16[1584,128]{1,0:T(8,128)(2,1)}) %tuple.60), branch_computations={%region_6.0_spmd, %region_7.0_spmd} | conditional | flops 7 | bytes 1622139 | solution.py:250
  42.6 1.8 %add_packed.6 = bf16[1584,128]{1,0:T(8,128)(2,1)S(1)} custom-call(s32[1]{0:T(128)S(6)} %sub.3.where, f32[1552,128]{1,0:T(8,128)} %get-tuple-element.74.keep_ref, bf16[1584,128]{1,0:T(8,128)(2,1)} %get-tuple-element.75.refs_0_, bf16[1584,128]{1,0:T(8,128)(2,1)} %get-tuple-element.76.refs_1_, bf16[1584,128]{1,0:T(8,128)(2,1)} %get-tuple-element.77.refs_2_), custom_call_target="tpu_custom_call" | custom-call | tf_op jit(solution)/shard_map/cond/branch_1_fun/add_packed/pallas_call | solution.py:264
  44.4 1.6 %collective-permute-start.3 = (bf16[1584,128]{1,0:T(8,128)(2,1)S(1)}, bf16[1584,128]{1,0:T(8,128)(2,1)}, u32[]{:S(2)}, u32[]{:S(2)}) collective-permute-start(bf16[1584,128]{1,0:T(8,128)(2,1)S(1)} %add_packed.6), channel_id=1, source_target_pairs={{0,2},{2,0},{4,6},{6,4},{8,10},{10,8},{12,14},{14,12},{1,3},{3,1},... | collective-permute-start | bytes 1216520 | tf_op jit(solution)/shard_map/cond/branch_1_fun/ppermute | solution.py:239
  46.0 23.8 %collective-permute-done.3 = bf16[1584,128]{1,0:T(8,128)(2,1)} collective-permute-done((bf16[1584,128]{1,0:T(8,128)(2,1)S(1)}, bf16[1584,128]{1,0:T(8,128)(2,1)}, u32[]{:S(2)}, u32[]{:S(2)}) %collective-permute-start.3) | collective-permute-done | bytes 405536 | tf_op jit(solution)/shard_map/cond/branch_1_fun/ppermute | solution.py:239
  69.8 0.0 copy-start.5
  69.8 23.2 %collective-permute-start.10 = (bf16[128,3072]{1,0:T(8,128)(2,1)}, bf16[128,3072]{1,0:T(8,128)(2,1)S(1)}, u32[]{:S(2)}, u32[]{:S(2)}) collective-permute-start(bf16[128,3072]{1,0:T(8,128)(2,1)} %refs_4_.1), channel_id=1, source_target_pairs={{4,0},{6,2},{12,4},{14,6},{8,12},{10,14},{0,8},{2,10},{5,1},{7,3},... | collective-permute-start | bytes 2359304 | tf_op jit(solution)/shard_map/ppermute | solution.py:239
  93.1 0.0 copy-done
  93.1 0.0 copy-done.1
  93.1 4.7 %linear.1.linear_ref = f32[128,3072]{1,0:T(8,128)S(1)} custom-call(s32[1]{0:T(128)} %bitcast.where, f32[24]{0:T(128)S(1)} %copy-done.1, bf16[128,3072]{1,0:T(8,128)(2,1)S(1)} %copy-done, bf16[1584,128]{1,0:T(8,128)(2,1)} %copy-done.3, bf16[1584,128]{1,0:T(8,128)(2,1)} %get-tuple-element.104.refs_1_, bf16[1584,128]{1,0:T(8,128)(2,1)} %get-tuple-element.105.refs_2_, ...), custom_call_target="tpu_custom_call" | custom-call | tf_op jit(solution)/shard_map/linear/pallas_call | solution.py:314
  97.8 0.0 collective-permute-done.4.refs_1_
  97.8 0.0 collective-permute-done.8.refs_5_
  97.8 0.0 collective-permute-done.7.refs_3_
  97.9 0.0 copy-done.5
  97.9 10.8 %scores.1 = (bf16[128,3072]{1,0:T(8,128)(2,1)S(1)}, bf16[128,3072]{1,0:T(8,128)(2,1)S(1)}, f32[128,768]{1,0:T(8,128)S(1)}, f32[128,3072]{1,0:T(8,128)S(1)}) custom-call(s32[1]{0:T(128)} %bitcast.where, s32[8]{0:T(128)S(1)} %copy-done.5, bf16[128,3072]{1,0:T(8,128)(2,1)S(1)} %copy-done, bf16[128,3072]{1,0:T(8,128)(2,1)} %refs_0_.1, ...), custom_call_target="tpu_custom_call" | custom-call | tf_op jit(solution)/shard_map/scores/pallas_call | solution.py:302
  108.6 0.0 collective-permute-done.9.refs_2_
  108.7 0.0 collective-permute-done.10.refs_3_
  108.7 3.3 %finish.1 = bf16[128,3072]{1,0:T(8,128)(2,1)} custom-call(f32[128,768]{1,0:T(8,128)S(1)} %get-tuple-element.95.factor_ref, f32[128,3072]{1,0:T(8,128)S(1)} %get-tuple-element.96.base_ref, f32[128,3072]{1,0:T(8,128)S(1)} %linear.1.linear_ref, bf16[128,3072]{1,0:T(8,128)(2,1)S(1)} %get-tuple-element.97.refs_0_, ...), custom_call_target="tpu_custom_call" | custom-call | tf_op jit(solution)/shard_map/finish/pallas_call | solution.py:326
Async XLA Ops:
  0.0 21.8 %collective-permute-start.5 = (bf16[128,3072]{1,0:T(8,128)(2,1)}, bf16[128,3072]{1,0:T(8,128)(2,1)S(1)}, u32[]{:S(2)}, u32[]{:S(2)}) collective-permute-start(bf16[128,3072]{1,0:T(8,128)(2,1)} %refs_0_.1), channel_id=1, source_target_pairs={{0,4},{2,6},{4,12},{6,14},{12,8},{14,10},{8,0},{10,2},{1,5},{3,7},... | collective-permute-start | bytes 2359304 | tf_op jit(solution)/shard_map/ppermute | solution.py:239
  6.4 11.0 %collective-permute-start = (bf16[1584,128]{1,0:T(8,128)(2,1)S(1)}, bf16[1584,128]{1,0:T(8,128)(2,1)}, u32[]{:S(2)}, u32[]{:S(2)}) collective-permute-start(bf16[1584,128]{1,0:T(8,128)(2,1)S(1)} %get-tuple-element.65), channel_id=1, source_target_pairs={{0,2},{2,0},{4,6},{6,4},{8,10},{10,8},{12,14},{14,12},{1,3},{3,1},... | collective-permute-start | bytes 1216520 | tf_op jit(solution)/shard_map/cond/branch_1_fun/ppermute | solution.py:239
  17.4 22.3 %copy-start.2 = (f32[1552,128]{1,0:T(8,128)}, f32[1552,128]{1,0:T(8,128)S(1)}, u32[]{:S(2)}) copy-start(f32[1552,128]{1,0:T(8,128)S(1)} %get-tuple-element.91.keep_ref) | copy-start | bytes 2383876
  22.9 12.7 %collective-permute-start.6 = (bf16[1584,128]{1,0:T(8,128)(2,1)S(1)}, bf16[1584,128]{1,0:T(8,128)(2,1)S(1)}, u32[]{:S(2)}, u32[]{:S(2)}) collective-permute-start(bf16[1584,128]{1,0:T(8,128)(2,1)S(1)} %add_packed.7), channel_id=1, source_target_pairs={{0,4},{2,6},{1,5},{3,7},{16,20},{18,22},{17,21},{19,23}} | collective-permute-start | bytes 1216520 | tf_op jit(solution)/shard_map/ppermute | solution.py:239
  25.8 72.1 %collective-permute-start.8 = (bf16[128,3072]{1,0:T(8,128)(2,1)}, bf16[128,3072]{1,0:T(8,128)(2,1)S(1)}, u32[]{:S(2)}, u32[]{:S(2)}) collective-permute-start(bf16[128,3072]{1,0:T(8,128)(2,1)} %refs_4_.1), channel_id=1, source_target_pairs={{0,2},{2,0},{4,6},{6,4},{8,10},{10,8},{12,14},{14,12},{1,3},{3,1},... | collective-permute-start | bytes 2359304 | tf_op jit(solution)/shard_map/ppermute | solution.py:239
  27.4 81.3 %collective-permute-start.9 = (bf16[128,3072]{1,0:T(8,128)(2,1)}, bf16[128,3072]{1,0:T(8,128)(2,1)S(1)}, u32[]{:S(2)}, u32[]{:S(2)}) collective-permute-start(bf16[128,3072]{1,0:T(8,128)(2,1)} %refs_4_.1), channel_id=1, source_target_pairs={{0,4},{2,6},{4,12},{6,14},{12,8},{14,10},{8,0},{10,2},{1,5},{3,7},... | collective-permute-start | bytes 2359304 | tf_op jit(solution)/shard_map/ppermute | solution.py:239
  27.4 70.5 %collective-permute-start.4 = (bf16[128,3072]{1,0:T(8,128)(2,1)}, bf16[128,3072]{1,0:T(8,128)(2,1)}, u32[]{:S(2)}, u32[]{:S(2)}) collective-permute-start(bf16[128,3072]{1,0:T(8,128)(2,1)} %refs_0_.1), channel_id=1, source_target_pairs={{0,2},{2,0},{4,6},{6,4},{8,10},{10,8},{12,14},{14,12},{1,3},{3,1},... | collective-permute-start | bytes 2359304 | tf_op jit(solution)/shard_map/ppermute | solution.py:239
  35.6 0.7 copy-start.3
  35.6 62.3 %collective-permute-start.7 = (bf16[128,3072]{1,0:T(8,128)(2,1)}, bf16[128,3072]{1,0:T(8,128)(2,1)}, u32[]{:S(2)}, u32[]{:S(2)}) collective-permute-start(bf16[128,3072]{1,0:T(8,128)(2,1)} %refs_0_.1), channel_id=1, source_target_pairs={{4,0},{6,2},{12,4},{14,6},{8,12},{10,14},{0,8},{2,10},{5,1},{7,3},... | collective-permute-start | bytes 2359304 | tf_op jit(solution)/shard_map/ppermute | solution.py:239
  36.3 0.7 copy-start.4
  38.3 1.4 %collective-permute-start.1 = (bf16[1584,128]{1,0:T(8,128)(2,1)S(1)}, bf16[1584,128]{1,0:T(8,128)(2,1)}, u32[]{:S(2)}, u32[]{:S(2)}) collective-permute-start(bf16[1584,128]{1,0:T(8,128)(2,1)S(1)} %add_packed.4), channel_id=1, source_target_pairs={{4,8},{6,10},{5,9},{7,11},{20,24},{22,26},{21,25},{23,27}} | collective-permute-start | bytes 1216520 | tf_op jit(solution)/shard_map/cond/branch_1_fun/ppermute | solution.py:239
  41.2 1.4 %collective-permute-start.2 = (bf16[1584,128]{1,0:T(8,128)(2,1)S(1)}, bf16[1584,128]{1,0:T(8,128)(2,1)}, u32[]{:S(2)}, u32[]{:S(2)}) collective-permute-start(bf16[1584,128]{1,0:T(8,128)(2,1)S(1)} %add_packed.5), channel_id=1, source_target_pairs={{8,12},{10,14},{9,13},{11,15},{24,28},{26,30},{25,29},{27,31}} | collective-permute-start | bytes 1216520 | tf_op jit(solution)/shard_map/cond/branch_1_fun/ppermute | solution.py:239
  42.6 50.4 %copy-start = (bf16[128,3072]{1,0:T(8,128)(2,1)S(1)}, bf16[128,3072]{1,0:T(8,128)(2,1)}, u32[]{:S(2)}) copy-start(bf16[128,3072]{1,0:T(8,128)(2,1)} %q_ref.3) | copy-start | bytes 2359300
  42.6 50.4 %copy-start.1 = (f32[24]{0:T(128)S(1)}, f32[24]{0:T(128)}, u32[]{:S(2)}) copy-start(f32[24]{0:T(128)} %scale.1) | copy-start | bytes 292
  44.4 25.4 %collective-permute-start.3 = (bf16[1584,128]{1,0:T(8,128)(2,1)S(1)}, bf16[1584,128]{1,0:T(8,128)(2,1)}, u32[]{:S(2)}, u32[]{:S(2)}) collective-permute-start(bf16[1584,128]{1,0:T(8,128)(2,1)S(1)} %add_packed.6), channel_id=1, source_target_pairs={{0,2},{2,0},{4,6},{6,4},{8,10},{10,8},{12,14},{14,12},{1,3},{3,1},... | collective-permute-start | bytes 1216520 | tf_op jit(solution)/shard_map/cond/branch_1_fun/ppermute | solution.py:239
  69.8 28.0 %copy-start.5 = (s32[8]{0:T(128)S(1)}, s32[8]{0:T(128)}, u32[]{:S(2)}) copy-start(s32[8]{0:T(128)} %lengths.1) | copy-start | bytes 100
  69.8 38.8 %collective-permute-start.10 = (bf16[128,3072]{1,0:T(8,128)(2,1)}, bf16[128,3072]{1,0:T(8,128)(2,1)S(1)}, u32[]{:S(2)}, u32[]{:S(2)}) collective-permute-start(bf16[128,3072]{1,0:T(8,128)(2,1)} %refs_4_.1), channel_id=1, source_target_pairs={{4,0},{6,2},{12,4},{14,6},{8,12},{10,14},{0,8},{2,10},{5,1},{7,3},... | collective-permute-start | bytes 2359304 | tf_op jit(solution)/shard_map/ppermute | solution.py:239

commit v4 on v3

--- a/solution.py
+++ b/solution.py
@@ -104,14 +104,14 @@
         return [me] + [jnp.bitwise_xor(me, 1 << level) for level in range(levels)]
     pair = me // 2
     inner = lax.rem(pair + pair // 2, 2)
-    return [me, jnp.bitwise_xor(me, 1), jnp.bitwise_xor(me, 4 - 2 * inner), jnp.bitwise_xor(me, 2 + 2 * inner)]
+    return [me, jnp.bitwise_xor(me, 1), jnp.bitwise_xor(me, 2 + 2 * inner), jnp.bitwise_xor(me, 4 - 2 * inner)]
 
 
 def exchanges(levels):
     count = 1 << levels
     if levels != 3:
         return [[(i, i ^ 1 << level) for i in range(count)] for level in range(1, levels)]
-    cycle = [(0, 1), (1, 3), (3, 2), (2, 0)]
+    cycle = [(0, 2), (2, 3), (3, 1), (1, 0)]
     return [
         [(2 * a + y, 2 * b + y) for a, b in cycle for y in (0, 1)],
         [(2 * b + y, 2 * a + y) for a, b in cycle for y in (0, 1)],
@@ -120,8 +120,8 @@
 
 def scores_kernel(width, levels, where, lengths, q_ref, *refs):
     key_refs, refs = refs[: levels + 1], refs[levels + 1 :]
-    value_refs, refs = refs[:2], refs[2:]
-    weight_refs, (factor_ref, base_ref) = refs[: levels - 1], refs[levels - 1 :]
+    value_ref, refs = refs[0], refs[1:]
+    weight_refs, (factor_ref, base_ref) = refs[:levels], refs[levels:]
     row_count = q_ref.shape[0]
     a_step = q_ref.shape[1] // width
     column = lax.broadcasted_iota(jnp.int32, (row_count, row_count), 1)
@@ -148,15 +148,14 @@
         shares = [jnp.exp(one - peak) for one in peaks]
         whole = functools.reduce(jnp.add, [a * b for a, b in zip(shares, totals)])
         shares = [share / whole for share in shares]
-        base = shares[0] * jnp.dot(weights[0], value_refs[0][:, at], preferred_element_type=F32)
-        base_ref[:, at] = base + shares[1] * jnp.dot(weights[1], value_refs[1][:, at], preferred_element_type=F32)
-        for which in range(2, levels + 1):
-            weight_refs[which - 2][:, at] = weights[which]
-            factors = jnp.where(lane == (which - 2) * a_step + h, shares[which], factors)
+        base_ref[:, at] = shares[0] * jnp.dot(weights[0], value_ref[:, at], preferred_element_type=F32)
+        for which in range(levels):
+            weight_refs[which][:, at] = weights[which + 1]
+            factors = jnp.where(lane == which * a_step + h, shares[which + 1], factors)
     factor_ref[...] = factors
 
 
-def linear_kernel(heads, width, hops, tokens, where, scale, q_ref, *refs):
+def linear_kernel(heads, width, hops, tokens, where, scale, q_ref, factor_ref, base_ref, weight_ref, value_ref, *refs):
     hop_refs, (near_ref, far_ref, out_ref) = refs[:hops], refs[hops:]
     side = lax.rem(where[0], 2)
     half_heads = heads // 2
@@ -186,17 +185,19 @@
         ) + jnp.dot(high, prefix_low, preferred_element_type=F32)
         value_sum = jnp.sum(jnp.where(sum_row == in_half + h, sums, 0.0), axis=0, keepdims=True)
         linear = linear + jnp.sum(mapped, axis=1, keepdims=True) * (CENTER * value_sum)
-        out_ref[:, at] = linear * (scale[first + h] * (1.0 / (width * math.sqrt(tokens))))
-
-
-def finish_kernel(late, width, factor_ref, base_ref, linear_ref, *refs):
+        near = jnp.dot(weight_ref[:, at], value_ref[:, at], preferred_element_type=F32)
+        total = base_ref[:, at] + factor_ref[:, h : h + 1] * near
+        out_ref[:, at] = total + linear * (scale[first + h] * (1.0 / (width * math.sqrt(tokens))))
+
+
+def finish_kernel(late, width, factor_ref, base_ref, *refs):
     out_ref = refs[2 * late]
     a_step = base_ref.shape[1] // width
     for h in range(a_step):
         at = slice(h * width, (h + 1) * width)
-        total = base_ref[:, at] + linear_ref[:, at]
+        total = base_ref[:, at]
         for which in range(late):
-            lane = which * a_step + h
+            lane = (which + 1) * a_step + h
             total = total + factor_ref[:, lane : lane + 1] * jnp.dot(
                 refs[which][:, at], refs[late + which][:, at], preferred_element_type=F32
             )
@@ -270,28 +271,6 @@
             name="add_packed",
         )(flag, keep, *parts)
 
-    one = jnp.ones((1,), jnp.int32)
-    far_keys = [moved(key_rows, turns[0])]
-    keep, near = fenced(block_sums, where, key_len, key_rows, value_rows)
-    near_keys = moved(after(key_rows, near), swaps)
-    near_values = moved(after(value_rows, near), swaps)
-    hops = [moved(add_packed(one, keep, after(near, *far_keys)), steps[0])]
-    far_values = [moved(after(value_rows, near), turns[0])]
-    far_keys += [moved(after(key_rows, hops[0]), turn) for turn in turns[1:]]
-    for pairs in steps[1:]:
-        hops.append(
-            fenced(
-                lambda keep, *parts: moved(add_packed(one, keep, *parts), pairs), keep, near, *hops
-            )
-        )
-    far_values += [moved(after(value_rows, hops[-1]), turn) for turn in turns[1:]]
-    far = fenced(
-        lambda flag, keep, *parts: moved(add_packed(flag, keep, *parts), swaps),
-        1 - lax.rem(where, 2),
-        keep,
-        *hops,
-    )
-
     a_step = math.gcd(HEADS_A_STEP, half_heads)
     grid = (heads // a_step,)
     wide = pl.BlockSpec((row_count, a_step * width), lambda i, *_: (0, i))
@@ -299,39 +278,67 @@
     whole = pl.BlockSpec(packed.shape, lambda i, *_: (0, 0))
     full = jax.ShapeDtypeStruct((row_count, columns), BF16)
     full_f32 = jax.ShapeDtypeStruct((row_count, columns), F32)
-    *weights, factors, base = pl.pallas_call(
-        functools.partial(scores_kernel, width, levels),
-        grid_spec=pltpu.PrefetchScalarGridSpec(
-            num_scalar_prefetch=2,
-            grid=grid,
-            in_specs=[wide] * (1 + levels + 1 + 2),
-            out_specs=[wide] * late + [narrow, wide],
-        ),
-        out_shape=[full] * late + [jax.ShapeDtypeStruct((row_count, grid[0] * 128), F32), full_f32],
-        compiler_params=params(),
-        name="scores",
-    )(where, key_len, query_rows, key_rows, near_keys, *far_keys, value_rows, near_values)
-    linear = pl.pallas_call(
+
+    def scores(where, key_len, query_rows, key_rows, value_rows, *keys):
+        return pl.pallas_call(
+            functools.partial(scores_kernel, width, levels),
+            grid_spec=pltpu.PrefetchScalarGridSpec(
+                num_scalar_prefetch=2,
+                grid=grid,
+                in_specs=[wide] * (1 + levels + 1 + 1),
+                out_specs=[wide] * levels + [narrow, wide],
+            ),
+            out_shape=[full] * levels + [jax.ShapeDtypeStruct((row_count, grid[0] * 128), F32), full_f32],
+            compiler_params=params(),
+            name="scores",
+        )(where, key_len, query_rows, key_rows, *keys, value_rows)
+
+    one = jnp.ones((1,), jnp.int32)
+    far_keys = [moved(key_rows, turns[0])]
+    keep, near = fenced(block_sums, where, key_len, key_rows, value_rows)
+    near_keys = moved(after(key_rows, near), swaps)
+    near_values = moved(after(value_rows, near), swaps)
+    hops = [moved(add_packed(one, keep, after(near, *far_keys)), steps[0])]
+    far_keys += [moved(after(key_rows, near), turn) for turn in turns[1:]]
+    hops.append(moved(add_packed(one, keep, near, *hops), steps[1]))
+    far_values = [moved(after(value_rows, *far_keys), turns[0])]
+    far_values += [moved(after(value_rows, *hops), turn) for turn in turns[1:]]
+
+    def last_hop(keep, parts, *operands):
+        for pairs in steps[2:]:
+            parts = [*parts, moved(add_packed(one, keep, *parts), pairs)]
+        return parts[1:], scores(*operands)
+
+    hops, (*weights, factors, base) = fenced(
+        last_hop, keep, [near, *hops], where, key_len, query_rows, key_rows, value_rows, near_keys, *far_keys
+    )
+    far = fenced(
+        lambda flag, keep, *parts: moved(add_packed(flag, keep, *parts), swaps),
+        1 - lax.rem(where, 2),
+        keep,
+        *hops,
+    )
+    base = pl.pallas_call(
         functools.partial(linear_kernel, heads, width, len(hops), tokens),
         grid_spec=pltpu.PrefetchScalarGridSpec(
             num_scalar_prefetch=2,
             grid=grid,
-            in_specs=[wide] + [whole] * (len(hops) + 2),
+            in_specs=[wide, narrow] + [wide] * 3 + [whole] * (len(hops) + 2),
             out_specs=wide,
         ),
         out_shape=full_f32,
         compiler_params=params(),
         name="linear",
-    )(where, linear_scale, query_rows, *hops, near, far)
+    )(where, linear_scale, query_rows, factors, base, weights[0], near_values, *hops, near, far)
     return pl.pallas_call(
         functools.partial(finish_kernel, late, width),
         grid=grid,
-        in_specs=[narrow, wide, wide] + [wide] * (2 * late),
+        in_specs=[narrow, wide] + [wide] * (2 * late),
         out_specs=wide,
         out_shape=full,
         compiler_params=params(),
         name="finish",
-    )(factors, base, linear, *weights, *far_values)
+    )(factors, base, *weights[1:], *far_values)
 
 
 def solution(mesh):

time: 112 us -> 106 us (0.946)
  the two profiles are of different devices: /device:TPU:0 before, /device:TPU:24 now
where the time goes in v4:
time: 106 us
  waiting for transfers between devices  57.1 us (54%)
  Pallas kernels  26.3 us (25%)
  starting transfers between devices  19 us (18%)
  local copies, waits for them, and re-layouts  2.42 us (2%)
    ppermute x11, waiting for transfers between devices, moved(): return lax.ppermute(x, 'seq', pairs)  57.1 us
    ppermute x11, starting transfers between devices, moved(): return lax.ppermute(x, 'seq', pairs)  19 us
    pallas_call x1, Pallas kernels, scores(): pl.pallas_call(functools.partial(scores_kernel, width, levels), grid_spec...  8.85 us
    pallas_call x1, Pallas kernels, shards(): pl.pallas_call(functools.partial(linear_kernel, heads, width, len(hops),...  6.59 us
    pallas_call x4, Pallas kernels, add_packed(): pl.pallas_call(functools.partial(add_packed_kernel, rows, extra, len(part...  4.93 us
    pallas_call x1, Pallas kernels, shards(): pl.pallas_call(functools.partial(finish_kernel, late, width), grid=grid,...  3.25 us
    pallas_call x1, Pallas kernels, block_sums(): pl.pallas_call(functools.partial(block_sums_kernel, heads, width), in_spe...  2.71 us
  transfers between devices with their start and end apart: 11, of which 5 were waited for; matrix products, arithmetic and copies ran while one was open for 1% of the time, Pallas kernels for 21%

profile of v4, /device:TPU:24, one launch (start us, length us, event | category | flops | bytes accessed | tf_op | source)
XLA Modules:
  0.0 105.7 jit_solution(15100503215504974201)
XLA Ops:
  0.0 0.3 collective-permute-start.3
  1.0 13.7 %conditional.3 = (f32[1552,128]{1,0:T(8,128)S(1)}, bf16[1584,128]{1,0:T(8,128)(2,1)}) conditional(s32[]{:T(128)} %bitcast, () %tuple.34, (s32[1]{0:T(128)}, s32[8]{0:T(128)}, bf16[128,3072]{1,0:T(8,128)(2,1)}, bf16[128,3072]{1,0:T(8,128)(2,1)}) %tuple.35), branch_computations={%region_0.0_spmd, %region_1.0_spmd} | conditional | bytes 1622072 | solution.py:251
  1.0 2.7 %block_sums.1 = (bf16[1584,128]{1,0:T(8,128)(2,1)S(1)}, f32[1552,128]{1,0:T(8,128)S(1)}) custom-call(s32[1]{0:T(128)} %get-tuple-element.64.where, s32[8]{0:T(128)} %get-tuple-element.65.lengths, bf16[128,3072]{1,0:T(8,128)(2,1)} %get-tuple-element.66.k_ref, bf16[128,3072]{1,0:T(8,128)(2,1)} %get-tuple-element.67.v_ref), custom_call_target="tpu_custom_call" | custom-call | tf_op jit(solution)/shard_map/cond/branch_1_fun/block_sums/pallas_call | solution.py:254
  3.7 1.6 %collective-permute-start = (bf16[1584,128]{1,0:T(8,128)(2,1)S(1)}, bf16[1584,128]{1,0:T(8,128)(2,1)}, u32[]{:S(2)}, u32[]{:S(2)}) collective-permute-start(bf16[1584,128]{1,0:T(8,128)(2,1)S(1)} %get-tuple-element.69), channel_id=1, source_target_pairs={{0,2},{2,0},{4,6},{6,4},{8,10},{10,8},{12,14},{14,12},{1,3},{3,1},... | collective-permute-start | bytes 1216520 | tf_op jit(solution)/shard_map/cond/branch_1_fun/ppermute | solution.py:240
  5.3 9.4 %collective-permute-done = bf16[1584,128]{1,0:T(8,128)(2,1)} collective-permute-done((bf16[1584,128]{1,0:T(8,128)(2,1)S(1)}, bf16[1584,128]{1,0:T(8,128)(2,1)}, u32[]{:S(2)}, u32[]{:S(2)}) %collective-permute-start) | collective-permute-done | bytes 405536 | tf_op jit(solution)/shard_map/cond/branch_1_fun/ppermute | solution.py:240
  14.7 0.0 copy-start.3
  14.7 4.8 %collective-permute-done.3 = bf16[128,3072]{1,0:T(8,128)(2,1)S(1)} collective-permute-done((bf16[128,3072]{1,0:T(8,128)(2,1)}, bf16[128,3072]{1,0:T(8,128)(2,1)S(1)}, u32[]{:S(2)}, u32[]{:S(2)}) %collective-permute-start.3) | collective-permute-done | bytes 786464 | tf_op jit(solution)/shard_map/ppermute | solution.py:240
  19.5 0.9 copy-done.6
  20.4 0.0 copy-start.7
  20.4 0.0 copy-start.8
  20.4 1.2 %add_packed.6 = bf16[1584,128]{1,0:T(8,128)(2,1)S(1)} custom-call(s32[1]{0:T(128)} %constant.32.clone.1.where, f32[1552,128]{1,0:T(8,128)S(1)} %get-tuple-element.107.keep_ref, bf16[1584,128]{1,0:T(8,128)(2,1)} %get-tuple-element.109.refs_0_.refs_3_), custom_call_target="tpu_custom_call" | custom-call | tf_op jit(solution)/shard_map/add_packed/pallas_call | solution.py:265
  21.6 0.7 collective-permute-start.4
  22.3 0.0 copy-done.3
  22.3 1.4 %collective-permute-start.7 = (bf16[128,3072]{1,0:T(8,128)(2,1)S(1)}, bf16[128,3072]{1,0:T(8,128)(2,1)S(1)}, u32[]{:S(2)}, u32[]{:S(2)}) collective-permute-start(bf16[128,3072]{1,0:T(8,128)(2,1)S(1)} %copy-done.3), channel_id=1, source_target_pairs={{8,0},{10,2},{12,8},{14,10},{4,12},{6,14},{0,4},{2,6},{9,1},{11,3}... | collective-permute-start | bytes 2359304 | tf_op jit(solution)/shard_map/ppermute | solution.py:240
  23.7 0.0 collective-permute-done.4.refs_1_
  23.7 1.2 %add_packed.7 = bf16[1584,128]{1,0:T(8,128)(2,1)S(1)} custom-call(s32[1]{0:T(128)} %constant.32.clone.1.where, f32[1552,128]{1,0:T(8,128)S(1)} %get-tuple-element.107.keep_ref, bf16[1584,128]{1,0:T(8,128)(2,1)} %get-tuple-element.109.refs_0_.refs_3_, bf16[1584,128]{1,0:T(8,128)(2,1)S(1)} %collective-permute-done.4.refs_1_), custom_call_target="tpu_custom_call" | custom-call | tf_op jit(solution)/shard_map/add_packed/pallas_call | solution.py:265
  24.9 0.7 collective-permute-start.5
  25.6 1.6 %collective-permute-start.6 = (bf16[128,3072]{1,0:T(8,128)(2,1)S(1)}, bf16[128,3072]{1,0:T(8,128)(2,1)S(1)}, u32[]{:S(2)}, u32[]{:S(2)}) collective-permute-start(bf16[128,3072]{1,0:T(8,128)(2,1)S(1)} %copy-done.3), channel_id=1, source_target_pairs={{0,2},{2,0},{4,6},{6,4},{8,10},{10,8},{12,14},{14,12},{1,3},{3,1},... | collective-permute-start | bytes 2359304 | tf_op jit(solution)/shard_map/ppermute | solution.py:240
  27.1 0.5 collective-permute-start.8
  27.6 16.1 %collective-permute-done.7 = bf16[128,3072]{1,0:T(8,128)(2,1)S(1)} collective-permute-done((bf16[128,3072]{1,0:T(8,128)(2,1)S(1)}, bf16[128,3072]{1,0:T(8,128)(2,1)S(1)}, u32[]{:S(2)}, u32[]{:S(2)}) %collective-permute-start.7) | collective-permute-done | bytes 786464 | tf_op jit(solution)/shard_map/ppermute | solution.py:240
  43.7 9.4 %collective-permute-start.9 = (bf16[128,3072]{1,0:T(8,128)(2,1)}, bf16[128,3072]{1,0:T(8,128)(2,1)S(1)}, u32[]{:S(2)}, u32[]{:S(2)}) collective-permute-start(bf16[128,3072]{1,0:T(8,128)(2,1)} %param.13), channel_id=1, source_target_pairs={{0,8},{2,10},{8,12},{10,14},{12,4},{14,6},{4,0},{6,2},{1,9},{3,11}... | collective-permute-start | bytes 2359304 | tf_op jit(solution)/shard_map/ppermute | solution.py:240
  53.1 0.0 collective-permute-done.5
  53.1 0.0 collective-permute-start.10
  53.1 0.0 collective-permute-done.6
  53.1 0.0 copy-done.2
  53.1 0.0 copy-done.7
  53.1 0.0 copy-done.8
  53.2 32.5 %conditional.4 = (bf16[1584,128]{1,0:T(8,128)(2,1)S(1)}, bf16[1584,128]{1,0:T(8,128)(2,1)}, bf16[1584,128]{1,0:T(8,128)(2,1)}, bf16[128,3072]{1,0:T(8,128)(2,1)}...) conditional(s32[]{:T(128)} %bitcast, () %tuple.33, ...), branch_computations={%region_2.0_spmd, %region_3.0_spmd} | conditional | bytes 5541972 | solution.py:251
  53.2 1.2 %add_packed.4 = bf16[1584,128]{1,0:T(8,128)(2,1)S(1)} custom-call(s32[1]{0:T(128)} %constant.19.clone.where, f32[1552,128]{1,0:T(8,128)S(1)} %get-tuple-element.72.keep_ref, bf16[1584,128]{1,0:T(8,128)(2,1)} %get-tuple-element.73.refs_0_, bf16[1584,128]{1,0:T(8,128)(2,1)S(1)} %get-tuple-element.134.refs_1_, bf16[1584,128]{1,0:T(8,128)(2,1)S(1)} %get-tuple-element.135.refs_2_), custom_call_target="tpu_custom_call" | custom-call | tf_op jit(solution)/shard_map/cond/branch_1_fun/add_packed/pallas_call | solution.py:265
  54.4 1.3 %collective-permute-start.1 = (bf16[1584,128]{1,0:T(8,128)(2,1)S(1)}, bf16[1584,128]{1,0:T(8,128)(2,1)}, u32[]{:S(2)}, u32[]{:S(2)}) collective-permute-start(bf16[1584,128]{1,0:T(8,128)(2,1)S(1)} %add_packed.4), channel_id=1, source_target_pairs={{8,12},{10,14},{9,13},{11,15},{24,28},{26,30},{25,29},{27,31}} | collective-permute-start | bytes 1216520 | tf_op jit(solution)/shard_map/cond/branch_1_fun/ppermute | solution.py:240
  55.7 0.7 copy.19
  56.5 8.8 %scores.1 = (bf16[128,3072]{1,0:T(8,128)(2,1)}, bf16[128,3072]{1,0:T(8,128)(2,1)}, bf16[128,3072]{1,0:T(8,128)(2,1)}, f32[128,768]{1,0:T(8,128)S(1)}, f32[128,3072]{1,0:T(8,128)}) custom-call(s32[1]{0:T(128)} %get-tuple-element.74.where, s32[8]{0:T(128)S(1)} %get-tuple-element.75.lengths, bf16[128,3072]{1,0:T(8,128)(2,1)S(1)} %get-tuple-element.76.q_ref, ...), custom_call_target="tpu_custom_call" | custom-call | tf_op jit(solution)/shard_map/cond/branch_1_fun/scores/pallas_call | solution.py:283
  65.3 20.3 %collective-permute-done.1 = bf16[1584,128]{1,0:T(8,128)(2,1)} collective-permute-done((bf16[1584,128]{1,0:T(8,128)(2,1)S(1)}, bf16[1584,128]{1,0:T(8,128)(2,1)}, u32[]{:S(2)}, u32[]{:S(2)}) %collective-permute-start.1) | collective-permute-done | bytes 405536 | tf_op jit(solution)/shard_map/cond/branch_1_fun/ppermute | solution.py:240
  85.6 0.0 copy-start.1
  85.6 0.7 copy-done.1
  86.4 9.4 %conditional.5 = (bf16[1584,128]{1,0:T(8,128)(2,1)}) conditional(s32[]{:T(128)} %bitcast, () %tuple.40, (s32[1]{0:T(128)}, f32[1552,128]{1,0:T(8,128)S(1)}, bf16[1584,128]{1,0:T(8,128)(2,1)S(1)}, bf16[1584,128]{1,0:T(8,128)(2,1)}, bf16[1584,128]{1,0:T(8,128)(2,1)}) %tuple.41), branch_computations={%region_4.0_spmd, %region_5.0_spmd} | conditional | flops 7 | bytes 1622139 | solution.py:251
  86.4 1.3 %add_packed.5 = bf16[1584,128]{1,0:T(8,128)(2,1)S(1)} custom-call(s32[1]{0:T(128)S(6)} %sub.3.where, f32[1552,128]{1,0:T(8,128)S(1)} %get-tuple-element.88.keep_ref, bf16[1584,128]{1,0:T(8,128)(2,1)S(1)} %get-tuple-element.89.refs_0_, bf16[1584,128]{1,0:T(8,128)(2,1)} %get-tuple-element.90.refs_1_, bf16[1584,128]{1,0:T(8,128)(2,1)} %get-tuple-element.91.refs_2_), custom_call_target="tpu_custom_call" | custom-call | tf_op jit(solution)/shard_map/cond/branch_1_fun/add_packed/pallas_call | solution.py:265
  87.7 1.6 %collective-permute-start.2 = (bf16[1584,128]{1,0:T(8,128)(2,1)S(1)}, bf16[1584,128]{1,0:T(8,128)(2,1)}, u32[]{:S(2)}, u32[]{:S(2)}) collective-permute-start(bf16[1584,128]{1,0:T(8,128)(2,1)S(1)} %add_packed.5), channel_id=1, source_target_pairs={{0,2},{2,0},{4,6},{6,4},{8,10},{10,8},{12,14},{14,12},{1,3},{3,1},... | collective-permute-start | bytes 1216520 | tf_op jit(solution)/shard_map/cond/branch_1_fun/ppermute | solution.py:240
  89.3 6.5 %collective-permute-done.2 = bf16[1584,128]{1,0:T(8,128)(2,1)} collective-permute-done((bf16[1584,128]{1,0:T(8,128)(2,1)S(1)}, bf16[1584,128]{1,0:T(8,128)(2,1)}, u32[]{:S(2)}, u32[]{:S(2)}) %collective-permute-start.2) | collective-permute-done | bytes 405536 | tf_op jit(solution)/shard_map/cond/branch_1_fun/ppermute | solution.py:240
  95.8 0.0 collective-permute-done.8.value_ref
  95.8 0.0 copy-done
  95.8 0.0 copy-start.5
  95.8 6.6 %linear.1.base_ref = f32[128,3072]{1,0:T(8,128)S(1)} custom-call(s32[1]{0:T(128)} %bitcast.1.where, f32[24]{0:T(128)S(1)} %copy-done, bf16[128,3072]{1,0:T(8,128)(2,1)} %q_ref.1, f32[128,768]{1,0:T(8,128)S(1)} %get-tuple-element.111.factor_ref, f32[128,3072]{1,0:T(8,128)} %get-tuple-element.112.base_ref, bf16[128,3072]{1,0:T(8,128)(2,1)} %get-tuple-element.113.weight_ref, ...), custom_call_target="tpu_custom_call" | custom-call | tf_op jit(solution)/shard_map/linear/pallas_call | solution.py:321
  102.4 0.0 collective-permute-done.9.refs_2_
  102.4 0.0 collective-permute-done.10.refs_3_
  102.4 0.0 copy-done.4
  102.4 0.0 copy-done.5
  102.4 3.2 %finish.1 = bf16[128,3072]{1,0:T(8,128)(2,1)} custom-call(f32[128,768]{1,0:T(8,128)S(1)} %get-tuple-element.111.factor_ref, f32[128,3072]{1,0:T(8,128)S(1)} %linear.1.base_ref, bf16[128,3072]{1,0:T(8,128)(2,1)S(1)} %copy-done.4, bf16[128,3072]{1,0:T(8,128)(2,1)S(1)} %copy-done.5, bf16[128,3072]{1,0:T(8,128)(2,1)S(1)} %collective-permute-done.9.refs_2_, ...), custom_call_target="tpu_custom_call" | custom-call | tf_op jit(solution)/shard_map/finish/pallas_call | solution.py:333
  (5 shorter events, 0.0 us)
Async XLA Ops:
  0.0 19.5 %collective-permute-start.3 = (bf16[128,3072]{1,0:T(8,128)(2,1)}, bf16[128,3072]{1,0:T(8,128)(2,1)S(1)}, u32[]{:S(2)}, u32[]{:S(2)}) collective-permute-start(bf16[128,3072]{1,0:T(8,128)(2,1)} %param.12), channel_id=1, source_target_pairs={{0,8},{2,10},{8,12},{10,14},{12,4},{14,6},{4,0},{6,2},{1,9},{3,11}... | collective-permute-start | bytes 2359304 | tf_op jit(solution)/shard_map/ppermute | solution.py:240
  3.7 11.0 %collective-permute-start = (bf16[1584,128]{1,0:T(8,128)(2,1)S(1)}, bf16[1584,128]{1,0:T(8,128)(2,1)}, u32[]{:S(2)}, u32[]{:S(2)}) collective-permute-start(bf16[1584,128]{1,0:T(8,128)(2,1)S(1)} %get-tuple-element.69), channel_id=1, source_target_pairs={{0,2},{2,0},{4,6},{6,4},{8,10},{10,8},{12,14},{14,12},{1,3},{3,1},... | collective-permute-start | bytes 1216520 | tf_op jit(solution)/shard_map/cond/branch_1_fun/ppermute | solution.py:240
  14.7 7.6 %copy-start.3 = (bf16[128,3072]{1,0:T(8,128)(2,1)S(1)}, bf16[128,3072]{1,0:T(8,128)(2,1)}, u32[]{:S(2)}) copy-start(bf16[128,3072]{1,0:T(8,128)(2,1)} %param.12) | copy-start | bytes 2359300
  19.5 0.9 copy-start.6
  20.4 32.8 %copy-start.2 = (bf16[128,3072]{1,0:T(8,128)(2,1)S(1)}, bf16[128,3072]{1,0:T(8,128)(2,1)}, u32[]{:S(2)}) copy-start(bf16[128,3072]{1,0:T(8,128)(2,1)} %q_ref.1) | copy-start | bytes 2359300
  20.4 32.8 %copy-start.7 = (bf16[128,3072]{1,0:T(8,128)(2,1)S(1)}, bf16[128,3072]{1,0:T(8,128)(2,1)}, u32[]{:S(2)}) copy-start(bf16[128,3072]{1,0:T(8,128)(2,1)} %copy-done.6) | copy-start | bytes 2359300
  20.4 32.8 %copy-start.8 = (s32[8]{0:T(128)S(1)}, s32[8]{0:T(128)}, u32[]{:S(2)}) copy-start(s32[8]{0:T(128)} %param.14) | copy-start | bytes 100
  21.6 2.1 %collective-permute-start.4 = (bf16[1584,128]{1,0:T(8,128)(2,1)S(1)}, bf16[1584,128]{1,0:T(8,128)(2,1)S(1)}, u32[]{:S(2)}, u32[]{:S(2)}) collective-permute-start(bf16[1584,128]{1,0:T(8,128)(2,1)S(1)} %add_packed.6), channel_id=1, source_target_pairs={{0,4},{2,6},{1,5},{3,7},{16,20},{18,22},{17,21},{19,23}} | collective-permute-start | bytes 1216520 | tf_op jit(solution)/shard_map/ppermute | solution.py:240
  22.3 21.4 %collective-permute-start.7 = (bf16[128,3072]{1,0:T(8,128)(2,1)S(1)}, bf16[128,3072]{1,0:T(8,128)(2,1)S(1)}, u32[]{:S(2)}, u32[]{:S(2)}) collective-permute-start(bf16[128,3072]{1,0:T(8,128)(2,1)S(1)} %copy-done.3), channel_id=1, source_target_pairs={{8,0},{10,2},{12,8},{14,10},{4,12},{6,14},{0,4},{2,6},{9,1},{11,3}... | collective-permute-start | bytes 2359304 | tf_op jit(solution)/shard_map/ppermute | solution.py:240
  24.9 28.2 %collective-permute-start.5 = (bf16[1584,128]{1,0:T(8,128)(2,1)S(1)}, bf16[1584,128]{1,0:T(8,128)(2,1)S(1)}, u32[]{:S(2)}, u32[]{:S(2)}) collective-permute-start(bf16[1584,128]{1,0:T(8,128)(2,1)S(1)} %add_packed.7), channel_id=1, source_target_pairs={{4,8},{6,10},{5,9},{7,11},{20,24},{22,26},{21,25},{23,27}} | collective-permute-start | bytes 1216520 | tf_op jit(solution)/shard_map/ppermute | solution.py:240
  25.6 27.6 %collective-permute-start.6 = (bf16[128,3072]{1,0:T(8,128)(2,1)S(1)}, bf16[128,3072]{1,0:T(8,128)(2,1)S(1)}, u32[]{:S(2)}, u32[]{:S(2)}) collective-permute-start(bf16[128,3072]{1,0:T(8,128)(2,1)S(1)} %copy-done.3), channel_id=1, source_target_pairs={{0,2},{2,0},{4,6},{6,4},{8,10},{10,8},{12,14},{14,12},{1,3},{3,1},... | collective-permute-start | bytes 2359304 | tf_op jit(solution)/shard_map/ppermute | solution.py:240
  27.1 68.6 %collective-permute-start.8 = (bf16[128,3072]{1,0:T(8,128)(2,1)}, bf16[128,3072]{1,0:T(8,128)(2,1)S(1)}, u32[]{:S(2)}, u32[]{:S(2)}) collective-permute-start(bf16[128,3072]{1,0:T(8,128)(2,1)} %param.13), channel_id=1, source_target_pairs={{0,2},{2,0},{4,6},{6,4},{8,10},{10,8},{12,14},{14,12},{1,3},{3,1},... | collective-permute-start | bytes 2359304 | tf_op jit(solution)/shard_map/ppermute | solution.py:240
  43.7 58.7 %collective-permute-start.9 = (bf16[128,3072]{1,0:T(8,128)(2,1)}, bf16[128,3072]{1,0:T(8,128)(2,1)S(1)}, u32[]{:S(2)}, u32[]{:S(2)}) collective-permute-start(bf16[128,3072]{1,0:T(8,128)(2,1)} %param.13), channel_id=1, source_target_pairs={{0,8},{2,10},{8,12},{10,14},{12,4},{14,6},{4,0},{6,2},{1,9},{3,11}... | collective-permute-start | bytes 2359304 | tf_op jit(solution)/shard_map/ppermute | solution.py:240
  53.1 49.3 %collective-permute-start.10 = (bf16[128,3072]{1,0:T(8,128)(2,1)}, bf16[128,3072]{1,0:T(8,128)(2,1)S(1)}, u32[]{:S(2)}, u32[]{:S(2)}) collective-permute-start(bf16[128,3072]{1,0:T(8,128)(2,1)} %param.13), channel_id=1, source_target_pairs={{8,0},{10,2},{12,8},{14,10},{4,12},{6,14},{0,4},{2,6},{9,1},{11,3}... | collective-permute-start | bytes 2359304 | tf_op jit(solution)/shard_map/ppermute | solution.py:240
  54.4 31.2 %collective-permute-start.1 = (bf16[1584,128]{1,0:T(8,128)(2,1)S(1)}, bf16[1584,128]{1,0:T(8,128)(2,1)}, u32[]{:S(2)}, u32[]{:S(2)}) collective-permute-start(bf16[1584,128]{1,0:T(8,128)(2,1)S(1)} %add_packed.4), channel_id=1, source_target_pairs={{8,12},{10,14},{9,13},{11,15},{24,28},{26,30},{25,29},{27,31}} | collective-permute-start | bytes 1216520 | tf_op jit(solution)/shard_map/cond/branch_1_fun/ppermute | solution.py:240
  85.6 0.7 copy-start.1
  85.6 10.2 %copy-start = (f32[24]{0:T(128)S(1)}, f32[24]{0:T(128)}, u32[]{:S(2)}) copy-start(f32[24]{0:T(128)} %scale.1) | copy-start | bytes 292
  87.7 8.1 %collective-permute-start.2 = (bf16[1584,128]{1,0:T(8,128)(2,1)S(1)}, bf16[1584,128]{1,0:T(8,128)(2,1)}, u32[]{:S(2)}, u32[]{:S(2)}) collective-permute-start(bf16[1584,128]{1,0:T(8,128)(2,1)S(1)} %add_packed.5), channel_id=1, source_target_pairs={{0,2},{2,0},{4,6},{6,4},{8,10},{10,8},{12,14},{14,12},{1,3},{3,1},... | collective-permute-start | bytes 1216520 | tf_op jit(solution)/shard_map/cond/branch_1_fun/ppermute | solution.py:240
  95.8 6.6 %copy-start.4 = (bf16[128,3072]{1,0:T(8,128)(2,1)S(1)}, bf16[128,3072]{1,0:T(8,128)(2,1)}, u32[]{:S(2)}) copy-start(bf16[128,3072]{1,0:T(8,128)(2,1)} %get-tuple-element.118.refs_0_) | copy-start | bytes 2359300
  95.8 6.6 %copy-start.5 = (bf16[128,3072]{1,0:T(8,128)(2,1)S(1)}, bf16[128,3072]{1,0:T(8,128)(2,1)}, u32[]{:S(2)}) copy-start(bf16[128,3072]{1,0:T(8,128)(2,1)} %get-tuple-element.119.refs_1_) | copy-start | bytes 2359300

commit v5 on v4

--- a/solution.py
+++ b/solution.py
@@ -155,34 +155,38 @@
     factor_ref[...] = factors
 
 
-def linear_kernel(heads, width, hops, tokens, where, scale, q_ref, factor_ref, base_ref, weight_ref, value_ref, *refs):
-    hop_refs, (near_ref, far_ref, out_ref) = refs[:hops], refs[hops:]
+def linear_kernel(heads, width, own, parts, tokens, where, scale, q_ref, factor_ref, base_ref, weight_ref, value_ref, *refs):
+    part_refs, out_ref = refs[:parts], refs[parts]
     side = lax.rem(where[0], 2)
     half_heads = heads // 2
     rows, extra = half_heads * width, padded(half_heads)
     a_step = q_ref.shape[1] // width
-    first = pl.program_id(0) * a_step
-    mine = (first // half_heads == side).astype(F32)
-    upper = mine * side.astype(F32)
-    in_half = lax.rem(first, half_heads)
-    sums = (1.0 - mine) * packed_sums(far_ref, rows, extra) + upper * packed_sums(near_ref, rows, extra)
-    for ref in hop_refs:
-        sums = sums + mine * packed_sums(ref, rows, extra)
+    in_half = pl.program_id(0) * a_step
+    first = (side if own else 1 - side) * half_heads + in_half
+    flags = [1.0] * (parts - 1) + [side.astype(F32) if own else 1.0]
+    sums = functools.reduce(
+        jnp.add, [flag * packed_sums(ref, rows, extra) for flag, ref in zip(flags, part_refs)]
+    )
     sum_row = lax.broadcasted_iota(jnp.int32, sums.shape, 0)
     for h in range(a_step):
         at = slice(h * width, (h + 1) * width)
         block = pl.ds(pl.multiple_of((in_half + h) * width, width), width)
-        prefix = (1.0 - mine) * far_ref[block, :].astype(F32) + upper * near_ref[block, :].astype(F32)
-        for ref in hop_refs:
-            prefix = prefix + mine * ref[block, :].astype(F32)
         mapped = feature(q_ref[:, at].astype(F32))
         high, low = halves(mapped)
-        prefix_high, prefix_low = halves(prefix)
+        if own:
+            prefix = functools.reduce(
+                jnp.add, [flag * ref[block, :].astype(F32) for flag, ref in zip(flags, part_refs)]
+            )
+            prefix, rest = halves(prefix)
+        else:
+            prefix = part_refs[0][block, :]
         linear = jnp.dot(
             jnp.concatenate([high, low], axis=1),
-            jnp.concatenate([prefix_high, prefix_high], axis=0),
+            jnp.concatenate([prefix, prefix], axis=0),
             preferred_element_type=F32,
-        ) + jnp.dot(high, prefix_low, preferred_element_type=F32)
+        )
+        if own:
+            linear = linear + jnp.dot(high, rest, preferred_element_type=F32)
         value_sum = jnp.sum(jnp.where(sum_row == in_half + h, sums, 0.0), axis=0, keepdims=True)
         linear = linear + jnp.sum(mapped, axis=1, keepdims=True) * (CENTER * value_sum)
         near = jnp.dot(weight_ref[:, at], value_ref[:, at], preferred_element_type=F32)
@@ -190,12 +194,13 @@
         out_ref[:, at] = total + linear * (scale[first + h] * (1.0 / (width * math.sqrt(tokens))))
 
 
-def finish_kernel(late, width, factor_ref, base_ref, *refs):
+def finish_kernel(late, width, where, factor_ref, own_ref, other_ref, *refs):
     out_ref = refs[2 * late]
-    a_step = base_ref.shape[1] // width
+    a_step = own_ref.shape[1] // width
+    own = pl.program_id(0) // (pl.num_programs(0) // 2) == lax.rem(where[0], 2)
     for h in range(a_step):
         at = slice(h * width, (h + 1) * width)
-        total = base_ref[:, at]
+        total = jnp.where(own, own_ref[:, at], other_ref[:, at])
         for which in range(late):
             lane = (which + 1) * a_step + h
             total = total + factor_ref[:, lane : lane + 1] * jnp.dot(
@@ -298,11 +303,10 @@
     keep, near = fenced(block_sums, where, key_len, key_rows, value_rows)
     near_keys = moved(after(key_rows, near), swaps)
     near_values = moved(after(value_rows, near), swaps)
-    hops = [moved(add_packed(one, keep, after(near, *far_keys)), steps[0])]
+    hops = [moved(add_packed(one, keep, near), steps[0])]
     far_keys += [moved(after(key_rows, near), turn) for turn in turns[1:]]
-    hops.append(moved(add_packed(one, keep, near, *hops), steps[1]))
-    far_values = [moved(after(value_rows, *far_keys), turns[0])]
-    far_values += [moved(after(value_rows, *hops), turn) for turn in turns[1:]]
+    hops.append(moved(add_packed(one, keep, after(near, far_keys[0]), *hops), steps[1]))
+    far_values = [moved(after(value_rows, near_keys, *far_keys), turns[0])]
 
     def last_hop(keep, parts, *operands):
         for pairs in steps[2:]:
@@ -312,33 +316,50 @@
     hops, (*weights, factors, base) = fenced(
         last_hop, keep, [near, *hops], where, key_len, query_rows, key_rows, value_rows, near_keys, *far_keys
     )
-    far = fenced(
-        lambda flag, keep, *parts: moved(add_packed(flag, keep, *parts), swaps),
-        1 - lax.rem(where, 2),
-        keep,
-        *hops,
-    )
-    base = pl.pallas_call(
-        functools.partial(linear_kernel, heads, width, len(hops), tokens),
+    far_values += [moved(after(value_rows, *hops), turn) for turn in turns[1:]]
+
+    half_grid = grid[0] // 2
+    half_f32 = jax.ShapeDtypeStruct((row_count, columns // 2), F32)
+
+    def linear(own, where, linear_scale, query_rows, factors, base, weights, near_values, *parts):
+        def at(i, where, scale):
+            side = lax.rem(where[0], 2)
+            return 0, (side if own else 1 - side) * half_grid + i
+
+        chosen = pl.BlockSpec((row_count, a_step * width), at)
+        return pl.pallas_call(
+            functools.partial(linear_kernel, heads, width, own, len(parts), tokens),
+            grid_spec=pltpu.PrefetchScalarGridSpec(
+                num_scalar_prefetch=2,
+                grid=(half_grid,),
+                in_specs=[chosen, pl.BlockSpec((row_count, 128), at)] + [chosen] * 3 + [whole] * len(parts),
+                out_specs=wide,
+            ),
+            out_shape=half_f32,
+            compiler_params=params(),
+            name="linear_own" if own else "linear_other",
+        )(where, linear_scale, query_rows, factors, base, weights, near_values, *parts)
+
+    operands = (where, linear_scale, query_rows, factors, base, weights[0], near_values)
+
+    def last_exchange(flag, keep, near, hops, *operands):
+        return moved(add_packed(flag, keep, *hops), swaps), linear(True, *operands, *hops, near)
+
+    far, own = fenced(last_exchange, 1 - lax.rem(where, 2), keep, near, hops, *operands)
+    other = linear(False, *operands, far)
+    half = pl.BlockSpec((row_count, a_step * width), lambda i, *_: (0, lax.rem(i, half_grid)))
+    return pl.pallas_call(
+        functools.partial(finish_kernel, late, width),
         grid_spec=pltpu.PrefetchScalarGridSpec(
-            num_scalar_prefetch=2,
+            num_scalar_prefetch=1,
             grid=grid,
-            in_specs=[wide, narrow] + [wide] * 3 + [whole] * (len(hops) + 2),
+            in_specs=[narrow, half, half] + [wide] * (2 * late),
             out_specs=wide,
         ),
-        out_shape=full_f32,
-        compiler_params=params(),
-        name="linear",
-    )(where, linear_scale, query_rows, factors, base, weights[0], near_values, *hops, near, far)
-    return pl.pallas_call(
-        functools.partial(finish_kernel, late, width),
-        grid=grid,
-        in_specs=[narrow, wide] + [wide] * (2 * late),
-        out_specs=wide,
         out_shape=full,
         compiler_params=params(),
         name="finish",
-    )(factors, base, *weights[1:], *far_values)
+    )(where, factors, own, other, *weights[1:], *far_values)
 
 
 def solution(mesh):

time: 106 us -> 97.4 us (0.919)
  the two profiles are of different devices: /device:TPU:24 before, /device:TPU:10 now
where the time goes in v5:
time: 97.4 us; the launch traced here: 97 us
  waiting for transfers between devices  49.4 us (51%)
  Pallas kernels  27.6 us (28%)
  starting transfers between devices  18.2 us (19%)
    ppermute x11, waiting for transfers between devices, moved(): return lax.ppermute(x, 'seq', pairs)  49.4 us
    ppermute x11, starting transfers between devices, moved(): return lax.ppermute(x, 'seq', pairs)  18.2 us
    pallas_call x1, Pallas kernels, scores(): pl.pallas_call(functools.partial(scores_kernel, width, levels), grid_spec...  8.84 us
    pallas_call x2, Pallas kernels, linear(): pl.pallas_call(functools.partial(linear_kernel, heads, width, own, len(pa...  7.82 us
    pallas_call x4, Pallas kernels, add_packed(): pl.pallas_call(functools.partial(add_packed_kernel, rows, extra, len(part...  4.9 us
    pallas_call x1, Pallas kernels, shards(): pl.pallas_call(functools.partial(finish_kernel, late, width), grid_spec=p...  3.34 us
    pallas_call x1, Pallas kernels, block_sums(): pl.pallas_call(functools.partial(block_sums_kernel, heads, width), in_spe...  2.7 us
  transfers between devices with their start and end apart: 11, of which 6 were waited for; matrix products, arithmetic and copies ran while one was open for 0% of the time, Pallas kernels for 25%

profile of v5, /device:TPU:10, one launch (start us, length us, event | category | flops | bytes accessed | tf_op | source)
XLA Modules:
  0.0 97.0 jit_solution(9628165738032414513)
XLA Ops:
  0.0 0.4 collective-permute-start.4
  1.1 13.7 %conditional.3 = (f32[1552,128]{1,0:T(8,128)S(1)}, bf16[1584,128]{1,0:T(8,128)(2,1)}) conditional(s32[]{:T(128)} %bitcast.1, () %tuple.36, (s32[1]{0:T(128)}, s32[8]{0:T(128)}, bf16[128,3072]{1,0:T(8,128)(2,1)}, bf16[128,3072]{1,0:T(8,128)(2,1)}) %tuple.37), branch_computations={%region_0.0_spmd, %region_1.0_spmd} | conditional | bytes 1622072 | solution.py:256
  1.1 2.7 %block_sums.1 = (bf16[1584,128]{1,0:T(8,128)(2,1)S(1)}, f32[1552,128]{1,0:T(8,128)S(1)}) custom-call(s32[1]{0:T(128)} %get-tuple-element.76.where, s32[8]{0:T(128)} %get-tuple-element.77.lengths, bf16[128,3072]{1,0:T(8,128)(2,1)} %get-tuple-element.78.k_ref, bf16[128,3072]{1,0:T(8,128)(2,1)} %get-tuple-element.79.v_ref), custom_call_target="tpu_custom_call" | custom-call | tf_op jit(solution)/shard_map/cond/branch_1_fun/block_sums/pallas_call | solution.py:259
  3.8 1.6 %collective-permute-start = (bf16[1584,128]{1,0:T(8,128)(2,1)S(1)}, bf16[1584,128]{1,0:T(8,128)(2,1)}, u32[]{:S(2)}, u32[]{:S(2)}) collective-permute-start(bf16[1584,128]{1,0:T(8,128)(2,1)S(1)} %get-tuple-element.81), channel_id=1, source_target_pairs={{0,2},{2,0},{4,6},{6,4},{8,10},{10,8},{12,14},{14,12},{1,3},{3,1},... | collective-permute-start | bytes 1216520 | tf_op jit(solution)/shard_map/cond/branch_1_fun/ppermute | solution.py:245
  5.4 9.4 %collective-permute-done = bf16[1584,128]{1,0:T(8,128)(2,1)} collective-permute-done((bf16[1584,128]{1,0:T(8,128)(2,1)S(1)}, bf16[1584,128]{1,0:T(8,128)(2,1)}, u32[]{:S(2)}, u32[]{:S(2)}) %collective-permute-start) | collective-permute-done | bytes 405536 | tf_op jit(solution)/shard_map/cond/branch_1_fun/ppermute | solution.py:245
  14.8 0.0 copy-start.1
  14.8 0.0 copy-start
  14.9 0.0 copy-start.8
  14.9 1.2 %add_packed.6 = bf16[1584,128]{1,0:T(8,128)(2,1)S(1)} custom-call(s32[1]{0:T(128)} %constant.34.clone.1.where, f32[1552,128]{1,0:T(8,128)S(1)} %get-tuple-element.128.keep_ref, bf16[1584,128]{1,0:T(8,128)(2,1)} %get-tuple-element.130.refs_0_), custom_call_target="tpu_custom_call" | custom-call | tf_op jit(solution)/shard_map/add_packed/pallas_call | solution.py:270
  16.1 1.3 %collective-permute-start.3 = (bf16[1584,128]{1,0:T(8,128)(2,1)S(1)}, bf16[1584,128]{1,0:T(8,128)(2,1)S(1)}, u32[]{:S(2)}, u32[]{:S(2)}) collective-permute-start(bf16[1584,128]{1,0:T(8,128)(2,1)S(1)} %add_packed.6), channel_id=1, source_target_pairs={{0,4},{2,6},{1,5},{3,7},{16,20},{18,22},{17,21},{19,23}} | collective-permute-start | bytes 1216520 | tf_op jit(solution)/shard_map/ppermute | solution.py:245
  17.4 0.0 copy-done.1
  17.4 1.6 %collective-permute-start.6 = (bf16[128,3072]{1,0:T(8,128)(2,1)S(1)}, bf16[128,3072]{1,0:T(8,128)(2,1)S(1)}, u32[]{:S(2)}, u32[]{:S(2)}) collective-permute-start(bf16[128,3072]{1,0:T(8,128)(2,1)S(1)} %copy-done.1), channel_id=1, source_target_pairs={{0,2},{2,0},{4,6},{6,4},{8,10},{10,8},{12,14},{14,12},{1,3},{3,1},... | collective-permute-start | bytes 2359304 | tf_op jit(solution)/shard_map/ppermute | solution.py:245
  19.0 1.9 %collective-permute-start.7 = (bf16[128,3072]{1,0:T(8,128)(2,1)S(1)}, bf16[128,3072]{1,0:T(8,128)(2,1)S(1)}, u32[]{:S(2)}, u32[]{:S(2)}) collective-permute-start(bf16[128,3072]{1,0:T(8,128)(2,1)S(1)} %copy-done.1), channel_id=1, source_target_pairs={{8,0},{10,2},{12,8},{14,10},{4,12},{6,14},{0,4},{2,6},{9,1},{11,3}... | collective-permute-start | bytes 2359304 | tf_op jit(solution)/shard_map/ppermute | solution.py:245
  20.8 0.0 collective-permute-done.4
  20.8 0.0 copy-start.6
  20.8 9.4 %collective-permute-done.3.refs_1_ = bf16[1584,128]{1,0:T(8,128)(2,1)S(1)} collective-permute-done((bf16[1584,128]{1,0:T(8,128)(2,1)S(1)}, bf16[1584,128]{1,0:T(8,128)(2,1)S(1)}, u32[]{:S(2)}, u32[]{:S(2)}) %collective-permute-start.3) | collective-permute-done | bytes 405536 | tf_op jit(solution)/shard_map/ppermute | solution.py:245
  30.3 1.2 %add_packed.7 = bf16[1584,128]{1,0:T(8,128)(2,1)S(1)} custom-call(s32[1]{0:T(128)} %constant.34.clone.1.where, f32[1552,128]{1,0:T(8,128)S(1)} %get-tuple-element.128.keep_ref, bf16[1584,128]{1,0:T(8,128)(2,1)} %get-tuple-element.130.refs_0_, bf16[1584,128]{1,0:T(8,128)(2,1)S(1)} %collective-permute-done.3.refs_1_), custom_call_target="tpu_custom_call" | custom-call | tf_op jit(solution)/shard_map/add_packed/pallas_call | solution.py:270
  31.5 1.3 %collective-permute-start.5 = (bf16[1584,128]{1,0:T(8,128)(2,1)S(1)}, bf16[1584,128]{1,0:T(8,128)(2,1)S(1)}, u32[]{:S(2)}, u32[]{:S(2)}) collective-permute-start(bf16[1584,128]{1,0:T(8,128)(2,1)S(1)} %add_packed.7), channel_id=1, source_target_pairs={{4,8},{6,10},{5,9},{7,11},{20,24},{22,26},{21,25},{23,27}} | collective-permute-start | bytes 1216520 | tf_op jit(solution)/shard_map/ppermute | solution.py:245
  32.8 1.6 %collective-permute-start.8 = (bf16[128,3072]{1,0:T(8,128)(2,1)}, bf16[128,3072]{1,0:T(8,128)(2,1)}, u32[]{:S(2)}, u32[]{:S(2)}) collective-permute-start(bf16[128,3072]{1,0:T(8,128)(2,1)} %param.13), channel_id=1, source_target_pairs={{0,2},{2,0},{4,6},{6,4},{8,10},{10,8},{12,14},{14,12},{1,3},{3,1},... | collective-permute-start | bytes 2359304 | tf_op jit(solution)/shard_map/ppermute | solution.py:245
  34.4 3.1 %collective-permute-done.6 = bf16[128,3072]{1,0:T(8,128)(2,1)S(1)} collective-permute-done((bf16[128,3072]{1,0:T(8,128)(2,1)S(1)}, bf16[128,3072]{1,0:T(8,128)(2,1)S(1)}, u32[]{:S(2)}, u32[]{:S(2)}) %collective-permute-start.6) | collective-permute-done | bytes 786464 | tf_op jit(solution)/shard_map/ppermute | solution.py:245
  37.4 0.0 copy-done.6
  37.4 8.9 %collective-permute-done.7 = bf16[128,3072]{1,0:T(8,128)(2,1)S(1)} collective-permute-done((bf16[128,3072]{1,0:T(8,128)(2,1)S(1)}, bf16[128,3072]{1,0:T(8,128)(2,1)S(1)}, u32[]{:S(2)}, u32[]{:S(2)}) %collective-permute-start.7) | collective-permute-done | bytes 786464 | tf_op jit(solution)/shard_map/ppermute | solution.py:245
  46.4 0.0 collective-permute-start.9
  46.4 14.5 %collective-permute-done.5 = bf16[1584,128]{1,0:T(8,128)(2,1)S(1)} collective-permute-done((bf16[1584,128]{1,0:T(8,128)(2,1)S(1)}, bf16[1584,128]{1,0:T(8,128)(2,1)S(1)}, u32[]{:S(2)}, u32[]{:S(2)}) %collective-permute-start.5) | collective-permute-done | bytes 405536 | tf_op jit(solution)/shard_map/ppermute | solution.py:245
  60.9 0.0 copy-done
  60.9 0.0 copy-done.8
  60.9 11.6 %conditional.4 = (bf16[1584,128]{1,0:T(8,128)(2,1)S(1)}, bf16[1584,128]{1,0:T(8,128)(2,1)S(1)}, bf16[1584,128]{1,0:T(8,128)(2,1)}, bf16[128,3072]{1,0:T(8,128)(2...) conditional(s32[]{:T(128)} %bitcast.1, () %tuple.35, ...), branch_computations={%region_2.0_spmd, %region_3.0_spmd} | conditional | bytes 6389892 | solution.py:256
  60.9 1.3 %add_packed.4 = bf16[1584,128]{1,0:T(8,128)(2,1)S(1)} custom-call(s32[1]{0:T(128)} %constant.19.clone.where, f32[1552,128]{1,0:T(8,128)S(1)} %get-tuple-element.84.keep_ref, bf16[1584,128]{1,0:T(8,128)(2,1)} %get-tuple-element.85.refs_0_, bf16[1584,128]{1,0:T(8,128)(2,1)S(1)} %get-tuple-element.157.refs_1_, bf16[1584,128]{1,0:T(8,128)(2,1)S(1)} %get-tuple-element.158.refs_2_), custom_call_target="tpu_custom_call" | custom-call | tf_op jit(solution)/shard_map/cond/branch_1_fun/add_packed/pallas_call | solution.py:270
  62.2 1.4 %collective-permute-start.1 = (bf16[1584,128]{1,0:T(8,128)(2,1)S(1)}, bf16[1584,128]{1,0:T(8,128)(2,1)}, u32[]{:S(2)}, u32[]{:S(2)}) collective-permute-start(bf16[1584,128]{1,0:T(8,128)(2,1)S(1)} %add_packed.4), channel_id=1, source_target_pairs={{8,12},{10,14},{9,13},{11,15},{24,28},{26,30},{25,29},{27,31}} | collective-permute-start | bytes 1216520 | tf_op jit(solution)/shard_map/cond/branch_1_fun/ppermute | solution.py:245
  63.7 0.0 copy-done.7
  63.7 8.8 %scores.1 = (bf16[128,3072]{1,0:T(8,128)(2,1)}, bf16[128,3072]{1,0:T(8,128)(2,1)}, bf16[128,3072]{1,0:T(8,128)(2,1)}, f32[128,768]{1,0:T(8,128)S(1)}, f32[128,3072]{1,0:T(8,128)}) custom-call(s32[1]{0:T(128)} %get-tuple-element.86.where, s32[8]{0:T(128)S(1)} %get-tuple-element.87.lengths, bf16[128,3072]{1,0:T(8,128)(2,1)S(1)} %get-tuple-element.88.q_ref, ...), custom_call_target="tpu_custom_call" | custom-call | tf_op jit(solution)/shard_map/cond/branch_1_fun/scores/pallas_call | solution.py:288
  72.5 0.0 collective-permute-done.1
  72.6 7.0 %collective-permute-start.10 = (bf16[128,3072]{1,0:T(8,128)(2,1)}, bf16[128,3072]{1,0:T(8,128)(2,1)S(1)}, u32[]{:S(2)}, u32[]{:S(2)}) collective-permute-start(bf16[128,3072]{1,0:T(8,128)(2,1)} %param.13), channel_id=1, source_target_pairs={{8,0},{10,2},{12,8},{14,10},{4,12},{6,14},{0,4},{2,6},{9,1},{11,3}... | collective-permute-start | bytes 2359304 | tf_op jit(solution)/shard_map/ppermute | solution.py:245
  79.6 0.0 collective-permute-done.8.value_ref
  79.6 0.0 copy-done.9
  79.6 9.3 %conditional.5 = (bf16[1584,128]{1,0:T(8,128)(2,1)}, f32[128,1536]{1,0:T(8,128)S(1)}) conditional(s32[]{:T(128)} %bitcast.1, () %tuple.41, (s32[1]{0:T(128)}, f32[1552,128]{1,0:T(8,128)S(1)}, bf16[1584,128]{1,0:T(8,128)(2,1)S(1)}, bf16[1584,128]{1,0:T(8,128)(2,1)S(1)}, bf16[1584,128]{1,0:T(8,128)(2,1)}, /*index=5*/f32[24]{0:T(128)S(1)}, ...), branch_computations={%region_4.0_spmd, %region_5.0_spmd} | conditional | flops 7 | bytes 1622147 | solution.py:256
  79.6 1.2 %add_packed.5 = bf16[1584,128]{1,0:T(8,128)(2,1)S(1)} custom-call(s32[1]{0:T(128)S(6)} %sub.3.where, f32[1552,128]{1,0:T(8,128)S(1)} %get-tuple-element.100.keep_ref, bf16[1584,128]{1,0:T(8,128)(2,1)S(1)} %get-tuple-element.101.refs_0_, bf16[1584,128]{1,0:T(8,128)(2,1)S(1)} %get-tuple-element.102.refs_1_, bf16[1584,128]{1,0:T(8,128)(2,1)} %get-tuple-element.103.refs_2_), custom_call_target="tpu_custom_call" | custom-call | tf_op jit(solution)/shard_map/cond/branch_1_fun/add_packed/pallas_call | solution.py:270
  80.8 0.1 collective-permute-start.2
  80.9 4.0 %linear_own.1 = f32[128,1536]{1,0:T(8,128)S(1)} custom-call(s32[1]{0:T(128)} %get-tuple-element.99.where, f32[24]{0:T(128)S(1)} %get-tuple-element.104.scale, bf16[128,3072]{1,0:T(8,128)(2,1)S(1)} %get-tuple-element.105.q_ref, f32[128,768]{1,0:T(8,128)S(1)} %get-tuple-element.106.factor_ref, f32[128,3072]{1,0:T(8,128)} %get-tuple-element.107.base_ref, ...), custom_call_target="tpu_custom_call" | custom-call | tf_op jit(solution)/shard_map/cond/branch_1_fun/linear_own/pallas_call | solution.py:330
  84.9 4.0 %collective-permute-done.2 = bf16[1584,128]{1,0:T(8,128)(2,1)} collective-permute-done((bf16[1584,128]{1,0:T(8,128)(2,1)S(1)}, bf16[1584,128]{1,0:T(8,128)(2,1)}, u32[]{:S(2)}, u32[]{:S(2)}) %collective-permute-start.2) | collective-permute-done | bytes 405536 | tf_op jit(solution)/shard_map/cond/branch_1_fun/ppermute | solution.py:245
  88.9 0.9 copy-done.4
  89.8 3.8 %linear_other.1.other_ref = f32[128,1536]{1,0:T(8,128)S(1)} custom-call(s32[1]{0:T(128)} %bitcast.where, f32[24]{0:T(128)S(1)} %copy-done.9, bf16[128,3072]{1,0:T(8,128)(2,1)S(1)} %copy-done, f32[128,768]{1,0:T(8,128)S(1)} %get-tuple-element.132.factor_ref, f32[128,3072]{1,0:T(8,128)} %get-tuple-element.136.base_ref, ...), custom_call_target="tpu_custom_call" | custom-call | tf_op jit(solution)/shard_map/linear_other/pallas_call | solution.py:330
  93.6 0.0 collective-permute-done.9.refs_2_
  93.6 0.0 collective-permute-done.10.refs_3_
  93.6 0.0 copy-done.2
  93.6 0.0 copy-done.3
  93.6 0.0 copy-done.5
  93.6 3.3 %finish.1 = bf16[128,3072]{1,0:T(8,128)(2,1)} custom-call(s32[1]{0:T(128)} %bitcast.where, f32[128,768]{1,0:T(8,128)S(1)} %get-tuple-element.132.factor_ref, f32[128,1536]{1,0:T(8,128)S(1)} %copy-done.5, f32[128,1536]{1,0:T(8,128)S(1)} %linear_other.1.other_ref, bf16[128,3072]{1,0:T(8,128)(2,1)S(1)} %copy-done.2, bf16[128,3072]{1,0:T(8,128)(2,1)S(1)} %copy-done.3, ...), custom_call_target="tpu_custom_call" | custom-call | tf_op jit(solution)/shard_map/finish/pallas_call | solution.py:351
  (8 shorter events, 0.1 us)
Async XLA Ops:
  0.0 20.8 %collective-permute-start.4 = (bf16[128,3072]{1,0:T(8,128)(2,1)}, bf16[128,3072]{1,0:T(8,128)(2,1)S(1)}, u32[]{:S(2)}, u32[]{:S(2)}) collective-permute-start(bf16[128,3072]{1,0:T(8,128)(2,1)} %param.12), channel_id=1, source_target_pairs={{0,8},{2,10},{8,12},{10,14},{12,4},{14,6},{4,0},{6,2},{1,9},{3,11}... | collective-permute-start | bytes 2359304 | tf_op jit(solution)/shard_map/ppermute | solution.py:245
  3.8 11.0 %collective-permute-start = (bf16[1584,128]{1,0:T(8,128)(2,1)S(1)}, bf16[1584,128]{1,0:T(8,128)(2,1)}, u32[]{:S(2)}, u32[]{:S(2)}) collective-permute-start(bf16[1584,128]{1,0:T(8,128)(2,1)S(1)} %get-tuple-element.81), channel_id=1, source_target_pairs={{0,2},{2,0},{4,6},{6,4},{8,10},{10,8},{12,14},{14,12},{1,3},{3,1},... | collective-permute-start | bytes 1216520 | tf_op jit(solution)/shard_map/cond/branch_1_fun/ppermute | solution.py:245
  14.8 2.5 %copy-start.1 = (bf16[128,3072]{1,0:T(8,128)(2,1)S(1)}, bf16[128,3072]{1,0:T(8,128)(2,1)}, u32[]{:S(2)}) copy-start(bf16[128,3072]{1,0:T(8,128)(2,1)} %param.12) | copy-start | bytes 2359300
  14.8 46.0 %copy-start = (bf16[128,3072]{1,0:T(8,128)(2,1)S(1)}, bf16[128,3072]{1,0:T(8,128)(2,1)}, u32[]{:S(2)}) copy-start(bf16[128,3072]{1,0:T(8,128)(2,1)} %q_ref.1) | copy-start | bytes 2359300
  14.9 46.0 %copy-start.8 = (s32[8]{0:T(128)S(1)}, s32[8]{0:T(128)}, u32[]{:S(2)}) copy-start(s32[8]{0:T(128)} %param.14) | copy-start | bytes 100
  16.1 14.2 %collective-permute-start.3 = (bf16[1584,128]{1,0:T(8,128)(2,1)S(1)}, bf16[1584,128]{1,0:T(8,128)(2,1)S(1)}, u32[]{:S(2)}, u32[]{:S(2)}) collective-permute-start(bf16[1584,128]{1,0:T(8,128)(2,1)S(1)} %add_packed.6), channel_id=1, source_target_pairs={{0,4},{2,6},{1,5},{3,7},{16,20},{18,22},{17,21},{19,23}} | collective-permute-start | bytes 1216520 | tf_op jit(solution)/shard_map/ppermute | solution.py:245
  17.4 20.0 %collective-permute-start.6 = (bf16[128,3072]{1,0:T(8,128)(2,1)S(1)}, bf16[128,3072]{1,0:T(8,128)(2,1)S(1)}, u32[]{:S(2)}, u32[]{:S(2)}) collective-permute-start(bf16[128,3072]{1,0:T(8,128)(2,1)S(1)} %copy-done.1), channel_id=1, source_target_pairs={{0,2},{2,0},{4,6},{6,4},{8,10},{10,8},{12,14},{14,12},{1,3},{3,1},... | collective-permute-start | bytes 2359304 | tf_op jit(solution)/shard_map/ppermute | solution.py:245
  19.0 27.4 %collective-permute-start.7 = (bf16[128,3072]{1,0:T(8,128)(2,1)S(1)}, bf16[128,3072]{1,0:T(8,128)(2,1)S(1)}, u32[]{:S(2)}, u32[]{:S(2)}) collective-permute-start(bf16[128,3072]{1,0:T(8,128)(2,1)S(1)} %copy-done.1), channel_id=1, source_target_pairs={{8,0},{10,2},{12,8},{14,10},{4,12},{6,14},{0,4},{2,6},{9,1},{11,3}... | collective-permute-start | bytes 2359304 | tf_op jit(solution)/shard_map/ppermute | solution.py:245
  20.8 16.6 %copy-start.6 = (bf16[128,3072]{1,0:T(8,128)(2,1)}, bf16[128,3072]{1,0:T(8,128)(2,1)S(1)}, u32[]{:S(2)}) copy-start(bf16[128,3072]{1,0:T(8,128)(2,1)S(1)} %collective-permute-done.4) | copy-start | bytes 2359300
  31.5 29.4 %collective-permute-start.5 = (bf16[1584,128]{1,0:T(8,128)(2,1)S(1)}, bf16[1584,128]{1,0:T(8,128)(2,1)S(1)}, u32[]{:S(2)}, u32[]{:S(2)}) collective-permute-start(bf16[1584,128]{1,0:T(8,128)(2,1)S(1)} %add_packed.7), channel_id=1, source_target_pairs={{4,8},{6,10},{5,9},{7,11},{20,24},{22,26},{21,25},{23,27}} | collective-permute-start | bytes 1216520 | tf_op jit(solution)/shard_map/ppermute | solution.py:245
  32.8 46.8 %collective-permute-start.8 = (bf16[128,3072]{1,0:T(8,128)(2,1)}, bf16[128,3072]{1,0:T(8,128)(2,1)}, u32[]{:S(2)}, u32[]{:S(2)}) collective-permute-start(bf16[128,3072]{1,0:T(8,128)(2,1)} %param.13), channel_id=1, source_target_pairs={{0,2},{2,0},{4,6},{6,4},{8,10},{10,8},{12,14},{14,12},{1,3},{3,1},... | collective-permute-start | bytes 2359304 | tf_op jit(solution)/shard_map/ppermute | solution.py:245
  46.4 47.2 %collective-permute-start.9 = (bf16[128,3072]{1,0:T(8,128)(2,1)}, bf16[128,3072]{1,0:T(8,128)(2,1)S(1)}, u32[]{:S(2)}, u32[]{:S(2)}) collective-permute-start(bf16[128,3072]{1,0:T(8,128)(2,1)} %param.13), channel_id=1, source_target_pairs={{0,8},{2,10},{8,12},{10,14},{12,4},{14,6},{4,0},{6,2},{1,9},{3,11}... | collective-permute-start | bytes 2359304 | tf_op jit(solution)/shard_map/ppermute | solution.py:245
  60.9 18.7 %copy-start.9 = (f32[24]{0:T(128)S(1)}, f32[24]{0:T(128)}, u32[]{:S(2)}) copy-start(f32[24]{0:T(128)} %scale.1) | copy-start | bytes 292
  60.9 2.8 %copy-start.7 = (bf16[128,3072]{1,0:T(8,128)(2,1)S(1)}, bf16[128,3072]{1,0:T(8,128)(2,1)}, u32[]{:S(2)}) copy-start(bf16[128,3072]{1,0:T(8,128)(2,1)} %get-tuple-element.91.refs_2_) | copy-start | bytes 2359300 | tf_op jit(solution)/shard_map/cond
  62.2 10.3 %collective-permute-start.1 = (bf16[1584,128]{1,0:T(8,128)(2,1)S(1)}, bf16[1584,128]{1,0:T(8,128)(2,1)}, u32[]{:S(2)}, u32[]{:S(2)}) collective-permute-start(bf16[1584,128]{1,0:T(8,128)(2,1)S(1)} %add_packed.4), channel_id=1, source_target_pairs={{8,12},{10,14},{9,13},{11,15},{24,28},{26,30},{25,29},{27,31}} | collective-permute-start | bytes 1216520 | tf_op jit(solution)/shard_map/cond/branch_1_fun/ppermute | solution.py:245
  72.6 21.1 %collective-permute-start.10 = (bf16[128,3072]{1,0:T(8,128)(2,1)}, bf16[128,3072]{1,0:T(8,128)(2,1)S(1)}, u32[]{:S(2)}, u32[]{:S(2)}) collective-permute-start(bf16[128,3072]{1,0:T(8,128)(2,1)} %param.13), channel_id=1, source_target_pairs={{8,0},{10,2},{12,8},{14,10},{4,12},{6,14},{0,4},{2,6},{9,1},{11,3}... | collective-permute-start | bytes 2359304 | tf_op jit(solution)/shard_map/ppermute | solution.py:245
  80.8 8.1 %collective-permute-start.2 = (bf16[1584,128]{1,0:T(8,128)(2,1)S(1)}, bf16[1584,128]{1,0:T(8,128)(2,1)}, u32[]{:S(2)}, u32[]{:S(2)}) collective-permute-start(bf16[1584,128]{1,0:T(8,128)(2,1)S(1)} %add_packed.5), channel_id=1, source_target_pairs={{0,2},{2,0},{4,6},{6,4},{8,10},{10,8},{12,14},{14,12},{1,3},{3,1},... | collective-permute-start | bytes 1216520 | tf_op jit(solution)/shard_map/cond/branch_1_fun/ppermute | solution.py:245
  88.9 0.9 copy-start.4
  89.8 3.9 %copy-start.2 = (bf16[128,3072]{1,0:T(8,128)(2,1)S(1)}, bf16[128,3072]{1,0:T(8,128)(2,1)}, u32[]{:S(2)}) copy-start(bf16[128,3072]{1,0:T(8,128)(2,1)} %get-tuple-element.141.refs_0_) | copy-start | bytes 2359300
  89.8 3.9 %copy-start.3 = (bf16[128,3072]{1,0:T(8,128)(2,1)S(1)}, bf16[128,3072]{1,0:T(8,128)(2,1)}, u32[]{:S(2)}) copy-start(bf16[128,3072]{1,0:T(8,128)(2,1)} %get-tuple-element.142.refs_1_) | copy-start | bytes 2359300
  89.8 3.9 %copy-start.5 = (f32[128,1536]{1,0:T(8,128)S(1)}, f32[128,1536]{1,0:T(8,128)}, u32[]{:S(2)}) copy-start(f32[128,1536]{1,0:T(8,128)} %copy-done.4) | copy-start | bytes 2359300

commit v6 on v5

--- a/solution.py
+++ b/solution.py
@@ -195,16 +195,19 @@
 
 
 def finish_kernel(late, width, where, factor_ref, own_ref, other_ref, *refs):
-    out_ref = refs[2 * late]
+    weight_refs, first_refs, value_refs = refs[:late], refs[late:-late], refs[-late:-1]
+    out_ref = refs[-1]
     a_step = own_ref.shape[1] // width
     own = pl.program_id(0) // (pl.num_programs(0) // 2) == lax.rem(where[0], 2)
     for h in range(a_step):
         at = slice(h * width, (h + 1) * width)
         total = jnp.where(own, own_ref[:, at], other_ref[:, at])
+        values = [functools.reduce(jnp.add, [ref[:, at] for ref in first_refs])]
+        values += [ref[:, at] for ref in value_refs]
         for which in range(late):
             lane = (which + 1) * a_step + h
             total = total + factor_ref[:, lane : lane + 1] * jnp.dot(
-                refs[which][:, at], refs[late + which][:, at], preferred_element_type=F32
+                weight_refs[which][:, at], values[which], preferred_element_type=F32
             )
         out_ref[:, at] = total.astype(BF16)
 
@@ -306,17 +309,20 @@
     hops = [moved(add_packed(one, keep, near), steps[0])]
     far_keys += [moved(after(key_rows, near), turn) for turn in turns[1:]]
     hops.append(moved(add_packed(one, keep, after(near, far_keys[0]), *hops), steps[1]))
-    far_values = [moved(after(value_rows, near_keys, *far_keys), turns[0])]
+    held = [pair for pair in turns[0] if pair[0] < 2 and levels == 3]
+    early = [pair for pair in turns[0] if pair not in held]
+    first_values = [moved(after(value_rows, near_keys, *far_keys), early)]
 
     def last_hop(keep, parts, *operands):
         for pairs in steps[2:]:
             parts = [*parts, moved(add_packed(one, keep, *parts), pairs)]
-        return parts[1:], scores(*operands)
-
-    hops, (*weights, factors, base) = fenced(
+        return parts[1:], scores(*operands), [moved(operands[4], held)] if held else []
+
+    hops, (*weights, factors, base), rest = fenced(
         last_hop, keep, [near, *hops], where, key_len, query_rows, key_rows, value_rows, near_keys, *far_keys
     )
-    far_values += [moved(after(value_rows, *hops), turn) for turn in turns[1:]]
+    first_values += rest
+    far_values = [moved(after(value_rows, *hops), turn) for turn in turns[1:]]
 
     half_grid = grid[0] // 2
     half_f32 = jax.ShapeDtypeStruct((row_count, columns // 2), F32)
@@ -353,13 +359,13 @@
         grid_spec=pltpu.PrefetchScalarGridSpec(
             num_scalar_prefetch=1,
             grid=grid,
-            in_specs=[narrow, half, half] + [wide] * (2 * late),
+            in_specs=[narrow, half, half] + [wide] * (late + len(first_values) + late - 1),
             out_specs=wide,
         ),
         out_shape=full,
         compiler_params=params(),
         name="finish",
-    )(where, factors, own, other, *weights[1:], *far_values)
+    )(where, factors, own, other, *weights[1:], *first_values, *far_values)
 
 
 def solution(mesh):

time: 97.4 us -> 92.6 us (0.951)
  the two profiles are of different devices: /device:TPU:10 before, /device:TPU:0 now
where the time goes in v6:
time: 92.6 us; the launch traced here: 92.1 us
  waiting for transfers between devices  40.8 us (44%)
  Pallas kernels  29.4 us (32%)
  starting transfers between devices  20.1 us (22%)
  local copies, waits for them, and re-layouts  0.97 us (1%)
    ppermute x12, waiting for transfers between devices, moved(): return lax.ppermute(x, 'seq', pairs)  40.8 us
    ppermute x12, starting transfers between devices, moved(): return lax.ppermute(x, 'seq', pairs)  20.1 us
    pallas_call x1, Pallas kernels, scores(): pl.pallas_call(functools.partial(scores_kernel, width, levels), grid_spec...  8.85 us
    pallas_call x2, Pallas kernels, linear(): pl.pallas_call(functools.partial(linear_kernel, heads, width, own, len(pa...  7.81 us
    pallas_call x1, Pallas kernels, shards(): pl.pallas_call(functools.partial(finish_kernel, late, width), grid_spec=p...  5.09 us
    pallas_call x4, Pallas kernels, add_packed(): pl.pallas_call(functools.partial(add_packed_kernel, rows, extra, len(part...  4.9 us
    pallas_call x1, Pallas kernels, block_sums(): pl.pallas_call(functools.partial(block_sums_kernel, heads, width), in_spe...  2.7 us
  transfers between devices with their start and end apart: 12, of which 7 were waited for; matrix products, arithmetic and copies ran while one was open for 0% of the time, Pallas kernels for 26%

profile of v6, /device:TPU:0, one launch (start us, length us, event | category | flops | bytes accessed | tf_op | source)
XLA Modules:
  0.0 92.1 jit_solution(14012556705193091812)
XLA Ops:
  0.0 4.0 %collective-permute-start.5 = (bf16[128,3072]{1,0:T(8,128)(2,1)}, bf16[128,3072]{1,0:T(8,128)(2,1)S(1)}, u32[]{:S(2)}, u32[]{:S(2)}) collective-permute-start(bf16[128,3072]{1,0:T(8,128)(2,1)} %param.12), channel_id=1, source_target_pairs={{0,8},{2,10},{8,12},{10,14},{12,4},{14,6},{4,0},{6,2},{1,9},{3,11}... | collective-permute-start | bytes 2359304 | tf_op jit(solution)/shard_map/ppermute | solution.py:248
  4.7 13.7 %conditional.3 = (f32[1552,128]{1,0:T(8,128)S(1)}, bf16[1584,128]{1,0:T(8,128)(2,1)}) conditional(s32[]{:T(128)} %bitcast.1, () %tuple.36, (s32[1]{0:T(128)}, s32[8]{0:T(128)}, bf16[128,3072]{1,0:T(8,128)(2,1)}, bf16[128,3072]{1,0:T(8,128)(2,1)}) %tuple.37), branch_computations={%region_0.0_spmd, %region_1.0_spmd} | conditional | bytes 1622072 | solution.py:259
  4.7 2.7 %block_sums.1 = (bf16[1584,128]{1,0:T(8,128)(2,1)S(1)}, f32[1552,128]{1,0:T(8,128)S(1)}) custom-call(s32[1]{0:T(128)} %get-tuple-element.76.where, s32[8]{0:T(128)} %get-tuple-element.77.lengths, bf16[128,3072]{1,0:T(8,128)(2,1)} %get-tuple-element.78.k_ref, bf16[128,3072]{1,0:T(8,128)(2,1)} %get-tuple-element.79.v_ref), custom_call_target="tpu_custom_call" | custom-call | tf_op jit(solution)/shard_map/cond/branch_1_fun/block_sums/pallas_call | solution.py:262
  7.4 1.6 %collective-permute-start = (bf16[1584,128]{1,0:T(8,128)(2,1)S(1)}, bf16[1584,128]{1,0:T(8,128)(2,1)}, u32[]{:S(2)}, u32[]{:S(2)}) collective-permute-start(bf16[1584,128]{1,0:T(8,128)(2,1)S(1)} %get-tuple-element.81), channel_id=1, source_target_pairs={{0,2},{2,0},{4,6},{6,4},{8,10},{10,8},{12,14},{14,12},{1,3},{3,1},... | collective-permute-start | bytes 1216520 | tf_op jit(solution)/shard_map/cond/branch_1_fun/ppermute | solution.py:248
  9.0 9.4 %collective-permute-done = bf16[1584,128]{1,0:T(8,128)(2,1)} collective-permute-done((bf16[1584,128]{1,0:T(8,128)(2,1)S(1)}, bf16[1584,128]{1,0:T(8,128)(2,1)}, u32[]{:S(2)}, u32[]{:S(2)}) %collective-permute-start) | collective-permute-done | bytes 405536 | tf_op jit(solution)/shard_map/cond/branch_1_fun/ppermute | solution.py:248
  18.4 0.0 copy-start.1
  18.4 1.2 %add_packed.6 = bf16[1584,128]{1,0:T(8,128)(2,1)S(1)} custom-call(s32[1]{0:T(128)} %constant.34.clone.1.where, f32[1552,128]{1,0:T(8,128)S(1)} %get-tuple-element.129.keep_ref, bf16[1584,128]{1,0:T(8,128)(2,1)} %get-tuple-element.131.refs_0_), custom_call_target="tpu_custom_call" | custom-call | tf_op jit(solution)/shard_map/add_packed/pallas_call | solution.py:273
  19.7 1.3 %collective-permute-start.4 = (bf16[1584,128]{1,0:T(8,128)(2,1)S(1)}, bf16[1584,128]{1,0:T(8,128)(2,1)S(1)}, u32[]{:S(2)}, u32[]{:S(2)}) collective-permute-start(bf16[1584,128]{1,0:T(8,128)(2,1)S(1)} %add_packed.6), channel_id=1, source_target_pairs={{0,4},{2,6},{1,5},{3,7},{16,20},{18,22},{17,21},{19,23}} | collective-permute-start | bytes 1216520 | tf_op jit(solution)/shard_map/ppermute | solution.py:248
  21.0 0.0 copy-done.1
  21.0 1.6 %collective-permute-start.7 = (bf16[128,3072]{1,0:T(8,128)(2,1)S(1)}, bf16[128,3072]{1,0:T(8,128)(2,1)S(1)}, u32[]{:S(2)}, u32[]{:S(2)}) collective-permute-start(bf16[128,3072]{1,0:T(8,128)(2,1)S(1)} %copy-done.1), channel_id=1, source_target_pairs={{0,2},{2,0},{4,6},{6,4},{8,10},{10,8},{12,14},{14,12},{1,3},{3,1},... | collective-permute-start | bytes 2359304 | tf_op jit(solution)/shard_map/ppermute | solution.py:248
  22.6 0.0 collective-permute-start.8
  22.6 0.0 collective-permute-done.5
  22.6 8.1 %collective-permute-done.4.refs_1_ = bf16[1584,128]{1,0:T(8,128)(2,1)S(1)} collective-permute-done((bf16[1584,128]{1,0:T(8,128)(2,1)S(1)}, bf16[1584,128]{1,0:T(8,128)(2,1)S(1)}, u32[]{:S(2)}, u32[]{:S(2)}) %collective-permute-start.4) | collective-permute-done | bytes 405536 | tf_op jit(solution)/shard_map/ppermute | solution.py:248
  30.7 1.2 %add_packed.7 = bf16[1584,128]{1,0:T(8,128)(2,1)S(1)} custom-call(s32[1]{0:T(128)} %constant.34.clone.1.where, f32[1552,128]{1,0:T(8,128)S(1)} %get-tuple-element.129.keep_ref, bf16[1584,128]{1,0:T(8,128)(2,1)} %get-tuple-element.131.refs_0_, bf16[1584,128]{1,0:T(8,128)(2,1)S(1)} %collective-permute-done.4.refs_1_), custom_call_target="tpu_custom_call" | custom-call | tf_op jit(solution)/shard_map/add_packed/pallas_call | solution.py:273
  31.9 0.7 collective-permute-start.6
  32.6 1.7 %collective-permute-start.9 = (bf16[128,3072]{1,0:T(8,128)(2,1)}, bf16[128,3072]{1,0:T(8,128)(2,1)}, u32[]{:S(2)}, u32[]{:S(2)}) collective-permute-start(bf16[128,3072]{1,0:T(8,128)(2,1)} %param.13), channel_id=1, source_target_pairs={{0,2},{2,0},{4,6},{6,4},{8,10},{10,8},{12,14},{14,12},{1,3},{3,1},... | collective-permute-start | bytes 2359304 | tf_op jit(solution)/shard_map/ppermute | solution.py:248
  34.3 7.3 %collective-permute-done.7 = bf16[128,3072]{1,0:T(8,128)(2,1)S(1)} collective-permute-done((bf16[128,3072]{1,0:T(8,128)(2,1)S(1)}, bf16[128,3072]{1,0:T(8,128)(2,1)S(1)}, u32[]{:S(2)}, u32[]{:S(2)}) %collective-permute-start.7) | collective-permute-done | bytes 786464 | tf_op jit(solution)/shard_map/ppermute | solution.py:248
  41.5 0.0 copy-done.6
  41.5 5.1 %collective-permute-done.8 = bf16[128,3072]{1,0:T(8,128)(2,1)S(1)} collective-permute-done((bf16[128,3072]{1,0:T(8,128)(2,1)S(1)}, bf16[128,3072]{1,0:T(8,128)(2,1)S(1)}, u32[]{:S(2)}, u32[]{:S(2)}) %collective-permute-start.8) | collective-permute-done | bytes 786464 | tf_op jit(solution)/shard_map/ppermute | solution.py:248
  46.6 1.3 %collective-permute-start.10 = (bf16[128,3072]{1,0:T(8,128)(2,1)}, bf16[128,3072]{1,0:T(8,128)(2,1)S(1)}, u32[]{:S(2)}, u32[]{:S(2)}) collective-permute-start(bf16[128,3072]{1,0:T(8,128)(2,1)} %param.13), channel_id=1, source_target_pairs={{8,12},{10,14},{12,4},{14,6},{4,0},{6,2},{9,13},{11,15},{13,5},{15... | collective-permute-start | bytes 2359304 | tf_op jit(solution)/shard_map/ppermute | solution.py:248
  47.9 0.0 collective-permute-done.6
  47.9 0.0 copy-done
  47.9 0.0 copy-done.8
  47.9 0.0 copy-start.9
  47.9 21.8 %conditional.4 = (bf16[1584,128]{1,0:T(8,128)(2,1)S(1)}, bf16[1584,128]{1,0:T(8,128)(2,1)S(1)}, bf16[1584,128]{1,0:T(8,128)(2,1)}, bf16[128,3072]{1,0:T(8,128)(2...) conditional(s32[]{:T(128)} %bitcast.1, () %tuple.35, ...), branch_computations={%region_2.0_spmd, %region_3.0_spmd} | conditional | bytes 9535668 | solution.py:259
  47.9 5.3 %collective-permute-start.2 = (bf16[128,3072]{1,0:T(8,128)(2,1)}, bf16[128,3072]{1,0:T(8,128)(2,1)}, u32[]{:S(2)}, u32[]{:S(2)}) collective-permute-start(bf16[128,3072]{1,0:T(8,128)(2,1)} %get-tuple-element.93.refs_4_), channel_id=1, source_target_pairs={{0,8},{2,10},{1,9},{3,11},{16,24},{18,26},{17,25},{19,27}} | collective-permute-start | bytes 2359304 | tf_op jit(solution)/shard_map/cond/branch_1_fun/ppermute | solution.py:248
  53.2 1.3 %add_packed.4 = bf16[1584,128]{1,0:T(8,128)(2,1)S(1)} custom-call(s32[1]{0:T(128)} %constant.19.clone.where, f32[1552,128]{1,0:T(8,128)S(1)} %get-tuple-element.84.keep_ref, bf16[1584,128]{1,0:T(8,128)(2,1)} %get-tuple-element.85.refs_0_, bf16[1584,128]{1,0:T(8,128)(2,1)S(1)} %get-tuple-element.160.refs_1_, bf16[1584,128]{1,0:T(8,128)(2,1)S(1)} %get-tuple-element.161.refs_2_), custom_call_target="tpu_custom_call" | custom-call | tf_op jit(solution)/shard_map/cond/branch_1_fun/add_packed/pallas_call | solution.py:273
  54.5 1.4 %collective-permute-start.1 = (bf16[1584,128]{1,0:T(8,128)(2,1)S(1)}, bf16[1584,128]{1,0:T(8,128)(2,1)}, u32[]{:S(2)}, u32[]{:S(2)}) collective-permute-start(bf16[1584,128]{1,0:T(8,128)(2,1)S(1)} %add_packed.4), channel_id=1, source_target_pairs={{8,12},{10,14},{9,13},{11,15},{24,28},{26,30},{25,29},{27,31}} | collective-permute-start | bytes 1216520 | tf_op jit(solution)/shard_map/cond/branch_1_fun/ppermute | solution.py:248
  56.0 0.0 copy-done.7
  56.0 8.8 %scores.1 = (bf16[128,3072]{1,0:T(8,128)(2,1)}, bf16[128,3072]{1,0:T(8,128)(2,1)}, bf16[128,3072]{1,0:T(8,128)(2,1)}, f32[128,768]{1,0:T(8,128)S(1)}, f32[128,3072]{1,0:T(8,128)}) custom-call(s32[1]{0:T(128)} %get-tuple-element.86.where, s32[8]{0:T(128)S(1)} %get-tuple-element.87.lengths, bf16[128,3072]{1,0:T(8,128)(2,1)S(1)} %get-tuple-element.88.q_ref, ...), custom_call_target="tpu_custom_call" | custom-call | tf_op jit(solution)/shard_map/cond/branch_1_fun/scores/pallas_call | solution.py:291
  64.9 0.0 collective-permute-done.1
  64.9 4.8 %collective-permute-done.2 = bf16[128,3072]{1,0:T(8,128)(2,1)} collective-permute-done((bf16[128,3072]{1,0:T(8,128)(2,1)}, bf16[128,3072]{1,0:T(8,128)(2,1)}, u32[]{:S(2)}, u32[]{:S(2)}) %collective-permute-start.2) | collective-permute-done | bytes 786464 | tf_op jit(solution)/shard_map/cond/branch_1_fun/ppermute | solution.py:248
  69.7 0.0 collective-permute-start.11
  69.7 0.0 collective-permute-done.9.value_ref
  69.7 0.0 copy-done.9
  69.7 9.3 %conditional.5 = (bf16[1584,128]{1,0:T(8,128)(2,1)}, f32[128,1536]{1,0:T(8,128)S(1)}) conditional(s32[]{:T(128)} %bitcast.1, () %tuple.41, (s32[1]{0:T(128)}, f32[1552,128]{1,0:T(8,128)S(1)}, bf16[1584,128]{1,0:T(8,128)(2,1)S(1)}, bf16[1584,128]{1,0:T(8,128)(2,1)S(1)}, bf16[1584,128]{1,0:T(8,128)(2,1)}, /*index=5*/f32[24]{0:T(128)S(1)}, ...), branch_computations={%region_4.0_spmd, %region_5.0_spmd} | conditional | flops 7 | bytes 1622147 | solution.py:259
  69.8 1.2 %add_packed.5 = bf16[1584,128]{1,0:T(8,128)(2,1)S(1)} custom-call(s32[1]{0:T(128)S(6)} %sub.3.where, f32[1552,128]{1,0:T(8,128)S(1)} %get-tuple-element.100.keep_ref, bf16[1584,128]{1,0:T(8,128)(2,1)S(1)} %get-tuple-element.101.refs_0_, bf16[1584,128]{1,0:T(8,128)(2,1)S(1)} %get-tuple-element.102.refs_1_, bf16[1584,128]{1,0:T(8,128)(2,1)} %get-tuple-element.103.refs_2_), custom_call_target="tpu_custom_call" | custom-call | tf_op jit(solution)/shard_map/cond/branch_1_fun/add_packed/pallas_call | solution.py:273
  71.0 1.2 %collective-permute-start.3 = (bf16[1584,128]{1,0:T(8,128)(2,1)S(1)}, bf16[1584,128]{1,0:T(8,128)(2,1)}, u32[]{:S(2)}, u32[]{:S(2)}) collective-permute-start(bf16[1584,128]{1,0:T(8,128)(2,1)S(1)} %add_packed.5), channel_id=1, source_target_pairs={{0,2},{2,0},{4,6},{6,4},{8,10},{10,8},{12,14},{14,12},{1,3},{3,1},... | collective-permute-start | bytes 1216520 | tf_op jit(solution)/shard_map/cond/branch_1_fun/ppermute | solution.py:248
  72.1 4.0 %linear_own.1 = f32[128,1536]{1,0:T(8,128)S(1)} custom-call(s32[1]{0:T(128)} %get-tuple-element.99.where, f32[24]{0:T(128)S(1)} %get-tuple-element.104.scale, bf16[128,3072]{1,0:T(8,128)(2,1)S(1)} %get-tuple-element.105.q_ref, f32[128,768]{1,0:T(8,128)S(1)} %get-tuple-element.106.factor_ref, f32[128,3072]{1,0:T(8,128)} %get-tuple-element.107.base_ref, ...), custom_call_target="tpu_custom_call" | custom-call | tf_op jit(solution)/shard_map/cond/branch_1_fun/linear_own/pallas_call | solution.py:336
  76.1 2.9 %collective-permute-done.3 = bf16[1584,128]{1,0:T(8,128)(2,1)} collective-permute-done((bf16[1584,128]{1,0:T(8,128)(2,1)S(1)}, bf16[1584,128]{1,0:T(8,128)(2,1)}, u32[]{:S(2)}, u32[]{:S(2)}) %collective-permute-start.3) | collective-permute-done | bytes 405536 | tf_op jit(solution)/shard_map/cond/branch_1_fun/ppermute | solution.py:248
  79.1 0.9 copy-done.4
  79.9 3.8 %linear_other.1.other_ref = f32[128,1536]{1,0:T(8,128)S(1)} custom-call(s32[1]{0:T(128)} %bitcast.where, f32[24]{0:T(128)S(1)} %copy-done.9, bf16[128,3072]{1,0:T(8,128)(2,1)S(1)} %copy-done, f32[128,768]{1,0:T(8,128)S(1)} %get-tuple-element.133.factor_ref, f32[128,3072]{1,0:T(8,128)} %get-tuple-element.137.base_ref, ...), custom_call_target="tpu_custom_call" | custom-call | tf_op jit(solution)/shard_map/linear_other/pallas_call | solution.py:336
  83.8 0.0 collective-permute-done.10.refs_2_
  83.8 3.2 %collective-permute-done.11.refs_4_ = bf16[128,3072]{1,0:T(8,128)(2,1)S(1)} collective-permute-done((bf16[128,3072]{1,0:T(8,128)(2,1)}, bf16[128,3072]{1,0:T(8,128)(2,1)S(1)}, u32[]{:S(2)}, u32[]{:S(2)}) %collective-permute-start.11) | collective-permute-done | bytes 786464 | tf_op jit(solution)/shard_map/ppermute | solution.py:248
  87.0 0.0 copy-done.2
  87.0 0.0 copy-done.3
  87.0 0.0 copy-done.5
  87.0 5.1 %finish.1 = bf16[128,3072]{1,0:T(8,128)(2,1)} custom-call(s32[1]{0:T(128)} %bitcast.where, f32[128,768]{1,0:T(8,128)S(1)} %get-tuple-element.133.factor_ref, f32[128,1536]{1,0:T(8,128)S(1)} %copy-done.5, f32[128,1536]{1,0:T(8,128)S(1)} %linear_other.1.other_ref, bf16[128,3072]{1,0:T(8,128)(2,1)S(1)} %copy-done.2, bf16[128,3072]{1,0:T(8,128)(2,1)S(1)} %copy-done.3, ...), custom_call_target="tpu_custom_call" | custom-call | tf_op jit(solution)/shard_map/finish/pallas_call | solution.py:357
  (10 shorter events, 0.1 us)
Async XLA Ops:
  0.0 22.6 %collective-permute-start.5 = (bf16[128,3072]{1,0:T(8,128)(2,1)}, bf16[128,3072]{1,0:T(8,128)(2,1)S(1)}, u32[]{:S(2)}, u32[]{:S(2)}) collective-permute-start(bf16[128,3072]{1,0:T(8,128)(2,1)} %param.12), channel_id=1, source_target_pairs={{0,8},{2,10},{8,12},{10,14},{12,4},{14,6},{4,0},{6,2},{1,9},{3,11}... | collective-permute-start | bytes 2359304 | tf_op jit(solution)/shard_map/ppermute | solution.py:248
  7.4 11.0 %collective-permute-start = (bf16[1584,128]{1,0:T(8,128)(2,1)S(1)}, bf16[1584,128]{1,0:T(8,128)(2,1)}, u32[]{:S(2)}, u32[]{:S(2)}) collective-permute-start(bf16[1584,128]{1,0:T(8,128)(2,1)S(1)} %get-tuple-element.81), channel_id=1, source_target_pairs={{0,2},{2,0},{4,6},{6,4},{8,10},{10,8},{12,14},{14,12},{1,3},{3,1},... | collective-permute-start | bytes 1216520 | tf_op jit(solution)/shard_map/cond/branch_1_fun/ppermute | solution.py:248
  18.4 2.5 %copy-start.1 = (bf16[128,3072]{1,0:T(8,128)(2,1)S(1)}, bf16[128,3072]{1,0:T(8,128)(2,1)}, u32[]{:S(2)}) copy-start(bf16[128,3072]{1,0:T(8,128)(2,1)} %param.12) | copy-start | bytes 2359300
  18.4 29.5 %copy-start = (bf16[128,3072]{1,0:T(8,128)(2,1)S(1)}, bf16[128,3072]{1,0:T(8,128)(2,1)}, u32[]{:S(2)}) copy-start(bf16[128,3072]{1,0:T(8,128)(2,1)} %q_ref.1) | copy-start | bytes 2359300
  18.4 29.5 %copy-start.8 = (s32[8]{0:T(128)S(1)}, s32[8]{0:T(128)}, u32[]{:S(2)}) copy-start(s32[8]{0:T(128)} %param.14) | copy-start | bytes 100
  19.7 11.1 %collective-permute-start.4 = (bf16[1584,128]{1,0:T(8,128)(2,1)S(1)}, bf16[1584,128]{1,0:T(8,128)(2,1)S(1)}, u32[]{:S(2)}, u32[]{:S(2)}) collective-permute-start(bf16[1584,128]{1,0:T(8,128)(2,1)S(1)} %add_packed.6), channel_id=1, source_target_pairs={{0,4},{2,6},{1,5},{3,7},{16,20},{18,22},{17,21},{19,23}} | collective-permute-start | bytes 1216520 | tf_op jit(solution)/shard_map/ppermute | solution.py:248
  21.0 20.5 %collective-permute-start.7 = (bf16[128,3072]{1,0:T(8,128)(2,1)S(1)}, bf16[128,3072]{1,0:T(8,128)(2,1)S(1)}, u32[]{:S(2)}, u32[]{:S(2)}) collective-permute-start(bf16[128,3072]{1,0:T(8,128)(2,1)S(1)} %copy-done.1), channel_id=1, source_target_pairs={{0,2},{2,0},{4,6},{6,4},{8,10},{10,8},{12,14},{14,12},{1,3},{3,1},... | collective-permute-start | bytes 2359304 | tf_op jit(solution)/shard_map/ppermute | solution.py:248
  22.6 24.0 %collective-permute-start.8 = (bf16[128,3072]{1,0:T(8,128)(2,1)S(1)}, bf16[128,3072]{1,0:T(8,128)(2,1)S(1)}, u32[]{:S(2)}, u32[]{:S(2)}) collective-permute-start(bf16[128,3072]{1,0:T(8,128)(2,1)S(1)} %copy-done.1), channel_id=1, source_target_pairs={{8,0},{10,2},{12,8},{14,10},{4,12},{6,14},{0,4},{2,6},{9,1},{11,3}... | collective-permute-start | bytes 2359304 | tf_op jit(solution)/shard_map/ppermute | solution.py:248
  22.6 18.9 %copy-start.6 = (bf16[128,3072]{1,0:T(8,128)(2,1)}, bf16[128,3072]{1,0:T(8,128)(2,1)S(1)}, u32[]{:S(2)}) copy-start(bf16[128,3072]{1,0:T(8,128)(2,1)S(1)} %collective-permute-done.5) | copy-start | bytes 2359300
  31.9 16.0 %collective-permute-start.6 = (bf16[1584,128]{1,0:T(8,128)(2,1)S(1)}, bf16[1584,128]{1,0:T(8,128)(2,1)S(1)}, u32[]{:S(2)}, u32[]{:S(2)}) collective-permute-start(bf16[1584,128]{1,0:T(8,128)(2,1)S(1)} %add_packed.7), channel_id=1, source_target_pairs={{4,8},{6,10},{5,9},{7,11},{20,24},{22,26},{21,25},{23,27}} | collective-permute-start | bytes 1216520 | tf_op jit(solution)/shard_map/ppermute | solution.py:248
  32.6 37.1 %collective-permute-start.9 = (bf16[128,3072]{1,0:T(8,128)(2,1)}, bf16[128,3072]{1,0:T(8,128)(2,1)}, u32[]{:S(2)}, u32[]{:S(2)}) collective-permute-start(bf16[128,3072]{1,0:T(8,128)(2,1)} %param.13), channel_id=1, source_target_pairs={{0,2},{2,0},{4,6},{6,4},{8,10},{10,8},{12,14},{14,12},{1,3},{3,1},... | collective-permute-start | bytes 2359304 | tf_op jit(solution)/shard_map/ppermute | solution.py:248
  46.6 37.2 %collective-permute-start.10 = (bf16[128,3072]{1,0:T(8,128)(2,1)}, bf16[128,3072]{1,0:T(8,128)(2,1)S(1)}, u32[]{:S(2)}, u32[]{:S(2)}) collective-permute-start(bf16[128,3072]{1,0:T(8,128)(2,1)} %param.13), channel_id=1, source_target_pairs={{8,12},{10,14},{12,4},{14,6},{4,0},{6,2},{9,13},{11,15},{13,5},{15... | collective-permute-start | bytes 2359304 | tf_op jit(solution)/shard_map/ppermute | solution.py:248
  47.9 21.8 %copy-start.9 = (f32[24]{0:T(128)S(1)}, f32[24]{0:T(128)}, u32[]{:S(2)}) copy-start(f32[24]{0:T(128)} %scale.1) | copy-start | bytes 292
  47.9 21.8 %collective-permute-start.2 = (bf16[128,3072]{1,0:T(8,128)(2,1)}, bf16[128,3072]{1,0:T(8,128)(2,1)}, u32[]{:S(2)}, u32[]{:S(2)}) collective-permute-start(bf16[128,3072]{1,0:T(8,128)(2,1)} %get-tuple-element.93.refs_4_), channel_id=1, source_target_pairs={{0,8},{2,10},{1,9},{3,11},{16,24},{18,26},{17,25},{19,27}} | collective-permute-start | bytes 2359304 | tf_op jit(solution)/shard_map/cond/branch_1_fun/ppermute | solution.py:248
  53.2 2.8 %copy-start.7 = (bf16[128,3072]{1,0:T(8,128)(2,1)S(1)}, bf16[128,3072]{1,0:T(8,128)(2,1)}, u32[]{:S(2)}) copy-start(bf16[128,3072]{1,0:T(8,128)(2,1)} %get-tuple-element.91.refs_2_) | copy-start | bytes 2359300 | tf_op jit(solution)/shard_map/cond
  54.5 10.3 %collective-permute-start.1 = (bf16[1584,128]{1,0:T(8,128)(2,1)S(1)}, bf16[1584,128]{1,0:T(8,128)(2,1)}, u32[]{:S(2)}, u32[]{:S(2)}) collective-permute-start(bf16[1584,128]{1,0:T(8,128)(2,1)S(1)} %add_packed.4), channel_id=1, source_target_pairs={{8,12},{10,14},{9,13},{11,15},{24,28},{26,30},{25,29},{27,31}} | collective-permute-start | bytes 1216520 | tf_op jit(solution)/shard_map/cond/branch_1_fun/ppermute | solution.py:248
  69.7 17.3 %collective-permute-start.11 = (bf16[128,3072]{1,0:T(8,128)(2,1)}, bf16[128,3072]{1,0:T(8,128)(2,1)S(1)}, u32[]{:S(2)}, u32[]{:S(2)}) collective-permute-start(bf16[128,3072]{1,0:T(8,128)(2,1)} %param.13), channel_id=1, source_target_pairs={{8,0},{10,2},{12,8},{14,10},{4,12},{6,14},{0,4},{2,6},{9,1},{11,3}... | collective-permute-start | bytes 2359304 | tf_op jit(solution)/shard_map/ppermute | solution.py:248
  71.0 8.1 %collective-permute-start.3 = (bf16[1584,128]{1,0:T(8,128)(2,1)S(1)}, bf16[1584,128]{1,0:T(8,128)(2,1)}, u32[]{:S(2)}, u32[]{:S(2)}) collective-permute-start(bf16[1584,128]{1,0:T(8,128)(2,1)S(1)} %add_packed.5), channel_id=1, source_target_pairs={{0,2},{2,0},{4,6},{6,4},{8,10},{10,8},{12,14},{14,12},{1,3},{3,1},... | collective-permute-start | bytes 1216520 | tf_op jit(solution)/shard_map/cond/branch_1_fun/ppermute | solution.py:248
  79.1 0.9 copy-start.4
  79.9 7.1 %copy-start.2 = (bf16[128,3072]{1,0:T(8,128)(2,1)S(1)}, bf16[128,3072]{1,0:T(8,128)(2,1)}, u32[]{:S(2)}) copy-start(bf16[128,3072]{1,0:T(8,128)(2,1)} %get-tuple-element.142.refs_0_) | copy-start | bytes 2359300
  79.9 7.1 %copy-start.3 = (bf16[128,3072]{1,0:T(8,128)(2,1)S(1)}, bf16[128,3072]{1,0:T(8,128)(2,1)}, u32[]{:S(2)}) copy-start(bf16[128,3072]{1,0:T(8,128)(2,1)} %get-tuple-element.143.refs_1_) | copy-start | bytes 2359300
  79.9 7.1 %copy-start.5 = (f32[128,1536]{1,0:T(8,128)S(1)}, f32[128,1536]{1,0:T(8,128)}, u32[]{:S(2)}) copy-start(f32[128,1536]{1,0:T(8,128)} %copy-done.4) | copy-start | bytes 2359300

commit v7 on v5

--- a/solution.py
+++ b/solution.py
@@ -155,22 +155,36 @@
     factor_ref[...] = factors
 
 
-def linear_kernel(heads, width, own, parts, tokens, where, scale, q_ref, factor_ref, base_ref, weight_ref, value_ref, *refs):
+def parts_kernel(width, counts, factor_ref, base_ref, *refs):
+    weight_refs, value_refs, out_ref = refs[: len(counts)], refs[len(counts) : -1], refs[-1]
+    a_step = base_ref.shape[1] // width
+    for h in range(a_step):
+        at = slice(h * width, (h + 1) * width)
+        total = base_ref[:, at]
+        first = 0
+        for which, count in enumerate(counts):
+            values = functools.reduce(jnp.add, [ref[:, at] for ref in value_refs[first : first + count]])
+            first += count
+            lane = which * a_step + h
+            total = total + factor_ref[:, lane : lane + 1] * jnp.dot(
+                weight_refs[which][:, at], values, preferred_element_type=F32
+            )
+        out_ref[:, at] = total
+
+
+def linear_kernel(heads, width, own, parts, tokens, where, scale, q_ref, *refs):
     part_refs, out_ref = refs[:parts], refs[parts]
     side = lax.rem(where[0], 2)
     half_heads = heads // 2
     rows, extra = half_heads * width, padded(half_heads)
-    a_step = q_ref.shape[1] // width
-    in_half = pl.program_id(0) * a_step
-    first = (side if own else 1 - side) * half_heads + in_half
+    start = (side if own else 1 - side) * half_heads
     flags = [1.0] * (parts - 1) + [side.astype(F32) if own else 1.0]
     sums = functools.reduce(
         jnp.add, [flag * packed_sums(ref, rows, extra) for flag, ref in zip(flags, part_refs)]
     )
-    sum_row = lax.broadcasted_iota(jnp.int32, sums.shape, 0)
-    for h in range(a_step):
-        at = slice(h * width, (h + 1) * width)
-        block = pl.ds(pl.multiple_of((in_half + h) * width, width), width)
+    for h in range(half_heads):
+        at = pl.ds(pl.multiple_of((start + h) * width, width), width)
+        block = slice(h * width, (h + 1) * width)
         mapped = feature(q_ref[:, at].astype(F32))
         high, low = halves(mapped)
         if own:
@@ -187,26 +201,27 @@
         )
         if own:
             linear = linear + jnp.dot(high, rest, preferred_element_type=F32)
-        value_sum = jnp.sum(jnp.where(sum_row == in_half + h, sums, 0.0), axis=0, keepdims=True)
-        linear = linear + jnp.sum(mapped, axis=1, keepdims=True) * (CENTER * value_sum)
-        near = jnp.dot(weight_ref[:, at], value_ref[:, at], preferred_element_type=F32)
-        total = base_ref[:, at] + factor_ref[:, h : h + 1] * near
-        out_ref[:, at] = total + linear * (scale[first + h] * (1.0 / (width * math.sqrt(tokens))))
-
-
-def finish_kernel(late, width, where, factor_ref, own_ref, other_ref, *refs):
-    out_ref = refs[2 * late]
-    a_step = own_ref.shape[1] // width
-    own = pl.program_id(0) // (pl.num_programs(0) // 2) == lax.rem(where[0], 2)
-    for h in range(a_step):
-        at = slice(h * width, (h + 1) * width)
-        total = jnp.where(own, own_ref[:, at], other_ref[:, at])
-        for which in range(late):
-            lane = (which + 1) * a_step + h
-            total = total + factor_ref[:, lane : lane + 1] * jnp.dot(
-                refs[which][:, at], refs[late + which][:, at], preferred_element_type=F32
-            )
-        out_ref[:, at] = total.astype(BF16)
+        linear = linear + jnp.sum(mapped, axis=1, keepdims=True) * (CENTER * sums[h : h + 1, :])
+        out_ref[:, block] = linear * (scale[start + h] * (1.0 / (width * math.sqrt(tokens))))
+
+
+def finish_kernel(heads, width, late, a_step, where, factor_ref, base_ref, own_ref, other_ref, *refs):
+    weight_refs, value_refs, out_ref = refs[: late - 1], refs[late - 1 : -1], refs[-1]
+    side = lax.rem(where[0], 2)
+    half_heads = heads // 2
+    for own, linear_ref in ((True, own_ref), (False, other_ref)):
+        start = (side if own else 1 - side) * half_heads
+        for h in range(half_heads):
+            at = pl.ds(pl.multiple_of((start + h) * width, width), width)
+            total = base_ref[:, at] + linear_ref[:, h * width : (h + 1) * width]
+            column = pl.ds(pl.multiple_of((start + h) // a_step * 128, 128), 128)
+            factors = factor_ref[:, column]
+            for which in range(late - 1):
+                lane = (which + 2) * a_step + h % a_step
+                total = total + factors[:, lane : lane + 1] * jnp.dot(
+                    weight_refs[which][:, at], value_refs[which][:, at], preferred_element_type=F32
+                )
+            out_ref[:, at] = total.astype(BF16)
 
 
 def params():
@@ -302,11 +317,15 @@
     far_keys = [moved(key_rows, turns[0])]
     keep, near = fenced(block_sums, where, key_len, key_rows, value_rows)
     near_keys = moved(after(key_rows, near), swaps)
-    near_values = moved(after(value_rows, near), swaps)
     hops = [moved(add_packed(one, keep, near), steps[0])]
     far_keys += [moved(after(key_rows, near), turn) for turn in turns[1:]]
     hops.append(moved(add_packed(one, keep, after(near, far_keys[0]), *hops), steps[1]))
-    far_values = [moved(after(value_rows, near_keys, *far_keys), turns[0])]
+    held = [pair for pair in turns[0] if pair[0] < 2 and levels == 3]
+    early = [pair for pair in turns[0] if pair not in held]
+    first_values = [moved(after(value_rows, near_keys), early)]
+    near_values = moved(after(value_rows, near_keys, *far_keys), swaps)
+    if held:
+        first_values.append(moved(after(value_rows, near_keys, *far_keys), held))
 
     def last_hop(keep, parts, *operands):
         for pairs in steps[2:]:
@@ -316,50 +335,39 @@
     hops, (*weights, factors, base) = fenced(
         last_hop, keep, [near, *hops], where, key_len, query_rows, key_rows, value_rows, near_keys, *far_keys
     )
-    far_values += [moved(after(value_rows, *hops), turn) for turn in turns[1:]]
-
-    half_grid = grid[0] // 2
-    half_f32 = jax.ShapeDtypeStruct((row_count, columns // 2), F32)
-
-    def linear(own, where, linear_scale, query_rows, factors, base, weights, near_values, *parts):
-        def at(i, where, scale):
-            side = lax.rem(where[0], 2)
-            return 0, (side if own else 1 - side) * half_grid + i
-
-        chosen = pl.BlockSpec((row_count, a_step * width), at)
+    far_values = [moved(after(value_rows, *hops), turn) for turn in turns[1:]]
+
+    far = moved(add_packed(1 - lax.rem(where, 2), keep, *hops), swaps)
+    def linear(own, *parts):
         return pl.pallas_call(
             functools.partial(linear_kernel, heads, width, own, len(parts), tokens),
-            grid_spec=pltpu.PrefetchScalarGridSpec(
-                num_scalar_prefetch=2,
-                grid=(half_grid,),
-                in_specs=[chosen, pl.BlockSpec((row_count, 128), at)] + [chosen] * 3 + [whole] * len(parts),
-                out_specs=wide,
-            ),
-            out_shape=half_f32,
+            in_specs=[smem, smem] + [vmem] * (1 + len(parts)),
+            out_specs=vmem,
+            out_shape=jax.ShapeDtypeStruct((row_count, columns // 2), F32),
             compiler_params=params(),
             name="linear_own" if own else "linear_other",
-        )(where, linear_scale, query_rows, factors, base, weights, near_values, *parts)
-
-    operands = (where, linear_scale, query_rows, factors, base, weights[0], near_values)
-
-    def last_exchange(flag, keep, near, hops, *operands):
-        return moved(add_packed(flag, keep, *hops), swaps), linear(True, *operands, *hops, near)
-
-    far, own = fenced(last_exchange, 1 - lax.rem(where, 2), keep, near, hops, *operands)
-    other = linear(False, *operands, far)
-    half = pl.BlockSpec((row_count, a_step * width), lambda i, *_: (0, lax.rem(i, half_grid)))
+        )(where, linear_scale, query_rows, *parts)
+
+    own = linear(True, *hops, after(near, first_values[0]))
+    base = pl.pallas_call(
+        functools.partial(parts_kernel, width, [1, len(first_values)]),
+        grid=grid,
+        in_specs=[narrow] + [wide] * (1 + 2 + 1 + len(first_values)),
+        out_specs=wide,
+        out_shape=full_f32,
+        compiler_params=params(),
+        name="parts",
+    )(factors, after(base, own), *weights[:2], near_values, *first_values)
+
+    other = linear(False, far)
     return pl.pallas_call(
-        functools.partial(finish_kernel, late, width),
-        grid_spec=pltpu.PrefetchScalarGridSpec(
-            num_scalar_prefetch=1,
-            grid=grid,
-            in_specs=[narrow, half, half] + [wide] * (2 * late),
-            out_specs=wide,
-        ),
+        functools.partial(finish_kernel, heads, width, late, a_step),
+        in_specs=[smem] + [vmem] * (4 + 2 * (late - 1)),
+        out_specs=vmem,
         out_shape=full,
         compiler_params=params(),
         name="finish",
-    )(where, factors, own, other, *weights[1:], *far_values)
+    )(where, factors, base, own, other, *weights[2:], *far_values)
 
 
 def solution(mesh):

time: 97.4 us -> 85.4 us (0.88)
  the two profiles are of different devices: /device:TPU:10 before, /device:TPU:0 now
where the time goes in v7:
time: 85.4 us; the launch traced here: 84.9 us
  waiting for transfers between devices  39.3 us (46%)
  Pallas kernels  25.8 us (30%)
  starting transfers between devices  17.3 us (20%)
  local copies, waits for them, and re-layouts  1.59 us (2%)
    ppermute x12, waiting for transfers between devices, moved(): return lax.ppermute(x, 'seq', pairs)  39.3 us
    ppermute x12, starting transfers between devices, moved(): return lax.ppermute(x, 'seq', pairs)  17.3 us
    pallas_call x1, Pallas kernels, scores(): pl.pallas_call(functools.partial(scores_kernel, width, levels), grid_spec...  8.85 us
    pallas_call x4, Pallas kernels, add_packed(): pl.pallas_call(functools.partial(add_packed_kernel, rows, extra, len(part...  5.16 us
    pallas_call x1, Pallas kernels, shards(): pl.pallas_call(functools.partial(parts_kernel, width, [1, len(first_value...  4.03 us
    pallas_call x2, Pallas kernels, linear(): pl.pallas_call(functools.partial(linear_kernel, heads, width, own, len(pa...  3.2 us
    pallas_call x1, Pallas kernels, block_sums(): pl.pallas_call(functools.partial(block_sums_kernel, heads, width), in_spe...  2.71 us
    pallas_call x1, Pallas kernels, shards(): pl.pallas_call(functools.partial(finish_kernel, heads, width, late, a_ste...  1.85 us
  transfers between devices with their start and end apart: 12, of which 6 were waited for; matrix products, arithmetic and copies ran while one was open for 2% of the time, Pallas kernels for 28%

profile of v7, /device:TPU:0, one launch (start us, length us, event | category | flops | bytes accessed | tf_op | source)
XLA Modules:
  0.0 84.9 jit_solution(6806330402914553672)
XLA Ops:
  0.0 4.0 %collective-permute-start.3 = (bf16[128,3072]{1,0:T(8,128)(2,1)}, bf16[128,3072]{1,0:T(8,128)(2,1)S(1)}, u32[]{:S(2)}, u32[]{:S(2)}) collective-permute-start(bf16[128,3072]{1,0:T(8,128)(2,1)} %param.10), channel_id=1, source_target_pairs={{0,8},{2,10},{8,12},{10,14},{12,4},{14,6},{4,0},{6,2},{1,9},{3,11}... | collective-permute-start | bytes 2359304 | tf_op jit(solution)/shard_map/ppermute | solution.py:260
  4.7 13.7 %conditional.2 = (f32[1552,128]{1,0:T(8,128)S(1)}, bf16[1584,128]{1,0:T(8,128)(2,1)}) conditional(s32[]{:T(128)} %bitcast.1, () %tuple.29, (s32[1]{0:T(128)}, s32[8]{0:T(128)}, bf16[128,3072]{1,0:T(8,128)(2,1)}, bf16[128,3072]{1,0:T(8,128)(2,1)}) %tuple.30), branch_computations={%region_0.0_spmd, %region_1.0_spmd} | conditional | bytes 1622072 | solution.py:271
  4.7 2.7 %block_sums.1 = (bf16[1584,128]{1,0:T(8,128)(2,1)S(1)}, f32[1552,128]{1,0:T(8,128)S(1)}) custom-call(s32[1]{0:T(128)} %get-tuple-element.37.where, s32[8]{0:T(128)} %get-tuple-element.38.lengths, bf16[128,3072]{1,0:T(8,128)(2,1)} %get-tuple-element.39.k_ref, bf16[128,3072]{1,0:T(8,128)(2,1)} %get-tuple-element.40.v_ref), custom_call_target="tpu_custom_call" | custom-call | tf_op jit(solution)/shard_map/cond/branch_1_fun/block_sums/pallas_call | solution.py:274
  7.4 1.6 %collective-permute-start = (bf16[1584,128]{1,0:T(8,128)(2,1)S(1)}, bf16[1584,128]{1,0:T(8,128)(2,1)}, u32[]{:S(2)}, u32[]{:S(2)}) collective-permute-start(bf16[1584,128]{1,0:T(8,128)(2,1)S(1)} %get-tuple-element.42), channel_id=1, source_target_pairs={{0,2},{2,0},{4,6},{6,4},{8,10},{10,8},{12,14},{14,12},{1,3},{3,1},... | collective-permute-start | bytes 1216520 | tf_op jit(solution)/shard_map/cond/branch_1_fun/ppermute | solution.py:260
  9.0 9.4 %collective-permute-done = bf16[1584,128]{1,0:T(8,128)(2,1)} collective-permute-done((bf16[1584,128]{1,0:T(8,128)(2,1)S(1)}, bf16[1584,128]{1,0:T(8,128)(2,1)}, u32[]{:S(2)}, u32[]{:S(2)}) %collective-permute-start) | collective-permute-done | bytes 405536 | tf_op jit(solution)/shard_map/cond/branch_1_fun/ppermute | solution.py:260
  18.4 1.2 %add_packed.5 = bf16[1584,128]{1,0:T(8,128)(2,1)S(1)} custom-call(s32[1]{0:T(128)} %constant.27.clone.1.where, f32[1552,128]{1,0:T(8,128)S(1)} %get-tuple-element.77.keep_ref, bf16[1584,128]{1,0:T(8,128)(2,1)} %get-tuple-element.87.refs_0_.refs_3_), custom_call_target="tpu_custom_call" | custom-call | tf_op jit(solution)/shard_map/add_packed/pallas_call | solution.py:285
  19.7 1.3 %collective-permute-start.2 = (bf16[1584,128]{1,0:T(8,128)(2,1)S(1)}, bf16[1584,128]{1,0:T(8,128)(2,1)S(1)}, u32[]{:S(2)}, u32[]{:S(2)}) collective-permute-start(bf16[1584,128]{1,0:T(8,128)(2,1)S(1)} %add_packed.5), channel_id=1, source_target_pairs={{0,4},{2,6},{1,5},{3,7},{16,20},{18,22},{17,21},{19,23}} | collective-permute-start | bytes 1216520 | tf_op jit(solution)/shard_map/ppermute | solution.py:260
  21.0 0.0 copy-done.3
  21.0 1.6 %collective-permute-start.5 = (bf16[128,3072]{1,0:T(8,128)(2,1)S(1)}, bf16[128,3072]{1,0:T(8,128)(2,1)S(1)}, u32[]{:S(2)}, u32[]{:S(2)}) collective-permute-start(bf16[128,3072]{1,0:T(8,128)(2,1)S(1)} %copy-done.3), channel_id=1, source_target_pairs={{0,2},{2,0},{4,6},{6,4},{8,10},{10,8},{12,14},{14,12},{1,3},{3,1},... | collective-permute-start | bytes 2359304 | tf_op jit(solution)/shard_map/ppermute | solution.py:260
  22.6 0.0 collective-permute-start.6
  22.6 0.0 collective-permute-done.3
  22.6 8.1 %collective-permute-done.2.refs_1_ = bf16[1584,128]{1,0:T(8,128)(2,1)S(1)} collective-permute-done((bf16[1584,128]{1,0:T(8,128)(2,1)S(1)}, bf16[1584,128]{1,0:T(8,128)(2,1)S(1)}, u32[]{:S(2)}, u32[]{:S(2)}) %collective-permute-start.2) | collective-permute-done | bytes 405536 | tf_op jit(solution)/shard_map/ppermute | solution.py:260
  30.8 1.2 %add_packed.6 = bf16[1584,128]{1,0:T(8,128)(2,1)S(1)} custom-call(s32[1]{0:T(128)} %constant.27.clone.1.where, f32[1552,128]{1,0:T(8,128)S(1)} %get-tuple-element.77.keep_ref, bf16[1584,128]{1,0:T(8,128)(2,1)} %get-tuple-element.87.refs_0_.refs_3_, bf16[1584,128]{1,0:T(8,128)(2,1)S(1)} %collective-permute-done.2.refs_1_), custom_call_target="tpu_custom_call" | custom-call | tf_op jit(solution)/shard_map/add_packed/pallas_call | solution.py:285
  32.0 0.7 collective-permute-start.4
  32.7 6.5 %collective-permute-done.5 = bf16[128,3072]{1,0:T(8,128)(2,1)S(1)} collective-permute-done((bf16[128,3072]{1,0:T(8,128)(2,1)S(1)}, bf16[128,3072]{1,0:T(8,128)(2,1)S(1)}, u32[]{:S(2)}, u32[]{:S(2)}) %collective-permute-start.5) | collective-permute-done | bytes 786464 | tf_op jit(solution)/shard_map/ppermute | solution.py:260
  39.1 1.3 %collective-permute-start.7 = (bf16[128,3072]{1,0:T(8,128)(2,1)}, bf16[128,3072]{1,0:T(8,128)(2,1)S(1)}, u32[]{:S(2)}, u32[]{:S(2)}) collective-permute-start(bf16[128,3072]{1,0:T(8,128)(2,1)} %param.11), channel_id=1, source_target_pairs={{8,12},{10,14},{12,4},{14,6},{4,0},{6,2},{9,13},{11,15},{13,5},{15... | collective-permute-start | bytes 2359304 | tf_op jit(solution)/shard_map/ppermute | solution.py:260
  40.4 6.2 %collective-permute-done.6 = bf16[128,3072]{1,0:T(8,128)(2,1)S(1)} collective-permute-done((bf16[128,3072]{1,0:T(8,128)(2,1)S(1)}, bf16[128,3072]{1,0:T(8,128)(2,1)S(1)}, u32[]{:S(2)}, u32[]{:S(2)}) %collective-permute-start.6) | collective-permute-done | bytes 786464 | tf_op jit(solution)/shard_map/ppermute | solution.py:260
  46.6 1.5 %collective-permute-start.8 = (bf16[128,3072]{1,0:T(8,128)(2,1)}, bf16[128,3072]{1,0:T(8,128)(2,1)S(1)}, u32[]{:S(2)}, u32[]{:S(2)}) collective-permute-start(bf16[128,3072]{1,0:T(8,128)(2,1)} %param.11), channel_id=1, source_target_pairs={{0,2},{2,0},{4,6},{6,4},{8,10},{10,8},{12,14},{14,12},{1,3},{3,1},... | collective-permute-start | bytes 2359304 | tf_op jit(solution)/shard_map/ppermute | solution.py:260
  48.1 1.3 %collective-permute-start.9 = (bf16[128,3072]{1,0:T(8,128)(2,1)}, bf16[128,3072]{1,0:T(8,128)(2,1)S(1)}, u32[]{:S(2)}, u32[]{:S(2)}) collective-permute-start(bf16[128,3072]{1,0:T(8,128)(2,1)} %param.11), channel_id=1, source_target_pairs={{0,8},{2,10},{1,9},{3,11},{16,24},{18,26},{17,25},{19,27}} | collective-permute-start | bytes 2359304 | tf_op jit(solution)/shard_map/ppermute | solution.py:260
  49.4 0.0 collective-permute-done.4
  49.5 0.0 copy-done.1
  49.5 0.0 copy-done.9
  49.5 13.1 %conditional.3 = (bf16[1584,128]{1,0:T(8,128)(2,1)}, bf16[1584,128]{1,0:T(8,128)(2,1)}, bf16[1584,128]{1,0:T(8,128)(2,1)}, bf16[128,3072]{1,0:T(8,128)(2,1)}, bf...) conditional(s32[]{:T(128)} %bitcast.1, () %tuple.28, ...), branch_computations={%region_2.0_spmd, %region_3.0_spmd} | conditional | bytes 6389892 | solution.py:271
  49.5 0.0 copy-start.8
  49.5 1.3 %add_packed.4 = bf16[1584,128]{1,0:T(8,128)(2,1)S(1)} custom-call(s32[1]{0:T(128)} %constant.17.clone.where, f32[1552,128]{1,0:T(8,128)S(1)} %get-tuple-element.45.keep_ref, bf16[1584,128]{1,0:T(8,128)(2,1)} %get-tuple-element.46.refs_0_, bf16[1584,128]{1,0:T(8,128)(2,1)S(1)} %get-tuple-element.106.refs_1_, bf16[1584,128]{1,0:T(8,128)(2,1)S(1)} %get-tuple-element.107.refs_2_), custom_call_target="tpu_custom_call" | custom-call | tf_op jit(solution)/shard_map/cond/branch_1_fun/add_packed/pallas_call | solution.py:285
  50.8 1.4 %collective-permute-start.1 = (bf16[1584,128]{1,0:T(8,128)(2,1)S(1)}, bf16[1584,128]{1,0:T(8,128)(2,1)}, u32[]{:S(2)}, u32[]{:S(2)}) collective-permute-start(bf16[1584,128]{1,0:T(8,128)(2,1)S(1)} %add_packed.4), channel_id=1, source_target_pairs={{8,12},{10,14},{9,13},{11,15},{24,28},{26,30},{25,29},{27,31}} | collective-permute-start | bytes 1216520 | tf_op jit(solution)/shard_map/cond/branch_1_fun/ppermute | solution.py:260
  52.2 0.8 copy.18
  53.0 0.8 copy.19
  53.8 0.0 copy-done.8
  53.8 8.8 %scores.1 = (bf16[128,3072]{1,0:T(8,128)(2,1)}, bf16[128,3072]{1,0:T(8,128)(2,1)}, bf16[128,3072]{1,0:T(8,128)(2,1)}, f32[128,768]{1,0:T(8,128)S(1)}, f32[128,3072]{1,0:T(8,128)}) custom-call(s32[1]{0:T(128)} %get-tuple-element.47.where, s32[8]{0:T(128)S(1)} %get-tuple-element.48.lengths, bf16[128,3072]{1,0:T(8,128)(2,1)S(1)} %get-tuple-element.49.q_ref, ...), custom_call_target="tpu_custom_call" | custom-call | tf_op jit(solution)/shard_map/cond/branch_1_fun/scores/pallas_call | solution.py:303
  62.6 0.0 collective-permute-done.1
  62.6 0.0 copy-start.2
  62.6 1.9 %collective-permute-start.11 = (bf16[128,3072]{1,0:T(8,128)(2,1)}, bf16[128,3072]{1,0:T(8,128)(2,1)S(1)}, u32[]{:S(2)}, u32[]{:S(2)}) collective-permute-start(bf16[128,3072]{1,0:T(8,128)(2,1)} %param.11), channel_id=1, source_target_pairs={{8,0},{10,2},{12,8},{14,10},{4,12},{6,14},{0,4},{2,6},{9,1},{11,3}... | collective-permute-start | bytes 2359304 | tf_op jit(solution)/shard_map/ppermute | solution.py:260
  64.5 1.4 %add_packed.7 = bf16[1584,128]{1,0:T(8,128)(2,1)S(1)} custom-call(s32[1]{0:T(128)S(6)} %sub.3.where, f32[1552,128]{1,0:T(8,128)S(1)} %get-tuple-element.77.keep_ref, bf16[1584,128]{1,0:T(8,128)(2,1)} %get-tuple-element.83.refs_0_, bf16[1584,128]{1,0:T(8,128)(2,1)} %get-tuple-element.84.refs_1_, bf16[1584,128]{1,0:T(8,128)(2,1)} %get-tuple-element.85.refs_2_), custom_call_target="tpu_custom_call" | custom-call | tf_op jit(solution)/shard_map/add_packed/pallas_call | solution.py:285
  66.0 0.6 collective-permute-start.10
  66.6 0.0 collective-permute-done.7.refs_3_
  66.6 0.0 copy-done.2
  66.6 2.2 %linear_own.1.own_ref = f32[128,1536]{1,0:T(8,128)S(1)} custom-call(s32[1]{0:T(128)} %bitcast.where, f32[24]{0:T(128)S(1)} %copy-done, bf16[128,3072]{1,0:T(8,128)(2,1)S(1)} %copy-done.2, bf16[1584,128]{1,0:T(8,128)(2,1)} %get-tuple-element.83.refs_0_, bf16[1584,128]{1,0:T(8,128)(2,1)} %get-tuple-element.84.refs_1_, ...), custom_call_target="tpu_custom_call" | custom-call | tf_op jit(solution)/shard_map/linear_own/pallas_call | solution.py:342
  68.8 0.0 collective-permute-done.8.refs_2_
  68.8 0.0 collective-permute-done.9.refs_4_
  68.8 0.0 copy-done.4
  68.8 0.0 copy-done.5
  68.8 4.0 %parts.1.base_ref = f32[128,3072]{1,0:T(8,128)S(1)} custom-call(f32[128,768]{1,0:T(8,128)S(1)} %get-tuple-element.81.factor_ref, f32[128,3072]{1,0:T(8,128)} %get-tuple-element.88.base_ref, bf16[128,3072]{1,0:T(8,128)(2,1)S(1)} %copy-done.4, bf16[128,3072]{1,0:T(8,128)(2,1)S(1)} %copy-done.5, bf16[128,3072]{1,0:T(8,128)(2,1)S(1)} %collective-permute-done.8.refs_2_, ...), custom_call_target="tpu_custom_call" | custom-call | tf_op jit(solution)/shard_map/parts/pallas_call | solution.py:352
  72.9 2.9 %collective-permute-done.10.refs_0_ = bf16[1584,128]{1,0:T(8,128)(2,1)S(1)} collective-permute-done((bf16[1584,128]{1,0:T(8,128)(2,1)S(1)}, bf16[1584,128]{1,0:T(8,128)(2,1)S(1)}, u32[]{:S(2)}, u32[]{:S(2)}) %collective-permute-start.10) | collective-permute-done | bytes 405536 | tf_op jit(solution)/shard_map/ppermute | solution.py:260
  75.8 1.0 %linear_other.1.other_ref = f32[128,1536]{1,0:T(8,128)S(1)} custom-call(s32[1]{0:T(128)} %bitcast.where, f32[24]{0:T(128)S(1)} %copy-done, bf16[128,3072]{1,0:T(8,128)(2,1)S(1)} %copy-done.2, bf16[1584,128]{1,0:T(8,128)(2,1)S(1)} %collective-permute-done.10.refs_0_), custom_call_target="tpu_custom_call" | custom-call | tf_op jit(solution)/shard_map/linear_other/pallas_call | solution.py:342
  76.8 6.2 %collective-permute-done.11.refs_1_ = bf16[128,3072]{1,0:T(8,128)(2,1)S(1)} collective-permute-done((bf16[128,3072]{1,0:T(8,128)(2,1)}, bf16[128,3072]{1,0:T(8,128)(2,1)S(1)}, u32[]{:S(2)}, u32[]{:S(2)}) %collective-permute-start.11) | collective-permute-done | bytes 786464 | tf_op jit(solution)/shard_map/ppermute | solution.py:260
  83.0 0.0 copy-done.6
  83.0 1.8 %finish.1 = bf16[128,3072]{1,0:T(8,128)(2,1)} custom-call(s32[1]{0:T(128)} %bitcast.where, f32[128,768]{1,0:T(8,128)S(1)} %get-tuple-element.81.factor_ref, f32[128,3072]{1,0:T(8,128)S(1)} %parts.1.base_ref, f32[128,1536]{1,0:T(8,128)S(1)} %linear_own.1.own_ref, f32[128,1536]{1,0:T(8,128)S(1)} %linear_other.1.other_ref, bf16[128,3072]{1,0:T(8,128)(2,1)S(1)} %copy-done.6, ...), custom_call_target="tpu_custom_call" | custom-call | tf_op jit(solution)/shard_map/finish/pallas_call | solution.py:363
  (10 shorter events, 0.0 us)
Async XLA Ops:
  0.0 22.6 %collective-permute-start.3 = (bf16[128,3072]{1,0:T(8,128)(2,1)}, bf16[128,3072]{1,0:T(8,128)(2,1)S(1)}, u32[]{:S(2)}, u32[]{:S(2)}) collective-permute-start(bf16[128,3072]{1,0:T(8,128)(2,1)} %param.10), channel_id=1, source_target_pairs={{0,8},{2,10},{8,12},{10,14},{12,4},{14,6},{4,0},{6,2},{1,9},{3,11}... | collective-permute-start | bytes 2359304 | tf_op jit(solution)/shard_map/ppermute | solution.py:260
  7.4 11.0 %collective-permute-start = (bf16[1584,128]{1,0:T(8,128)(2,1)S(1)}, bf16[1584,128]{1,0:T(8,128)(2,1)}, u32[]{:S(2)}, u32[]{:S(2)}) collective-permute-start(bf16[1584,128]{1,0:T(8,128)(2,1)S(1)} %get-tuple-element.42), channel_id=1, source_target_pairs={{0,2},{2,0},{4,6},{6,4},{8,10},{10,8},{12,14},{14,12},{1,3},{3,1},... | collective-permute-start | bytes 1216520 | tf_op jit(solution)/shard_map/cond/branch_1_fun/ppermute | solution.py:260
  18.4 2.5 %copy-start.3 = (bf16[128,3072]{1,0:T(8,128)(2,1)S(1)}, bf16[128,3072]{1,0:T(8,128)(2,1)}, u32[]{:S(2)}) copy-start(bf16[128,3072]{1,0:T(8,128)(2,1)} %param.10) | copy-start | bytes 2359300
  18.4 31.0 %copy-start.1 = (bf16[128,3072]{1,0:T(8,128)(2,1)S(1)}, bf16[128,3072]{1,0:T(8,128)(2,1)}, u32[]{:S(2)}) copy-start(bf16[128,3072]{1,0:T(8,128)(2,1)} %q_ref.3) | copy-start | bytes 2359300
  18.4 31.0 %copy-start.9 = (s32[8]{0:T(128)S(1)}, s32[8]{0:T(128)}, u32[]{:S(2)}) copy-start(s32[8]{0:T(128)} %param.12) | copy-start | bytes 100
  19.7 11.1 %collective-permute-start.2 = (bf16[1584,128]{1,0:T(8,128)(2,1)S(1)}, bf16[1584,128]{1,0:T(8,128)(2,1)S(1)}, u32[]{:S(2)}, u32[]{:S(2)}) collective-permute-start(bf16[1584,128]{1,0:T(8,128)(2,1)S(1)} %add_packed.5), channel_id=1, source_target_pairs={{0,4},{2,6},{1,5},{3,7},{16,20},{18,22},{17,21},{19,23}} | collective-permute-start | bytes 1216520 | tf_op jit(solution)/shard_map/ppermute | solution.py:260
  21.0 18.2 %collective-permute-start.5 = (bf16[128,3072]{1,0:T(8,128)(2,1)S(1)}, bf16[128,3072]{1,0:T(8,128)(2,1)S(1)}, u32[]{:S(2)}, u32[]{:S(2)}) collective-permute-start(bf16[128,3072]{1,0:T(8,128)(2,1)S(1)} %copy-done.3), channel_id=1, source_target_pairs={{0,2},{2,0},{4,6},{6,4},{8,10},{10,8},{12,14},{14,12},{1,3},{3,1},... | collective-permute-start | bytes 2359304 | tf_op jit(solution)/shard_map/ppermute | solution.py:260
  22.6 24.0 %collective-permute-start.6 = (bf16[128,3072]{1,0:T(8,128)(2,1)S(1)}, bf16[128,3072]{1,0:T(8,128)(2,1)S(1)}, u32[]{:S(2)}, u32[]{:S(2)}) collective-permute-start(bf16[128,3072]{1,0:T(8,128)(2,1)S(1)} %copy-done.3), channel_id=1, source_target_pairs={{8,0},{10,2},{12,8},{14,10},{4,12},{6,14},{0,4},{2,6},{9,1},{11,3}... | collective-permute-start | bytes 2359304 | tf_op jit(solution)/shard_map/ppermute | solution.py:260
  22.6 10.0 %copy-start.7 = (bf16[128,3072]{1,0:T(8,128)(2,1)}, bf16[128,3072]{1,0:T(8,128)(2,1)S(1)}, u32[]{:S(2)}) copy-start(bf16[128,3072]{1,0:T(8,128)(2,1)S(1)} %collective-permute-done.3) | copy-start | bytes 2359300
  32.0 17.5 %collective-permute-start.4 = (bf16[1584,128]{1,0:T(8,128)(2,1)S(1)}, bf16[1584,128]{1,0:T(8,128)(2,1)S(1)}, u32[]{:S(2)}, u32[]{:S(2)}) collective-permute-start(bf16[1584,128]{1,0:T(8,128)(2,1)S(1)} %add_packed.6), channel_id=1, source_target_pairs={{4,8},{6,10},{5,9},{7,11},{20,24},{22,26},{21,25},{23,27}} | collective-permute-start | bytes 1216520 | tf_op jit(solution)/shard_map/ppermute | solution.py:260
  39.1 27.5 %collective-permute-start.7 = (bf16[128,3072]{1,0:T(8,128)(2,1)}, bf16[128,3072]{1,0:T(8,128)(2,1)S(1)}, u32[]{:S(2)}, u32[]{:S(2)}) collective-permute-start(bf16[128,3072]{1,0:T(8,128)(2,1)} %param.11), channel_id=1, source_target_pairs={{8,12},{10,14},{12,4},{14,6},{4,0},{6,2},{9,13},{11,15},{13,5},{15... | collective-permute-start | bytes 2359304 | tf_op jit(solution)/shard_map/ppermute | solution.py:260
  46.6 22.2 %collective-permute-start.8 = (bf16[128,3072]{1,0:T(8,128)(2,1)}, bf16[128,3072]{1,0:T(8,128)(2,1)S(1)}, u32[]{:S(2)}, u32[]{:S(2)}) collective-permute-start(bf16[128,3072]{1,0:T(8,128)(2,1)} %param.11), channel_id=1, source_target_pairs={{0,2},{2,0},{4,6},{6,4},{8,10},{10,8},{12,14},{14,12},{1,3},{3,1},... | collective-permute-start | bytes 2359304 | tf_op jit(solution)/shard_map/ppermute | solution.py:260
  48.1 20.7 %collective-permute-start.9 = (bf16[128,3072]{1,0:T(8,128)(2,1)}, bf16[128,3072]{1,0:T(8,128)(2,1)S(1)}, u32[]{:S(2)}, u32[]{:S(2)}) collective-permute-start(bf16[128,3072]{1,0:T(8,128)(2,1)} %param.11), channel_id=1, source_target_pairs={{0,8},{2,10},{1,9},{3,11},{16,24},{18,26},{17,25},{19,27}} | collective-permute-start | bytes 2359304 | tf_op jit(solution)/shard_map/ppermute | solution.py:260
  49.5 4.3 %copy-start.8 = (bf16[128,3072]{1,0:T(8,128)(2,1)S(1)}, bf16[128,3072]{1,0:T(8,128)(2,1)}, u32[]{:S(2)}) copy-start(bf16[128,3072]{1,0:T(8,128)(2,1)} %get-tuple-element.52.refs_2_) | copy-start | bytes 2359300 | tf_op jit(solution)/shard_map/cond
  50.8 11.8 %collective-permute-start.1 = (bf16[1584,128]{1,0:T(8,128)(2,1)S(1)}, bf16[1584,128]{1,0:T(8,128)(2,1)}, u32[]{:S(2)}, u32[]{:S(2)}) collective-permute-start(bf16[1584,128]{1,0:T(8,128)(2,1)S(1)} %add_packed.4), channel_id=1, source_target_pairs={{8,12},{10,14},{9,13},{11,15},{24,28},{26,30},{25,29},{27,31}} | collective-permute-start | bytes 1216520 | tf_op jit(solution)/shard_map/cond/branch_1_fun/ppermute | solution.py:260
  62.6 4.0 %copy-start = (f32[24]{0:T(128)S(1)}, f32[24]{0:T(128)}, u32[]{:S(2)}) copy-start(f32[24]{0:T(128)} %scale.3) | copy-start | bytes 292
  62.6 4.0 %copy-start.2 = (bf16[128,3072]{1,0:T(8,128)(2,1)S(1)}, bf16[128,3072]{1,0:T(8,128)(2,1)}, u32[]{:S(2)}) copy-start(bf16[128,3072]{1,0:T(8,128)(2,1)} %q_ref.3) | copy-start | bytes 2359300
  62.6 20.4 %collective-permute-start.11 = (bf16[128,3072]{1,0:T(8,128)(2,1)}, bf16[128,3072]{1,0:T(8,128)(2,1)S(1)}, u32[]{:S(2)}, u32[]{:S(2)}) collective-permute-start(bf16[128,3072]{1,0:T(8,128)(2,1)} %param.11), channel_id=1, source_target_pairs={{8,0},{10,2},{12,8},{14,10},{4,12},{6,14},{0,4},{2,6},{9,1},{11,3}... | collective-permute-start | bytes 2359304 | tf_op jit(solution)/shard_map/ppermute | solution.py:260
  66.0 2.8 %copy-start.4 = (bf16[128,3072]{1,0:T(8,128)(2,1)S(1)}, bf16[128,3072]{1,0:T(8,128)(2,1)}, u32[]{:S(2)}) copy-start(bf16[128,3072]{1,0:T(8,128)(2,1)} %get-tuple-element.89.refs_0_) | copy-start | bytes 2359300
  66.0 2.8 %copy-start.5 = (bf16[128,3072]{1,0:T(8,128)(2,1)S(1)}, bf16[128,3072]{1,0:T(8,128)(2,1)}, u32[]{:S(2)}) copy-start(bf16[128,3072]{1,0:T(8,128)(2,1)} %get-tuple-element.90.refs_1_) | copy-start | bytes 2359300
  66.0 9.8 %collective-permute-start.10 = (bf16[1584,128]{1,0:T(8,128)(2,1)S(1)}, bf16[1584,128]{1,0:T(8,128)(2,1)S(1)}, u32[]{:S(2)}, u32[]{:S(2)}) collective-permute-start(bf16[1584,128]{1,0:T(8,128)(2,1)S(1)} %add_packed.7), channel_id=1, source_target_pairs={{0,2},{2,0},{4,6},{6,4},{8,10},{10,8},{12,14},{14,12},{1,3},{3,1},... | collective-permute-start | bytes 1216520 | tf_op jit(solution)/shard_map/ppermute | solution.py:260
  72.9 10.1 %copy-start.6 = (bf16[128,3072]{1,0:T(8,128)(2,1)S(1)}, bf16[128,3072]{1,0:T(8,128)(2,1)}, u32[]{:S(2)}) copy-start(bf16[128,3072]{1,0:T(8,128)(2,1)} %get-tuple-element.92.refs_0_) | copy-start | bytes 2359300

commit v8 on v7

--- a/solution.py
+++ b/solution.py
@@ -326,6 +326,7 @@
     near_values = moved(after(value_rows, near_keys, *far_keys), swaps)
     if held:
         first_values.append(moved(after(value_rows, near_keys, *far_keys), held))
+    far_values = [moved(after(value_rows, hops[1]), turn) for turn in turns[1:]]
 
     def last_hop(keep, parts, *operands):
         for pairs in steps[2:]:
@@ -335,9 +336,9 @@
     hops, (*weights, factors, base) = fenced(
         last_hop, keep, [near, *hops], where, key_len, query_rows, key_rows, value_rows, near_keys, *far_keys
     )
-    far_values = [moved(after(value_rows, *hops), turn) for turn in turns[1:]]
 
     far = moved(add_packed(1 - lax.rem(where, 2), keep, *hops), swaps)
+
     def linear(own, *parts):
         return pl.pallas_call(
             functools.partial(linear_kernel, heads, width, own, len(parts), tokens),

time: 85.4 us -> 84.7 us (level)
    cond x4, local copies, waits for them, and re-layouts: 1.56 us -> 0.06 us
  transfers between devices with their start and end apart: 12 -> 12, of which waited for: 6 -> 6; matrix products, arithmetic and copies ran while one was open for 2% -> 0% of each run, Pallas kernels for 28% -> 29%
where the time goes in v8:
time: 84.7 us; the launch traced here: 84.2 us
  waiting for transfers between devices  39 us (46%)
  Pallas kernels  26.2 us (31%)
  starting transfers between devices  17.3 us (20%)
  between operations  0.86 us (1%)
    ppermute x12, waiting for transfers between devices, moved(): return lax.ppermute(x, 'seq', pairs)  39 us
    ppermute x12, starting transfers between devices, moved(): return lax.ppermute(x, 'seq', pairs)  17.3 us
    pallas_call x1, Pallas kernels, scores(): pl.pallas_call(functools.partial(scores_kernel, width, levels), grid_spec...  8.79 us
    pallas_call x4, Pallas kernels, add_packed(): pl.pallas_call(functools.partial(add_packed_kernel, rows, extra, len(part...  5.73 us
    pallas_call x1, Pallas kernels, shards(): pl.pallas_call(functools.partial(parts_kernel, width, [1, len(first_value...  3.98 us
    pallas_call x2, Pallas kernels, linear(): pl.pallas_call(functools.partial(linear_kernel, heads, width, own, len(pa...  3.17 us
    pallas_call x1, Pallas kernels, block_sums(): pl.pallas_call(functools.partial(block_sums_kernel, heads, width), in_spe...  2.7 us
    pallas_call x1, Pallas kernels, shards(): pl.pallas_call(functools.partial(finish_kernel, heads, width, late, a_ste...  1.83 us
  transfers between devices with their start and end apart: 12, of which 6 were waited for; matrix products, arithmetic and copies ran while one was open for 0% of the time, Pallas kernels for 29%

profile of v8, /device:TPU:0, one launch (start us, length us, event | category | flops | bytes accessed | tf_op | source)
XLA Modules:
  0.0 84.2 jit_solution(7140415338839358041)
XLA Ops:
  0.0 4.0 %collective-permute-start.3 = (bf16[128,3072]{1,0:T(8,128)(2,1)}, bf16[128,3072]{1,0:T(8,128)(2,1)S(1)}, u32[]{:S(2)}, u32[]{:S(2)}) collective-permute-start(bf16[128,3072]{1,0:T(8,128)(2,1)} %param.10), channel_id=1, source_target_pairs={{0,8},{2,10},{8,12},{10,14},{12,4},{14,6},{4,0},{6,2},{1,9},{3,11}... | collective-permute-start | bytes 2359304 | tf_op jit(solution)/shard_map/ppermute | solution.py:260
  4.7 13.7 %conditional.2 = (f32[1552,128]{1,0:T(8,128)S(1)}, bf16[1584,128]{1,0:T(8,128)(2,1)}) conditional(s32[]{:T(128)} %bitcast.1, () %tuple.29, (s32[1]{0:T(128)}, s32[8]{0:T(128)}, bf16[128,3072]{1,0:T(8,128)(2,1)}, bf16[128,3072]{1,0:T(8,128)(2,1)}) %tuple.30), branch_computations={%region_0.0_spmd, %region_1.0_spmd} | conditional | bytes 1622072 | solution.py:271
  4.7 2.7 %block_sums.1 = (bf16[1584,128]{1,0:T(8,128)(2,1)S(1)}, f32[1552,128]{1,0:T(8,128)S(1)}) custom-call(s32[1]{0:T(128)} %get-tuple-element.37.where, s32[8]{0:T(128)} %get-tuple-element.38.lengths, bf16[128,3072]{1,0:T(8,128)(2,1)} %get-tuple-element.39.k_ref, bf16[128,3072]{1,0:T(8,128)(2,1)} %get-tuple-element.40.v_ref), custom_call_target="tpu_custom_call" | custom-call | tf_op jit(solution)/shard_map/cond/branch_1_fun/block_sums/pallas_call | solution.py:274
  7.4 1.6 %collective-permute-start = (bf16[1584,128]{1,0:T(8,128)(2,1)S(1)}, bf16[1584,128]{1,0:T(8,128)(2,1)}, u32[]{:S(2)}, u32[]{:S(2)}) collective-permute-start(bf16[1584,128]{1,0:T(8,128)(2,1)S(1)} %get-tuple-element.42), channel_id=1, source_target_pairs={{0,2},{2,0},{4,6},{6,4},{8,10},{10,8},{12,14},{14,12},{1,3},{3,1},... | collective-permute-start | bytes 1216520 | tf_op jit(solution)/shard_map/cond/branch_1_fun/ppermute | solution.py:260
  9.0 9.4 %collective-permute-done = bf16[1584,128]{1,0:T(8,128)(2,1)} collective-permute-done((bf16[1584,128]{1,0:T(8,128)(2,1)S(1)}, bf16[1584,128]{1,0:T(8,128)(2,1)}, u32[]{:S(2)}, u32[]{:S(2)}) %collective-permute-start) | collective-permute-done | bytes 405536 | tf_op jit(solution)/shard_map/cond/branch_1_fun/ppermute | solution.py:260
  18.4 1.4 %add_packed.5 = bf16[1584,128]{1,0:T(8,128)(2,1)S(1)} custom-call(s32[1]{0:T(128)} %constant.27.clone.1.where, f32[1552,128]{1,0:T(8,128)S(1)} %get-tuple-element.77.keep_ref, bf16[1584,128]{1,0:T(8,128)(2,1)} %get-tuple-element.87.refs_0_.refs_3_), custom_call_target="tpu_custom_call" | custom-call | tf_op jit(solution)/shard_map/add_packed/pallas_call | solution.py:285
  19.9 1.3 %collective-permute-start.2 = (bf16[1584,128]{1,0:T(8,128)(2,1)S(1)}, bf16[1584,128]{1,0:T(8,128)(2,1)S(1)}, u32[]{:S(2)}, u32[]{:S(2)}) collective-permute-start(bf16[1584,128]{1,0:T(8,128)(2,1)S(1)} %add_packed.5), channel_id=1, source_target_pairs={{0,4},{2,6},{1,5},{3,7},{16,20},{18,22},{17,21},{19,23}} | collective-permute-start | bytes 1216520 | tf_op jit(solution)/shard_map/ppermute | solution.py:260
  21.2 0.0 copy-done.8
  21.2 1.6 %collective-permute-start.5 = (bf16[128,3072]{1,0:T(8,128)(2,1)S(1)}, bf16[128,3072]{1,0:T(8,128)(2,1)S(1)}, u32[]{:S(2)}, u32[]{:S(2)}) collective-permute-start(bf16[128,3072]{1,0:T(8,128)(2,1)S(1)} %copy-done.8), channel_id=1, source_target_pairs={{0,2},{2,0},{4,6},{6,4},{8,10},{10,8},{12,14},{14,12},{1,3},{3,1},... | collective-permute-start | bytes 2359304 | tf_op jit(solution)/shard_map/ppermute | solution.py:260
  22.8 0.0 collective-permute-start.6
  22.8 0.0 collective-permute-done.3
  22.9 8.1 %collective-permute-done.2.refs_1_ = bf16[1584,128]{1,0:T(8,128)(2,1)S(1)} collective-permute-done((bf16[1584,128]{1,0:T(8,128)(2,1)S(1)}, bf16[1584,128]{1,0:T(8,128)(2,1)S(1)}, u32[]{:S(2)}, u32[]{:S(2)}) %collective-permute-start.2) | collective-permute-done | bytes 405536 | tf_op jit(solution)/shard_map/ppermute | solution.py:260
  31.0 1.2 %add_packed.6 = bf16[1584,128]{1,0:T(8,128)(2,1)S(1)} custom-call(s32[1]{0:T(128)} %constant.27.clone.1.where, f32[1552,128]{1,0:T(8,128)S(1)} %get-tuple-element.77.keep_ref, bf16[1584,128]{1,0:T(8,128)(2,1)} %get-tuple-element.87.refs_0_.refs_3_, bf16[1584,128]{1,0:T(8,128)(2,1)S(1)} %collective-permute-done.2.refs_1_), custom_call_target="tpu_custom_call" | custom-call | tf_op jit(solution)/shard_map/add_packed/pallas_call | solution.py:285
  32.1 0.0 copy-done.1
  32.2 0.7 collective-permute-start.4
  32.8 6.5 %collective-permute-done.5 = bf16[128,3072]{1,0:T(8,128)(2,1)S(1)} collective-permute-done((bf16[128,3072]{1,0:T(8,128)(2,1)S(1)}, bf16[128,3072]{1,0:T(8,128)(2,1)S(1)}, u32[]{:S(2)}, u32[]{:S(2)}) %collective-permute-start.5) | collective-permute-done | bytes 786464 | tf_op jit(solution)/shard_map/ppermute | solution.py:260
  39.4 1.3 %collective-permute-start.7 = (bf16[128,3072]{1,0:T(8,128)(2,1)}, bf16[128,3072]{1,0:T(8,128)(2,1)S(1)}, u32[]{:S(2)}, u32[]{:S(2)}) collective-permute-start(bf16[128,3072]{1,0:T(8,128)(2,1)} %param.11), channel_id=1, source_target_pairs={{8,12},{10,14},{12,4},{14,6},{4,0},{6,2},{9,13},{11,15},{13,5},{15... | collective-permute-start | bytes 2359304 | tf_op jit(solution)/shard_map/ppermute | solution.py:260
  40.7 0.0 copy-done.11
  40.7 5.9 %collective-permute-done.6 = bf16[128,3072]{1,0:T(8,128)(2,1)S(1)} collective-permute-done((bf16[128,3072]{1,0:T(8,128)(2,1)S(1)}, bf16[128,3072]{1,0:T(8,128)(2,1)S(1)}, u32[]{:S(2)}, u32[]{:S(2)}) %collective-permute-start.6) | collective-permute-done | bytes 786464 | tf_op jit(solution)/shard_map/ppermute | solution.py:260
  46.6 1.5 %collective-permute-start.8 = (bf16[128,3072]{1,0:T(8,128)(2,1)}, bf16[128,3072]{1,0:T(8,128)(2,1)S(1)}, u32[]{:S(2)}, u32[]{:S(2)}) collective-permute-start(bf16[128,3072]{1,0:T(8,128)(2,1)} %param.11), channel_id=1, source_target_pairs={{0,2},{2,0},{4,6},{6,4},{8,10},{10,8},{12,14},{14,12},{1,3},{3,1},... | collective-permute-start | bytes 2359304 | tf_op jit(solution)/shard_map/ppermute | solution.py:260
  48.1 1.3 %collective-permute-start.9 = (bf16[128,3072]{1,0:T(8,128)(2,1)}, bf16[128,3072]{1,0:T(8,128)(2,1)S(1)}, u32[]{:S(2)}, u32[]{:S(2)}) collective-permute-start(bf16[128,3072]{1,0:T(8,128)(2,1)} %param.11), channel_id=1, source_target_pairs={{0,8},{2,10},{1,9},{3,11},{16,24},{18,26},{17,25},{19,27}} | collective-permute-start | bytes 2359304 | tf_op jit(solution)/shard_map/ppermute | solution.py:260
  49.4 0.0 collective-permute-done.4
  49.5 1.9 %collective-permute-start.11 = (bf16[128,3072]{1,0:T(8,128)(2,1)}, bf16[128,3072]{1,0:T(8,128)(2,1)S(1)}, u32[]{:S(2)}, u32[]{:S(2)}) collective-permute-start(bf16[128,3072]{1,0:T(8,128)(2,1)} %param.11), channel_id=1, source_target_pairs={{8,0},{10,2},{12,8},{14,10},{4,12},{6,14},{0,4},{2,6},{9,1},{11,3}... | collective-permute-start | bytes 2359304 | tf_op jit(solution)/shard_map/ppermute | solution.py:260
  51.4 0.0 copy-done.2
  51.4 0.0 copy-done.13
  51.4 11.8 %conditional.3 = (bf16[1584,128]{1,0:T(8,128)(2,1)S(1)}, bf16[1584,128]{1,0:T(8,128)(2,1)S(1)}, bf16[1584,128]{1,0:T(8,128)(2,1)}, bf16[128,3072]{1,0:T(8,128)(2...) conditional(s32[]{:T(128)} %bitcast.1, () %tuple.28, ...), branch_computations={%region_2.0_spmd, %region_3.0_spmd} | conditional | bytes 6389892 | solution.py:271
  51.4 1.5 %add_packed.4 = bf16[1584,128]{1,0:T(8,128)(2,1)S(1)} custom-call(s32[1]{0:T(128)} %constant.17.clone.where, f32[1552,128]{1,0:T(8,128)} %get-tuple-element.45.keep_ref, bf16[1584,128]{1,0:T(8,128)(2,1)} %get-tuple-element.46.refs_0_, bf16[1584,128]{1,0:T(8,128)(2,1)S(1)} %get-tuple-element.106.refs_1_, bf16[1584,128]{1,0:T(8,128)(2,1)S(1)} %get-tuple-element.107.refs_2_), custom_call_target="tpu_custom_call" | custom-call | tf_op jit(solution)/shard_map/cond/branch_1_fun/add_packed/pallas_call | solution.py:285
  52.9 1.4 %collective-permute-start.1 = (bf16[1584,128]{1,0:T(8,128)(2,1)S(1)}, bf16[1584,128]{1,0:T(8,128)(2,1)}, u32[]{:S(2)}, u32[]{:S(2)}) collective-permute-start(bf16[1584,128]{1,0:T(8,128)(2,1)S(1)} %add_packed.4), channel_id=1, source_target_pairs={{8,12},{10,14},{9,13},{11,15},{24,28},{26,30},{25,29},{27,31}} | collective-permute-start | bytes 1216520 | tf_op jit(solution)/shard_map/cond/branch_1_fun/ppermute | solution.py:260
  54.4 0.0 copy-done.12
  54.4 8.8 %scores.1 = (bf16[128,3072]{1,0:T(8,128)(2,1)}, bf16[128,3072]{1,0:T(8,128)(2,1)}, bf16[128,3072]{1,0:T(8,128)(2,1)}, f32[128,768]{1,0:T(8,128)}, f32[128,3072]{1,0:T(8,128)}) custom-call(s32[1]{0:T(128)} %get-tuple-element.47.where, s32[8]{0:T(128)S(1)} %get-tuple-element.48.lengths, bf16[128,3072]{1,0:T(8,128)(2,1)S(1)} %get-tuple-element.49.q_ref, ...), custom_call_target="tpu_custom_call" | custom-call | tf_op jit(solution)/shard_map/cond/branch_1_fun/scores/pallas_call | solution.py:303
  63.2 0.0 collective-permute-done.1
  63.2 0.0 copy-start
  63.2 0.0 copy-start.3
  63.2 0.7 copy-done.5
  64.0 1.6 %add_packed.7 = bf16[1584,128]{1,0:T(8,128)(2,1)S(1)} custom-call(s32[1]{0:T(128)S(6)} %sub.3.where, f32[1552,128]{1,0:T(8,128)} %copy-done.1, bf16[1584,128]{1,0:T(8,128)(2,1)S(1)} %get-tuple-element.83.refs_0_, bf16[1584,128]{1,0:T(8,128)(2,1)} %copy-done.5, bf16[1584,128]{1,0:T(8,128)(2,1)} %get-tuple-element.85.refs_2_), custom_call_target="tpu_custom_call" | custom-call | tf_op jit(solution)/shard_map/add_packed/pallas_call | solution.py:285
  65.6 0.0 copy-start.7
  65.6 0.6 collective-permute-start.10
  66.2 0.0 collective-permute-done.7.refs_3_
  66.2 0.0 copy-done.3
  66.2 0.0 copy-done.6
  66.2 2.2 %linear_own.1.own_ref = f32[128,1536]{1,0:T(8,128)S(1)} custom-call(s32[1]{0:T(128)} %bitcast.where, f32[24]{0:T(128)S(1)} %copy-done, bf16[128,3072]{1,0:T(8,128)(2,1)S(1)} %copy-done.3, bf16[1584,128]{1,0:T(8,128)(2,1)S(1)} %get-tuple-element.83.refs_0_, bf16[1584,128]{1,0:T(8,128)(2,1)S(1)} %copy-done.6, bf16[1584,128]{1,0:T(8,128)(2,1)} %get-tuple-element.85.refs_2_, ...), custom_call_target="tpu_custom_call" | custom-call | tf_op jit(solution)/shard_map/linear_own/pallas_call | solution.py:343
  68.4 0.0 collective-permute-done.8.refs_2_
  68.4 0.0 collective-permute-done.9.refs_4_
  68.4 4.0 %parts.1.base_ref = f32[128,3072]{1,0:T(8,128)S(1)} custom-call(f32[128,768]{1,0:T(8,128)S(1)} %copy-done.7, f32[128,3072]{1,0:T(8,128)S(1)} %copy-done.4, bf16[128,3072]{1,0:T(8,128)(2,1)S(1)} %copy-done.9, bf16[128,3072]{1,0:T(8,128)(2,1)} %get-tuple-element.90.refs_1_, bf16[128,3072]{1,0:T(8,128)(2,1)S(1)} %collective-permute-done.8.refs_2_, ...), custom_call_target="tpu_custom_call" | custom-call | tf_op jit(solution)/shard_map/parts/pallas_call | solution.py:353
  72.4 2.8 %collective-permute-done.10.refs_0_ = bf16[1584,128]{1,0:T(8,128)(2,1)S(1)} collective-permute-done((bf16[1584,128]{1,0:T(8,128)(2,1)S(1)}, bf16[1584,128]{1,0:T(8,128)(2,1)S(1)}, u32[]{:S(2)}, u32[]{:S(2)}) %collective-permute-start.10) | collective-permute-done | bytes 405536 | tf_op jit(solution)/shard_map/ppermute | solution.py:260
  75.2 1.0 %linear_other.1.other_ref = f32[128,1536]{1,0:T(8,128)S(1)} custom-call(s32[1]{0:T(128)} %bitcast.where, f32[24]{0:T(128)S(1)} %copy-done, bf16[128,3072]{1,0:T(8,128)(2,1)S(1)} %copy-done.3, bf16[1584,128]{1,0:T(8,128)(2,1)S(1)} %collective-permute-done.10.refs_0_), custom_call_target="tpu_custom_call" | custom-call | tf_op jit(solution)/shard_map/linear_other/pallas_call | solution.py:343
  76.2 6.1 %collective-permute-done.11.refs_1_ = bf16[128,3072]{1,0:T(8,128)(2,1)S(1)} collective-permute-done((bf16[128,3072]{1,0:T(8,128)(2,1)}, bf16[128,3072]{1,0:T(8,128)(2,1)S(1)}, u32[]{:S(2)}, u32[]{:S(2)}) %collective-permute-start.11) | collective-permute-done | bytes 786464 | tf_op jit(solution)/shard_map/ppermute | solution.py:260
  82.4 1.8 %finish.1 = bf16[128,3072]{1,0:T(8,128)(2,1)} custom-call(s32[1]{0:T(128)} %bitcast.where, f32[128,768]{1,0:T(8,128)S(1)} %copy-done.7, f32[128,3072]{1,0:T(8,128)S(1)} %parts.1.base_ref, f32[128,1536]{1,0:T(8,128)S(1)} %linear_own.1.own_ref, f32[128,1536]{1,0:T(8,128)S(1)} %linear_other.1.other_ref, bf16[128,3072]{1,0:T(8,128)(2,1)S(1)} %copy-done.10, ...), custom_call_target="tpu_custom_call" | custom-call | tf_op jit(solution)/shard_map/finish/pallas_call | solution.py:364
  (18 shorter events, 0.1 us)
Async XLA Ops:
  0.0 22.8 %collective-permute-start.3 = (bf16[128,3072]{1,0:T(8,128)(2,1)}, bf16[128,3072]{1,0:T(8,128)(2,1)S(1)}, u32[]{:S(2)}, u32[]{:S(2)}) collective-permute-start(bf16[128,3072]{1,0:T(8,128)(2,1)} %param.10), channel_id=1, source_target_pairs={{0,8},{2,10},{8,12},{10,14},{12,4},{14,6},{4,0},{6,2},{1,9},{3,11}... | collective-permute-start | bytes 2359304 | tf_op jit(solution)/shard_map/ppermute | solution.py:260
  7.4 11.0 %collective-permute-start = (bf16[1584,128]{1,0:T(8,128)(2,1)S(1)}, bf16[1584,128]{1,0:T(8,128)(2,1)}, u32[]{:S(2)}, u32[]{:S(2)}) collective-permute-start(bf16[1584,128]{1,0:T(8,128)(2,1)S(1)} %get-tuple-element.42), channel_id=1, source_target_pairs={{0,2},{2,0},{4,6},{6,4},{8,10},{10,8},{12,14},{14,12},{1,3},{3,1},... | collective-permute-start | bytes 1216520 | tf_op jit(solution)/shard_map/cond/branch_1_fun/ppermute | solution.py:260
  18.4 13.7 %copy-start.1 = (f32[1552,128]{1,0:T(8,128)}, f32[1552,128]{1,0:T(8,128)S(1)}, u32[]{:S(2)}) copy-start(f32[1552,128]{1,0:T(8,128)S(1)} %get-tuple-element.77.keep_ref) | copy-start | bytes 2383876
  18.4 2.8 %copy-start.8 = (bf16[128,3072]{1,0:T(8,128)(2,1)S(1)}, bf16[128,3072]{1,0:T(8,128)(2,1)}, u32[]{:S(2)}) copy-start(bf16[128,3072]{1,0:T(8,128)(2,1)} %param.10) | copy-start | bytes 2359300
  18.4 32.9 %copy-start.2 = (bf16[128,3072]{1,0:T(8,128)(2,1)S(1)}, bf16[128,3072]{1,0:T(8,128)(2,1)}, u32[]{:S(2)}) copy-start(bf16[128,3072]{1,0:T(8,128)(2,1)} %q_ref.3) | copy-start | bytes 2359300
  18.4 32.9 %copy-start.13 = (s32[8]{0:T(128)S(1)}, s32[8]{0:T(128)}, u32[]{:S(2)}) copy-start(s32[8]{0:T(128)} %param.12) | copy-start | bytes 100
  19.9 11.1 %collective-permute-start.2 = (bf16[1584,128]{1,0:T(8,128)(2,1)S(1)}, bf16[1584,128]{1,0:T(8,128)(2,1)S(1)}, u32[]{:S(2)}, u32[]{:S(2)}) collective-permute-start(bf16[1584,128]{1,0:T(8,128)(2,1)S(1)} %add_packed.5), channel_id=1, source_target_pairs={{0,4},{2,6},{1,5},{3,7},{16,20},{18,22},{17,21},{19,23}} | collective-permute-start | bytes 1216520 | tf_op jit(solution)/shard_map/ppermute | solution.py:260
  21.2 18.2 %collective-permute-start.5 = (bf16[128,3072]{1,0:T(8,128)(2,1)S(1)}, bf16[128,3072]{1,0:T(8,128)(2,1)S(1)}, u32[]{:S(2)}, u32[]{:S(2)}) collective-permute-start(bf16[128,3072]{1,0:T(8,128)(2,1)S(1)} %copy-done.8), channel_id=1, source_target_pairs={{0,2},{2,0},{4,6},{6,4},{8,10},{10,8},{12,14},{14,12},{1,3},{3,1},... | collective-permute-start | bytes 2359304 | tf_op jit(solution)/shard_map/ppermute | solution.py:260
  22.8 23.7 %collective-permute-start.6 = (bf16[128,3072]{1,0:T(8,128)(2,1)S(1)}, bf16[128,3072]{1,0:T(8,128)(2,1)S(1)}, u32[]{:S(2)}, u32[]{:S(2)}) collective-permute-start(bf16[128,3072]{1,0:T(8,128)(2,1)S(1)} %copy-done.8), channel_id=1, source_target_pairs={{8,0},{10,2},{12,8},{14,10},{4,12},{6,14},{0,4},{2,6},{9,1},{11,3}... | collective-permute-start | bytes 2359304 | tf_op jit(solution)/shard_map/ppermute | solution.py:260
  22.8 17.8 %copy-start.11 = (bf16[128,3072]{1,0:T(8,128)(2,1)}, bf16[128,3072]{1,0:T(8,128)(2,1)S(1)}, u32[]{:S(2)}) copy-start(bf16[128,3072]{1,0:T(8,128)(2,1)S(1)} %collective-permute-done.3) | copy-start | bytes 2359300
  32.2 17.3 %collective-permute-start.4 = (bf16[1584,128]{1,0:T(8,128)(2,1)S(1)}, bf16[1584,128]{1,0:T(8,128)(2,1)S(1)}, u32[]{:S(2)}, u32[]{:S(2)}) collective-permute-start(bf16[1584,128]{1,0:T(8,128)(2,1)S(1)} %add_packed.6), channel_id=1, source_target_pairs={{4,8},{6,10},{5,9},{7,11},{20,24},{22,26},{21,25},{23,27}} | collective-permute-start | bytes 1216520 | tf_op jit(solution)/shard_map/ppermute | solution.py:260
  39.4 26.8 %collective-permute-start.7 = (bf16[128,3072]{1,0:T(8,128)(2,1)}, bf16[128,3072]{1,0:T(8,128)(2,1)S(1)}, u32[]{:S(2)}, u32[]{:S(2)}) collective-permute-start(bf16[128,3072]{1,0:T(8,128)(2,1)} %param.11), channel_id=1, source_target_pairs={{8,12},{10,14},{12,4},{14,6},{4,0},{6,2},{9,13},{11,15},{13,5},{15... | collective-permute-start | bytes 2359304 | tf_op jit(solution)/shard_map/ppermute | solution.py:260
  46.6 21.8 %collective-permute-start.8 = (bf16[128,3072]{1,0:T(8,128)(2,1)}, bf16[128,3072]{1,0:T(8,128)(2,1)S(1)}, u32[]{:S(2)}, u32[]{:S(2)}) collective-permute-start(bf16[128,3072]{1,0:T(8,128)(2,1)} %param.11), channel_id=1, source_target_pairs={{0,2},{2,0},{4,6},{6,4},{8,10},{10,8},{12,14},{14,12},{1,3},{3,1},... | collective-permute-start | bytes 2359304 | tf_op jit(solution)/shard_map/ppermute | solution.py:260
  48.1 20.3 %collective-permute-start.9 = (bf16[128,3072]{1,0:T(8,128)(2,1)}, bf16[128,3072]{1,0:T(8,128)(2,1)S(1)}, u32[]{:S(2)}, u32[]{:S(2)}) collective-permute-start(bf16[128,3072]{1,0:T(8,128)(2,1)} %param.11), channel_id=1, source_target_pairs={{0,8},{2,10},{1,9},{3,11},{16,24},{18,26},{17,25},{19,27}} | collective-permute-start | bytes 2359304 | tf_op jit(solution)/shard_map/ppermute | solution.py:260
  49.5 32.9 %collective-permute-start.11 = (bf16[128,3072]{1,0:T(8,128)(2,1)}, bf16[128,3072]{1,0:T(8,128)(2,1)S(1)}, u32[]{:S(2)}, u32[]{:S(2)}) collective-permute-start(bf16[128,3072]{1,0:T(8,128)(2,1)} %param.11), channel_id=1, source_target_pairs={{8,0},{10,2},{12,8},{14,10},{4,12},{6,14},{0,4},{2,6},{9,1},{11,3}... | collective-permute-start | bytes 2359304 | tf_op jit(solution)/shard_map/ppermute | solution.py:260
  51.4 3.0 %copy-start.12 = (bf16[128,3072]{1,0:T(8,128)(2,1)S(1)}, bf16[128,3072]{1,0:T(8,128)(2,1)}, u32[]{:S(2)}) copy-start(bf16[128,3072]{1,0:T(8,128)(2,1)} %get-tuple-element.52.refs_2_) | copy-start | bytes 2359300 | tf_op jit(solution)/shard_map/cond
  52.9 10.3 %collective-permute-start.1 = (bf16[1584,128]{1,0:T(8,128)(2,1)S(1)}, bf16[1584,128]{1,0:T(8,128)(2,1)}, u32[]{:S(2)}, u32[]{:S(2)}) collective-permute-start(bf16[1584,128]{1,0:T(8,128)(2,1)S(1)} %add_packed.4), channel_id=1, source_target_pairs={{8,12},{10,14},{9,13},{11,15},{24,28},{26,30},{25,29},{27,31}} | collective-permute-start | bytes 1216520 | tf_op jit(solution)/shard_map/cond/branch_1_fun/ppermute | solution.py:260
  63.2 0.8 copy-start.5
  63.2 3.0 %copy-start = (f32[24]{0:T(128)S(1)}, f32[24]{0:T(128)}, u32[]{:S(2)}) copy-start(f32[24]{0:T(128)} %scale.3) | copy-start | bytes 292
  63.2 3.0 %copy-start.3 = (bf16[128,3072]{1,0:T(8,128)(2,1)S(1)}, bf16[128,3072]{1,0:T(8,128)(2,1)}, u32[]{:S(2)}) copy-start(bf16[128,3072]{1,0:T(8,128)(2,1)} %q_ref.3) | copy-start | bytes 2359300
  64.0 2.2 %copy-start.6 = (bf16[1584,128]{1,0:T(8,128)(2,1)S(1)}, bf16[1584,128]{1,0:T(8,128)(2,1)}, u32[]{:S(2)}) copy-start(bf16[1584,128]{1,0:T(8,128)(2,1)} %copy-done.5) | copy-start | bytes 1216516
  65.6 2.8 %copy-start.4 = (f32[128,3072]{1,0:T(8,128)S(1)}, f32[128,3072]{1,0:T(8,128)}, u32[]{:S(2)}) copy-start(f32[128,3072]{1,0:T(8,128)} %get-tuple-element.88.base_ref) | copy-start | bytes 4718596
  65.6 2.8 %copy-start.7 = (f32[128,768]{1,0:T(8,128)S(1)}, f32[128,768]{1,0:T(8,128)}, u32[]{:S(2)}) copy-start(f32[128,768]{1,0:T(8,128)} %get-tuple-element.81.factor_ref) | copy-start | bytes 1179652
  65.6 2.8 %copy-start.9 = (bf16[128,3072]{1,0:T(8,128)(2,1)S(1)}, bf16[128,3072]{1,0:T(8,128)(2,1)}, u32[]{:S(2)}) copy-start(bf16[128,3072]{1,0:T(8,128)(2,1)} %get-tuple-element.89.refs_0_) | copy-start | bytes 2359300
  65.6 9.6 %collective-permute-start.10 = (bf16[1584,128]{1,0:T(8,128)(2,1)S(1)}, bf16[1584,128]{1,0:T(8,128)(2,1)S(1)}, u32[]{:S(2)}, u32[]{:S(2)}) collective-permute-start(bf16[1584,128]{1,0:T(8,128)(2,1)S(1)} %add_packed.7), channel_id=1, source_target_pairs={{0,2},{2,0},{4,6},{6,4},{8,10},{10,8},{12,14},{14,12},{1,3},{3,1},... | collective-permute-start | bytes 1216520 | tf_op jit(solution)/shard_map/ppermute | solution.py:260
  72.4 10.0 %copy-start.10 = (bf16[128,3072]{1,0:T(8,128)(2,1)S(1)}, bf16[128,3072]{1,0:T(8,128)(2,1)}, u32[]{:S(2)}) copy-start(bf16[128,3072]{1,0:T(8,128)(2,1)} %get-tuple-element.92.refs_0_) | copy-start | bytes 2359300

commit v9 on v8

--- a/solution.py
+++ b/solution.py
@@ -30,8 +30,13 @@
 
 
 def store_packed(ref, main, sums):
-    rows, extra = main.shape[0], sums.shape[0]
+    rows = main.shape[0]
     ref[0:rows, :] = main.astype(BF16)
+    store_sums(ref, rows, sums)
+
+
+def store_sums(ref, rows, sums):
+    extra = sums.shape[0]
     for term in range(TERMS):
         part = sums.astype(BF16)
         sums = sums - part.astype(F32)
@@ -45,48 +50,34 @@
     return total
 
 
-def block_sums_kernel(heads, width, where, lengths, k_ref, v_ref, send_ref, keep_ref):
+def block_sums_kernel(heads, width, sent, where, lengths, k_ref, v_ref, out_ref):
     half_heads = heads // 2
     me = where[0]
     side = lax.rem(me, 2)
     length = lengths[me]
     rows = half_heads * width
     extra = padded(half_heads)
+    first = (1 - side if sent else side) * half_heads
     live = lax.broadcasted_iota(jnp.int32, (k_ref.shape[0], width), 0) < length
-
-    def one_half(first, store):
-        sums = []
-        for i in range(half_heads):
-            columns = pl.ds(pl.multiple_of((first + i) * width, width), width)
-            mapped = jnp.where(live, feature(k_ref[:, columns].astype(F32)) - CENTER, 0.0)
-            values = jnp.where(live, v_ref[:, columns].astype(F32), 0.0)
-            sums.append(jnp.sum(values, axis=0, keepdims=True))
-            high, low = halves(mapped)
-            values = values.astype(BF16)
-            store(
-                i,
-                lax.dot_general(
-                    jnp.concatenate([high, low], axis=0),
-                    jnp.concatenate([values, values], axis=0),
-                    (((0,), (0,)), ((), ())),
-                    preferred_element_type=F32,
-                ),
-            )
-        sums += [jnp.zeros((1, width), F32)] * (extra - half_heads)
-        return jnp.concatenate(sums, axis=0)
-
-    def store_send(i, value):
-        send_ref[i * width : (i + 1) * width, :] = value.astype(BF16)
-
-    def store_keep(i, value):
-        keep_ref[i * width : (i + 1) * width, :] = value
-
-    sums = one_half((1 - side) * half_heads, store_send)
-    for term in range(TERMS):
-        part = sums.astype(BF16)
-        sums = sums - part.astype(F32)
-        send_ref[rows + term * extra : rows + (term + 1) * extra, :] = part
-    keep_ref[rows : rows + extra, :] = one_half(side * half_heads, store_keep)
+    sums = []
+    for i in range(half_heads):
+        columns = pl.ds(pl.multiple_of((first + i) * width, width), width)
+        mapped = jnp.where(live, feature(k_ref[:, columns].astype(F32)) - CENTER, 0.0)
+        values = jnp.where(live, v_ref[:, columns].astype(F32), 0.0)
+        sums.append(jnp.sum(values, axis=0, keepdims=True))
+        high, low = halves(mapped)
+        values = values.astype(BF16)
+        out_ref[i * width : (i + 1) * width, :] = lax.dot_general(
+            jnp.concatenate([high, low], axis=0),
+            jnp.concatenate([values, values], axis=0),
+            (((0,), (0,)), ((), ())),
+            preferred_element_type=F32,
+        ).astype(out_ref.dtype)
+    sums = jnp.concatenate(sums + [jnp.zeros((1, width), F32)] * (extra - half_heads), axis=0)
+    if sent:
+        store_sums(out_ref, rows, sums)
+    else:
+        out_ref[rows : rows + extra, :] = sums
 
 
 def add_packed_kernel(rows, extra, count, where, keep_ref, *refs):
@@ -155,8 +146,12 @@
     factor_ref[...] = factors
 
 
-def parts_kernel(width, counts, factor_ref, base_ref, *refs):
-    weight_refs, value_refs, out_ref = refs[: len(counts)], refs[len(counts) : -1], refs[-1]
+def parts_kernel(width, counts, passed, factor_ref, base_ref, *refs):
+    weight_refs, refs = refs[: len(counts)], refs[len(counts) :]
+    last = len(refs) - 1 - 2 * passed
+    value_refs, out_ref = refs[:last], refs[last + passed]
+    for source, target in zip(refs[last : last + passed], refs[last + passed + 1 :]):
+        target[...] = source[...]
     a_step = base_ref.shape[1] // width
     for h in range(a_step):
         at = slice(h * width, (h + 1) * width)
@@ -270,16 +265,22 @@
 
         return lax.cond(key_len[0] > 0, run, nothing, *operands)
 
+    one = jnp.ones((1,), jnp.int32)
+
     def block_sums(where, key_len, key_rows, value_rows):
-        send, keep = pl.pallas_call(
-            functools.partial(block_sums_kernel, heads, width),
-            in_specs=[smem, smem, vmem, vmem],
-            out_specs=[vmem, vmem],
-            out_shape=[packed, jax.ShapeDtypeStruct((rows + extra, width), F32)],
-            compiler_params=params(),
-            name="block_sums",
-        )(where, key_len, key_rows, value_rows)
-        return keep, moved(send, swaps)
+        def half(sent, shape):
+            return pl.pallas_call(
+                functools.partial(block_sums_kernel, heads, width, sent),
+                in_specs=[smem, smem, vmem, vmem],
+                out_specs=vmem,
+                out_shape=shape,
+                compiler_params=params(),
+                name="sums_sent" if sent else "sums_kept",
+            )(where, key_len, key_rows, value_rows)
+
+        near = moved(half(True, packed), swaps)
+        keep = half(False, jax.ShapeDtypeStruct((rows + extra, width), F32))
+        return keep, near, add_packed(one, keep, near)
 
     def add_packed(flag, keep, *parts):
         return pl.pallas_call(
@@ -313,11 +314,10 @@
             name="scores",
         )(where, key_len, query_rows, key_rows, *keys, value_rows)
 
-    one = jnp.ones((1,), jnp.int32)
     far_keys = [moved(key_rows, turns[0])]
-    keep, near = fenced(block_sums, where, key_len, key_rows, value_rows)
+    keep, near, payload = fenced(block_sums, where, key_len, key_rows, value_rows)
     near_keys = moved(after(key_rows, near), swaps)
-    hops = [moved(add_packed(one, keep, near), steps[0])]
+    hops = [moved(payload, steps[0])]
     far_keys += [moved(after(key_rows, near), turn) for turn in turns[1:]]
     hops.append(moved(add_packed(one, keep, after(near, far_keys[0]), *hops), steps[1]))
     held = [pair for pair in turns[0] if pair[0] < 2 and levels == 3]
@@ -350,15 +350,15 @@
         )(where, linear_scale, query_rows, *parts)
 
     own = linear(True, *hops, after(near, first_values[0]))
-    base = pl.pallas_call(
-        functools.partial(parts_kernel, width, [1, len(first_values)]),
+    base, *weights[2:] = pl.pallas_call(
+        functools.partial(parts_kernel, width, [1, len(first_values)], late - 1),
         grid=grid,
-        in_specs=[narrow] + [wide] * (1 + 2 + 1 + len(first_values)),
-        out_specs=wide,
-        out_shape=full_f32,
+        in_specs=[narrow] + [wide] * (1 + 2 + 1 + len(first_values) + late - 1),
+        out_specs=[wide] * late,
+        out_shape=[full_f32] + [full] * (late - 1),
         compiler_params=params(),
         name="parts",
-    )(factors, after(base, own), *weights[:2], near_values, *first_values)
+    )(factors, after(base, own), *weights[:2], near_values, *first_values, *weights[2:])
 
     other = linear(False, far)
     return pl.pallas_call(

time: 84.7 us -> 84.8 us (level)
    pallas_call x1 -> x2, Pallas kernels: 2.7 us -> 4.97 us  [half(): pl.pallas_call(functools.partial(block_sums_kernel, heads, width, sent),...]
    pallas_call x1, Pallas kernels: 3.98 us -> 2.27 us  [shards(): pl.pallas_call(functools.partial(parts_kernel, width, [1, len(first_value...]
  transfers between devices with their start and end apart: 12 -> 12, of which waited for: 6 -> 7; matrix products, arithmetic and copies ran while one was open for 0% -> 0% of each run, Pallas kernels for 29% -> 30%
where the time goes in v9:
time: 84.8 us; the launch traced here: 84.4 us
  waiting for transfers between devices  39.1 us (46%)
  Pallas kernels  26.8 us (32%)
  starting transfers between devices  17.4 us (21%)
    ppermute x12, waiting for transfers between devices, moved(): return lax.ppermute(x, 'seq', pairs)  39.1 us
    ppermute x12, starting transfers between devices, moved(): return lax.ppermute(x, 'seq', pairs)  17.4 us
    pallas_call x1, Pallas kernels, scores(): pl.pallas_call(functools.partial(scores_kernel, width, levels), grid_spec...  8.75 us
    pallas_call x4, Pallas kernels, add_packed(): pl.pallas_call(functools.partial(add_packed_kernel, rows, extra, len(part...  5.79 us
    pallas_call x2, Pallas kernels, half(): pl.pallas_call(functools.partial(block_sums_kernel, heads, width, sent),...  4.97 us
    pallas_call x2, Pallas kernels, linear(): pl.pallas_call(functools.partial(linear_kernel, heads, width, own, len(pa...  3.16 us
    pallas_call x1, Pallas kernels, shards(): pl.pallas_call(functools.partial(parts_kernel, width, [1, len(first_value...  2.27 us
    pallas_call x1, Pallas kernels, shards(): pl.pallas_call(functools.partial(finish_kernel, heads, width, late, a_ste...  1.85 us
  transfers between devices with their start and end apart: 12, of which 7 were waited for; matrix products, arithmetic and copies ran while one was open for 0% of the time, Pallas kernels for 30%

profile of v9, /device:TPU:0, one launch (start us, length us, event | category | flops | bytes accessed | tf_op | source)
XLA Modules:
  0.0 84.4 jit_solution(2653368769322717673)
XLA Ops:
  0.0 4.0 %collective-permute-start.3 = (bf16[128,3072]{1,0:T(8,128)(2,1)}, bf16[128,3072]{1,0:T(8,128)(2,1)S(1)}, u32[]{:S(2)}, u32[]{:S(2)}) collective-permute-start(bf16[128,3072]{1,0:T(8,128)(2,1)} %param.10), channel_id=1, source_target_pairs={{0,8},{2,10},{8,12},{10,14},{12,4},{14,6},{4,0},{6,2},{1,9},{3,11}... | collective-permute-start | bytes 2359304 | tf_op jit(solution)/shard_map/ppermute | solution.py:255
  4.7 0.0 copy-start.1
  4.7 14.6 %conditional.2 = (f32[1552,128]{1,0:T(8,128)}, bf16[1584,128]{1,0:T(8,128)(2,1)}, bf16[1584,128]{1,0:T(8,128)(2,1)S(1)}) conditional(s32[]{:T(128)} %bitcast.1, () %tuple.29, (s32[1]{0:T(128)}, s32[8]{0:T(128)}, bf16[128,3072]{1,0:T(8,128)(2,1)}, bf16[128,3072]{1,0:T(8,128)(2,1)}) %tuple.30), branch_computations={%region_0.0_spmd, %region_1.0_spmd} | conditional | bytes 4767992 | solution.py:266
  4.7 0.0 copy-start.3
  4.7 0.0 copy-start.13
  4.7 2.2 %sums_sent.1 = bf16[1584,128]{1,0:T(8,128)(2,1)S(1)} custom-call(s32[1]{0:T(128)} %get-tuple-element.37.where, s32[8]{0:T(128)} %get-tuple-element.38.lengths, bf16[128,3072]{1,0:T(8,128)(2,1)} %get-tuple-element.39.k_ref, bf16[128,3072]{1,0:T(8,128)(2,1)} %get-tuple-element.40.v_ref), custom_call_target="tpu_custom_call" | custom-call | tf_op jit(solution)/shard_map/cond/branch_1_fun/sums_sent/pallas_call | solution.py:272
  7.0 1.6 %collective-permute-start = (bf16[1584,128]{1,0:T(8,128)(2,1)S(1)}, bf16[1584,128]{1,0:T(8,128)(2,1)}, u32[]{:S(2)}, u32[]{:S(2)}) collective-permute-start(bf16[1584,128]{1,0:T(8,128)(2,1)S(1)} %sums_sent.1), channel_id=1, source_target_pairs={{0,2},{2,0},{4,6},{6,4},{8,10},{10,8},{12,14},{14,12},{1,3},{3,1},... | collective-permute-start | bytes 1216520 | tf_op jit(solution)/shard_map/cond/branch_1_fun/ppermute | solution.py:255
  8.5 0.0 copy-done.3
  8.5 2.8 %sums_kept.1.keep_ref = f32[1552,128]{1,0:T(8,128)} custom-call(s32[1]{0:T(128)} %get-tuple-element.37.where, s32[8]{0:T(128)S(1)} %copy-done.13, bf16[128,3072]{1,0:T(8,128)(2,1)S(1)} %copy-done.3, bf16[128,3072]{1,0:T(8,128)(2,1)} %get-tuple-element.40.v_ref), custom_call_target="tpu_custom_call" | custom-call | tf_op jit(solution)/shard_map/cond/branch_1_fun/sums_kept/pallas_call | solution.py:272
  11.3 6.7 %collective-permute-done.refs_0_ = bf16[1584,128]{1,0:T(8,128)(2,1)} collective-permute-done((bf16[1584,128]{1,0:T(8,128)(2,1)S(1)}, bf16[1584,128]{1,0:T(8,128)(2,1)}, u32[]{:S(2)}, u32[]{:S(2)}) %collective-permute-start) | collective-permute-done | bytes 405536 | tf_op jit(solution)/shard_map/cond/branch_1_fun/ppermute | solution.py:255
  18.0 1.3 %add_packed.4 = bf16[1584,128]{1,0:T(8,128)(2,1)S(1)} custom-call(s32[1]{0:T(128)} %constant.12.clone.where, f32[1552,128]{1,0:T(8,128)} %sums_kept.1.keep_ref, bf16[1584,128]{1,0:T(8,128)(2,1)} %collective-permute-done.refs_0_), custom_call_target="tpu_custom_call" | custom-call | tf_op jit(solution)/shard_map/cond/branch_1_fun/add_packed/pallas_call | solution.py:286
  19.3 0.0 copy-start.4
  19.3 0.0 copy-start.12
  19.3 1.4 %collective-permute-start.2 = (bf16[1584,128]{1,0:T(8,128)(2,1)S(1)}, bf16[1584,128]{1,0:T(8,128)(2,1)S(1)}, u32[]{:S(2)}, u32[]{:S(2)}) collective-permute-start(bf16[1584,128]{1,0:T(8,128)(2,1)S(1)} %get-tuple-element.80), channel_id=1, source_target_pairs={{0,4},{2,6},{1,5},{3,7},{16,20},{18,22},{17,21},{19,23}} | collective-permute-start | bytes 1216520 | tf_op jit(solution)/shard_map/ppermute | solution.py:255
  20.8 1.6 %collective-permute-start.5 = (bf16[128,3072]{1,0:T(8,128)(2,1)}, bf16[128,3072]{1,0:T(8,128)(2,1)S(1)}, u32[]{:S(2)}, u32[]{:S(2)}) collective-permute-start(bf16[128,3072]{1,0:T(8,128)(2,1)} %param.10), channel_id=1, source_target_pairs={{0,2},{2,0},{4,6},{6,4},{8,10},{10,8},{12,14},{14,12},{1,3},{3,1},... | collective-permute-start | bytes 2359304 | tf_op jit(solution)/shard_map/ppermute | solution.py:255
  22.4 0.0 collective-permute-start.6
  22.4 0.0 collective-permute-done.3
  22.4 0.0 copy-start.10
  22.5 8.4 %collective-permute-done.2.refs_1_ = bf16[1584,128]{1,0:T(8,128)(2,1)S(1)} collective-permute-done((bf16[1584,128]{1,0:T(8,128)(2,1)S(1)}, bf16[1584,128]{1,0:T(8,128)(2,1)S(1)}, u32[]{:S(2)}, u32[]{:S(2)}) %collective-permute-start.2) | collective-permute-done | bytes 405536 | tf_op jit(solution)/shard_map/ppermute | solution.py:255
  30.9 1.4 %add_packed.6 = bf16[1584,128]{1,0:T(8,128)(2,1)S(1)} custom-call(s32[1]{0:T(128)} %constant.29.clone.1.where, f32[1552,128]{1,0:T(8,128)} %get-tuple-element.78.keep_ref, bf16[1584,128]{1,0:T(8,128)(2,1)} %get-tuple-element.89.refs_0_.refs_3_, bf16[1584,128]{1,0:T(8,128)(2,1)S(1)} %collective-permute-done.2.refs_1_), custom_call_target="tpu_custom_call" | custom-call | tf_op jit(solution)/shard_map/add_packed/pallas_call | solution.py:286
  32.3 0.7 collective-permute-start.4
  33.0 6.2 %collective-permute-done.5 = bf16[128,3072]{1,0:T(8,128)(2,1)S(1)} collective-permute-done((bf16[128,3072]{1,0:T(8,128)(2,1)}, bf16[128,3072]{1,0:T(8,128)(2,1)S(1)}, u32[]{:S(2)}, u32[]{:S(2)}) %collective-permute-start.5) | collective-permute-done | bytes 786464 | tf_op jit(solution)/shard_map/ppermute | solution.py:255
  39.2 1.3 %collective-permute-start.7 = (bf16[128,3072]{1,0:T(8,128)(2,1)}, bf16[128,3072]{1,0:T(8,128)(2,1)S(1)}, u32[]{:S(2)}, u32[]{:S(2)}) collective-permute-start(bf16[128,3072]{1,0:T(8,128)(2,1)} %param.11), channel_id=1, source_target_pairs={{8,12},{10,14},{12,4},{14,6},{4,0},{6,2},{9,13},{11,15},{13,5},{15... | collective-permute-start | bytes 2359304 | tf_op jit(solution)/shard_map/ppermute | solution.py:255
  40.4 6.1 %collective-permute-done.6 = bf16[128,3072]{1,0:T(8,128)(2,1)S(1)} collective-permute-done((bf16[128,3072]{1,0:T(8,128)(2,1)S(1)}, bf16[128,3072]{1,0:T(8,128)(2,1)S(1)}, u32[]{:S(2)}, u32[]{:S(2)}) %collective-permute-start.6) | collective-permute-done | bytes 786464 | tf_op jit(solution)/shard_map/ppermute | solution.py:255
  46.6 1.5 %collective-permute-start.8 = (bf16[128,3072]{1,0:T(8,128)(2,1)}, bf16[128,3072]{1,0:T(8,128)(2,1)S(1)}, u32[]{:S(2)}, u32[]{:S(2)}) collective-permute-start(bf16[128,3072]{1,0:T(8,128)(2,1)} %param.11), channel_id=1, source_target_pairs={{0,2},{2,0},{4,6},{6,4},{8,10},{10,8},{12,14},{14,12},{1,3},{3,1},... | collective-permute-start | bytes 2359304 | tf_op jit(solution)/shard_map/ppermute | solution.py:255
  48.1 1.3 %collective-permute-start.9 = (bf16[128,3072]{1,0:T(8,128)(2,1)}, bf16[128,3072]{1,0:T(8,128)(2,1)S(1)}, u32[]{:S(2)}, u32[]{:S(2)}) collective-permute-start(bf16[128,3072]{1,0:T(8,128)(2,1)} %param.11), channel_id=1, source_target_pairs={{0,8},{2,10},{1,9},{3,11},{16,24},{18,26},{17,25},{19,27}} | collective-permute-start | bytes 2359304 | tf_op jit(solution)/shard_map/ppermute | solution.py:255
  49.4 0.0 collective-permute-done.4
  49.5 1.9 %collective-permute-start.11 = (bf16[128,3072]{1,0:T(8,128)(2,1)}, bf16[128,3072]{1,0:T(8,128)(2,1)S(1)}, u32[]{:S(2)}, u32[]{:S(2)}) collective-permute-start(bf16[128,3072]{1,0:T(8,128)(2,1)} %param.11), channel_id=1, source_target_pairs={{8,0},{10,2},{12,8},{14,10},{4,12},{6,14},{0,4},{2,6},{9,1},{11,3}... | collective-permute-start | bytes 2359304 | tf_op jit(solution)/shard_map/ppermute | solution.py:255
  51.4 0.0 copy-done.4
  51.4 11.8 %conditional.3 = (bf16[1584,128]{1,0:T(8,128)(2,1)S(1)}, bf16[1584,128]{1,0:T(8,128)(2,1)S(1)}, bf16[1584,128]{1,0:T(8,128)(2,1)}, bf16[128,3072]{1,0:T(8,128)(2...) conditional(s32[]{:T(128)} %bitcast.1, () %tuple.28, ...), branch_computations={%region_2.0_spmd, %region_3.0_spmd} | conditional | bytes 6389892 | solution.py:266
  51.4 0.0 copy-start.11
  51.4 1.5 %add_packed.5 = bf16[1584,128]{1,0:T(8,128)(2,1)S(1)} custom-call(s32[1]{0:T(128)} %constant.19.clone.where, f32[1552,128]{1,0:T(8,128)} %get-tuple-element.43.keep_ref, bf16[1584,128]{1,0:T(8,128)(2,1)} %get-tuple-element.44.refs_0_, bf16[1584,128]{1,0:T(8,128)(2,1)S(1)} %get-tuple-element.112.refs_1_, bf16[1584,128]{1,0:T(8,128)(2,1)S(1)} %get-tuple-element.113.refs_2_), custom_call_target="tpu_custom_call" | custom-call | tf_op jit(solution)/shard_map/cond/branch_1_fun/add_packed/pallas_call | solution.py:286
  52.9 1.4 %collective-permute-start.1 = (bf16[1584,128]{1,0:T(8,128)(2,1)S(1)}, bf16[1584,128]{1,0:T(8,128)(2,1)}, u32[]{:S(2)}, u32[]{:S(2)}) collective-permute-start(bf16[1584,128]{1,0:T(8,128)(2,1)S(1)} %add_packed.5), channel_id=1, source_target_pairs={{8,12},{10,14},{9,13},{11,15},{24,28},{26,30},{25,29},{27,31}} | collective-permute-start | bytes 1216520 | tf_op jit(solution)/shard_map/cond/branch_1_fun/ppermute | solution.py:255
  54.4 8.8 %scores.1 = (bf16[128,3072]{1,0:T(8,128)(2,1)}, bf16[128,3072]{1,0:T(8,128)(2,1)}, bf16[128,3072]{1,0:T(8,128)(2,1)}, f32[128,768]{1,0:T(8,128)}, f32[128,3072]{1,0:T(8,128)S(1)}) custom-call(s32[1]{0:T(128)} %get-tuple-element.45.where, s32[8]{0:T(128)S(1)} %get-tuple-element.46.lengths, bf16[128,3072]{1,0:T(8,128)(2,1)S(1)} %get-tuple-element.47.q_ref, ...), custom_call_target="tpu_custom_call" | custom-call | tf_op jit(solution)/shard_map/cond/branch_1_fun/scores/pallas_call | solution.py:304
  63.2 0.0 collective-permute-done.1
  63.2 0.0 copy-start.5
  63.2 1.5 %add_packed.7 = bf16[1584,128]{1,0:T(8,128)(2,1)S(1)} custom-call(s32[1]{0:T(128)S(6)} %sub.3.where, f32[1552,128]{1,0:T(8,128)} %get-tuple-element.78.keep_ref, bf16[1584,128]{1,0:T(8,128)(2,1)S(1)} %get-tuple-element.85.refs_0_, bf16[1584,128]{1,0:T(8,128)(2,1)S(1)} %get-tuple-element.86.refs_1_, bf16[1584,128]{1,0:T(8,128)(2,1)} %get-tuple-element.87.refs_2_), custom_call_target="tpu_custom_call" | custom-call | tf_op jit(solution)/shard_map/add_packed/pallas_call | solution.py:286
  64.8 0.6 collective-permute-start.10
  65.3 0.0 collective-permute-done.7.refs_3_
  65.3 0.0 copy-done
  65.4 2.2 %linear_own.1.own_ref = f32[128,1536]{1,0:T(8,128)S(1)} custom-call(s32[1]{0:T(128)} %bitcast.where, f32[24]{0:T(128)S(1)} %copy-done, bf16[128,3072]{1,0:T(8,128)(2,1)S(1)} %copy-done.5, bf16[1584,128]{1,0:T(8,128)(2,1)S(1)} %get-tuple-element.85.refs_0_, bf16[1584,128]{1,0:T(8,128)(2,1)S(1)} %get-tuple-element.86.refs_1_, ...), custom_call_target="tpu_custom_call" | custom-call | tf_op jit(solution)/shard_map/linear_own/pallas_call | solution.py:343
  67.5 0.0 collective-permute-done.8.refs_2_
  67.5 0.2 collective-permute-done.9.refs_4_
  67.8 2.3 %parts.1 = (f32[128,3072]{1,0:T(8,128)S(1)}, bf16[128,3072]{1,0:T(8,128)(2,1)S(1)}) custom-call(f32[128,768]{1,0:T(8,128)S(1)} %copy-done.6, f32[128,3072]{1,0:T(8,128)S(1)} %get-tuple-element.90.base_ref, bf16[128,3072]{1,0:T(8,128)(2,1)S(1)} %copy-done.7, bf16[128,3072]{1,0:T(8,128)(2,1)S(1)} %copy-done.8, ...), custom_call_target="tpu_custom_call" | custom-call | tf_op jit(solution)/shard_map/parts/pallas_call | solution.py:353
  70.0 4.5 %collective-permute-done.10.refs_0_ = bf16[1584,128]{1,0:T(8,128)(2,1)S(1)} collective-permute-done((bf16[1584,128]{1,0:T(8,128)(2,1)S(1)}, bf16[1584,128]{1,0:T(8,128)(2,1)S(1)}, u32[]{:S(2)}, u32[]{:S(2)}) %collective-permute-start.10) | collective-permute-done | bytes 405536 | tf_op jit(solution)/shard_map/ppermute | solution.py:255
  74.5 1.0 %linear_other.1.other_ref = f32[128,1536]{1,0:T(8,128)S(1)} custom-call(s32[1]{0:T(128)} %bitcast.where, f32[24]{0:T(128)S(1)} %copy-done, bf16[128,3072]{1,0:T(8,128)(2,1)S(1)} %copy-done.5, bf16[1584,128]{1,0:T(8,128)(2,1)S(1)} %collective-permute-done.10.refs_0_), custom_call_target="tpu_custom_call" | custom-call | tf_op jit(solution)/shard_map/linear_other/pallas_call | solution.py:343
  75.5 7.0 %collective-permute-done.11.refs_1_ = bf16[128,3072]{1,0:T(8,128)(2,1)S(1)} collective-permute-done((bf16[128,3072]{1,0:T(8,128)(2,1)}, bf16[128,3072]{1,0:T(8,128)(2,1)S(1)}, u32[]{:S(2)}, u32[]{:S(2)}) %collective-permute-start.11) | collective-permute-done | bytes 786464 | tf_op jit(solution)/shard_map/ppermute | solution.py:255
  82.5 1.9 %finish.1 = bf16[128,3072]{1,0:T(8,128)(2,1)} custom-call(s32[1]{0:T(128)} %bitcast.where, f32[128,768]{1,0:T(8,128)S(1)} %copy-done.6, f32[128,3072]{1,0:T(8,128)S(1)} %get-tuple-element.95.base_ref, f32[128,1536]{1,0:T(8,128)S(1)} %linear_own.1.own_ref, f32[128,1536]{1,0:T(8,128)S(1)} %linear_other.1.other_ref, ...), custom_call_target="tpu_custom_call" | custom-call | tf_op jit(solution)/shard_map/finish/pallas_call | solution.py:364
  (19 shorter events, 0.1 us)
Async XLA Ops:
  0.0 22.4 %collective-permute-start.3 = (bf16[128,3072]{1,0:T(8,128)(2,1)}, bf16[128,3072]{1,0:T(8,128)(2,1)S(1)}, u32[]{:S(2)}, u32[]{:S(2)}) collective-permute-start(bf16[128,3072]{1,0:T(8,128)(2,1)} %param.10), channel_id=1, source_target_pairs={{0,8},{2,10},{8,12},{10,14},{12,4},{14,6},{4,0},{6,2},{1,9},{3,11}... | collective-permute-start | bytes 2359304 | tf_op jit(solution)/shard_map/ppermute | solution.py:255
  4.7 17.7 %copy-start.1 = (bf16[128,3072]{1,0:T(8,128)(2,1)S(1)}, bf16[128,3072]{1,0:T(8,128)(2,1)}, u32[]{:S(2)}) copy-start(bf16[128,3072]{1,0:T(8,128)(2,1)} %param.10) | copy-start | bytes 2359300
  4.7 3.8 %copy-start.3 = (bf16[128,3072]{1,0:T(8,128)(2,1)S(1)}, bf16[128,3072]{1,0:T(8,128)(2,1)}, u32[]{:S(2)}) copy-start(bf16[128,3072]{1,0:T(8,128)(2,1)} %get-tuple-element.39.k_ref) | copy-start | bytes 2359300 | tf_op jit(solution)/shard_map/cond
  4.7 3.8 %copy-start.13 = (s32[8]{0:T(128)S(1)}, s32[8]{0:T(128)}, u32[]{:S(2)}) copy-start(s32[8]{0:T(128)} %get-tuple-element.38.lengths) | copy-start | bytes 100 | tf_op jit(solution)/shard_map/cond
  7.0 11.0 %collective-permute-start = (bf16[1584,128]{1,0:T(8,128)(2,1)S(1)}, bf16[1584,128]{1,0:T(8,128)(2,1)}, u32[]{:S(2)}, u32[]{:S(2)}) collective-permute-start(bf16[1584,128]{1,0:T(8,128)(2,1)S(1)} %sums_sent.1), channel_id=1, source_target_pairs={{0,2},{2,0},{4,6},{6,4},{8,10},{10,8},{12,14},{14,12},{1,3},{3,1},... | collective-permute-start | bytes 1216520 | tf_op jit(solution)/shard_map/cond/branch_1_fun/ppermute | solution.py:255
  19.3 32.1 %copy-start.2 = (bf16[128,3072]{1,0:T(8,128)(2,1)S(1)}, bf16[128,3072]{1,0:T(8,128)(2,1)}, u32[]{:S(2)}) copy-start(bf16[128,3072]{1,0:T(8,128)(2,1)} %param.10) | copy-start | bytes 2359300
  19.3 32.1 %copy-start.4 = (bf16[128,3072]{1,0:T(8,128)(2,1)S(1)}, bf16[128,3072]{1,0:T(8,128)(2,1)}, u32[]{:S(2)}) copy-start(bf16[128,3072]{1,0:T(8,128)(2,1)} %q_ref.3) | copy-start | bytes 2359300
  19.3 32.0 %copy-start.12 = (s32[8]{0:T(128)S(1)}, s32[8]{0:T(128)}, u32[]{:S(2)}) copy-start(s32[8]{0:T(128)} %param.12) | copy-start | bytes 100
  19.3 11.5 %collective-permute-start.2 = (bf16[1584,128]{1,0:T(8,128)(2,1)S(1)}, bf16[1584,128]{1,0:T(8,128)(2,1)S(1)}, u32[]{:S(2)}, u32[]{:S(2)}) collective-permute-start(bf16[1584,128]{1,0:T(8,128)(2,1)S(1)} %get-tuple-element.80), channel_id=1, source_target_pairs={{0,4},{2,6},{1,5},{3,7},{16,20},{18,22},{17,21},{19,23}} | collective-permute-start | bytes 1216520 | tf_op jit(solution)/shard_map/ppermute | solution.py:255
  20.8 18.4 %collective-permute-start.5 = (bf16[128,3072]{1,0:T(8,128)(2,1)}, bf16[128,3072]{1,0:T(8,128)(2,1)S(1)}, u32[]{:S(2)}, u32[]{:S(2)}) collective-permute-start(bf16[128,3072]{1,0:T(8,128)(2,1)} %param.10), channel_id=1, source_target_pairs={{0,2},{2,0},{4,6},{6,4},{8,10},{10,8},{12,14},{14,12},{1,3},{3,1},... | collective-permute-start | bytes 2359304 | tf_op jit(solution)/shard_map/ppermute | solution.py:255
  22.4 24.2 %collective-permute-start.6 = (bf16[128,3072]{1,0:T(8,128)(2,1)S(1)}, bf16[128,3072]{1,0:T(8,128)(2,1)S(1)}, u32[]{:S(2)}, u32[]{:S(2)}) collective-permute-start(bf16[128,3072]{1,0:T(8,128)(2,1)S(1)} %copy-done.1), channel_id=1, source_target_pairs={{8,0},{10,2},{12,8},{14,10},{4,12},{6,14},{0,4},{2,6},{9,1},{11,3}... | collective-permute-start | bytes 2359304 | tf_op jit(solution)/shard_map/ppermute | solution.py:255
  22.4 10.5 %copy-start.10 = (bf16[128,3072]{1,0:T(8,128)(2,1)}, bf16[128,3072]{1,0:T(8,128)(2,1)S(1)}, u32[]{:S(2)}) copy-start(bf16[128,3072]{1,0:T(8,128)(2,1)S(1)} %collective-permute-done.3) | copy-start | bytes 2359300
  32.3 17.2 %collective-permute-start.4 = (bf16[1584,128]{1,0:T(8,128)(2,1)S(1)}, bf16[1584,128]{1,0:T(8,128)(2,1)S(1)}, u32[]{:S(2)}, u32[]{:S(2)}) collective-permute-start(bf16[1584,128]{1,0:T(8,128)(2,1)S(1)} %add_packed.6), channel_id=1, source_target_pairs={{4,8},{6,10},{5,9},{7,11},{20,24},{22,26},{21,25},{23,27}} | collective-permute-start | bytes 1216520 | tf_op jit(solution)/shard_map/ppermute | solution.py:255
  39.2 26.2 %collective-permute-start.7 = (bf16[128,3072]{1,0:T(8,128)(2,1)}, bf16[128,3072]{1,0:T(8,128)(2,1)S(1)}, u32[]{:S(2)}, u32[]{:S(2)}) collective-permute-start(bf16[128,3072]{1,0:T(8,128)(2,1)} %param.11), channel_id=1, source_target_pairs={{8,12},{10,14},{12,4},{14,6},{4,0},{6,2},{9,13},{11,15},{13,5},{15... | collective-permute-start | bytes 2359304 | tf_op jit(solution)/shard_map/ppermute | solution.py:255
  46.6 20.9 %collective-permute-start.8 = (bf16[128,3072]{1,0:T(8,128)(2,1)}, bf16[128,3072]{1,0:T(8,128)(2,1)S(1)}, u32[]{:S(2)}, u32[]{:S(2)}) collective-permute-start(bf16[128,3072]{1,0:T(8,128)(2,1)} %param.11), channel_id=1, source_target_pairs={{0,2},{2,0},{4,6},{6,4},{8,10},{10,8},{12,14},{14,12},{1,3},{3,1},... | collective-permute-start | bytes 2359304 | tf_op jit(solution)/shard_map/ppermute | solution.py:255
  48.1 19.6 %collective-permute-start.9 = (bf16[128,3072]{1,0:T(8,128)(2,1)}, bf16[128,3072]{1,0:T(8,128)(2,1)S(1)}, u32[]{:S(2)}, u32[]{:S(2)}) collective-permute-start(bf16[128,3072]{1,0:T(8,128)(2,1)} %param.11), channel_id=1, source_target_pairs={{0,8},{2,10},{1,9},{3,11},{16,24},{18,26},{17,25},{19,27}} | collective-permute-start | bytes 2359304 | tf_op jit(solution)/shard_map/ppermute | solution.py:255
  49.5 33.1 %collective-permute-start.11 = (bf16[128,3072]{1,0:T(8,128)(2,1)}, bf16[128,3072]{1,0:T(8,128)(2,1)S(1)}, u32[]{:S(2)}, u32[]{:S(2)}) collective-permute-start(bf16[128,3072]{1,0:T(8,128)(2,1)} %param.11), channel_id=1, source_target_pairs={{8,0},{10,2},{12,8},{14,10},{4,12},{6,14},{0,4},{2,6},{9,1},{11,3}... | collective-permute-start | bytes 2359304 | tf_op jit(solution)/shard_map/ppermute | solution.py:255
  51.4 3.0 %copy-start.11 = (bf16[128,3072]{1,0:T(8,128)(2,1)S(1)}, bf16[128,3072]{1,0:T(8,128)(2,1)}, u32[]{:S(2)}) copy-start(bf16[128,3072]{1,0:T(8,128)(2,1)} %get-tuple-element.50.refs_2_) | copy-start | bytes 2359300 | tf_op jit(solution)/shard_map/cond
  52.9 10.3 %collective-permute-start.1 = (bf16[1584,128]{1,0:T(8,128)(2,1)S(1)}, bf16[1584,128]{1,0:T(8,128)(2,1)}, u32[]{:S(2)}, u32[]{:S(2)}) collective-permute-start(bf16[1584,128]{1,0:T(8,128)(2,1)S(1)} %add_packed.5), channel_id=1, source_target_pairs={{8,12},{10,14},{9,13},{11,15},{24,28},{26,30},{25,29},{27,31}} | collective-permute-start | bytes 1216520 | tf_op jit(solution)/shard_map/cond/branch_1_fun/ppermute | solution.py:255
  63.2 2.2 %copy-start = (f32[24]{0:T(128)S(1)}, f32[24]{0:T(128)}, u32[]{:S(2)}) copy-start(f32[24]{0:T(128)} %scale.3) | copy-start | bytes 292
  63.2 2.2 %copy-start.5 = (bf16[128,3072]{1,0:T(8,128)(2,1)S(1)}, bf16[128,3072]{1,0:T(8,128)(2,1)}, u32[]{:S(2)}) copy-start(bf16[128,3072]{1,0:T(8,128)(2,1)} %q_ref.3) | copy-start | bytes 2359300
  64.7 3.0 %copy-start.6 = (f32[128,768]{1,0:T(8,128)S(1)}, f32[128,768]{1,0:T(8,128)}, u32[]{:S(2)}) copy-start(f32[128,768]{1,0:T(8,128)} %get-tuple-element.83.factor_ref) | copy-start | bytes 1179652
  64.7 3.0 %copy-start.7 = (bf16[128,3072]{1,0:T(8,128)(2,1)S(1)}, bf16[128,3072]{1,0:T(8,128)(2,1)}, u32[]{:S(2)}) copy-start(bf16[128,3072]{1,0:T(8,128)(2,1)} %get-tuple-element.91.refs_0_) | copy-start | bytes 2359300
  64.8 3.0 %copy-start.8 = (bf16[128,3072]{1,0:T(8,128)(2,1)S(1)}, bf16[128,3072]{1,0:T(8,128)(2,1)}, u32[]{:S(2)}) copy-start(bf16[128,3072]{1,0:T(8,128)(2,1)} %get-tuple-element.92.refs_1_) | copy-start | bytes 2359300
  64.8 3.0 %copy-start.9 = (bf16[128,3072]{1,0:T(8,128)(2,1)S(1)}, bf16[128,3072]{1,0:T(8,128)(2,1)}, u32[]{:S(2)}) copy-start(bf16[128,3072]{1,0:T(8,128)(2,1)} %get-tuple-element.94.refs_5_) | copy-start | bytes 2359300
  64.8 9.8 %collective-permute-start.10 = (bf16[1584,128]{1,0:T(8,128)(2,1)S(1)}, bf16[1584,128]{1,0:T(8,128)(2,1)S(1)}, u32[]{:S(2)}, u32[]{:S(2)}) collective-permute-start(bf16[1584,128]{1,0:T(8,128)(2,1)S(1)} %add_packed.7), channel_id=1, source_target_pairs={{0,2},{2,0},{4,6},{6,4},{8,10},{10,8},{12,14},{14,12},{1,3},{3,1},... | collective-permute-start | bytes 1216520 | tf_op jit(solution)/shard_map/ppermute | solution.py:255

commit v10 on v9

--- a/solution.py
+++ b/solution.py
@@ -9,7 +9,7 @@
 from jax.sharding import PartitionSpec as P
 
 CENTER = 1.125
-TERMS = 3
+TERMS = 2
 HEADS_A_STEP = 4
 VMEM_BYTES = 40 * 1024 * 1024
 F32 = jnp.float32
@@ -202,21 +202,21 @@
 
 def finish_kernel(heads, width, late, a_step, where, factor_ref, base_ref, own_ref, other_ref, *refs):
     weight_refs, value_refs, out_ref = refs[: late - 1], refs[late - 1 : -1], refs[-1]
-    side = lax.rem(where[0], 2)
+    step = pl.program_id(0)
     half_heads = heads // 2
-    for own, linear_ref in ((True, own_ref), (False, other_ref)):
-        start = (side if own else 1 - side) * half_heads
-        for h in range(half_heads):
-            at = pl.ds(pl.multiple_of((start + h) * width, width), width)
-            total = base_ref[:, at] + linear_ref[:, h * width : (h + 1) * width]
-            column = pl.ds(pl.multiple_of((start + h) // a_step * 128, 128), 128)
-            factors = factor_ref[:, column]
-            for which in range(late - 1):
-                lane = (which + 2) * a_step + h % a_step
-                total = total + factors[:, lane : lane + 1] * jnp.dot(
-                    weight_refs[which][:, at], value_refs[which][:, at], preferred_element_type=F32
-                )
-            out_ref[:, at] = total.astype(BF16)
+    own = step == lax.rem(where[0], 2)
+    for h in range(half_heads):
+        block = slice(h * width, (h + 1) * width)
+        at = pl.ds(pl.multiple_of((step * half_heads + h) * width, width), width)
+        total = base_ref[:, at] + jnp.where(own, own_ref[:, block], other_ref[:, block])
+        column = pl.ds(pl.multiple_of((step * half_heads + h) // a_step * 128, 128), 128)
+        factors = factor_ref[:, column]
+        for which in range(late - 1):
+            lane = (which + 2) * a_step + h % a_step
+            total = total + factors[:, lane : lane + 1] * jnp.dot(
+                weight_refs[which][:, at], value_refs[which][:, at], preferred_element_type=F32
+            )
+        out_ref[:, block] = total.astype(BF16)
 
 
 def params():
@@ -363,8 +363,9 @@
     other = linear(False, far)
     return pl.pallas_call(
         functools.partial(finish_kernel, heads, width, late, a_step),
+        grid=(2,),
         in_specs=[smem] + [vmem] * (4 + 2 * (late - 1)),
-        out_specs=vmem,
+        out_specs=pl.BlockSpec((row_count, columns // 2), lambda i: (0, i)),
         out_shape=full,
         compiler_params=params(),
         name="finish",

time: 84.8 us -> 84.6 us (level)
  no operation moved by 1% of the time
where the time goes in v10:
time: 84.6 us; the launch traced here: 84.2 us
  waiting for transfers between devices  39 us (46%)
  Pallas kernels  26.7 us (32%)
  starting transfers between devices  17.4 us (21%)
    ppermute x12, waiting for transfers between devices, moved(): return lax.ppermute(x, 'seq', pairs)  39 us
    ppermute x12, starting transfers between devices, moved(): return lax.ppermute(x, 'seq', pairs)  17.4 us
    pallas_call x1, Pallas kernels, scores(): pl.pallas_call(functools.partial(scores_kernel, width, levels), grid_spec...  8.76 us
    pallas_call x4, Pallas kernels, add_packed(): pl.pallas_call(functools.partial(add_packed_kernel, rows, extra, len(part...  5.78 us
    pallas_call x2, Pallas kernels, half(): pl.pallas_call(functools.partial(block_sums_kernel, heads, width, sent),...  4.97 us
    pallas_call x2, Pallas kernels, linear(): pl.pallas_call(functools.partial(linear_kernel, heads, width, own, len(pa...  3.16 us
    pallas_call x1, Pallas kernels, shards(): pl.pallas_call(functools.partial(parts_kernel, width, [1, len(first_value...  2.26 us
    pallas_call x1, Pallas kernels, shards(): pl.pallas_call(functools.partial(finish_kernel, heads, width, late, a_ste...  1.78 us
  transfers between devices with their start and end apart: 12, of which 7 were waited for; matrix products, arithmetic and copies ran while one was open for 0% of the time, Pallas kernels for 30%

profile of v10, /device:TPU:0, one launch (start us, length us, event | category | flops | bytes accessed | tf_op | source)
XLA Modules:
  0.0 84.2 jit_solution(13561892572912444584)
XLA Ops:
  0.0 4.0 %collective-permute-start.3 = (bf16[128,3072]{1,0:T(8,128)(2,1)}, bf16[128,3072]{1,0:T(8,128)(2,1)S(1)}, u32[]{:S(2)}, u32[]{:S(2)}) collective-permute-start(bf16[128,3072]{1,0:T(8,128)(2,1)} %param.10), channel_id=1, source_target_pairs={{0,8},{2,10},{8,12},{10,14},{12,4},{14,6},{4,0},{6,2},{1,9},{3,11}... | collective-permute-start | bytes 2359304 | tf_op jit(solution)/shard_map/ppermute | solution.py:255
  4.7 0.0 copy-start.1
  4.7 14.5 %conditional.2 = (f32[1552,128]{1,0:T(8,128)}, bf16[1568,128]{1,0:T(8,128)(2,1)}, bf16[1568,128]{1,0:T(8,128)(2,1)S(1)}) conditional(s32[]{:T(128)} %bitcast.1, () %tuple.29, (s32[1]{0:T(128)}, s32[8]{0:T(128)}, bf16[128,3072]{1,0:T(8,128)(2,1)}, bf16[128,3072]{1,0:T(8,128)(2,1)}) %tuple.30), branch_computations={%region_0.0_spmd, %region_1.0_spmd} | conditional | bytes 4751608 | solution.py:266
  4.7 0.0 copy-start.3
  4.7 0.0 copy-start.13
  4.7 2.2 %sums_sent.1 = bf16[1568,128]{1,0:T(8,128)(2,1)S(1)} custom-call(s32[1]{0:T(128)} %get-tuple-element.37.where, s32[8]{0:T(128)} %get-tuple-element.38.lengths, bf16[128,3072]{1,0:T(8,128)(2,1)} %get-tuple-element.39.k_ref, bf16[128,3072]{1,0:T(8,128)(2,1)} %get-tuple-element.40.v_ref), custom_call_target="tpu_custom_call" | custom-call | tf_op jit(solution)/shard_map/cond/branch_1_fun/sums_sent/pallas_call | solution.py:272
  7.0 1.6 %collective-permute-start = (bf16[1568,128]{1,0:T(8,128)(2,1)S(1)}, bf16[1568,128]{1,0:T(8,128)(2,1)}, u32[]{:S(2)}, u32[]{:S(2)}) collective-permute-start(bf16[1568,128]{1,0:T(8,128)(2,1)S(1)} %sums_sent.1), channel_id=1, source_target_pairs={{0,2},{2,0},{4,6},{6,4},{8,10},{10,8},{12,14},{14,12},{1,3},{3,1},... | collective-permute-start | bytes 1204232 | tf_op jit(solution)/shard_map/cond/branch_1_fun/ppermute | solution.py:255
  8.5 2.8 %sums_kept.1.keep_ref = f32[1552,128]{1,0:T(8,128)} custom-call(s32[1]{0:T(128)} %get-tuple-element.37.where, s32[8]{0:T(128)S(1)} %copy-done.13, bf16[128,3072]{1,0:T(8,128)(2,1)S(1)} %copy-done.3, bf16[128,3072]{1,0:T(8,128)(2,1)} %get-tuple-element.40.v_ref), custom_call_target="tpu_custom_call" | custom-call | tf_op jit(solution)/shard_map/cond/branch_1_fun/sums_kept/pallas_call | solution.py:272
  11.3 6.6 %collective-permute-done.refs_0_ = bf16[1568,128]{1,0:T(8,128)(2,1)} collective-permute-done((bf16[1568,128]{1,0:T(8,128)(2,1)S(1)}, bf16[1568,128]{1,0:T(8,128)(2,1)}, u32[]{:S(2)}, u32[]{:S(2)}) %collective-permute-start) | collective-permute-done | bytes 401440 | tf_op jit(solution)/shard_map/cond/branch_1_fun/ppermute | solution.py:255
  17.9 1.3 %add_packed.4 = bf16[1568,128]{1,0:T(8,128)(2,1)S(1)} custom-call(s32[1]{0:T(128)} %constant.12.clone.where, f32[1552,128]{1,0:T(8,128)} %sums_kept.1.keep_ref, bf16[1568,128]{1,0:T(8,128)(2,1)} %collective-permute-done.refs_0_), custom_call_target="tpu_custom_call" | custom-call | tf_op jit(solution)/shard_map/cond/branch_1_fun/add_packed/pallas_call | solution.py:286
  19.2 0.0 copy-start.2
  19.2 0.0 copy-start.4
  19.2 0.0 copy-start.12
  19.2 1.4 %collective-permute-start.2 = (bf16[1568,128]{1,0:T(8,128)(2,1)S(1)}, bf16[1568,128]{1,0:T(8,128)(2,1)S(1)}, u32[]{:S(2)}, u32[]{:S(2)}) collective-permute-start(bf16[1568,128]{1,0:T(8,128)(2,1)S(1)} %get-tuple-element.80), channel_id=1, source_target_pairs={{0,4},{2,6},{1,5},{3,7},{16,20},{18,22},{17,21},{19,23}} | collective-permute-start | bytes 1204232 | tf_op jit(solution)/shard_map/ppermute | solution.py:255
  20.7 1.6 %collective-permute-start.5 = (bf16[128,3072]{1,0:T(8,128)(2,1)}, bf16[128,3072]{1,0:T(8,128)(2,1)S(1)}, u32[]{:S(2)}, u32[]{:S(2)}) collective-permute-start(bf16[128,3072]{1,0:T(8,128)(2,1)} %param.10), channel_id=1, source_target_pairs={{0,2},{2,0},{4,6},{6,4},{8,10},{10,8},{12,14},{14,12},{1,3},{3,1},... | collective-permute-start | bytes 2359304 | tf_op jit(solution)/shard_map/ppermute | solution.py:255
  22.3 0.0 copy-done.1
  22.3 0.0 collective-permute-start.6
  22.3 0.0 collective-permute-done.3
  22.3 0.0 copy-start.10
  22.4 8.4 %collective-permute-done.2.refs_1_ = bf16[1568,128]{1,0:T(8,128)(2,1)S(1)} collective-permute-done((bf16[1568,128]{1,0:T(8,128)(2,1)S(1)}, bf16[1568,128]{1,0:T(8,128)(2,1)S(1)}, u32[]{:S(2)}, u32[]{:S(2)}) %collective-permute-start.2) | collective-permute-done | bytes 401440 | tf_op jit(solution)/shard_map/ppermute | solution.py:255
  30.8 1.4 %add_packed.6 = bf16[1568,128]{1,0:T(8,128)(2,1)S(1)} custom-call(s32[1]{0:T(128)} %constant.29.clone.1.where, f32[1552,128]{1,0:T(8,128)} %get-tuple-element.78.keep_ref, bf16[1568,128]{1,0:T(8,128)(2,1)} %get-tuple-element.89.refs_0_.refs_3_, bf16[1568,128]{1,0:T(8,128)(2,1)S(1)} %collective-permute-done.2.refs_1_), custom_call_target="tpu_custom_call" | custom-call | tf_op jit(solution)/shard_map/add_packed/pallas_call | solution.py:286
  32.2 0.7 collective-permute-start.4
  32.9 6.2 %collective-permute-done.5 = bf16[128,3072]{1,0:T(8,128)(2,1)S(1)} collective-permute-done((bf16[128,3072]{1,0:T(8,128)(2,1)}, bf16[128,3072]{1,0:T(8,128)(2,1)S(1)}, u32[]{:S(2)}, u32[]{:S(2)}) %collective-permute-start.5) | collective-permute-done | bytes 786464 | tf_op jit(solution)/shard_map/ppermute | solution.py:255
  39.1 1.3 %collective-permute-start.7 = (bf16[128,3072]{1,0:T(8,128)(2,1)}, bf16[128,3072]{1,0:T(8,128)(2,1)S(1)}, u32[]{:S(2)}, u32[]{:S(2)}) collective-permute-start(bf16[128,3072]{1,0:T(8,128)(2,1)} %param.11), channel_id=1, source_target_pairs={{8,12},{10,14},{12,4},{14,6},{4,0},{6,2},{9,13},{11,15},{13,5},{15... | collective-permute-start | bytes 2359304 | tf_op jit(solution)/shard_map/ppermute | solution.py:255
  40.4 6.1 %collective-permute-done.6 = bf16[128,3072]{1,0:T(8,128)(2,1)S(1)} collective-permute-done((bf16[128,3072]{1,0:T(8,128)(2,1)S(1)}, bf16[128,3072]{1,0:T(8,128)(2,1)S(1)}, u32[]{:S(2)}, u32[]{:S(2)}) %collective-permute-start.6) | collective-permute-done | bytes 786464 | tf_op jit(solution)/shard_map/ppermute | solution.py:255
  46.5 1.5 %collective-permute-start.8 = (bf16[128,3072]{1,0:T(8,128)(2,1)}, bf16[128,3072]{1,0:T(8,128)(2,1)S(1)}, u32[]{:S(2)}, u32[]{:S(2)}) collective-permute-start(bf16[128,3072]{1,0:T(8,128)(2,1)} %param.11), channel_id=1, source_target_pairs={{0,2},{2,0},{4,6},{6,4},{8,10},{10,8},{12,14},{14,12},{1,3},{3,1},... | collective-permute-start | bytes 2359304 | tf_op jit(solution)/shard_map/ppermute | solution.py:255
  48.0 1.3 %collective-permute-start.9 = (bf16[128,3072]{1,0:T(8,128)(2,1)}, bf16[128,3072]{1,0:T(8,128)(2,1)S(1)}, u32[]{:S(2)}, u32[]{:S(2)}) collective-permute-start(bf16[128,3072]{1,0:T(8,128)(2,1)} %param.11), channel_id=1, source_target_pairs={{0,8},{2,10},{1,9},{3,11},{16,24},{18,26},{17,25},{19,27}} | collective-permute-start | bytes 2359304 | tf_op jit(solution)/shard_map/ppermute | solution.py:255
  49.4 0.0 collective-permute-done.4
  49.4 1.9 %collective-permute-start.11 = (bf16[128,3072]{1,0:T(8,128)(2,1)}, bf16[128,3072]{1,0:T(8,128)(2,1)S(1)}, u32[]{:S(2)}, u32[]{:S(2)}) collective-permute-start(bf16[128,3072]{1,0:T(8,128)(2,1)} %param.11), channel_id=1, source_target_pairs={{8,0},{10,2},{12,8},{14,10},{4,12},{6,14},{0,4},{2,6},{9,1},{11,3}... | collective-permute-start | bytes 2359304 | tf_op jit(solution)/shard_map/ppermute | solution.py:255
  51.3 11.8 %conditional.3 = (bf16[1568,128]{1,0:T(8,128)(2,1)S(1)}, bf16[1568,128]{1,0:T(8,128)(2,1)S(1)}, bf16[1568,128]{1,0:T(8,128)(2,1)}, bf16[128,3072]{1,0:T(8,128)(2...) conditional(s32[]{:T(128)} %bitcast.1, () %tuple.28, ...), branch_computations={%region_2.0_spmd, %region_3.0_spmd} | conditional | bytes 6357124 | solution.py:266
  51.3 0.0 copy-start.11
  51.3 1.5 %add_packed.5 = bf16[1568,128]{1,0:T(8,128)(2,1)S(1)} custom-call(s32[1]{0:T(128)} %constant.19.clone.where, f32[1552,128]{1,0:T(8,128)} %get-tuple-element.43.keep_ref, bf16[1568,128]{1,0:T(8,128)(2,1)} %get-tuple-element.44.refs_0_, bf16[1568,128]{1,0:T(8,128)(2,1)S(1)} %get-tuple-element.112.refs_1_, bf16[1568,128]{1,0:T(8,128)(2,1)S(1)} %get-tuple-element.113.refs_2_), custom_call_target="tpu_custom_call" | custom-call | tf_op jit(solution)/shard_map/cond/branch_1_fun/add_packed/pallas_call | solution.py:286
  52.8 1.4 %collective-permute-start.1 = (bf16[1568,128]{1,0:T(8,128)(2,1)S(1)}, bf16[1568,128]{1,0:T(8,128)(2,1)}, u32[]{:S(2)}, u32[]{:S(2)}) collective-permute-start(bf16[1568,128]{1,0:T(8,128)(2,1)S(1)} %add_packed.5), channel_id=1, source_target_pairs={{8,12},{10,14},{9,13},{11,15},{24,28},{26,30},{25,29},{27,31}} | collective-permute-start | bytes 1204232 | tf_op jit(solution)/shard_map/cond/branch_1_fun/ppermute | solution.py:255
  54.3 0.0 copy-done.11
  54.3 8.8 %scores.1 = (bf16[128,3072]{1,0:T(8,128)(2,1)}, bf16[128,3072]{1,0:T(8,128)(2,1)}, bf16[128,3072]{1,0:T(8,128)(2,1)}, f32[128,768]{1,0:T(8,128)}, f32[128,3072]{1,0:T(8,128)S(1)}) custom-call(s32[1]{0:T(128)} %get-tuple-element.45.where, s32[8]{0:T(128)S(1)} %get-tuple-element.46.lengths, bf16[128,3072]{1,0:T(8,128)(2,1)S(1)} %get-tuple-element.47.q_ref, ...), custom_call_target="tpu_custom_call" | custom-call | tf_op jit(solution)/shard_map/cond/branch_1_fun/scores/pallas_call | solution.py:304
  63.1 0.0 collective-permute-done.1
  63.1 0.0 copy-start.5
  63.1 1.5 %add_packed.7 = bf16[1568,128]{1,0:T(8,128)(2,1)S(1)} custom-call(s32[1]{0:T(128)S(6)} %sub.3.where, f32[1552,128]{1,0:T(8,128)} %get-tuple-element.78.keep_ref, bf16[1568,128]{1,0:T(8,128)(2,1)S(1)} %get-tuple-element.85.refs_0_, bf16[1568,128]{1,0:T(8,128)(2,1)S(1)} %get-tuple-element.86.refs_1_, bf16[1568,128]{1,0:T(8,128)(2,1)} %get-tuple-element.87.refs_2_), custom_call_target="tpu_custom_call" | custom-call | tf_op jit(solution)/shard_map/add_packed/pallas_call | solution.py:286
  64.7 0.6 collective-permute-start.10
  65.3 0.0 collective-permute-done.7.refs_3_
  65.3 2.2 %linear_own.1.own_ref = f32[128,1536]{1,0:T(8,128)S(1)} custom-call(s32[1]{0:T(128)} %bitcast.where, f32[24]{0:T(128)S(1)} %copy-done, bf16[128,3072]{1,0:T(8,128)(2,1)S(1)} %copy-done.5, bf16[1568,128]{1,0:T(8,128)(2,1)S(1)} %get-tuple-element.85.refs_0_, bf16[1568,128]{1,0:T(8,128)(2,1)S(1)} %get-tuple-element.86.refs_1_, ...), custom_call_target="tpu_custom_call" | custom-call | tf_op jit(solution)/shard_map/linear_own/pallas_call | solution.py:343
  67.4 0.0 collective-permute-done.8.refs_2_
  67.4 0.2 collective-permute-done.9.refs_4_
  67.7 2.3 %parts.1 = (f32[128,3072]{1,0:T(8,128)S(1)}, bf16[128,3072]{1,0:T(8,128)(2,1)S(1)}) custom-call(f32[128,768]{1,0:T(8,128)S(1)} %copy-done.6, f32[128,3072]{1,0:T(8,128)S(1)} %get-tuple-element.90.base_ref, bf16[128,3072]{1,0:T(8,128)(2,1)S(1)} %copy-done.7, bf16[128,3072]{1,0:T(8,128)(2,1)S(1)} %copy-done.8, ...), custom_call_target="tpu_custom_call" | custom-call | tf_op jit(solution)/shard_map/parts/pallas_call | solution.py:353
  69.9 4.4 %collective-permute-done.10.refs_0_ = bf16[1568,128]{1,0:T(8,128)(2,1)S(1)} collective-permute-done((bf16[1568,128]{1,0:T(8,128)(2,1)S(1)}, bf16[1568,128]{1,0:T(8,128)(2,1)S(1)}, u32[]{:S(2)}, u32[]{:S(2)}) %collective-permute-start.10) | collective-permute-done | bytes 401440 | tf_op jit(solution)/shard_map/ppermute | solution.py:255
  74.4 1.0 %linear_other.1.other_ref = f32[128,1536]{1,0:T(8,128)S(1)} custom-call(s32[1]{0:T(128)} %bitcast.where, f32[24]{0:T(128)S(1)} %copy-done, bf16[128,3072]{1,0:T(8,128)(2,1)S(1)} %copy-done.5, bf16[1568,128]{1,0:T(8,128)(2,1)S(1)} %collective-permute-done.10.refs_0_), custom_call_target="tpu_custom_call" | custom-call | tf_op jit(solution)/shard_map/linear_other/pallas_call | solution.py:343
  75.4 7.1 %collective-permute-done.11.refs_1_ = bf16[128,3072]{1,0:T(8,128)(2,1)S(1)} collective-permute-done((bf16[128,3072]{1,0:T(8,128)(2,1)}, bf16[128,3072]{1,0:T(8,128)(2,1)S(1)}, u32[]{:S(2)}, u32[]{:S(2)}) %collective-permute-start.11) | collective-permute-done | bytes 786464 | tf_op jit(solution)/shard_map/ppermute | solution.py:255
  82.4 1.8 %finish.1 = bf16[128,3072]{1,0:T(8,128)(2,1)} custom-call(s32[1]{0:T(128)} %bitcast.where, f32[128,768]{1,0:T(8,128)S(1)} %copy-done.6, f32[128,3072]{1,0:T(8,128)S(1)} %get-tuple-element.95.base_ref, f32[128,1536]{1,0:T(8,128)S(1)} %linear_own.1.own_ref, f32[128,1536]{1,0:T(8,128)S(1)} %linear_other.1.other_ref, ...), custom_call_target="tpu_custom_call" | custom-call | tf_op jit(solution)/shard_map/finish/pallas_call | solution.py:364
  (19 shorter events, 0.1 us)
Async XLA Ops:
  0.0 22.3 %collective-permute-start.3 = (bf16[128,3072]{1,0:T(8,128)(2,1)}, bf16[128,3072]{1,0:T(8,128)(2,1)S(1)}, u32[]{:S(2)}, u32[]{:S(2)}) collective-permute-start(bf16[128,3072]{1,0:T(8,128)(2,1)} %param.10), channel_id=1, source_target_pairs={{0,8},{2,10},{8,12},{10,14},{12,4},{14,6},{4,0},{6,2},{1,9},{3,11}... | collective-permute-start | bytes 2359304 | tf_op jit(solution)/shard_map/ppermute | solution.py:255
  4.7 17.6 %copy-start.1 = (bf16[128,3072]{1,0:T(8,128)(2,1)S(1)}, bf16[128,3072]{1,0:T(8,128)(2,1)}, u32[]{:S(2)}) copy-start(bf16[128,3072]{1,0:T(8,128)(2,1)} %param.10) | copy-start | bytes 2359300
  4.7 3.8 %copy-start.3 = (bf16[128,3072]{1,0:T(8,128)(2,1)S(1)}, bf16[128,3072]{1,0:T(8,128)(2,1)}, u32[]{:S(2)}) copy-start(bf16[128,3072]{1,0:T(8,128)(2,1)} %get-tuple-element.39.k_ref) | copy-start | bytes 2359300 | tf_op jit(solution)/shard_map/cond
  4.7 3.8 %copy-start.13 = (s32[8]{0:T(128)S(1)}, s32[8]{0:T(128)}, u32[]{:S(2)}) copy-start(s32[8]{0:T(128)} %get-tuple-element.38.lengths) | copy-start | bytes 100 | tf_op jit(solution)/shard_map/cond
  7.0 10.9 %collective-permute-start = (bf16[1568,128]{1,0:T(8,128)(2,1)S(1)}, bf16[1568,128]{1,0:T(8,128)(2,1)}, u32[]{:S(2)}, u32[]{:S(2)}) collective-permute-start(bf16[1568,128]{1,0:T(8,128)(2,1)S(1)} %sums_sent.1), channel_id=1, source_target_pairs={{0,2},{2,0},{4,6},{6,4},{8,10},{10,8},{12,14},{14,12},{1,3},{3,1},... | collective-permute-start | bytes 1204232 | tf_op jit(solution)/shard_map/cond/branch_1_fun/ppermute | solution.py:255
  19.2 32.1 %copy-start.2 = (bf16[128,3072]{1,0:T(8,128)(2,1)S(1)}, bf16[128,3072]{1,0:T(8,128)(2,1)}, u32[]{:S(2)}) copy-start(bf16[128,3072]{1,0:T(8,128)(2,1)} %param.10) | copy-start | bytes 2359300
  19.2 32.1 %copy-start.4 = (bf16[128,3072]{1,0:T(8,128)(2,1)S(1)}, bf16[128,3072]{1,0:T(8,128)(2,1)}, u32[]{:S(2)}) copy-start(bf16[128,3072]{1,0:T(8,128)(2,1)} %q_ref.3) | copy-start | bytes 2359300
  19.2 32.0 %copy-start.12 = (s32[8]{0:T(128)S(1)}, s32[8]{0:T(128)}, u32[]{:S(2)}) copy-start(s32[8]{0:T(128)} %param.12) | copy-start | bytes 100
  19.2 11.5 %collective-permute-start.2 = (bf16[1568,128]{1,0:T(8,128)(2,1)S(1)}, bf16[1568,128]{1,0:T(8,128)(2,1)S(1)}, u32[]{:S(2)}, u32[]{:S(2)}) collective-permute-start(bf16[1568,128]{1,0:T(8,128)(2,1)S(1)} %get-tuple-element.80), channel_id=1, source_target_pairs={{0,4},{2,6},{1,5},{3,7},{16,20},{18,22},{17,21},{19,23}} | collective-permute-start | bytes 1204232 | tf_op jit(solution)/shard_map/ppermute | solution.py:255
  20.7 18.4 %collective-permute-start.5 = (bf16[128,3072]{1,0:T(8,128)(2,1)}, bf16[128,3072]{1,0:T(8,128)(2,1)S(1)}, u32[]{:S(2)}, u32[]{:S(2)}) collective-permute-start(bf16[128,3072]{1,0:T(8,128)(2,1)} %param.10), channel_id=1, source_target_pairs={{0,2},{2,0},{4,6},{6,4},{8,10},{10,8},{12,14},{14,12},{1,3},{3,1},... | collective-permute-start | bytes 2359304 | tf_op jit(solution)/shard_map/ppermute | solution.py:255
  22.3 24.2 %collective-permute-start.6 = (bf16[128,3072]{1,0:T(8,128)(2,1)S(1)}, bf16[128,3072]{1,0:T(8,128)(2,1)S(1)}, u32[]{:S(2)}, u32[]{:S(2)}) collective-permute-start(bf16[128,3072]{1,0:T(8,128)(2,1)S(1)} %copy-done.1), channel_id=1, source_target_pairs={{8,0},{10,2},{12,8},{14,10},{4,12},{6,14},{0,4},{2,6},{9,1},{11,3}... | collective-permute-start | bytes 2359304 | tf_op jit(solution)/shard_map/ppermute | solution.py:255
  22.3 10.5 %copy-start.10 = (bf16[128,3072]{1,0:T(8,128)(2,1)}, bf16[128,3072]{1,0:T(8,128)(2,1)S(1)}, u32[]{:S(2)}) copy-start(bf16[128,3072]{1,0:T(8,128)(2,1)S(1)} %collective-permute-done.3) | copy-start | bytes 2359300
  32.2 17.2 %collective-permute-start.4 = (bf16[1568,128]{1,0:T(8,128)(2,1)S(1)}, bf16[1568,128]{1,0:T(8,128)(2,1)S(1)}, u32[]{:S(2)}, u32[]{:S(2)}) collective-permute-start(bf16[1568,128]{1,0:T(8,128)(2,1)S(1)} %add_packed.6), channel_id=1, source_target_pairs={{4,8},{6,10},{5,9},{7,11},{20,24},{22,26},{21,25},{23,27}} | collective-permute-start | bytes 1204232 | tf_op jit(solution)/shard_map/ppermute | solution.py:255
  39.1 26.2 %collective-permute-start.7 = (bf16[128,3072]{1,0:T(8,128)(2,1)}, bf16[128,3072]{1,0:T(8,128)(2,1)S(1)}, u32[]{:S(2)}, u32[]{:S(2)}) collective-permute-start(bf16[128,3072]{1,0:T(8,128)(2,1)} %param.11), channel_id=1, source_target_pairs={{8,12},{10,14},{12,4},{14,6},{4,0},{6,2},{9,13},{11,15},{13,5},{15... | collective-permute-start | bytes 2359304 | tf_op jit(solution)/shard_map/ppermute | solution.py:255
  46.5 20.9 %collective-permute-start.8 = (bf16[128,3072]{1,0:T(8,128)(2,1)}, bf16[128,3072]{1,0:T(8,128)(2,1)S(1)}, u32[]{:S(2)}, u32[]{:S(2)}) collective-permute-start(bf16[128,3072]{1,0:T(8,128)(2,1)} %param.11), channel_id=1, source_target_pairs={{0,2},{2,0},{4,6},{6,4},{8,10},{10,8},{12,14},{14,12},{1,3},{3,1},... | collective-permute-start | bytes 2359304 | tf_op jit(solution)/shard_map/ppermute | solution.py:255
  48.0 19.6 %collective-permute-start.9 = (bf16[128,3072]{1,0:T(8,128)(2,1)}, bf16[128,3072]{1,0:T(8,128)(2,1)S(1)}, u32[]{:S(2)}, u32[]{:S(2)}) collective-permute-start(bf16[128,3072]{1,0:T(8,128)(2,1)} %param.11), channel_id=1, source_target_pairs={{0,8},{2,10},{1,9},{3,11},{16,24},{18,26},{17,25},{19,27}} | collective-permute-start | bytes 2359304 | tf_op jit(solution)/shard_map/ppermute | solution.py:255
  49.4 33.1 %collective-permute-start.11 = (bf16[128,3072]{1,0:T(8,128)(2,1)}, bf16[128,3072]{1,0:T(8,128)(2,1)S(1)}, u32[]{:S(2)}, u32[]{:S(2)}) collective-permute-start(bf16[128,3072]{1,0:T(8,128)(2,1)} %param.11), channel_id=1, source_target_pairs={{8,0},{10,2},{12,8},{14,10},{4,12},{6,14},{0,4},{2,6},{9,1},{11,3}... | collective-permute-start | bytes 2359304 | tf_op jit(solution)/shard_map/ppermute | solution.py:255
  51.3 3.0 %copy-start.11 = (bf16[128,3072]{1,0:T(8,128)(2,1)S(1)}, bf16[128,3072]{1,0:T(8,128)(2,1)}, u32[]{:S(2)}) copy-start(bf16[128,3072]{1,0:T(8,128)(2,1)} %get-tuple-element.50.refs_2_) | copy-start | bytes 2359300 | tf_op jit(solution)/shard_map/cond
  52.8 10.3 %collective-permute-start.1 = (bf16[1568,128]{1,0:T(8,128)(2,1)S(1)}, bf16[1568,128]{1,0:T(8,128)(2,1)}, u32[]{:S(2)}, u32[]{:S(2)}) collective-permute-start(bf16[1568,128]{1,0:T(8,128)(2,1)S(1)} %add_packed.5), channel_id=1, source_target_pairs={{8,12},{10,14},{9,13},{11,15},{24,28},{26,30},{25,29},{27,31}} | collective-permute-start | bytes 1204232 | tf_op jit(solution)/shard_map/cond/branch_1_fun/ppermute | solution.py:255
  63.1 2.2 %copy-start = (f32[24]{0:T(128)S(1)}, f32[24]{0:T(128)}, u32[]{:S(2)}) copy-start(f32[24]{0:T(128)} %scale.3) | copy-start | bytes 292
  63.1 2.2 %copy-start.5 = (bf16[128,3072]{1,0:T(8,128)(2,1)S(1)}, bf16[128,3072]{1,0:T(8,128)(2,1)}, u32[]{:S(2)}) copy-start(bf16[128,3072]{1,0:T(8,128)(2,1)} %q_ref.3) | copy-start | bytes 2359300
  64.7 3.0 %copy-start.6 = (f32[128,768]{1,0:T(8,128)S(1)}, f32[128,768]{1,0:T(8,128)}, u32[]{:S(2)}) copy-start(f32[128,768]{1,0:T(8,128)} %get-tuple-element.83.factor_ref) | copy-start | bytes 1179652
  64.7 3.0 %copy-start.7 = (bf16[128,3072]{1,0:T(8,128)(2,1)S(1)}, bf16[128,3072]{1,0:T(8,128)(2,1)}, u32[]{:S(2)}) copy-start(bf16[128,3072]{1,0:T(8,128)(2,1)} %get-tuple-element.91.refs_0_) | copy-start | bytes 2359300
  64.7 3.0 %copy-start.8 = (bf16[128,3072]{1,0:T(8,128)(2,1)S(1)}, bf16[128,3072]{1,0:T(8,128)(2,1)}, u32[]{:S(2)}) copy-start(bf16[128,3072]{1,0:T(8,128)(2,1)} %get-tuple-element.92.refs_1_) | copy-start | bytes 2359300
  64.7 3.0 %copy-start.9 = (bf16[128,3072]{1,0:T(8,128)(2,1)S(1)}, bf16[128,3072]{1,0:T(8,128)(2,1)}, u32[]{:S(2)}) copy-start(bf16[128,3072]{1,0:T(8,128)(2,1)} %get-tuple-element.94.refs_5_) | copy-start | bytes 2359300
  64.7 9.7 %collective-permute-start.10 = (bf16[1568,128]{1,0:T(8,128)(2,1)S(1)}, bf16[1568,128]{1,0:T(8,128)(2,1)S(1)}, u32[]{:S(2)}, u32[]{:S(2)}) collective-permute-start(bf16[1568,128]{1,0:T(8,128)(2,1)S(1)} %add_packed.7), channel_id=1, source_target_pairs={{0,2},{2,0},{4,6},{6,4},{8,10},{10,8},{12,14},{14,12},{1,3},{3,1},... | collective-permute-start | bytes 1204232 | tf_op jit(solution)/shard_map/ppermute | solution.py:255

commit v11 on v10

--- a/solution.py
+++ b/solution.py
@@ -200,15 +200,22 @@
         out_ref[:, block] = linear * (scale[start + h] * (1.0 / (width * math.sqrt(tokens))))
 
 
-def finish_kernel(heads, width, late, a_step, where, factor_ref, base_ref, own_ref, other_ref, *refs):
+def join_kernel(where, base_ref, own_ref, other_ref, out_ref):
+    side = lax.rem(where[0], 2)
+    half = own_ref.shape[1]
+    for ref, start in ((own_ref, side * half), (other_ref, (1 - side) * half)):
+        at = pl.ds(pl.multiple_of(start, half), half)
+        out_ref[:, at] = base_ref[:, at] + ref[...]
+
+
+def finish_kernel(heads, width, late, a_step, factor_ref, base_ref, *refs):
     weight_refs, value_refs, out_ref = refs[: late - 1], refs[late - 1 : -1], refs[-1]
     step = pl.program_id(0)
     half_heads = heads // 2
-    own = step == lax.rem(where[0], 2)
     for h in range(half_heads):
         block = slice(h * width, (h + 1) * width)
         at = pl.ds(pl.multiple_of((step * half_heads + h) * width, width), width)
-        total = base_ref[:, at] + jnp.where(own, own_ref[:, block], other_ref[:, block])
+        total = base_ref[:, at]
         column = pl.ds(pl.multiple_of((step * half_heads + h) // a_step * 128, 128), 128)
         factors = factor_ref[:, column]
         for which in range(late - 1):
@@ -361,15 +368,23 @@
     )(factors, after(base, own), *weights[:2], near_values, *first_values, *weights[2:])
 
     other = linear(False, far)
+    base = pl.pallas_call(
+        join_kernel,
+        in_specs=[smem] + [vmem] * 3,
+        out_specs=vmem,
+        out_shape=full_f32,
+        compiler_params=params(),
+        name="join",
+    )(where, base, own, other)
     return pl.pallas_call(
         functools.partial(finish_kernel, heads, width, late, a_step),
         grid=(2,),
-        in_specs=[smem] + [vmem] * (4 + 2 * (late - 1)),
+        in_specs=[vmem] * (2 + 2 * (late - 1)),
         out_specs=pl.BlockSpec((row_count, columns // 2), lambda i: (0, i)),
         out_shape=full,
         compiler_params=params(),
         name="finish",
-    )(where, factors, base, own, other, *weights[2:], *far_values)
+    )(factors, base, *weights[2:], *far_values)
 
 
 def solution(mesh):

time: 84.6 us -> 85.6 us (1.012)
  Pallas kernels: 26.7 us -> 30 us
  waiting for transfers between devices: 39 us -> 36.7 us
    pallas_call x1, Pallas kernels: 2.26 us -> 4.65 us  [shards(): pl.pallas_call(functools.partial(parts_kernel, width, [1, len(first_value...]
    ppermute x12, waiting for transfers between devices: 39 us -> 36.7 us  [moved(): return lax.ppermute(x, 'seq', pairs)]
  transfers between devices with their start and end apart: 12 -> 12, of which waited for: 7 -> 7; matrix products, arithmetic and copies ran while one was open for 0% -> 0% of each run, Pallas kernels for 30% -> 32%
where the time goes in v11:
time: 85.6 us; the launch traced here: 85 us
  waiting for transfers between devices  36.7 us (43%)
  Pallas kernels  30 us (35%)
  starting transfers between devices  17.4 us (20%)
    ppermute x12, waiting for transfers between devices, moved(): return lax.ppermute(x, 'seq', pairs)  36.7 us
    ppermute x12, starting transfers between devices, moved(): return lax.ppermute(x, 'seq', pairs)  17.4 us
    pallas_call x1, Pallas kernels, scores(): pl.pallas_call(functools.partial(scores_kernel, width, levels), grid_spec...  8.82 us
    pallas_call x4, Pallas kernels, add_packed(): pl.pallas_call(functools.partial(add_packed_kernel, rows, extra, len(part...  5.78 us
    pallas_call x2, Pallas kernels, half(): pl.pallas_call(functools.partial(block_sums_kernel, heads, width, sent),...  4.96 us
    pallas_call x1, Pallas kernels, shards(): pl.pallas_call(functools.partial(parts_kernel, width, [1, len(first_value...  4.65 us
    pallas_call x2, Pallas kernels, linear(): pl.pallas_call(functools.partial(linear_kernel, heads, width, own, len(pa...  2.96 us
    pallas_call x1, Pallas kernels, shards(): pl.pallas_call(functools.partial(finish_kernel, heads, width, late, a_ste...  2.61 us
  transfers between devices with their start and end apart: 12, of which 7 were waited for; matrix products, arithmetic and copies ran while one was open for 0% of the time, Pallas kernels for 32%

profile of v11, /device:TPU:0, one launch (start us, length us, event | category | flops | bytes accessed | tf_op | source)
XLA Modules:
  0.0 85.0 jit_solution(1958624083397077639)
XLA Ops:
  0.0 4.0 %collective-permute-start.3 = (bf16[128,3072]{1,0:T(8,128)(2,1)}, bf16[128,3072]{1,0:T(8,128)(2,1)S(1)}, u32[]{:S(2)}, u32[]{:S(2)}) collective-permute-start(bf16[128,3072]{1,0:T(8,128)(2,1)} %param.10), channel_id=1, source_target_pairs={{0,8},{2,10},{8,12},{10,14},{12,4},{14,6},{4,0},{6,2},{1,9},{3,11}... | collective-permute-start | bytes 2359304 | tf_op jit(solution)/shard_map/ppermute | solution.py:262
  4.7 0.0 copy-start.1
  4.7 14.5 %conditional.2 = (f32[1552,128]{1,0:T(8,128)}, bf16[1568,128]{1,0:T(8,128)(2,1)}, bf16[1568,128]{1,0:T(8,128)(2,1)S(1)}) conditional(s32[]{:T(128)} %bitcast, () %tuple.29, (s32[1]{0:T(128)}, s32[8]{0:T(128)}, bf16[128,3072]{1,0:T(8,128)(2,1)}, bf16[128,3072]{1,0:T(8,128)(2,1)}) %tuple.30), branch_computations={%region_0.0_spmd, %region_1.0_spmd} | conditional | bytes 4751608 | solution.py:273
  4.7 0.0 copy-start.3
  4.7 0.0 copy-start.9
  4.7 2.2 %sums_sent.1 = bf16[1568,128]{1,0:T(8,128)(2,1)S(1)} custom-call(s32[1]{0:T(128)} %get-tuple-element.37.where, s32[8]{0:T(128)} %get-tuple-element.38.lengths, bf16[128,3072]{1,0:T(8,128)(2,1)} %get-tuple-element.39.k_ref, bf16[128,3072]{1,0:T(8,128)(2,1)} %get-tuple-element.40.v_ref), custom_call_target="tpu_custom_call" | custom-call | tf_op jit(solution)/shard_map/cond/branch_1_fun/sums_sent/pallas_call | solution.py:279
  7.0 1.6 %collective-permute-start = (bf16[1568,128]{1,0:T(8,128)(2,1)S(1)}, bf16[1568,128]{1,0:T(8,128)(2,1)}, u32[]{:S(2)}, u32[]{:S(2)}) collective-permute-start(bf16[1568,128]{1,0:T(8,128)(2,1)S(1)} %sums_sent.1), channel_id=1, source_target_pairs={{0,2},{2,0},{4,6},{6,4},{8,10},{10,8},{12,14},{14,12},{1,3},{3,1},... | collective-permute-start | bytes 1204232 | tf_op jit(solution)/shard_map/cond/branch_1_fun/ppermute | solution.py:262
  8.5 2.8 %sums_kept.1.keep_ref = f32[1552,128]{1,0:T(8,128)} custom-call(s32[1]{0:T(128)} %get-tuple-element.37.where, s32[8]{0:T(128)S(1)} %copy-done.9, bf16[128,3072]{1,0:T(8,128)(2,1)S(1)} %copy-done.3, bf16[128,3072]{1,0:T(8,128)(2,1)} %get-tuple-element.40.v_ref), custom_call_target="tpu_custom_call" | custom-call | tf_op jit(solution)/shard_map/cond/branch_1_fun/sums_kept/pallas_call | solution.py:279
  11.3 6.6 %collective-permute-done.refs_0_ = bf16[1568,128]{1,0:T(8,128)(2,1)} collective-permute-done((bf16[1568,128]{1,0:T(8,128)(2,1)S(1)}, bf16[1568,128]{1,0:T(8,128)(2,1)}, u32[]{:S(2)}, u32[]{:S(2)}) %collective-permute-start) | collective-permute-done | bytes 401440 | tf_op jit(solution)/shard_map/cond/branch_1_fun/ppermute | solution.py:262
  17.9 1.3 %add_packed.4 = bf16[1568,128]{1,0:T(8,128)(2,1)S(1)} custom-call(s32[1]{0:T(128)} %constant.12.clone.where, f32[1552,128]{1,0:T(8,128)} %sums_kept.1.keep_ref, bf16[1568,128]{1,0:T(8,128)(2,1)} %collective-permute-done.refs_0_), custom_call_target="tpu_custom_call" | custom-call | tf_op jit(solution)/shard_map/cond/branch_1_fun/add_packed/pallas_call | solution.py:293
  19.2 0.0 copy-start.2
  19.2 0.0 copy-start.4
  19.2 0.0 copy-start.8
  19.2 1.4 %collective-permute-start.2 = (bf16[1568,128]{1,0:T(8,128)(2,1)S(1)}, bf16[1568,128]{1,0:T(8,128)(2,1)S(1)}, u32[]{:S(2)}, u32[]{:S(2)}) collective-permute-start(bf16[1568,128]{1,0:T(8,128)(2,1)S(1)} %get-tuple-element.80), channel_id=1, source_target_pairs={{0,4},{2,6},{1,5},{3,7},{16,20},{18,22},{17,21},{19,23}} | collective-permute-start | bytes 1204232 | tf_op jit(solution)/shard_map/ppermute | solution.py:262
  20.7 1.6 %collective-permute-start.5 = (bf16[128,3072]{1,0:T(8,128)(2,1)}, bf16[128,3072]{1,0:T(8,128)(2,1)S(1)}, u32[]{:S(2)}, u32[]{:S(2)}) collective-permute-start(bf16[128,3072]{1,0:T(8,128)(2,1)} %param.10), channel_id=1, source_target_pairs={{0,2},{2,0},{4,6},{6,4},{8,10},{10,8},{12,14},{14,12},{1,3},{3,1},... | collective-permute-start | bytes 2359304 | tf_op jit(solution)/shard_map/ppermute | solution.py:262
  22.3 0.0 copy-done.1
  22.3 0.0 collective-permute-start.6
  22.3 0.0 collective-permute-done.3
  22.3 0.0 copy-start.6
  22.4 8.4 %collective-permute-done.2.refs_1_ = bf16[1568,128]{1,0:T(8,128)(2,1)S(1)} collective-permute-done((bf16[1568,128]{1,0:T(8,128)(2,1)S(1)}, bf16[1568,128]{1,0:T(8,128)(2,1)S(1)}, u32[]{:S(2)}, u32[]{:S(2)}) %collective-permute-start.2) | collective-permute-done | bytes 401440 | tf_op jit(solution)/shard_map/ppermute | solution.py:262
  30.8 1.4 %add_packed.6 = bf16[1568,128]{1,0:T(8,128)(2,1)S(1)} custom-call(s32[1]{0:T(128)} %constant.29.clone.1.where, f32[1552,128]{1,0:T(8,128)} %get-tuple-element.78.keep_ref, bf16[1568,128]{1,0:T(8,128)(2,1)} %get-tuple-element.89.refs_0_.refs_3_, bf16[1568,128]{1,0:T(8,128)(2,1)S(1)} %collective-permute-done.2.refs_1_), custom_call_target="tpu_custom_call" | custom-call | tf_op jit(solution)/shard_map/add_packed/pallas_call | solution.py:293
  32.2 0.7 collective-permute-start.4
  32.9 6.2 %collective-permute-done.5 = bf16[128,3072]{1,0:T(8,128)(2,1)S(1)} collective-permute-done((bf16[128,3072]{1,0:T(8,128)(2,1)}, bf16[128,3072]{1,0:T(8,128)(2,1)S(1)}, u32[]{:S(2)}, u32[]{:S(2)}) %collective-permute-start.5) | collective-permute-done | bytes 786464 | tf_op jit(solution)/shard_map/ppermute | solution.py:262
  39.1 1.3 %collective-permute-start.7 = (bf16[128,3072]{1,0:T(8,128)(2,1)}, bf16[128,3072]{1,0:T(8,128)(2,1)S(1)}, u32[]{:S(2)}, u32[]{:S(2)}) collective-permute-start(bf16[128,3072]{1,0:T(8,128)(2,1)} %param.11), channel_id=1, source_target_pairs={{8,12},{10,14},{12,4},{14,6},{4,0},{6,2},{9,13},{11,15},{13,5},{15... | collective-permute-start | bytes 2359304 | tf_op jit(solution)/shard_map/ppermute | solution.py:262
  40.4 6.1 %collective-permute-done.6 = bf16[128,3072]{1,0:T(8,128)(2,1)S(1)} collective-permute-done((bf16[128,3072]{1,0:T(8,128)(2,1)S(1)}, bf16[128,3072]{1,0:T(8,128)(2,1)S(1)}, u32[]{:S(2)}, u32[]{:S(2)}) %collective-permute-start.6) | collective-permute-done | bytes 786464 | tf_op jit(solution)/shard_map/ppermute | solution.py:262
  46.5 1.5 %collective-permute-start.8 = (bf16[128,3072]{1,0:T(8,128)(2,1)}, bf16[128,3072]{1,0:T(8,128)(2,1)S(1)}, u32[]{:S(2)}, u32[]{:S(2)}) collective-permute-start(bf16[128,3072]{1,0:T(8,128)(2,1)} %param.11), channel_id=1, source_target_pairs={{0,2},{2,0},{4,6},{6,4},{8,10},{10,8},{12,14},{14,12},{1,3},{3,1},... | collective-permute-start | bytes 2359304 | tf_op jit(solution)/shard_map/ppermute | solution.py:262
  48.0 1.3 %collective-permute-start.9 = (bf16[128,3072]{1,0:T(8,128)(2,1)}, bf16[128,3072]{1,0:T(8,128)(2,1)S(1)}, u32[]{:S(2)}, u32[]{:S(2)}) collective-permute-start(bf16[128,3072]{1,0:T(8,128)(2,1)} %param.11), channel_id=1, source_target_pairs={{0,8},{2,10},{1,9},{3,11},{16,24},{18,26},{17,25},{19,27}} | collective-permute-start | bytes 2359304 | tf_op jit(solution)/shard_map/ppermute | solution.py:262
  49.4 0.0 collective-permute-done.4
  49.4 1.9 %collective-permute-start.11 = (bf16[128,3072]{1,0:T(8,128)(2,1)}, bf16[128,3072]{1,0:T(8,128)(2,1)S(1)}, u32[]{:S(2)}, u32[]{:S(2)}) collective-permute-start(bf16[128,3072]{1,0:T(8,128)(2,1)} %param.11), channel_id=1, source_target_pairs={{8,0},{10,2},{12,8},{14,10},{4,12},{6,14},{0,4},{2,6},{9,1},{11,3}... | collective-permute-start | bytes 2359304 | tf_op jit(solution)/shard_map/ppermute | solution.py:262
  51.3 11.9 %conditional.3 = (bf16[1568,128]{1,0:T(8,128)(2,1)S(1)}, bf16[1568,128]{1,0:T(8,128)(2,1)S(1)}, bf16[1568,128]{1,0:T(8,128)(2,1)}, bf16[128,3072]{1,0:T(8,128)(2...) conditional(s32[]{:T(128)} %bitcast, () %tuple.28, ...), branch_computations={%region_2.0_spmd, %region_3.0_spmd} | conditional | bytes 6357124 | solution.py:273
  51.3 0.0 copy-start.7
  51.3 1.5 %add_packed.5 = bf16[1568,128]{1,0:T(8,128)(2,1)S(1)} custom-call(s32[1]{0:T(128)} %constant.19.clone.where, f32[1552,128]{1,0:T(8,128)} %get-tuple-element.43.keep_ref, bf16[1568,128]{1,0:T(8,128)(2,1)} %get-tuple-element.44.refs_0_, bf16[1568,128]{1,0:T(8,128)(2,1)S(1)} %get-tuple-element.112.refs_1_, bf16[1568,128]{1,0:T(8,128)(2,1)S(1)} %get-tuple-element.113.refs_2_), custom_call_target="tpu_custom_call" | custom-call | tf_op jit(solution)/shard_map/cond/branch_1_fun/add_packed/pallas_call | solution.py:293
  52.8 1.4 %collective-permute-start.1 = (bf16[1568,128]{1,0:T(8,128)(2,1)S(1)}, bf16[1568,128]{1,0:T(8,128)(2,1)}, u32[]{:S(2)}, u32[]{:S(2)}) collective-permute-start(bf16[1568,128]{1,0:T(8,128)(2,1)S(1)} %add_packed.5), channel_id=1, source_target_pairs={{8,12},{10,14},{9,13},{11,15},{24,28},{26,30},{25,29},{27,31}} | collective-permute-start | bytes 1204232 | tf_op jit(solution)/shard_map/cond/branch_1_fun/ppermute | solution.py:262
  54.3 8.8 %scores.1 = (bf16[128,3072]{1,0:T(8,128)(2,1)}, bf16[128,3072]{1,0:T(8,128)(2,1)}, bf16[128,3072]{1,0:T(8,128)(2,1)}, f32[128,768]{1,0:T(8,128)}, f32[128,3072]{1,0:T(8,128)}) custom-call(s32[1]{0:T(128)} %get-tuple-element.45.where, s32[8]{0:T(128)S(1)} %get-tuple-element.46.lengths, bf16[128,3072]{1,0:T(8,128)(2,1)S(1)} %get-tuple-element.47.q_ref, ...), custom_call_target="tpu_custom_call" | custom-call | tf_op jit(solution)/shard_map/cond/branch_1_fun/scores/pallas_call | solution.py:311
  63.2 0.0 collective-permute-done.1
  63.2 0.0 copy-start.5
  63.2 1.5 %add_packed.7 = bf16[1568,128]{1,0:T(8,128)(2,1)S(1)} custom-call(s32[1]{0:T(128)S(6)} %sub.3.where, f32[1552,128]{1,0:T(8,128)} %get-tuple-element.78.keep_ref, bf16[1568,128]{1,0:T(8,128)(2,1)S(1)} %get-tuple-element.85.refs_0_, bf16[1568,128]{1,0:T(8,128)(2,1)S(1)} %get-tuple-element.86.refs_1_, bf16[1568,128]{1,0:T(8,128)(2,1)} %get-tuple-element.87.refs_2_), custom_call_target="tpu_custom_call" | custom-call | tf_op jit(solution)/shard_map/add_packed/pallas_call | solution.py:293
  64.7 0.6 collective-permute-start.10
  65.3 0.0 collective-permute-done.7.refs_3_
  65.3 2.0 %linear_own.1.own_ref = f32[128,1536]{1,0:T(8,128)S(1)} custom-call(s32[1]{0:T(128)} %bitcast.1.where, f32[24]{0:T(128)S(1)} %copy-done, bf16[128,3072]{1,0:T(8,128)(2,1)S(1)} %copy-done.5, bf16[1568,128]{1,0:T(8,128)(2,1)S(1)} %get-tuple-element.85.refs_0_, bf16[1568,128]{1,0:T(8,128)(2,1)S(1)} %get-tuple-element.86.refs_1_, ...), custom_call_target="tpu_custom_call" | custom-call | tf_op jit(solution)/shard_map/linear_own/pallas_call | solution.py:350
  67.3 0.0 collective-permute-done.8.refs_2_
  67.3 0.4 collective-permute-done.9.refs_4_
  67.7 4.7 %parts.1 = (f32[128,3072]{1,0:T(8,128)S(1)}, bf16[128,3072]{1,0:T(8,128)(2,1)S(1)}) custom-call(f32[128,768]{1,0:T(8,128)} %get-tuple-element.83.factor_ref, f32[128,3072]{1,0:T(8,128)} %get-tuple-element.90.base_ref, bf16[128,3072]{1,0:T(8,128)(2,1)} %get-tuple-element.91.refs_0_, bf16[128,3072]{1,0:T(8,128)(2,1)} %get-tuple-element.92.refs_1_, ...), custom_call_target="tpu_custom_call" | custom-call | tf_op jit(solution)/shard_map/parts/pallas_call | solution.py:360
  72.3 2.1 %collective-permute-done.10.refs_0_ = bf16[1568,128]{1,0:T(8,128)(2,1)S(1)} collective-permute-done((bf16[1568,128]{1,0:T(8,128)(2,1)S(1)}, bf16[1568,128]{1,0:T(8,128)(2,1)S(1)}, u32[]{:S(2)}, u32[]{:S(2)}) %collective-permute-start.10) | collective-permute-done | bytes 401440 | tf_op jit(solution)/shard_map/ppermute | solution.py:262
  74.4 1.0 %linear_other.1.other_ref = f32[128,1536]{1,0:T(8,128)S(1)} custom-call(s32[1]{0:T(128)} %bitcast.1.where, f32[24]{0:T(128)S(1)} %copy-done, bf16[128,3072]{1,0:T(8,128)(2,1)S(1)} %copy-done.5, bf16[1568,128]{1,0:T(8,128)(2,1)S(1)} %collective-permute-done.10.refs_0_), custom_call_target="tpu_custom_call" | custom-call | tf_op jit(solution)/shard_map/linear_other/pallas_call | solution.py:350
  75.4 0.2 join.1.base_ref
  75.6 6.9 %collective-permute-done.11.refs_1_ = bf16[128,3072]{1,0:T(8,128)(2,1)S(1)} collective-permute-done((bf16[128,3072]{1,0:T(8,128)(2,1)}, bf16[128,3072]{1,0:T(8,128)(2,1)S(1)}, u32[]{:S(2)}, u32[]{:S(2)}) %collective-permute-start.11) | collective-permute-done | bytes 786464 | tf_op jit(solution)/shard_map/ppermute | solution.py:262
  82.4 2.6 %finish.1 = bf16[128,3072]{1,0:T(8,128)(2,1)} custom-call(f32[128,768]{1,0:T(8,128)} %get-tuple-element.83.factor_ref, f32[128,3072]{1,0:T(8,128)S(1)} %join.1.base_ref, bf16[128,3072]{1,0:T(8,128)(2,1)S(1)} %get-tuple-element.96.refs_0_, bf16[128,3072]{1,0:T(8,128)(2,1)S(1)} %collective-permute-done.11.refs_1_), custom_call_target="tpu_custom_call" | custom-call | tf_op jit(solution)/shard_map/finish/pallas_call | solution.py:379
  (12 shorter events, 0.1 us)
Async XLA Ops:
  0.0 22.3 %collective-permute-start.3 = (bf16[128,3072]{1,0:T(8,128)(2,1)}, bf16[128,3072]{1,0:T(8,128)(2,1)S(1)}, u32[]{:S(2)}, u32[]{:S(2)}) collective-permute-start(bf16[128,3072]{1,0:T(8,128)(2,1)} %param.10), channel_id=1, source_target_pairs={{0,8},{2,10},{8,12},{10,14},{12,4},{14,6},{4,0},{6,2},{1,9},{3,11}... | collective-permute-start | bytes 2359304 | tf_op jit(solution)/shard_map/ppermute | solution.py:262
  4.7 17.6 %copy-start.1 = (bf16[128,3072]{1,0:T(8,128)(2,1)S(1)}, bf16[128,3072]{1,0:T(8,128)(2,1)}, u32[]{:S(2)}) copy-start(bf16[128,3072]{1,0:T(8,128)(2,1)} %param.10) | copy-start | bytes 2359300
  4.7 3.8 %copy-start.3 = (bf16[128,3072]{1,0:T(8,128)(2,1)S(1)}, bf16[128,3072]{1,0:T(8,128)(2,1)}, u32[]{:S(2)}) copy-start(bf16[128,3072]{1,0:T(8,128)(2,1)} %get-tuple-element.39.k_ref) | copy-start | bytes 2359300 | tf_op jit(solution)/shard_map/cond
  4.7 3.8 %copy-start.9 = (s32[8]{0:T(128)S(1)}, s32[8]{0:T(128)}, u32[]{:S(2)}) copy-start(s32[8]{0:T(128)} %get-tuple-element.38.lengths) | copy-start | bytes 100 | tf_op jit(solution)/shard_map/cond
  7.0 10.9 %collective-permute-start = (bf16[1568,128]{1,0:T(8,128)(2,1)S(1)}, bf16[1568,128]{1,0:T(8,128)(2,1)}, u32[]{:S(2)}, u32[]{:S(2)}) collective-permute-start(bf16[1568,128]{1,0:T(8,128)(2,1)S(1)} %sums_sent.1), channel_id=1, source_target_pairs={{0,2},{2,0},{4,6},{6,4},{8,10},{10,8},{12,14},{14,12},{1,3},{3,1},... | collective-permute-start | bytes 1204232 | tf_op jit(solution)/shard_map/cond/branch_1_fun/ppermute | solution.py:262
  19.2 32.1 %copy-start.2 = (bf16[128,3072]{1,0:T(8,128)(2,1)S(1)}, bf16[128,3072]{1,0:T(8,128)(2,1)}, u32[]{:S(2)}) copy-start(bf16[128,3072]{1,0:T(8,128)(2,1)} %param.10) | copy-start | bytes 2359300
  19.2 32.1 %copy-start.4 = (bf16[128,3072]{1,0:T(8,128)(2,1)S(1)}, bf16[128,3072]{1,0:T(8,128)(2,1)}, u32[]{:S(2)}) copy-start(bf16[128,3072]{1,0:T(8,128)(2,1)} %q_ref.3) | copy-start | bytes 2359300
  19.2 32.0 %copy-start.8 = (s32[8]{0:T(128)S(1)}, s32[8]{0:T(128)}, u32[]{:S(2)}) copy-start(s32[8]{0:T(128)} %param.12) | copy-start | bytes 100
  19.2 11.5 %collective-permute-start.2 = (bf16[1568,128]{1,0:T(8,128)(2,1)S(1)}, bf16[1568,128]{1,0:T(8,128)(2,1)S(1)}, u32[]{:S(2)}, u32[]{:S(2)}) collective-permute-start(bf16[1568,128]{1,0:T(8,128)(2,1)S(1)} %get-tuple-element.80), channel_id=1, source_target_pairs={{0,4},{2,6},{1,5},{3,7},{16,20},{18,22},{17,21},{19,23}} | collective-permute-start | bytes 1204232 | tf_op jit(solution)/shard_map/ppermute | solution.py:262
  20.7 18.4 %collective-permute-start.5 = (bf16[128,3072]{1,0:T(8,128)(2,1)}, bf16[128,3072]{1,0:T(8,128)(2,1)S(1)}, u32[]{:S(2)}, u32[]{:S(2)}) collective-permute-start(bf16[128,3072]{1,0:T(8,128)(2,1)} %param.10), channel_id=1, source_target_pairs={{0,2},{2,0},{4,6},{6,4},{8,10},{10,8},{12,14},{14,12},{1,3},{3,1},... | collective-permute-start | bytes 2359304 | tf_op jit(solution)/shard_map/ppermute | solution.py:262
  22.3 24.2 %collective-permute-start.6 = (bf16[128,3072]{1,0:T(8,128)(2,1)S(1)}, bf16[128,3072]{1,0:T(8,128)(2,1)S(1)}, u32[]{:S(2)}, u32[]{:S(2)}) collective-permute-start(bf16[128,3072]{1,0:T(8,128)(2,1)S(1)} %copy-done.1), channel_id=1, source_target_pairs={{8,0},{10,2},{12,8},{14,10},{4,12},{6,14},{0,4},{2,6},{9,1},{11,3}... | collective-permute-start | bytes 2359304 | tf_op jit(solution)/shard_map/ppermute | solution.py:262
  22.3 10.5 %copy-start.6 = (bf16[128,3072]{1,0:T(8,128)(2,1)}, bf16[128,3072]{1,0:T(8,128)(2,1)S(1)}, u32[]{:S(2)}) copy-start(bf16[128,3072]{1,0:T(8,128)(2,1)S(1)} %collective-permute-done.3) | copy-start | bytes 2359300
  32.2 17.2 %collective-permute-start.4 = (bf16[1568,128]{1,0:T(8,128)(2,1)S(1)}, bf16[1568,128]{1,0:T(8,128)(2,1)S(1)}, u32[]{:S(2)}, u32[]{:S(2)}) collective-permute-start(bf16[1568,128]{1,0:T(8,128)(2,1)S(1)} %add_packed.6), channel_id=1, source_target_pairs={{4,8},{6,10},{5,9},{7,11},{20,24},{22,26},{21,25},{23,27}} | collective-permute-start | bytes 1204232 | tf_op jit(solution)/shard_map/ppermute | solution.py:262
  39.1 26.2 %collective-permute-start.7 = (bf16[128,3072]{1,0:T(8,128)(2,1)}, bf16[128,3072]{1,0:T(8,128)(2,1)S(1)}, u32[]{:S(2)}, u32[]{:S(2)}) collective-permute-start(bf16[128,3072]{1,0:T(8,128)(2,1)} %param.11), channel_id=1, source_target_pairs={{8,12},{10,14},{12,4},{14,6},{4,0},{6,2},{9,13},{11,15},{13,5},{15... | collective-permute-start | bytes 2359304 | tf_op jit(solution)/shard_map/ppermute | solution.py:262
  46.5 20.8 %collective-permute-start.8 = (bf16[128,3072]{1,0:T(8,128)(2,1)}, bf16[128,3072]{1,0:T(8,128)(2,1)S(1)}, u32[]{:S(2)}, u32[]{:S(2)}) collective-permute-start(bf16[128,3072]{1,0:T(8,128)(2,1)} %param.11), channel_id=1, source_target_pairs={{0,2},{2,0},{4,6},{6,4},{8,10},{10,8},{12,14},{14,12},{1,3},{3,1},... | collective-permute-start | bytes 2359304 | tf_op jit(solution)/shard_map/ppermute | solution.py:262
  48.0 19.6 %collective-permute-start.9 = (bf16[128,3072]{1,0:T(8,128)(2,1)}, bf16[128,3072]{1,0:T(8,128)(2,1)S(1)}, u32[]{:S(2)}, u32[]{:S(2)}) collective-permute-start(bf16[128,3072]{1,0:T(8,128)(2,1)} %param.11), channel_id=1, source_target_pairs={{0,8},{2,10},{1,9},{3,11},{16,24},{18,26},{17,25},{19,27}} | collective-permute-start | bytes 2359304 | tf_op jit(solution)/shard_map/ppermute | solution.py:262
  49.4 33.1 %collective-permute-start.11 = (bf16[128,3072]{1,0:T(8,128)(2,1)}, bf16[128,3072]{1,0:T(8,128)(2,1)S(1)}, u32[]{:S(2)}, u32[]{:S(2)}) collective-permute-start(bf16[128,3072]{1,0:T(8,128)(2,1)} %param.11), channel_id=1, source_target_pairs={{8,0},{10,2},{12,8},{14,10},{4,12},{6,14},{0,4},{2,6},{9,1},{11,3}... | collective-permute-start | bytes 2359304 | tf_op jit(solution)/shard_map/ppermute | solution.py:262
  51.3 3.0 %copy-start.7 = (bf16[128,3072]{1,0:T(8,128)(2,1)S(1)}, bf16[128,3072]{1,0:T(8,128)(2,1)}, u32[]{:S(2)}) copy-start(bf16[128,3072]{1,0:T(8,128)(2,1)} %get-tuple-element.50.refs_2_) | copy-start | bytes 2359300 | tf_op jit(solution)/shard_map/cond
  52.8 10.3 %collective-permute-start.1 = (bf16[1568,128]{1,0:T(8,128)(2,1)S(1)}, bf16[1568,128]{1,0:T(8,128)(2,1)}, u32[]{:S(2)}, u32[]{:S(2)}) collective-permute-start(bf16[1568,128]{1,0:T(8,128)(2,1)S(1)} %add_packed.5), channel_id=1, source_target_pairs={{8,12},{10,14},{9,13},{11,15},{24,28},{26,30},{25,29},{27,31}} | collective-permute-start | bytes 1204232 | tf_op jit(solution)/shard_map/cond/branch_1_fun/ppermute | solution.py:262
  63.2 2.1 %copy-start = (f32[24]{0:T(128)S(1)}, f32[24]{0:T(128)}, u32[]{:S(2)}) copy-start(f32[24]{0:T(128)} %scale.3) | copy-start | bytes 292
  63.2 2.1 %copy-start.5 = (bf16[128,3072]{1,0:T(8,128)(2,1)S(1)}, bf16[128,3072]{1,0:T(8,128)(2,1)}, u32[]{:S(2)}) copy-start(bf16[128,3072]{1,0:T(8,128)(2,1)} %q_ref.3) | copy-start | bytes 2359300
  64.7 9.7 %collective-permute-start.10 = (bf16[1568,128]{1,0:T(8,128)(2,1)S(1)}, bf16[1568,128]{1,0:T(8,128)(2,1)S(1)}, u32[]{:S(2)}, u32[]{:S(2)}) collective-permute-start(bf16[1568,128]{1,0:T(8,128)(2,1)S(1)} %add_packed.7), channel_id=1, source_target_pairs={{0,2},{2,0},{4,6},{6,4},{8,10},{10,8},{12,14},{14,12},{1,3},{3,1},... | collective-permute-start | bytes 1204232 | tf_op jit(solution)/shard_map/ppermute | solution.py:262

commit v12 on v9

--- a/solution.py
+++ b/solution.py
@@ -9,7 +9,7 @@
 from jax.sharding import PartitionSpec as P
 
 CENTER = 1.125
-TERMS = 3
+TERMS = 2
 HEADS_A_STEP = 4
 VMEM_BYTES = 40 * 1024 * 1024
 F32 = jnp.float32

time: 84.8 us -> 84.7 us (level)
  no operation moved by 1% of the time
where the time goes in v12:
time: 84.7 us; the launch traced here: 84.3 us
  waiting for transfers between devices  39 us (46%)
  Pallas kernels  26.8 us (32%)
  starting transfers between devices  17.4 us (21%)
    ppermute x12, waiting for transfers between devices, moved(): return lax.ppermute(x, 'seq', pairs)  39 us
    ppermute x12, starting transfers between devices, moved(): return lax.ppermute(x, 'seq', pairs)  17.4 us
    pallas_call x1, Pallas kernels, scores(): pl.pallas_call(functools.partial(scores_kernel, width, levels), grid_spec...  8.76 us
    pallas_call x4, Pallas kernels, add_packed(): pl.pallas_call(functools.partial(add_packed_kernel, rows, extra, len(part...  5.78 us
    pallas_call x2, Pallas kernels, half(): pl.pallas_call(functools.partial(block_sums_kernel, heads, width, sent),...  4.97 us
    pallas_call x2, Pallas kernels, linear(): pl.pallas_call(functools.partial(linear_kernel, heads, width, own, len(pa...  3.16 us
    pallas_call x1, Pallas kernels, shards(): pl.pallas_call(functools.partial(parts_kernel, width, [1, len(first_value...  2.26 us
    pallas_call x1, Pallas kernels, shards(): pl.pallas_call(functools.partial(finish_kernel, heads, width, late, a_ste...  1.85 us
  transfers between devices with their start and end apart: 12, of which 7 were waited for; matrix products, arithmetic and copies ran while one was open for 0% of the time, Pallas kernels for 30%

profile of v12, /device:TPU:0, one launch (start us, length us, event | category | flops | bytes accessed | tf_op | source)
XLA Modules:
  0.0 84.3 jit_solution(14123853804433927034)
XLA Ops:
  0.0 4.0 %collective-permute-start.3 = (bf16[128,3072]{1,0:T(8,128)(2,1)}, bf16[128,3072]{1,0:T(8,128)(2,1)S(1)}, u32[]{:S(2)}, u32[]{:S(2)}) collective-permute-start(bf16[128,3072]{1,0:T(8,128)(2,1)} %param.10), channel_id=1, source_target_pairs={{0,8},{2,10},{8,12},{10,14},{12,4},{14,6},{4,0},{6,2},{1,9},{3,11}... | collective-permute-start | bytes 2359304 | tf_op jit(solution)/shard_map/ppermute | solution.py:255
  4.7 0.0 copy-start.1
  4.7 14.5 %conditional.2 = (f32[1552,128]{1,0:T(8,128)}, bf16[1568,128]{1,0:T(8,128)(2,1)}, bf16[1568,128]{1,0:T(8,128)(2,1)S(1)}) conditional(s32[]{:T(128)} %bitcast.1, () %tuple.29, (s32[1]{0:T(128)}, s32[8]{0:T(128)}, bf16[128,3072]{1,0:T(8,128)(2,1)}, bf16[128,3072]{1,0:T(8,128)(2,1)}) %tuple.30), branch_computations={%region_0.0_spmd, %region_1.0_spmd} | conditional | bytes 4751608 | solution.py:266
  4.7 0.0 copy-start.3
  4.7 0.0 copy-start.13
  4.7 2.2 %sums_sent.1 = bf16[1568,128]{1,0:T(8,128)(2,1)S(1)} custom-call(s32[1]{0:T(128)} %get-tuple-element.37.where, s32[8]{0:T(128)} %get-tuple-element.38.lengths, bf16[128,3072]{1,0:T(8,128)(2,1)} %get-tuple-element.39.k_ref, bf16[128,3072]{1,0:T(8,128)(2,1)} %get-tuple-element.40.v_ref), custom_call_target="tpu_custom_call" | custom-call | tf_op jit(solution)/shard_map/cond/branch_1_fun/sums_sent/pallas_call | solution.py:272
  7.0 1.6 %collective-permute-start = (bf16[1568,128]{1,0:T(8,128)(2,1)S(1)}, bf16[1568,128]{1,0:T(8,128)(2,1)}, u32[]{:S(2)}, u32[]{:S(2)}) collective-permute-start(bf16[1568,128]{1,0:T(8,128)(2,1)S(1)} %sums_sent.1), channel_id=1, source_target_pairs={{0,2},{2,0},{4,6},{6,4},{8,10},{10,8},{12,14},{14,12},{1,3},{3,1},... | collective-permute-start | bytes 1204232 | tf_op jit(solution)/shard_map/cond/branch_1_fun/ppermute | solution.py:255
  8.5 0.0 copy-done.3
  8.5 2.8 %sums_kept.1.keep_ref = f32[1552,128]{1,0:T(8,128)} custom-call(s32[1]{0:T(128)} %get-tuple-element.37.where, s32[8]{0:T(128)S(1)} %copy-done.13, bf16[128,3072]{1,0:T(8,128)(2,1)S(1)} %copy-done.3, bf16[128,3072]{1,0:T(8,128)(2,1)} %get-tuple-element.40.v_ref), custom_call_target="tpu_custom_call" | custom-call | tf_op jit(solution)/shard_map/cond/branch_1_fun/sums_kept/pallas_call | solution.py:272
  11.3 6.6 %collective-permute-done.refs_0_ = bf16[1568,128]{1,0:T(8,128)(2,1)} collective-permute-done((bf16[1568,128]{1,0:T(8,128)(2,1)S(1)}, bf16[1568,128]{1,0:T(8,128)(2,1)}, u32[]{:S(2)}, u32[]{:S(2)}) %collective-permute-start) | collective-permute-done | bytes 401440 | tf_op jit(solution)/shard_map/cond/branch_1_fun/ppermute | solution.py:255
  17.9 1.3 %add_packed.4 = bf16[1568,128]{1,0:T(8,128)(2,1)S(1)} custom-call(s32[1]{0:T(128)} %constant.12.clone.where, f32[1552,128]{1,0:T(8,128)} %sums_kept.1.keep_ref, bf16[1568,128]{1,0:T(8,128)(2,1)} %collective-permute-done.refs_0_), custom_call_target="tpu_custom_call" | custom-call | tf_op jit(solution)/shard_map/cond/branch_1_fun/add_packed/pallas_call | solution.py:286
  19.2 0.0 copy-start.2
  19.2 0.0 copy-start.4
  19.2 0.0 copy-start.12
  19.2 1.4 %collective-permute-start.2 = (bf16[1568,128]{1,0:T(8,128)(2,1)S(1)}, bf16[1568,128]{1,0:T(8,128)(2,1)S(1)}, u32[]{:S(2)}, u32[]{:S(2)}) collective-permute-start(bf16[1568,128]{1,0:T(8,128)(2,1)S(1)} %get-tuple-element.80), channel_id=1, source_target_pairs={{0,4},{2,6},{1,5},{3,7},{16,20},{18,22},{17,21},{19,23}} | collective-permute-start | bytes 1204232 | tf_op jit(solution)/shard_map/ppermute | solution.py:255
  20.7 1.6 %collective-permute-start.5 = (bf16[128,3072]{1,0:T(8,128)(2,1)}, bf16[128,3072]{1,0:T(8,128)(2,1)S(1)}, u32[]{:S(2)}, u32[]{:S(2)}) collective-permute-start(bf16[128,3072]{1,0:T(8,128)(2,1)} %param.10), channel_id=1, source_target_pairs={{0,2},{2,0},{4,6},{6,4},{8,10},{10,8},{12,14},{14,12},{1,3},{3,1},... | collective-permute-start | bytes 2359304 | tf_op jit(solution)/shard_map/ppermute | solution.py:255
  22.3 0.0 collective-permute-start.6
  22.3 0.0 collective-permute-done.3
  22.3 0.0 copy-start.10
  22.4 8.4 %collective-permute-done.2.refs_1_ = bf16[1568,128]{1,0:T(8,128)(2,1)S(1)} collective-permute-done((bf16[1568,128]{1,0:T(8,128)(2,1)S(1)}, bf16[1568,128]{1,0:T(8,128)(2,1)S(1)}, u32[]{:S(2)}, u32[]{:S(2)}) %collective-permute-start.2) | collective-permute-done | bytes 401440 | tf_op jit(solution)/shard_map/ppermute | solution.py:255
  30.8 1.4 %add_packed.6 = bf16[1568,128]{1,0:T(8,128)(2,1)S(1)} custom-call(s32[1]{0:T(128)} %constant.29.clone.1.where, f32[1552,128]{1,0:T(8,128)} %get-tuple-element.78.keep_ref, bf16[1568,128]{1,0:T(8,128)(2,1)} %get-tuple-element.89.refs_0_.refs_3_, bf16[1568,128]{1,0:T(8,128)(2,1)S(1)} %collective-permute-done.2.refs_1_), custom_call_target="tpu_custom_call" | custom-call | tf_op jit(solution)/shard_map/add_packed/pallas_call | solution.py:286
  32.2 0.7 collective-permute-start.4
  32.9 6.2 %collective-permute-done.5 = bf16[128,3072]{1,0:T(8,128)(2,1)S(1)} collective-permute-done((bf16[128,3072]{1,0:T(8,128)(2,1)}, bf16[128,3072]{1,0:T(8,128)(2,1)S(1)}, u32[]{:S(2)}, u32[]{:S(2)}) %collective-permute-start.5) | collective-permute-done | bytes 786464 | tf_op jit(solution)/shard_map/ppermute | solution.py:255
  39.1 1.3 %collective-permute-start.7 = (bf16[128,3072]{1,0:T(8,128)(2,1)}, bf16[128,3072]{1,0:T(8,128)(2,1)S(1)}, u32[]{:S(2)}, u32[]{:S(2)}) collective-permute-start(bf16[128,3072]{1,0:T(8,128)(2,1)} %param.11), channel_id=1, source_target_pairs={{8,12},{10,14},{12,4},{14,6},{4,0},{6,2},{9,13},{11,15},{13,5},{15... | collective-permute-start | bytes 2359304 | tf_op jit(solution)/shard_map/ppermute | solution.py:255
  40.4 6.1 %collective-permute-done.6 = bf16[128,3072]{1,0:T(8,128)(2,1)S(1)} collective-permute-done((bf16[128,3072]{1,0:T(8,128)(2,1)S(1)}, bf16[128,3072]{1,0:T(8,128)(2,1)S(1)}, u32[]{:S(2)}, u32[]{:S(2)}) %collective-permute-start.6) | collective-permute-done | bytes 786464 | tf_op jit(solution)/shard_map/ppermute | solution.py:255
  46.5 1.5 %collective-permute-start.8 = (bf16[128,3072]{1,0:T(8,128)(2,1)}, bf16[128,3072]{1,0:T(8,128)(2,1)S(1)}, u32[]{:S(2)}, u32[]{:S(2)}) collective-permute-start(bf16[128,3072]{1,0:T(8,128)(2,1)} %param.11), channel_id=1, source_target_pairs={{0,2},{2,0},{4,6},{6,4},{8,10},{10,8},{12,14},{14,12},{1,3},{3,1},... | collective-permute-start | bytes 2359304 | tf_op jit(solution)/shard_map/ppermute | solution.py:255
  48.0 1.3 %collective-permute-start.9 = (bf16[128,3072]{1,0:T(8,128)(2,1)}, bf16[128,3072]{1,0:T(8,128)(2,1)S(1)}, u32[]{:S(2)}, u32[]{:S(2)}) collective-permute-start(bf16[128,3072]{1,0:T(8,128)(2,1)} %param.11), channel_id=1, source_target_pairs={{0,8},{2,10},{1,9},{3,11},{16,24},{18,26},{17,25},{19,27}} | collective-permute-start | bytes 2359304 | tf_op jit(solution)/shard_map/ppermute | solution.py:255
  49.4 0.0 collective-permute-done.4
  49.4 1.9 %collective-permute-start.11 = (bf16[128,3072]{1,0:T(8,128)(2,1)}, bf16[128,3072]{1,0:T(8,128)(2,1)S(1)}, u32[]{:S(2)}, u32[]{:S(2)}) collective-permute-start(bf16[128,3072]{1,0:T(8,128)(2,1)} %param.11), channel_id=1, source_target_pairs={{8,0},{10,2},{12,8},{14,10},{4,12},{6,14},{0,4},{2,6},{9,1},{11,3}... | collective-permute-start | bytes 2359304 | tf_op jit(solution)/shard_map/ppermute | solution.py:255
  51.3 0.0 copy-done.4
  51.3 11.8 %conditional.3 = (bf16[1568,128]{1,0:T(8,128)(2,1)S(1)}, bf16[1568,128]{1,0:T(8,128)(2,1)S(1)}, bf16[1568,128]{1,0:T(8,128)(2,1)}, bf16[128,3072]{1,0:T(8,128)(2...) conditional(s32[]{:T(128)} %bitcast.1, () %tuple.28, ...), branch_computations={%region_2.0_spmd, %region_3.0_spmd} | conditional | bytes 6357124 | solution.py:266
  51.3 0.0 copy-start.11
  51.3 1.5 %add_packed.5 = bf16[1568,128]{1,0:T(8,128)(2,1)S(1)} custom-call(s32[1]{0:T(128)} %constant.19.clone.where, f32[1552,128]{1,0:T(8,128)} %get-tuple-element.43.keep_ref, bf16[1568,128]{1,0:T(8,128)(2,1)} %get-tuple-element.44.refs_0_, bf16[1568,128]{1,0:T(8,128)(2,1)S(1)} %get-tuple-element.112.refs_1_, bf16[1568,128]{1,0:T(8,128)(2,1)S(1)} %get-tuple-element.113.refs_2_), custom_call_target="tpu_custom_call" | custom-call | tf_op jit(solution)/shard_map/cond/branch_1_fun/add_packed/pallas_call | solution.py:286
  52.8 1.4 %collective-permute-start.1 = (bf16[1568,128]{1,0:T(8,128)(2,1)S(1)}, bf16[1568,128]{1,0:T(8,128)(2,1)}, u32[]{:S(2)}, u32[]{:S(2)}) collective-permute-start(bf16[1568,128]{1,0:T(8,128)(2,1)S(1)} %add_packed.5), channel_id=1, source_target_pairs={{8,12},{10,14},{9,13},{11,15},{24,28},{26,30},{25,29},{27,31}} | collective-permute-start | bytes 1204232 | tf_op jit(solution)/shard_map/cond/branch_1_fun/ppermute | solution.py:255
  54.3 8.8 %scores.1 = (bf16[128,3072]{1,0:T(8,128)(2,1)}, bf16[128,3072]{1,0:T(8,128)(2,1)}, bf16[128,3072]{1,0:T(8,128)(2,1)}, f32[128,768]{1,0:T(8,128)}, f32[128,3072]{1,0:T(8,128)S(1)}) custom-call(s32[1]{0:T(128)} %get-tuple-element.45.where, s32[8]{0:T(128)S(1)} %get-tuple-element.46.lengths, bf16[128,3072]{1,0:T(8,128)(2,1)S(1)} %get-tuple-element.47.q_ref, ...), custom_call_target="tpu_custom_call" | custom-call | tf_op jit(solution)/shard_map/cond/branch_1_fun/scores/pallas_call | solution.py:304
  63.1 0.0 collective-permute-done.1
  63.1 0.0 copy-start.5
  63.1 1.5 %add_packed.7 = bf16[1568,128]{1,0:T(8,128)(2,1)S(1)} custom-call(s32[1]{0:T(128)S(6)} %sub.3.where, f32[1552,128]{1,0:T(8,128)} %get-tuple-element.78.keep_ref, bf16[1568,128]{1,0:T(8,128)(2,1)S(1)} %get-tuple-element.85.refs_0_, bf16[1568,128]{1,0:T(8,128)(2,1)S(1)} %get-tuple-element.86.refs_1_, bf16[1568,128]{1,0:T(8,128)(2,1)} %get-tuple-element.87.refs_2_), custom_call_target="tpu_custom_call" | custom-call | tf_op jit(solution)/shard_map/add_packed/pallas_call | solution.py:286
  64.7 0.6 collective-permute-start.10
  65.3 0.0 collective-permute-done.7.refs_3_
  65.3 2.2 %linear_own.1.own_ref = f32[128,1536]{1,0:T(8,128)S(1)} custom-call(s32[1]{0:T(128)} %bitcast.where, f32[24]{0:T(128)S(1)} %copy-done, bf16[128,3072]{1,0:T(8,128)(2,1)S(1)} %copy-done.5, bf16[1568,128]{1,0:T(8,128)(2,1)S(1)} %get-tuple-element.85.refs_0_, bf16[1568,128]{1,0:T(8,128)(2,1)S(1)} %get-tuple-element.86.refs_1_, ...), custom_call_target="tpu_custom_call" | custom-call | tf_op jit(solution)/shard_map/linear_own/pallas_call | solution.py:343
  67.4 0.0 collective-permute-done.8.refs_2_
  67.4 0.2 collective-permute-done.9.refs_4_
  67.7 2.3 %parts.1 = (f32[128,3072]{1,0:T(8,128)S(1)}, bf16[128,3072]{1,0:T(8,128)(2,1)S(1)}) custom-call(f32[128,768]{1,0:T(8,128)S(1)} %copy-done.6, f32[128,3072]{1,0:T(8,128)S(1)} %get-tuple-element.90.base_ref, bf16[128,3072]{1,0:T(8,128)(2,1)S(1)} %copy-done.7, bf16[128,3072]{1,0:T(8,128)(2,1)S(1)} %copy-done.8, ...), custom_call_target="tpu_custom_call" | custom-call | tf_op jit(solution)/shard_map/parts/pallas_call | solution.py:353
  69.9 4.4 %collective-permute-done.10.refs_0_ = bf16[1568,128]{1,0:T(8,128)(2,1)S(1)} collective-permute-done((bf16[1568,128]{1,0:T(8,128)(2,1)S(1)}, bf16[1568,128]{1,0:T(8,128)(2,1)S(1)}, u32[]{:S(2)}, u32[]{:S(2)}) %collective-permute-start.10) | collective-permute-done | bytes 401440 | tf_op jit(solution)/shard_map/ppermute | solution.py:255
  74.4 1.0 %linear_other.1.other_ref = f32[128,1536]{1,0:T(8,128)S(1)} custom-call(s32[1]{0:T(128)} %bitcast.where, f32[24]{0:T(128)S(1)} %copy-done, bf16[128,3072]{1,0:T(8,128)(2,1)S(1)} %copy-done.5, bf16[1568,128]{1,0:T(8,128)(2,1)S(1)} %collective-permute-done.10.refs_0_), custom_call_target="tpu_custom_call" | custom-call | tf_op jit(solution)/shard_map/linear_other/pallas_call | solution.py:343
  75.4 7.1 %collective-permute-done.11.refs_1_ = bf16[128,3072]{1,0:T(8,128)(2,1)S(1)} collective-permute-done((bf16[128,3072]{1,0:T(8,128)(2,1)}, bf16[128,3072]{1,0:T(8,128)(2,1)S(1)}, u32[]{:S(2)}, u32[]{:S(2)}) %collective-permute-start.11) | collective-permute-done | bytes 786464 | tf_op jit(solution)/shard_map/ppermute | solution.py:255
  82.4 1.9 %finish.1 = bf16[128,3072]{1,0:T(8,128)(2,1)} custom-call(s32[1]{0:T(128)} %bitcast.where, f32[128,768]{1,0:T(8,128)S(1)} %copy-done.6, f32[128,3072]{1,0:T(8,128)S(1)} %get-tuple-element.95.base_ref, f32[128,1536]{1,0:T(8,128)S(1)} %linear_own.1.own_ref, f32[128,1536]{1,0:T(8,128)S(1)} %linear_other.1.other_ref, ...), custom_call_target="tpu_custom_call" | custom-call | tf_op jit(solution)/shard_map/finish/pallas_call | solution.py:364
  (19 shorter events, 0.1 us)
Async XLA Ops:
  0.0 22.3 %collective-permute-start.3 = (bf16[128,3072]{1,0:T(8,128)(2,1)}, bf16[128,3072]{1,0:T(8,128)(2,1)S(1)}, u32[]{:S(2)}, u32[]{:S(2)}) collective-permute-start(bf16[128,3072]{1,0:T(8,128)(2,1)} %param.10), channel_id=1, source_target_pairs={{0,8},{2,10},{8,12},{10,14},{12,4},{14,6},{4,0},{6,2},{1,9},{3,11}... | collective-permute-start | bytes 2359304 | tf_op jit(solution)/shard_map/ppermute | solution.py:255
  4.7 17.6 %copy-start.1 = (bf16[128,3072]{1,0:T(8,128)(2,1)S(1)}, bf16[128,3072]{1,0:T(8,128)(2,1)}, u32[]{:S(2)}) copy-start(bf16[128,3072]{1,0:T(8,128)(2,1)} %param.10) | copy-start | bytes 2359300
  4.7 3.8 %copy-start.3 = (bf16[128,3072]{1,0:T(8,128)(2,1)S(1)}, bf16[128,3072]{1,0:T(8,128)(2,1)}, u32[]{:S(2)}) copy-start(bf16[128,3072]{1,0:T(8,128)(2,1)} %get-tuple-element.39.k_ref) | copy-start | bytes 2359300 | tf_op jit(solution)/shard_map/cond
  4.7 3.8 %copy-start.13 = (s32[8]{0:T(128)S(1)}, s32[8]{0:T(128)}, u32[]{:S(2)}) copy-start(s32[8]{0:T(128)} %get-tuple-element.38.lengths) | copy-start | bytes 100 | tf_op jit(solution)/shard_map/cond
  7.0 10.9 %collective-permute-start = (bf16[1568,128]{1,0:T(8,128)(2,1)S(1)}, bf16[1568,128]{1,0:T(8,128)(2,1)}, u32[]{:S(2)}, u32[]{:S(2)}) collective-permute-start(bf16[1568,128]{1,0:T(8,128)(2,1)S(1)} %sums_sent.1), channel_id=1, source_target_pairs={{0,2},{2,0},{4,6},{6,4},{8,10},{10,8},{12,14},{14,12},{1,3},{3,1},... | collective-permute-start | bytes 1204232 | tf_op jit(solution)/shard_map/cond/branch_1_fun/ppermute | solution.py:255
  19.2 32.1 %copy-start.2 = (bf16[128,3072]{1,0:T(8,128)(2,1)S(1)}, bf16[128,3072]{1,0:T(8,128)(2,1)}, u32[]{:S(2)}) copy-start(bf16[128,3072]{1,0:T(8,128)(2,1)} %param.10) | copy-start | bytes 2359300
  19.2 32.1 %copy-start.4 = (bf16[128,3072]{1,0:T(8,128)(2,1)S(1)}, bf16[128,3072]{1,0:T(8,128)(2,1)}, u32[]{:S(2)}) copy-start(bf16[128,3072]{1,0:T(8,128)(2,1)} %q_ref.3) | copy-start | bytes 2359300
  19.2 32.0 %copy-start.12 = (s32[8]{0:T(128)S(1)}, s32[8]{0:T(128)}, u32[]{:S(2)}) copy-start(s32[8]{0:T(128)} %param.12) | copy-start | bytes 100
  19.2 11.5 %collective-permute-start.2 = (bf16[1568,128]{1,0:T(8,128)(2,1)S(1)}, bf16[1568,128]{1,0:T(8,128)(2,1)S(1)}, u32[]{:S(2)}, u32[]{:S(2)}) collective-permute-start(bf16[1568,128]{1,0:T(8,128)(2,1)S(1)} %get-tuple-element.80), channel_id=1, source_target_pairs={{0,4},{2,6},{1,5},{3,7},{16,20},{18,22},{17,21},{19,23}} | collective-permute-start | bytes 1204232 | tf_op jit(solution)/shard_map/ppermute | solution.py:255
  20.7 18.4 %collective-permute-start.5 = (bf16[128,3072]{1,0:T(8,128)(2,1)}, bf16[128,3072]{1,0:T(8,128)(2,1)S(1)}, u32[]{:S(2)}, u32[]{:S(2)}) collective-permute-start(bf16[128,3072]{1,0:T(8,128)(2,1)} %param.10), channel_id=1, source_target_pairs={{0,2},{2,0},{4,6},{6,4},{8,10},{10,8},{12,14},{14,12},{1,3},{3,1},... | collective-permute-start | bytes 2359304 | tf_op jit(solution)/shard_map/ppermute | solution.py:255
  22.3 24.2 %collective-permute-start.6 = (bf16[128,3072]{1,0:T(8,128)(2,1)S(1)}, bf16[128,3072]{1,0:T(8,128)(2,1)S(1)}, u32[]{:S(2)}, u32[]{:S(2)}) collective-permute-start(bf16[128,3072]{1,0:T(8,128)(2,1)S(1)} %copy-done.1), channel_id=1, source_target_pairs={{8,0},{10,2},{12,8},{14,10},{4,12},{6,14},{0,4},{2,6},{9,1},{11,3}... | collective-permute-start | bytes 2359304 | tf_op jit(solution)/shard_map/ppermute | solution.py:255
  22.3 10.5 %copy-start.10 = (bf16[128,3072]{1,0:T(8,128)(2,1)}, bf16[128,3072]{1,0:T(8,128)(2,1)S(1)}, u32[]{:S(2)}) copy-start(bf16[128,3072]{1,0:T(8,128)(2,1)S(1)} %collective-permute-done.3) | copy-start | bytes 2359300
  32.2 17.2 %collective-permute-start.4 = (bf16[1568,128]{1,0:T(8,128)(2,1)S(1)}, bf16[1568,128]{1,0:T(8,128)(2,1)S(1)}, u32[]{:S(2)}, u32[]{:S(2)}) collective-permute-start(bf16[1568,128]{1,0:T(8,128)(2,1)S(1)} %add_packed.6), channel_id=1, source_target_pairs={{4,8},{6,10},{5,9},{7,11},{20,24},{22,26},{21,25},{23,27}} | collective-permute-start | bytes 1204232 | tf_op jit(solution)/shard_map/ppermute | solution.py:255
  39.1 26.2 %collective-permute-start.7 = (bf16[128,3072]{1,0:T(8,128)(2,1)}, bf16[128,3072]{1,0:T(8,128)(2,1)S(1)}, u32[]{:S(2)}, u32[]{:S(2)}) collective-permute-start(bf16[128,3072]{1,0:T(8,128)(2,1)} %param.11), channel_id=1, source_target_pairs={{8,12},{10,14},{12,4},{14,6},{4,0},{6,2},{9,13},{11,15},{13,5},{15... | collective-permute-start | bytes 2359304 | tf_op jit(solution)/shard_map/ppermute | solution.py:255
  46.5 20.9 %collective-permute-start.8 = (bf16[128,3072]{1,0:T(8,128)(2,1)}, bf16[128,3072]{1,0:T(8,128)(2,1)S(1)}, u32[]{:S(2)}, u32[]{:S(2)}) collective-permute-start(bf16[128,3072]{1,0:T(8,128)(2,1)} %param.11), channel_id=1, source_target_pairs={{0,2},{2,0},{4,6},{6,4},{8,10},{10,8},{12,14},{14,12},{1,3},{3,1},... | collective-permute-start | bytes 2359304 | tf_op jit(solution)/shard_map/ppermute | solution.py:255
  48.0 19.6 %collective-permute-start.9 = (bf16[128,3072]{1,0:T(8,128)(2,1)}, bf16[128,3072]{1,0:T(8,128)(2,1)S(1)}, u32[]{:S(2)}, u32[]{:S(2)}) collective-permute-start(bf16[128,3072]{1,0:T(8,128)(2,1)} %param.11), channel_id=1, source_target_pairs={{0,8},{2,10},{1,9},{3,11},{16,24},{18,26},{17,25},{19,27}} | collective-permute-start | bytes 2359304 | tf_op jit(solution)/shard_map/ppermute | solution.py:255
  49.4 33.1 %collective-permute-start.11 = (bf16[128,3072]{1,0:T(8,128)(2,1)}, bf16[128,3072]{1,0:T(8,128)(2,1)S(1)}, u32[]{:S(2)}, u32[]{:S(2)}) collective-permute-start(bf16[128,3072]{1,0:T(8,128)(2,1)} %param.11), channel_id=1, source_target_pairs={{8,0},{10,2},{12,8},{14,10},{4,12},{6,14},{0,4},{2,6},{9,1},{11,3}... | collective-permute-start | bytes 2359304 | tf_op jit(solution)/shard_map/ppermute | solution.py:255
  51.3 3.0 %copy-start.11 = (bf16[128,3072]{1,0:T(8,128)(2,1)S(1)}, bf16[128,3072]{1,0:T(8,128)(2,1)}, u32[]{:S(2)}) copy-start(bf16[128,3072]{1,0:T(8,128)(2,1)} %get-tuple-element.50.refs_2_) | copy-start | bytes 2359300 | tf_op jit(solution)/shard_map/cond
  52.8 10.3 %collective-permute-start.1 = (bf16[1568,128]{1,0:T(8,128)(2,1)S(1)}, bf16[1568,128]{1,0:T(8,128)(2,1)}, u32[]{:S(2)}, u32[]{:S(2)}) collective-permute-start(bf16[1568,128]{1,0:T(8,128)(2,1)S(1)} %add_packed.5), channel_id=1, source_target_pairs={{8,12},{10,14},{9,13},{11,15},{24,28},{26,30},{25,29},{27,31}} | collective-permute-start | bytes 1204232 | tf_op jit(solution)/shard_map/cond/branch_1_fun/ppermute | solution.py:255
  63.1 2.2 %copy-start = (f32[24]{0:T(128)S(1)}, f32[24]{0:T(128)}, u32[]{:S(2)}) copy-start(f32[24]{0:T(128)} %scale.3) | copy-start | bytes 292
  63.1 2.2 %copy-start.5 = (bf16[128,3072]{1,0:T(8,128)(2,1)S(1)}, bf16[128,3072]{1,0:T(8,128)(2,1)}, u32[]{:S(2)}) copy-start(bf16[128,3072]{1,0:T(8,128)(2,1)} %q_ref.3) | copy-start | bytes 2359300
  64.7 3.0 %copy-start.6 = (f32[128,768]{1,0:T(8,128)S(1)}, f32[128,768]{1,0:T(8,128)}, u32[]{:S(2)}) copy-start(f32[128,768]{1,0:T(8,128)} %get-tuple-element.83.factor_ref) | copy-start | bytes 1179652
  64.7 3.0 %copy-start.7 = (bf16[128,3072]{1,0:T(8,128)(2,1)S(1)}, bf16[128,3072]{1,0:T(8,128)(2,1)}, u32[]{:S(2)}) copy-start(bf16[128,3072]{1,0:T(8,128)(2,1)} %get-tuple-element.91.refs_0_) | copy-start | bytes 2359300
  64.7 3.0 %copy-start.8 = (bf16[128,3072]{1,0:T(8,128)(2,1)S(1)}, bf16[128,3072]{1,0:T(8,128)(2,1)}, u32[]{:S(2)}) copy-start(bf16[128,3072]{1,0:T(8,128)(2,1)} %get-tuple-element.92.refs_1_) | copy-start | bytes 2359300
  64.7 3.0 %copy-start.9 = (bf16[128,3072]{1,0:T(8,128)(2,1)S(1)}, bf16[128,3072]{1,0:T(8,128)(2,1)}, u32[]{:S(2)}) copy-start(bf16[128,3072]{1,0:T(8,128)(2,1)} %get-tuple-element.94.refs_5_) | copy-start | bytes 2359300
  64.7 9.7 %collective-permute-start.10 = (bf16[1568,128]{1,0:T(8,128)(2,1)S(1)}, bf16[1568,128]{1,0:T(8,128)(2,1)S(1)}, u32[]{:S(2)}, u32[]{:S(2)}) collective-permute-start(bf16[1568,128]{1,0:T(8,128)(2,1)S(1)} %add_packed.7), channel_id=1, source_target_pairs={{0,2},{2,0},{4,6},{6,4},{8,10},{10,8},{12,14},{14,12},{1,3},{3,1},... | collective-permute-start | bytes 1204232 | tf_op jit(solution)/shard_map/ppermute | solution.py:255
